TPU v7x, 32 devices: a whole 2x2x4 slice. The times are simulated.
32 devices in a mesh: comp: 2 (over x), sect: 4 (over y, core), slab: 4 (over z).
Axes of the slice: x: 2, y: 2, z: 4, core: 2. Of those that a mesh axis runs over, the one named last changes fastest.
Arguments:
- spectrum: float32 [1296, 256, 512], P('comp', 'slab', 'sect'), may hold values from 0 to 1
- land_mask: int32 [256, 512], P('slab', 'sect'), may hold values 0 or 1
- ice_mask: int32 [256, 512], P('slab', 'sect'), may hold values 0 or 1
- wind_u: float32 [256, 512], P('slab', 'sect'), may hold values from -6 to 6
- wind_v: float32 [256, 512], P('slab', 'sect'), may hold values from -6 to 6
- depth: float32 [256, 512], P('slab', 'sect'), may hold values from 2 to 20
Outputs:
- damped: float32 [1296, 256, 512], P('comp', 'slab', 'sect')
- level: float32 [256, 512], P('slab', 'sect')
All inputs are finite; a program needn't handle non-finite values. No bound on the sum of `land_mask` or of `ice_mask` on one device may be relied on, other than what follows from the above.
Results may differ from a plain program's by a relative error of at most 0.00011.
Values sent between devices are 32-bit elements; how exact they have to be, the bound alone decides.
No kernel may reach another device: no remote copies, remote signals or barrier semaphores. Data moves between devices by JAX's collectives and lax.ppermute only.
A program may use at most 192 MiB of HBM per device.

v0:
```python
import math

import jax
import jax.numpy as jnp
from jax import lax
from jax.sharding import PartitionSpec as P

ND = 36
NF = 36
STEPS = 2
JAC = 4


def extended(cells, sides, width):
    for axis, dim in sides:
        count = lax.axis_size(axis)
        ends = count - 1
        head = lax.slice_in_dim(cells, 0, width, axis=dim)
        tail = lax.slice_in_dim(cells, cells.shape[dim] - width, cells.shape[dim], axis=dim)
        cells = jnp.concatenate(
            [
                lax.ppermute(tail, axis, [(i, (i + 1) % count) for i in range(ends)]),
                cells,
                lax.ppermute(head, axis, [((i + 1) % count, i) for i in range(ends)]),
            ],
            axis=dim,
        )
    return cells


def tables(index):
    freq_index = (index // ND).astype(jnp.float32)
    angle_index = (index % ND).astype(jnp.float32)
    heading = 2.0 * math.pi * angle_index / ND
    return (
        jnp.cos(heading),
        jnp.sin(heading),
        jnp.power(1.1, -freq_index),
        jnp.power(1.1, freq_index - (NF - 1)),
        0.5 + 0.5 * freq_index / (NF - 1),
    )


def column(values):
    return values[:, None, None]


def advect(spectra, wet_cells, speed_x, speed_y):
    padded = extended(spectra, (("slab", 1), ("sect", 2)), 1)
    upper_rows = padded[:, :-2, 1:-1]
    lower_rows = padded[:, 2:, 1:-1]
    left_cells = padded[:, 1:-1, :-2]
    right_cells = padded[:, 1:-1, 2:]
    change = (
        jnp.maximum(speed_x, 0.0) * (spectra - upper_rows)
        + jnp.minimum(speed_x, 0.0) * (lower_rows - spectra)
        + jnp.maximum(speed_y, 0.0) * (spectra - left_cells)
        + jnp.minimum(speed_y, 0.0) * (right_cells - spectra)
    )
    return (spectra - change) * wet_cells


def forcing(spectra, energy, wind_east, wind_north, ice_cover, cosine, sine, high_ratio):
    project = cosine * wind_east + sine * wind_north
    growth = 0.5 * high_ratio * jnp.square(jnp.maximum(project, 0.0)) * (1.0 - ice_cover)
    return spectra * (1.0 + growth) / (1.0 + 2.0 * high_ratio * jnp.square(energy))


def stress_weights(cosine, sine, shoaling):
    return jnp.stack(
        [shoaling * (cosine * cosine + 1.0) - 0.5, shoaling * (sine * sine + 1.0) - 0.5]
    )


def surge_solve(stress):
    padded = extended(stress, (("slab", 1), ("sect", 2)), 1)
    source_term = -(
        padded[0, 2:, 1:-1]
        + padded[0, :-2, 1:-1]
        - 2.0 * stress[0]
        + (padded[1, 1:-1, 2:] + padded[1, 1:-1, :-2] - 2.0 * stress[1])
    )
    surge_level = source_term / 4.5
    for _ in range(JAC):
        neighbours = extended(surge_level, (("slab", 0), ("sect", 1)), 1)
        surge_level = (
            source_term
            + neighbours[2:, 1:-1]
            + neighbours[:-2, 1:-1]
            + neighbours[1:-1, 2:]
            + neighbours[1:-1, :-2]
        ) / 4.5
    return surge_level


def local(spectrum, land_mask, ice_mask, wind_u, wind_v, depth):
    groups = lax.axis_size("comp")
    member = lax.axis_index("comp")
    local_comp, block_rows, block_cols = spectrum.shape
    point_rows = block_rows // groups
    total_comp = ND * NF
    wet_cells = (1 - land_mask).astype(jnp.float32)
    ice_cover = ice_mask.astype(jnp.float32)

    def own_rows(values):
        return lax.dynamic_slice_in_dim(values, member * point_rows, point_rows, values.ndim - 2)

    own_index = member * local_comp + jnp.arange(local_comp, dtype=jnp.int32)
    cosine, sine, low_ratio, high_ratio, shoaling = tables(own_index)
    spectra = spectrum * wet_cells
    for _ in range(STEPS):
        spectra = advect(
            spectra, wet_cells, column(0.7 * low_ratio * cosine), column(0.7 * low_ratio * sine)
        )
    points = lax.all_to_all(spectra, "comp", split_axis=1, concat_axis=0, tiled=True)
    cosine_full, sine_full, _, high_full, shoal_full = tables(
        jnp.arange(total_comp, dtype=jnp.int32)
    )
    energy = jnp.sum(points, axis=0) / total_comp
    sourced = forcing(
        points,
        energy,
        own_rows(wind_u),
        own_rows(wind_v),
        own_rows(ice_cover),
        column(cosine_full),
        column(sine_full),
        column(high_full),
    )
    stress = (
        jnp.einsum(
            "sk,krc->src",
            stress_weights(cosine_full, sine_full, shoal_full),
            sourced,
            precision=lax.Precision.HIGHEST,
        )
        / total_comp
    )
    stress_block = lax.all_gather(stress, "comp", axis=1, tiled=True)
    level_block = surge_solve(stress_block)
    final_energy = jnp.sum(sourced, axis=0) / total_comp
    damped = sourced / (
        1.0 + 4.0 * final_energy / (jnp.square(own_rows(depth) + own_rows(level_block)) + 1.0)
    )
    result = lax.all_to_all(damped, "comp", split_axis=0, concat_axis=1, tiled=True)
    return (result, level_block)


def solution(mesh):
    in_specs = (
        P("comp", "slab", "sect"),
        P("slab", "sect"),
        P("slab", "sect"),
        P("slab", "sect"),
        P("slab", "sect"),
        P("slab", "sect"),
    )
    out_specs = (P("comp", "slab", "sect"), P("slab", "sect"))
    return jax.shard_map(local, mesh=mesh, in_specs=in_specs, out_specs=out_specs, check_vma=False)
```

profile of v0, /device:TPU:12, one launch (start us, length us, event | category | flops | bytes accessed | tf_op | source)
XLA Modules:
  0.0 1009.6 jit_solution(2733810476816461516)
XLA Ops:
  1.4 19.6 %copy_multiply_fusion = f32[648,64,128]{2,0,1:T(8,128)S(1)} fusion(f32[648,64,128]{2,1,0:T(8,128)} %param.6, f32[64,128]{1,0:T(8,128)S(1)} %subtract_convert_fusion), kind=kLoop, calls=%fused_computation.47 | loop fusion | flops 5308416 | bytes 42500096 | tf_op jit(solution)/shard_map/mul | solution.py:110
  21.0 7.6 copy-done.1
  28.7 3.5 collective-permute-start
  34.6 5.5 collective-permute-done
  40.1 3.2 collective-permute-done.1
  43.3 8.7 pad_maximum_fusion
  52.1 15.1 %fusion.100 = (f32[648,66,1]{2,0,1:T(8,128)}, f32[648,66,1]{2,0,1:T(8,128)}) fusion(f32[648,66,128]{2,0,1:T(8,128)S(1)} %pad_maximum_fusion), kind=kLoop, calls=%fused_computation.203 | loop fusion | bytes 684288 | tf_op jit(solution)/shard_map/slice | solution.py:19
  67.2 13.0 %copy.11 = f32[648,66,1]{0,1,2:T(8,128)S(1)} copy(f32[648,66,1]{2,0,1:T(8,128)} %get-tuple-element.4) | data formatting | bytes 342144 | tf_op jit(solution)/shard_map/slice | solution.py:19
  82.1 13.0 %copy.13 = f32[648,66,1]{0,1,2:T(8,128)S(1)} copy(f32[648,66,1]{2,0,1:T(8,128)} %get-tuple-element.5) | data formatting | bytes 342144 | tf_op jit(solution)/shard_map/slice | solution.py:18
  95.1 3.8 collective-permute-start.3
  99.1 11.0 %copy.12 = f32[648,66,1]{2,0,1:T(8,128)} copy(f32[648,66,1]{0,1,2:T(8,128)S(1)} %collective-permute-done.2) | data formatting | bytes 342144 | tf_op jit(solution)/shard_map/ppermute | solution.py:22
  110.1 11.0 %copy.14 = f32[648,66,1]{2,0,1:T(8,128)} copy(f32[648,66,1]{0,1,2:T(8,128)S(1)} %collective-permute-done.3) | data formatting | bytes 342144 | tf_op jit(solution)/shard_map/ppermute | solution.py:24
  121.1 57.0 %fusion.17 = f32[648,64,128]{2,0,1:T(8,128)} fusion(f32[648,64,128]{2,0,1:T(8,128)} %copy-done.1, f32[648,66,1]{2,0,1:T(8,128)} %copy.14, f32[648,1,128]{2,0,1:T(8,128)S(1)} %collective-permute-done.1, f32[648,1,128]{2,0,1:T(8,128)S(1)} %collective-permute-done, f32[648,66,1]{2,0,1:T(8,128)} %copy.12, f32[648]{0:T(1024)S(1)} %get-tuple-element.30, ...), kind=kLoop, calls=%fused_computation.28 | loop fusion | flops 111476736 | bytes 43516160 | tf_op jit(solution)/shard_map/mul | solution.py:60
  179.2 3.5 collective-permute-start.4
  185.1 4.5 collective-permute-done.4
  189.6 3.2 collective-permute-done.5
  192.8 8.7 pad_maximum_fusion.1
  201.5 15.0 %fusion.99 = (f32[648,66,1]{2,0,1:T(8,128)}, f32[648,66,1]{2,0,1:T(8,128)}) fusion(f32[648,66,128]{2,0,1:T(8,128)S(1)} %pad_maximum_fusion.1), kind=kLoop, calls=%fused_computation.202 | loop fusion | bytes 684288 | tf_op jit(solution)/shard_map/slice | solution.py:19
  216.5 13.0 %copy.15 = f32[648,66,1]{0,1,2:T(8,128)S(1)} copy(f32[648,66,1]{2,0,1:T(8,128)} %get-tuple-element.2) | data formatting | bytes 342144 | tf_op jit(solution)/shard_map/slice | solution.py:19
  231.4 13.0 %copy.17 = f32[648,66,1]{0,1,2:T(8,128)S(1)} copy(f32[648,66,1]{2,0,1:T(8,128)} %get-tuple-element.3) | data formatting | bytes 342144 | tf_op jit(solution)/shard_map/slice | solution.py:18
  244.5 3.9 collective-permute-start.7
  248.3 11.0 %copy.16 = f32[648,66,1]{2,0,1:T(8,128)} copy(f32[648,66,1]{0,1,2:T(8,128)S(1)} %collective-permute-done.6) | data formatting | bytes 342144 | tf_op jit(solution)/shard_map/ppermute | solution.py:22
  259.3 11.0 %copy.18 = f32[648,66,1]{2,0,1:T(8,128)} copy(f32[648,66,1]{0,1,2:T(8,128)S(1)} %collective-permute-done.7) | data formatting | bytes 342144 | tf_op jit(solution)/shard_map/ppermute | solution.py:24
  270.4 57.3 %fusion.4 = f32[648,64,128]{2,0,1:T(8,128)} fusion(f32[648,64,128]{2,0,1:T(8,128)} %fusion.17, f32[648,66,1]{2,0,1:T(8,128)} %copy.18, f32[648,1,128]{2,0,1:T(8,128)S(1)} %collective-permute-done.5, f32[648,1,128]{2,0,1:T(8,128)S(1)} %collective-permute-done.4, f32[648,66,1]{2,0,1:T(8,128)} %copy.16, f32[648]{0:T(1024)S(1)} %get-tuple-element.30, ...), kind=kLoop, calls=%fused_computation.7 | loop fusion | flops 111476736 | bytes 43516160 | tf_op jit(solution)/shard_map/mul | solution.py:60
  327.7 11.5 %all-to-all-start = ((f32[648,64,128]{2,0,1:T(8,128)}), f32[648,64,128]{2,0,1:T(8,128)}, u32[]{:S(2)}, u32[]{:S(2)}) async-start(f32[648,64,128]{2,0,1:T(8,128)} %fusion.4), calls=%async_computation | async-start | bytes 42467328 | tf_op jit(solution)/shard_map/all_to_all | solution.py:115
  339.5 228.8 %all-to-all-done = f32[648,64,128]{2,0,1:T(8,128)} async-done(((f32[648,64,128]{2,0,1:T(8,128)}), f32[648,64,128]{2,0,1:T(8,128)}, u32[]{:S(2)}, u32[]{:S(2)}) %all-to-all-start) | async-done | bytes 21233696 | tf_op jit(solution)/shard_map/all_to_all | solution.py:115
  568.3 20.7 %copy.19 = f32[2,648,32,128]{3,2,1,0:T(8,128)} copy(f32[2,648,32,128]{3,1,2,0:T(8,128)} %bitcast.1) | data formatting | bytes 42467328 | tf_op jit(solution)/shard_map/all_to_all | solution.py:115
  589.1 8.1 reduce_sum.18
  597.2 21.1 %fusion.28 = f32[1296,32,128]{2,1,0:T(8,128)} fusion(f32[32,128]{1,0:T(8,128)S(1)} %multiply_multiply_fusion, f32[1296]{0:T(1024)S(1)} %get-tuple-element.38, f32[32,128]{1,0:T(8,128)S(1)} %get-tuple-element.34, f32[32,128]{1,0:T(8,128)S(1)} %get-tuple-element.35, f32[1296]{0:T(1024)S(1)} %get-tuple-element.36, ...), kind=kLoop, calls=%fused_computation.51 | loop fusion | flops 63700992 | bytes 42553600 | tf_op jit(solution)/shard_map/div | solution.py:66
  618.3 33.6 %fusion.30 = f32[2,32,128]{2,0,1:T(2,128)S(1)} fusion(f32[1296,32,128]{2,1,0:T(8,128)} %fusion.28, f32[1,1296]{1,0:T(1,128)S(1)} %get-tuple-element.40, f32[1,1296]{1,0:T(1,128)S(1)} %get-tuple-element.41), kind=kOutput, calls=%fused_computation.53 | convolution fusion | flops 127412768 | bytes 21276800 | tf_op jit(solution)/shard_map/sk,krc->src/dot_general | solution.py:131
  651.9 4.6 all_gather.3
  658.7 3.6 collective-permute-start.8
  666.2 2.4 collective-permute-start.11
  668.6 3.2 collective-permute-done.11
  672.1 3.6 collective-permute-start.12
  678.0 3.2 collective-permute-done.13
  685.6 2.9 collective-permute-done.15
  690.5 3.9 collective-permute-start.17
  698.0 2.4 collective-permute-start.19
  700.4 2.9 collective-permute-done.19
  705.3 3.9 collective-permute-start.21
  712.7 2.6 collective-permute-start.23
  715.4 2.6 collective-permute-done.23
  720.1 3.9 collective-permute-start.25
  729.9 13.5 %fusion.29 = f32[32,128]{1,0:T(8,128)S(1)} fusion(f32[2,648,32,128]{3,1,2,0:T(8,128)} %bitcast.1, f32[32,128]{1,0:T(8,128)S(1)} %multiply_multiply_fusion, f32[2,648]{1,0:T(2,128)S(1)} %get-tuple-element.42, f32[32,128]{1,0:T(8,128)S(1)} %get-tuple-element.34, f32[32,128]{1,0:T(8,128)S(1)} %get-tuple-element.35, f32[2,648]{1,0:T(2,128)S(1)} %get-tuple-element.44, ...), kind=kLoop, calls=%fused_computation.52 | loop fusion | flops 69005312 | bytes 21336320 | tf_op jit(solution)/shard_map/reduce_sum | solution.py:141
  743.7 20.7 %multiply_divide_fusion = f32[1296,32,128]{2,1,0:T(8,128)} fusion(f32[32,128]{1,0:T(8,128)S(1)} %divide_add_fusion, f32[32,128]{1,0:T(8,128)S(1)} %multiply_multiply_fusion, f32[1296]{0:T(1024)S(1)} %get-tuple-element.38, f32[32,128]{1,0:T(8,128)S(1)} %get-tuple-element.34, f32[32,128]{1,0:T(8,128)S(1)} %get-tuple-element.35, ...), kind=kLoop, calls=%fused_computation.48 | loop fusion | flops 69009408 | bytes 42569984 | tf_op jit(solution)/shard_map/div | solution.py:142
  764.3 236.2 %all_to_all.36 = f32[1296,32,128]{2,1,0:T(8,128)S(1)} all-to-all(f32[1296,32,128]{2,1,0:T(8,128)} %multiply_divide_fusion), channel_id=1, replica_groups=mesh['comp'=2,'sect'=4,'slab'=4] {'comp'}, dimensions={0} | all-to-all | bytes 42467328 | tf_op jit(solution)/shard_map/all_to_all | solution.py:145
  1000.6 8.8 copy.21
  (96 shorter events, 43.1 us)
Async XLA Ops:
  0.6 338.6 %copy-start = (f32[64,128]{1,0:T(8,128)S(1)}, f32[64,128]{1,0:T(8,128)}, u32[]{:S(2)}) copy-start(f32[64,128]{1,0:T(8,128)} %param.9) | copy-start | bytes 98308
  21.0 7.6 copy-start.1
  28.7 11.4 %collective-permute-start = (f32[648,1,128]{2,0,1:T(8,128)S(1)}, f32[648,1,128]{2,0,1:T(8,128)S(1)}, u32[]{:S(2)}, u32[]{:S(2)}) collective-permute-start(f32[648,1,128]{2,0,1:T(8,128)S(1)} %get-tuple-element.8), channel_id=1, source_target_pairs={{0,1},{1,2},{2,3},{4,5},{5,6},{6,7},{8,9},{9,10},{10,11},{12,13},{... | collective-permute-start | bytes 995336 | tf_op jit(solution)/shard_map/ppermute | solution.py:22
  32.2 11.2 %collective-permute-start.1 = (f32[648,1,128]{2,0,1:T(8,128)S(1)}, f32[648,1,128]{2,0,1:T(8,128)S(1)}, u32[]{:S(2)}, u32[]{:S(2)}) collective-permute-start(f32[648,1,128]{2,0,1:T(8,128)S(1)} %get-tuple-element.9), channel_id=1, source_target_pairs={{1,0},{2,1},{3,2},{5,4},{6,5},{7,6},{9,8},{10,9},{11,10},{13,12},{... | collective-permute-start | bytes 995336 | tf_op jit(solution)/shard_map/ppermute | solution.py:24
  80.2 18.9 %collective-permute-start.2 = (f32[648,66,1]{0,1,2:T(8,128)S(1)}, f32[648,66,1]{0,1,2:T(8,128)S(1)}, u32[]{:S(2)}, u32[]{:S(2)}) collective-permute-start(f32[648,66,1]{0,1,2:T(8,128)S(1)} %copy.11), channel_id=1, source_target_pairs={{0,4},{4,8},{8,12},{1,5},{5,9},{9,13},{2,6},{6,10},{10,14},{3,7},{... | collective-permute-start | bytes 513224 | tf_op jit(solution)/shard_map/ppermute | solution.py:22
  95.1 14.9 %collective-permute-start.3 = (f32[648,66,1]{0,1,2:T(8,128)S(1)}, f32[648,66,1]{0,1,2:T(8,128)S(1)}, u32[]{:S(2)}, u32[]{:S(2)}) collective-permute-start(f32[648,66,1]{0,1,2:T(8,128)S(1)} %copy.13), channel_id=1, source_target_pairs={{4,0},{8,4},{12,8},{5,1},{9,5},{13,9},{6,2},{10,6},{14,10},{7,3},{... | collective-permute-start | bytes 513224 | tf_op jit(solution)/shard_map/ppermute | solution.py:24
  179.2 10.4 %collective-permute-start.4 = (f32[648,1,128]{2,0,1:T(8,128)S(1)}, f32[648,1,128]{2,0,1:T(8,128)S(1)}, u32[]{:S(2)}, u32[]{:S(2)}) collective-permute-start(f32[648,1,128]{2,0,1:T(8,128)S(1)} %get-tuple-element.6), channel_id=1, source_target_pairs={{0,1},{1,2},{2,3},{4,5},{5,6},{6,7},{8,9},{9,10},{10,11},{12,13},{... | collective-permute-start | bytes 995336 | tf_op jit(solution)/shard_map/ppermute | solution.py:22
  182.7 10.1 %collective-permute-start.5 = (f32[648,1,128]{2,0,1:T(8,128)S(1)}, f32[648,1,128]{2,0,1:T(8,128)S(1)}, u32[]{:S(2)}, u32[]{:S(2)}) collective-permute-start(f32[648,1,128]{2,0,1:T(8,128)S(1)} %get-tuple-element.7), channel_id=1, source_target_pairs={{1,0},{2,1},{3,2},{5,4},{6,5},{7,6},{9,8},{10,9},{11,10},{13,12},{... | collective-permute-start | bytes 995336 | tf_op jit(solution)/shard_map/ppermute | solution.py:24
  229.5 18.8 %collective-permute-start.6 = (f32[648,66,1]{0,1,2:T(8,128)S(1)}, f32[648,66,1]{0,1,2:T(8,128)S(1)}, u32[]{:S(2)}, u32[]{:S(2)}) collective-permute-start(f32[648,66,1]{0,1,2:T(8,128)S(1)} %copy.15), channel_id=1, source_target_pairs={{0,4},{4,8},{8,12},{1,5},{5,9},{9,13},{2,6},{6,10},{10,14},{3,7},{... | collective-permute-start | bytes 513224 | tf_op jit(solution)/shard_map/ppermute | solution.py:22
  244.5 14.9 %collective-permute-start.7 = (f32[648,66,1]{0,1,2:T(8,128)S(1)}, f32[648,66,1]{0,1,2:T(8,128)S(1)}, u32[]{:S(2)}, u32[]{:S(2)}) collective-permute-start(f32[648,66,1]{0,1,2:T(8,128)S(1)} %copy.17), channel_id=1, source_target_pairs={{4,0},{8,4},{12,8},{5,1},{9,5},{13,9},{6,2},{10,6},{14,10},{7,3},{... | collective-permute-start | bytes 513224 | tf_op jit(solution)/shard_map/ppermute | solution.py:24
  327.7 11.6 %copy-start.3 = (s32[64,128]{1,0:T(8,128)S(1)}, s32[64,128]{1,0:T(8,128)}, u32[]{:S(2)}) copy-start(s32[64,128]{1,0:T(8,128)} %param.8) | copy-start | bytes 98308
  327.7 11.6 %copy-start.4 = (f32[64,128]{1,0:T(8,128)S(1)}, f32[64,128]{1,0:T(8,128)}, u32[]{:S(2)}) copy-start(f32[64,128]{1,0:T(8,128)} %param.10) | copy-start | bytes 98308
  327.7 240.6 %all-to-all-start = ((f32[648,64,128]{2,0,1:T(8,128)}), f32[648,64,128]{2,0,1:T(8,128)}, u32[]{:S(2)}, u32[]{:S(2)}) async-start(f32[648,64,128]{2,0,1:T(8,128)} %fusion.4), calls=%async_computation | async-start | bytes 42467328 | tf_op jit(solution)/shard_map/all_to_all | solution.py:115
  597.2 146.4 %slice-start = ((s8[21233664]{0:T(1024)(128)(4,1)}), s8[262144]{0:T(1024)(128)(4,1)S(1)}, s32[]{:S(2)}) async-start(s8[21233664]{0:T(1024)(128)(4,1)} %bitcast.17), calls=%async_computation.2 | async-start | bytes 524288
  597.2 146.4 %slice-start.1 = ((s8[21233664]{0:T(1024)(128)(4,1)}), s8[4194304]{0:T(1024)(128)(4,1)S(1)}, s32[]{:S(2)}) async-start(s8[21233664]{0:T(1024)(128)(4,1)} %bitcast.17), calls=%async_computation.3 | async-start | bytes 8388608
  597.2 146.4 %slice-start.2 = ((s8[21233664]{0:T(1024)(128)(4,1)}), s8[4194304]{0:T(1024)(128)(4,1)S(1)}, s32[]{:S(2)}) async-start(s8[21233664]{0:T(1024)(128)(4,1)} %bitcast.17), calls=%async_computation.4 | async-start | bytes 8388608
  618.3 125.2 %copy-start.5 = (f32[64,128]{1,0:T(8,128)S(1)}, f32[64,128]{1,0:T(8,128)}, u32[]{:S(2)}) copy-start(f32[64,128]{1,0:T(8,128)} %param.11) | copy-start | bytes 98308
  618.3 125.3 %slice-start.3 = ((s8[21233664]{0:T(1024)(128)(4,1)}), s8[4194304]{0:T(1024)(128)(4,1)S(1)}, s32[]{:S(2)}) async-start(s8[21233664]{0:T(1024)(128)(4,1)} %bitcast.17), calls=%async_computation.5 | async-start | bytes 8388608
  618.3 125.3 %slice-start.4 = ((s8[21233664]{0:T(1024)(128)(4,1)}), s8[4194304]{0:T(1024)(128)(4,1)S(1)}, s32[]{:S(2)}) async-start(s8[21233664]{0:T(1024)(128)(4,1)} %bitcast.17), calls=%async_computation.6 | async-start | bytes 8388608
  656.5 5.8 collective-permute-start.9
  658.7 5.5 collective-permute-start.8
  664.3 4.3 collective-permute-start.10
  666.2 5.6 collective-permute-start.11
  672.1 5.9 collective-permute-start.12
  675.8 5.4 collective-permute-start.13
  681.3 4.3 collective-permute-start.14
  683.2 5.3 collective-permute-start.15
  688.6 5.9 collective-permute-start.16
  690.5 5.4 collective-permute-start.17
  696.1 4.3 collective-permute-start.18
  698.0 5.3 collective-permute-start.19
  703.4 5.9 collective-permute-start.20
  705.3 5.4 collective-permute-start.21
  710.8 4.5 collective-permute-start.22
  712.7 5.3 collective-permute-start.23
  718.1 6.0 collective-permute-start.24
  720.1 5.4 collective-permute-start.25
  725.6 17.8 %collective-permute-start.26 = (f32[66,1]{1,0:T(8,128)S(1)}, f32[66,1]{1,0:T(8,128)S(1)}, u32[]{:S(2)}, u32[]{:S(2)}) collective-permute-start(f32[66,1]{1,0:T(8,128)S(1)} %get-tuple-element.14), channel_id=1, source_target_pairs={{4,0},{8,4},{12,8},{5,1},{9,5},{13,9},{6,2},{10,6},{14,10},{7,3},{... | collective-permute-start | bytes 800 | tf_op jit(solution)/shard_map/ppermute | solution.py:24
  727.5 15.9 %collective-permute-start.27 = (f32[66,1]{1,0:T(8,128)S(1)}, f32[66,1]{1,0:T(8,128)S(1)}, u32[]{:S(2)}, u32[]{:S(2)}) collective-permute-start(f32[66,1]{1,0:T(8,128)S(1)} %get-tuple-element.15), channel_id=1, source_target_pairs={{0,4},{4,8},{8,12},{1,5},{5,9},{9,13},{2,6},{6,10},{10,14},{3,7},{... | collective-permute-start | bytes 800 | tf_op jit(solution)/shard_map/ppermute | solution.py:22
  729.9 13.7 %slice-start.5 = ((s8[21233664]{0:T(1024)(128)(4,1)}), s8[4194304]{0:T(1024)(128)(4,1)S(1)}, s32[]{:S(2)}) async-start(s8[21233664]{0:T(1024)(128)(4,1)} %bitcast.17), calls=%async_computation.7 | async-start | bytes 8388608
  743.5 20.8 %copy-start.2 = (f32[64,128]{1,0:T(8,128)}, f32[64,128]{1,0:T(8,128)S(1)}, u32[]{:S(2)}) copy-start(f32[64,128]{1,0:T(8,128)S(1)} %fusion.34) | copy-start | bytes 98308
where the time goes:
time: 1020 us; the launch traced here: 1010 us
  waiting for transfers between devices  266 us (26%)
  blocking collectives  241 us (24%)
  other arithmetic  217 us (21%)
  local copies, waits for them, and re-layouts  165 us (16%)
  starting transfers between devices  85.7 us (8%)
  matrix products  33.6 us (3%)
    all_to_all x1, blocking collectives, local(): lax.all_to_all(damped, 'comp', split_axis=0, concat_axis=1, tiled=True)  236 us
    all_to_all x1, waiting for transfers between devices, local(): lax.all_to_all(spectra, 'comp', split_axis=1, concat_axis=0, tiled=True)  229 us
    mul x2, other arithmetic, advect(): return (spectra - change) * wet_cells  114 us
    slice x10, local copies, waits for them, and re-layouts, extended(): lax.slice_in_dim(cells, cells.shape[dim] - width, cells.shape[dim], axis=...  57.2 us
    ppermute x14, starting transfers between devices, extended(): lax.ppermute(tail, axis, [(i, (i + 1) % count) for i in range(ends)])  39.2 us
    ppermute x14, starting transfers between devices, extended(): lax.ppermute(head, axis, [((i + 1) % count, i) for i in range(ends)])  35 us
    dot_general x1, matrix products, local(): jnp.einsum('sk,krc->src', stress_weights(cosine_full, sine_full, shoal_fu...  33.6 us
    ppermute x14, waiting for transfers between devices, extended(): lax.ppermute(tail, axis, [(i, (i + 1) % count) for i in range(ends)])  29.2 us
  transfers between devices with their start and end apart: 29, of which 14 were waited for; matrix products, arithmetic and copies ran while one was open for 6% of the time, Pallas kernels for 0%

commit v1 on v0

--- a/solution.py
+++ b/solution.py
@@ -1,8 +1,12 @@
+import functools
 import math
 
 import jax
 import jax.numpy as jnp
+import numpy as np
 from jax import lax
+from jax.experimental import pallas as pl
+from jax.experimental.pallas import tpu as pltpu
 from jax.sharding import PartitionSpec as P
 
 ND = 36
@@ -93,7 +97,7 @@
     return surge_level
 
 
-def local(spectrum, land_mask, ice_mask, wind_u, wind_v, depth):
+def general(spectrum, land_mask, ice_mask, wind_u, wind_v, depth):
     groups = lax.axis_size("comp")
     member = lax.axis_index("comp")
     local_comp, block_rows, block_cols = spectrum.shape
@@ -146,6 +150,775 @@
     return (result, level_block)
 
 
+LANES = 128
+SUB = 8
+CLASSES = 10
+KINDS = 5
+GROUP = 3
+GROUPS = ND // GROUP
+CORNERS = 8
+
+
+def class_of(direction):
+    folded = direction % 18
+    return folded if folded <= 9 else 18 - folded
+
+
+def heads_down(direction):
+    return direction < 9 or direction >= 27
+
+
+def heads_right(direction):
+    return direction < 18
+
+
+def row_slot(direction):
+    if direction < 9:
+        return direction
+    return direction - 18 if direction >= 27 else direction - 9
+
+
+def numpy_tables(members, freqs):
+    j = np.arange(members * freqs, dtype=np.float64)
+    heading = 2.0 * np.pi * np.arange(ND) / ND
+    cosine, sine = np.cos(heading), np.sin(heading)
+    low = 1.1 ** (-j)
+    high = 1.1 ** (j - (NF - 1))
+    shoal = 0.5 + 0.5 * j / (NF - 1)
+    step_x = 0.7 * low[:, None] * np.abs(cosine)
+    step_y = 0.7 * low[:, None] * np.abs(sine)
+    keep = 1.0 - step_x - step_y
+    alpha, beta, scale = step_x / keep, step_y / keep, keep * keep
+    classes = np.arange(CLASSES)
+    square = np.broadcast_to(cosine * cosine, alpha.shape)
+    scalars = np.stack(
+        [
+            alpha[:, classes],
+            beta[:, classes],
+            scale[:, classes],
+            np.broadcast_to(high[:, None], (j.size, CLASSES)),
+            np.broadcast_to(shoal[:, None], (j.size, CLASSES)),
+        ],
+        axis=-1,
+    ).astype(np.float32)
+
+    kinds = np.stack(
+        [
+            2.0 * beta,
+            beta * beta,
+            alpha * beta,
+            scale,
+            scale * square,
+            np.broadcast_to(high[:, None], alpha.shape),
+            np.broadcast_to(cosine, alpha.shape),
+            np.broadcast_to(sine, alpha.shape),
+        ]
+    )
+    lanes = np.zeros((members, GROUPS, 8, LANES), np.float32)
+    packed = kinds.reshape(8, members, freqs, GROUPS, GROUP)
+    packed = np.repeat(packed.transpose(1, 3, 0, 4, 2), 2, axis=-1)
+    lanes[..., : GROUP * 2 * freqs] = packed.reshape(members, GROUPS, 8, -1)
+
+    rows = np.stack(
+        [2.0 * alpha, alpha * alpha, alpha * beta, scale, np.broadcast_to(high[:, None], alpha.shape)]
+    )[:, :, classes]
+    rows = rows.reshape(5, members, freqs, CLASSES).transpose(1, 3, 0, 2)
+    rows = np.broadcast_to(rows[..., None], rows.shape + (LANES,)).astype(np.float32)
+    squares = (cosine * cosine)[classes].astype(np.float32)
+    return np.concatenate([scalars.reshape(-1), squares]), lanes, rows
+
+
+def iota(shape, axis):
+    return lax.broadcasted_iota(jnp.int32, shape, axis)
+
+
+def spread(values, column):
+    return jnp.broadcast_to(values[:, column : column + 1], values.shape)
+
+
+def shift_rows(values, step):
+    rows = values.shape[0]
+    edge = 0 if step > 0 else rows - 1
+    moved = pltpu.roll(values, step % rows, 0)
+    return jnp.where(iota(values.shape, 0) == edge, 0.0, moved)
+
+
+def shift_lanes(values, step):
+    lanes = values.shape[1]
+    edge = 0 if step > 0 else lanes - 1
+    moved = pltpu.roll(values, step % lanes, 1)
+    return jnp.where(iota(values.shape, 1) == edge, 0.0, moved)
+
+
+def slot_base(quadrant):
+    return (0, 9, 9, 18)[quadrant]
+
+
+def class_index(direction):
+    folded = lax.rem(direction, 18)
+    return jnp.where(folded <= 9, folded, 18 - folded)
+
+
+def pack_kernel(
+    freqs, member_ref, scalar_ref, lanes_ref, land_ref, ice_ref, east_ref, north_ref, spectrum_ref,
+    kept_ref, growth_ref, wet_ref, right_ref, left_ref, down_ref, up_ref, packed_ref, sems,
+):
+    member = member_ref[0]
+
+    def fetch(group):
+        part = (slice(None), pl.ds(group * GROUP, GROUP))
+        return pltpu.make_async_copy(spectrum_ref.at[part], kept_ref.at[part], sems.at[group])
+
+    for group in range(GROUPS):
+        fetch(group).start()
+
+    wet_cells = (1 - land_ref[...]).astype(jnp.float32)
+    wet_ref[...] = wet_cells
+    open_water = 0.5 * (1.0 - ice_ref[...].astype(jnp.float32))
+    shape = wet_cells.shape
+    rows = shape[0]
+    tiles = rows // SUB
+    for direction in range(ND):
+        angle = 2.0 * math.pi * direction / ND
+        project = math.cos(angle) * east_ref[...] + math.sin(angle) * north_ref[...]
+        growth_ref[direction] = open_water * jnp.square(jnp.maximum(project, 0.0))
+
+    lane = iota(shape, 1)
+    even = lane % 2 == 0
+    tile_lane = iota((SUB, LANES), 1)
+    down_ref[pl.ds(2 * 18 * freqs, CORNERS), :] = jnp.zeros((CORNERS, LANES), jnp.float32)
+    up_ref[pl.ds(2 * 18 * freqs, CORNERS), :] = jnp.zeros((CORNERS, LANES), jnp.float32)
+
+    for quadrant in range(4):
+        to_right, to_down = quadrant in (0, 1), quadrant in (0, 3)
+        side = 1 if to_right else -1
+        fore = 1 if to_down else -1
+        row_start = rows - SUB if to_down else 0
+        row_near = SUB - 1 if to_down else 0
+        wet_rows = wet_cells[row_start : row_start + SUB, :]
+        row_out = down_ref if to_down else up_ref
+        ahead, behind = (LANES - 1, LANES - 2) if to_right else (0, 1)
+        wet_near, wet_far = spread(wet_cells, ahead), spread(wet_cells, behind)
+        near_even = not to_right
+        wet_packed = jnp.where(even == near_even, wet_near, wet_far)
+
+        def one_group(index, carry):
+            group = quadrant * GROUP + index
+            fetch(group).wait()
+            packed = [jnp.zeros((SUB, LANES), jnp.float32) for _ in range(tiles)]
+            for i in range(GROUP):
+                direction = group * GROUP + i
+                kind = class_index(direction)
+                row_values = []
+                for j in range(freqs):
+                    base = ((member * freqs + j) * CLASSES + kind) * KINDS
+                    alpha, beta = scalar_ref[base], scalar_ref[base + 1]
+                    place = i * 2 * freqs + 2 * j
+                    here = (tile_lane >= place) & (tile_lane < place + 2)
+                    turn = (place + 2 if to_right else place) % LANES
+                    for tile in range(tiles):
+                        cells = kept_ref[j, direction, tile * SUB : (tile + 1) * SUB, :]
+                        packed[tile] = jnp.where(here, pltpu.roll(cells, turn, 1), packed[tile])
+                        if tile * SUB == row_start:
+                            near = cells * wet_rows
+                            far = pltpu.roll(near, fore % SUB, 0)
+                            beside = shift_lanes(near, side)
+                            follow = wet_rows * (alpha * alpha * far + alpha * beta * beside)
+                            row_values.append((near, follow))
+                slot = (direction - slot_base(quadrant)) * freqs
+                for j, (near, follow) in enumerate(row_values):
+                    row_out[pl.ds(slot + j, 1), :] = near[row_near : row_near + 1, :]
+                    row_out[pl.ds(18 * freqs + slot + j, 1), :] = follow[row_near : row_near + 1, :]
+            for tile in range(tiles):
+                packed_ref[tile * SUB : (tile + 1) * SUB, :] = packed[tile]
+            values = packed_ref[...] * wet_packed
+            near = pltpu.roll(values, 1 if near_even else LANES - 1, 1)
+            table = lanes_ref[member, group]
+            follow = wet_near * (table[1:2] * values + table[2:3] * shift_rows(near, fore))
+            message = jnp.where(even == near_even, values, follow)
+            message = jnp.where(lane == LANES - 1, wet_near, message)
+            if to_right:
+                right_ref[group] = message
+            else:
+                left_ref[group - GROUPS // 2] = message
+            return carry
+
+        lax.fori_loop(0, GROUP, one_group, 0)
+
+
+def corner_kernel(
+    freqs, wet_ref, right_ref, left_ref, down_in, up_in, down_ref, up_ref, rows_ref, sems
+):
+    rows = wet_ref.shape[0]
+    last = iota((1, LANES), 1) == LANES - 1
+    rows_ref[...] = jnp.zeros_like(rows_ref)
+    for which, row in ((0, rows - 1), (1, 0)):
+        for i in range(6):
+            source = right_ref if i < 3 else left_ref
+            if which == 0:
+                index = i if i < 3 else i
+            else:
+                index = i + 3 if i < 3 else i - 3
+            column = 0 if i < 3 else LANES - 1
+            own = jnp.broadcast_to(wet_ref[row : row + 1, column : column + 1], (1, LANES))
+            rows_ref[which, i : i + 1, :] = jnp.where(last, own, source[index, row : row + 1, :])
+    start = 2 * 18 * freqs
+    copies = [
+        pltpu.make_async_copy(
+            rows_ref.at[which], ref.at[pl.ds(start, CORNERS), :], sems.at[which]
+        )
+        for which, ref in ((0, down_ref), (1, up_ref))
+    ]
+    for copy in copies:
+        copy.start()
+    for copy in copies:
+        copy.wait()
+
+
+def main_kernel(
+    freqs, squares, member_ref, scalar_ref, wet_ref, growth_ref, kept_in, kept_ref, a_ref, b_ref,
+    energy_ref, first_ref,
+):
+    member = member_ref[0]
+    rows = wet_ref.shape[0]
+    tiles = rows // SUB
+    per_freq = CLASSES - 1
+    last = freqs * per_freq - 1
+    lane = iota((SUB, LANES), 1)
+    sub = iota((SUB, LANES), 0)
+    not_first = jnp.where(lane == 0, 0.0, 1.0)
+    not_last = jnp.where(lane == LANES - 1, 0.0, 1.0)
+    top, bottom = sub == 0, sub == SUB - 1
+    zero = jnp.zeros((SUB, LANES), jnp.float32)
+    energy_ref[...] = jnp.zeros_like(energy_ref)
+    a_ref[...] = jnp.zeros_like(a_ref)
+    b_ref[...] = jnp.zeros_like(b_ref)
+
+    def tile_at(tile):
+        return pl.ds(tile * SUB, SUB)
+
+    def unfold(item):
+        j = lax.div(item, per_freq)
+        index = lax.rem(item, per_freq)
+        flat = index == 0
+        directions = (
+            index,
+            jnp.where(flat, 9, 18 - index),
+            18 + index,
+            jnp.where(flat, 27, 36 - index),
+        )
+        kinds = (index, jnp.where(flat, 9, index))
+        bases = [((member * freqs + j) * CLASSES + kind) * KINDS for kind in kinds]
+        return j, directions, kinds, bases
+
+    def step(cells, quadrant, bases):
+        base = bases[quadrant % 2]
+        alpha, beta = scalar_ref[base], scalar_ref[base + 1]
+        to_down, to_right = quadrant in (0, 3), quadrant in (0, 1)
+        turn, edge = (1, top) if to_down else (SUB - 1, bottom)
+        side = 1 if to_right else LANES - 1
+        across = beta * (not_first if to_right else not_last)
+        turned = [pltpu.roll(values, turn, 0) for values in cells]
+        result = []
+        for tile in range(tiles):
+            source = tile - 1 if to_down else tile + 1
+            before = turned[source] if 0 <= source < tiles else zero
+            ahead = jnp.where(edge, before, turned[tile])
+            result.append(
+                cells[tile] + alpha * ahead + across * pltpu.roll(cells[tile], side, 1)
+            )
+        return result
+
+    def load_cells(j, directions):
+        return [[kept_in[j, d, tile_at(t), :] for t in range(tiles)] for d in directions]
+
+    def first_step(loaded, bases):
+        stepped = []
+        for quadrant in range(4):
+            cells = [loaded[quadrant][t] * wet_ref[tile_at(t), :] for t in range(tiles)]
+            stepped.append(
+                [wet_ref[tile_at(t), :] * v for t, v in enumerate(step(cells, quadrant, bases))]
+            )
+        return stepped
+
+    def store_first(slot, stepped):
+        for quadrant in range(4):
+            for tile in range(tiles):
+                first_ref[slot, quadrant, tile_at(tile), :] = stepped[quadrant][tile]
+
+    j, directions, kinds, bases = unfold(jnp.int32(0))
+    store_first(0, first_step(load_cells(j, directions), bases))
+
+    def body(item, carry):
+        slot = lax.rem(item, 2)
+        j, directions, kinds, bases = unfold(item)
+        ahead_j, ahead_directions, _, ahead_bases = unfold(jnp.minimum(item + 1, last))
+        first = [
+            [first_ref[slot, quadrant, tile_at(t), :] for t in range(tiles)]
+            for quadrant in range(4)
+        ]
+        loaded = load_cells(ahead_j, ahead_directions)
+        at = [pl.ds(pl.multiple_of(j * rows, SUB) + t * SUB, SUB) for t in range(tiles)]
+        growth = [[growth_ref[d, tile_at(t), :] for t in range(tiles)] for d in directions]
+        totals = [(energy_ref[tile_at(t), :], a_ref[at[t], :], b_ref[at[t], :]) for t in range(tiles)]
+
+        second = [step(first[quadrant], quadrant, bases) for quadrant in range(4)]
+        scale, high = scalar_ref[bases[0] + 2], scalar_ref[bases[0] + 3]
+        square_x, square_y = scalar_ref[squares + kinds[0]], scalar_ref[squares + kinds[1]]
+        scaled_high = scale * high
+        results = []
+        for t in range(tiles):
+            energy, whole, along = totals[t]
+            plain_x = scale * (second[0][t] + second[2][t])
+            plain_y = scale * (second[1][t] + second[3][t])
+            grown_x = plain_x + scaled_high * (
+                growth[0][t] * second[0][t] + growth[2][t] * second[2][t]
+            )
+            grown_y = plain_y + scaled_high * (
+                growth[1][t] * second[1][t] + growth[3][t] * second[3][t]
+            )
+            results.append(
+                (
+                    energy + (plain_x + plain_y),
+                    whole + (grown_x + grown_y),
+                    along + (square_x * grown_x + square_y * grown_y),
+                )
+            )
+        stepped = first_step(loaded, ahead_bases)
+
+        for t in range(tiles):
+            energy_ref[tile_at(t), :], a_ref[at[t], :], b_ref[at[t], :] = results[t]
+        for quadrant, direction in enumerate(directions):
+            for t in range(tiles):
+                kept_ref[j, direction, tile_at(t), :] = second[quadrant][t]
+        store_first(1 - slot, stepped)
+        return carry
+
+    lax.fori_loop(0, last + 1, body, 0)
+
+
+def border_kernel(
+    freqs, member_ref, lanes_ref, table_ref, wet_ref, ice_ref, east_ref, north_ref, growth_ref,
+    right_ref, left_ref, down_ref, up_ref, a_in, b_in, energy_in,
+    a_ref, b_ref, energy_ref, columns_ref, edges_ref,
+):
+    member = member_ref[0]
+    wet_cells = wet_ref[...]
+    shape = wet_cells.shape
+    rows = shape[0]
+    lane = iota(shape, 1)
+    row = iota(shape, 0)
+    even = lane % 2 == 0
+    used = lane < GROUP * 2 * freqs
+    a_ref[...] = a_in[...]
+    b_ref[...] = b_in[...]
+    energy_ref[...] = energy_in[...]
+    start = 2 * 18 * freqs
+
+    for to_right in (True, False):
+        near_column, far_column = (0, 1) if to_right else (LANES - 1, LANES - 2)
+        near_even = to_right
+        wet_near, wet_far = spread(wet_cells, near_column), spread(wet_cells, far_column)
+
+        def packed_field(values):
+            return jnp.where(
+                even == near_even, spread(values, near_column), spread(values, far_column)
+            )
+
+        east, north = packed_field(east_ref[...]), packed_field(north_ref[...])
+        open_water = 0.5 * (1.0 - packed_field(ice_ref[...].astype(jnp.float32)))
+        sums = [jnp.zeros(shape, jnp.float32) for _ in range(3)]
+        for index in range(GROUPS // 2):
+            group = index if to_right else index + GROUPS // 2
+            to_down = heads_down(group * GROUP)
+            fore = 1 if to_down else -1
+            message = (right_ref if to_right else left_ref)[index]
+            table = lanes_ref[member, group]
+            entered = pltpu.roll(message, LANES - 1 if near_even else 1, 1)
+            corner_index = index if to_down else (
+                index - 3 if to_right else index + 3
+            )
+            corner = (down_ref if to_down else up_ref)[pl.ds(start + corner_index, 1), :]
+            edge = 0 if to_down else rows - 1
+            paths = corner[:, LANES - 1 :] + message[edge : edge + 1, LANES - 1 :]
+            corner = pltpu.roll(
+                jnp.broadcast_to(corner, (SUB, LANES)), LANES - 1 if near_even else 1, 1
+            )[0:1]
+            corner = jnp.broadcast_to(paths, (1, LANES)) * corner
+            diagonal = shift_rows(wet_near * entered, fore)
+            diagonal = jnp.where(row == edge, jnp.broadcast_to(corner, shape), diagonal)
+            near = wet_near * (table[0:1] * entered + message + table[2:3] * diagonal)
+            far = wet_near * wet_far * (table[1:2] * message)
+            change = jnp.where(used, jnp.where(even == near_even, near, far), 0.0)
+            columns_ref[group] = change
+            project = table[6:7] * east + table[7:8] * north
+            grown = change * (1.0 + table[5:6] * (open_water * jnp.square(jnp.maximum(project, 0.0))))
+            sums[0] += table[3:4] * change
+            sums[1] += table[3:4] * grown
+            sums[2] += table[4:5] * grown
+        width = 2 * freqs
+        sums = [
+            part + pltpu.roll(part, LANES - width, 1) + pltpu.roll(part, LANES - 2 * width, 1)
+            for part in sums
+        ]
+        target = 0 if to_right else LANES - 2
+        inside = (lane >= target) & (lane < target + 2)
+
+        energy = jnp.zeros(shape, jnp.float32)
+        for j in range(freqs):
+            turn = (target - 2 * j) % LANES
+            block = slice(j * rows, (j + 1) * rows)
+            place = [jnp.where(inside, pltpu.roll(part, turn, 1), 0.0) for part in sums]
+            a_ref[block, :] += place[1]
+            b_ref[block, :] += place[2]
+            energy = energy + place[0]
+        energy_ref[...] += energy
+
+    for to_down in (True, False):
+        near_row, far_row = (0, 1) if to_down else (rows - 1, rows - 2)
+        message_ref = down_ref if to_down else up_ref
+        wet_near = wet_cells[near_row : near_row + 1, :]
+        wet_both = wet_near * wet_cells[far_row : far_row + 1, :]
+        directions = [d for d in range(ND) if heads_down(d) == to_down]
+        totals = [jnp.zeros((freqs, LANES), jnp.float32) for _ in range(6)]
+        for direction in directions:
+            slot = row_slot(direction) * freqs
+            entered = message_ref[slot : slot + freqs, :]
+            follow = message_ref[18 * freqs + slot : 18 * freqs + slot + freqs, :]
+            table = table_ref.at[member, class_of(direction)]
+            side = 1 if heads_right(direction) else -1
+            diagonal = shift_lanes(wet_near * entered, side)
+            near = wet_near * (table[0] * entered + follow + table[2] * diagonal)
+            far = wet_both * (table[1] * entered)
+            square = math.cos(2.0 * math.pi * direction / ND) ** 2
+            for place, (change, at) in enumerate(((near, near_row), (far, far_row))):
+                edges_ref[(0 if to_down else 2) + place, slot : slot + freqs, :] = change
+                growth = growth_ref[direction, at : at + 1, :]
+                plain = table[3] * change
+                grown = plain * (1.0 + table[4] * growth)
+                totals[3 * place] += plain
+                totals[3 * place + 1] += grown
+                totals[3 * place + 2] += square * grown
+        for place, at in enumerate((near_row, far_row)):
+            energy_ref[at : at + 1, :] += jnp.sum(totals[3 * place], axis=0, keepdims=True)
+            picked = pl.ds(at, freqs, stride=rows)
+            a_ref[picked, :] += totals[3 * place + 1]
+            b_ref[picked, :] += totals[3 * place + 2]
+
+
+def stress_kernel(
+    freqs, member_ref, scalar_ref, wet_ref, a_ref, b_ref, own_ref, other_ref, sums_ref, square_ref
+):
+    member = member_ref[0]
+    wet_cells = wet_ref[...]
+    rows = wet_cells.shape[0]
+    energy = wet_cells * (own_ref[...] + other_ref[...]) / (ND * NF)
+    square = jnp.square(energy)
+    square_ref[...] = square
+
+    def add(j, sums):
+        base = (member * freqs + j) * CLASSES * KINDS
+        high, shoal = scalar_ref[base + 3], scalar_ref[base + 4]
+        block = pl.ds(pl.multiple_of(j * rows, SUB), rows)
+        ratio = wet_cells / (1.0 + (2.0 * high) * square)
+        whole = ratio * a_ref[block, :]
+        along = ratio * b_ref[block, :]
+        return (
+            sums[0] + (shoal * along + (shoal - 0.5) * whole),
+            sums[1] + ((2.0 * shoal - 0.5) * whole - shoal * along),
+            sums[2] + whole,
+        )
+
+    zero = jnp.zeros(wet_cells.shape, jnp.float32)
+    sums = lax.fori_loop(0, freqs, add, (zero, zero, zero))
+    for index in range(3):
+        sums_ref[index] = sums[index] / (ND * NF)
+
+
+SLOTS = 3
+
+
+def final_kernel(
+    freqs, member_ref, scalar_ref, inside_ref, wet_ref, depth_ref, square_ref, sums_ref, left_ref,
+    right_ref, above_ref, below_ref, growth_ref, kept_ref, columns_ref, edges_ref,
+    result_ref, level_ref, ratio_ref, ring_ref, sems,
+):
+    member = member_ref[0]
+    wet_cells = wet_ref[...]
+    rows = wet_cells.shape[0]
+    low_half = iota((rows, LANES), 1) < LANES // 2
+
+    def framed(index):
+        block = sums_ref[index]
+        beside = jnp.where(low_half, right_ref[index], left_ref[index])
+        middle = jnp.concatenate([block, beside], axis=1)
+        return jnp.concatenate([middle, below_ref[index], above_ref[index]], axis=0)
+
+    def around(values, axis):
+        size = values.shape[axis]
+        return pltpu.roll(values, 1, axis) + pltpu.roll(values, size - 1, axis)
+
+    stress_x, stress_y = framed(0), framed(1)
+    frame = stress_x.shape
+    frame_row, frame_lane = iota(frame, 0), iota(frame, 1)
+    flag = lambda index: inside_ref[index]
+    row_ok = jnp.where(
+        frame_row < rows, 1.0, jnp.where(frame_row < rows + SUB, flag(1), flag(0))
+    )
+    lane_ok = jnp.where(
+        frame_lane < LANES, 1.0, jnp.where(frame_lane < LANES + LANES // 2, flag(3), flag(2))
+    )
+    inside = row_ok * lane_ok / 4.5
+    source = -((around(stress_x, 0) - 2.0 * stress_x) + (around(stress_y, 1) - 2.0 * stress_y))
+    level = inside * source
+    for _ in range(JAC):
+        level = inside * (source + around(level, 0) + around(level, 1))
+    level = level[:rows, :LANES]
+    level_ref[...] = level
+    damping = 1.0 + 4.0 * sums_ref[2] / (jnp.square(depth_ref[...] + level) + 1.0)
+    square = square_ref[...]
+    tiles = rows // SUB
+    for j in range(freqs):
+        high = scalar_ref[(member * freqs + j) * CLASSES * KINDS + 3]
+        ratio = wet_cells / ((1.0 + (2.0 * high) * square) * damping)
+        ratio_ref[0, j] = ratio
+        ratio_ref[1, j] = high * ratio
+
+    tile_row, tile_lane = iota((SUB, LANES), 0), iota((SUB, LANES), 1)
+    quarter = ND // 4
+
+    def send(direction, slot):
+        return pltpu.make_async_copy(
+            ring_ref.at[slot], result_ref.at[:, pl.ds(direction, 1)], sems.at[slot]
+        )
+
+    for quadrant in range(4):
+        to_right, to_down = quadrant in (0, 1), quadrant in (0, 3)
+        target = 0 if to_right else LANES - 2
+        at_side = (tile_lane >= target) & (tile_lane < target + 2)
+        bank, edge_tile = (0, 0) if to_down else (2, tiles - 1)
+        near_row = tile_row == (0 if to_down else SUB - 1)
+        far_row = tile_row == (1 if to_down else SUB - 2)
+
+        def one(index, carry):
+            direction = quadrant * quarter + index
+            slot = lax.rem(direction, SLOTS)
+
+            @pl.when(direction >= SLOTS)
+            def _():
+                send(direction - SLOTS, slot).wait()
+
+            kind = class_index(direction)
+            group = lax.div(direction, GROUP)
+            offset = 2 * freqs * lax.rem(direction, GROUP)
+            row_at = (direction - slot_base(quadrant)) * freqs
+            aligned = [
+                pltpu.roll(
+                    columns_ref[group, t * SUB : (t + 1) * SUB, :],
+                    lax.rem(target - offset + LANES, LANES),
+                    1,
+                )
+                for t in range(tiles)
+            ]
+            growth = [growth_ref[direction, t * SUB : (t + 1) * SUB, :] for t in range(tiles)]
+            for j in range(freqs):
+                scale = scalar_ref[((member * freqs + j) * CLASSES + kind) * KINDS + 2]
+                near = jnp.broadcast_to(edges_ref[bank, pl.ds(row_at + j, 1), :], (SUB, LANES))
+                far = jnp.broadcast_to(edges_ref[bank + 1, pl.ds(row_at + j, 1), :], (SUB, LANES))
+                for t in range(tiles):
+                    part = slice(t * SUB, (t + 1) * SUB)
+                    entered = pltpu.roll(aligned[t], (LANES - 2 * j) % LANES, 1)
+                    value = kept_ref[j, direction, part, :] + jnp.where(at_side, entered, 0.0)
+                    if t == edge_tile:
+                        value += jnp.where(near_row, near, jnp.where(far_row, far, 0.0))
+                    factor = ratio_ref[0, j, part, :] + ratio_ref[1, j, part, :] * growth[t]
+                    ring_ref[slot, j, 0, part, :] = value * (scale * factor)
+            send(direction, slot).start()
+            return carry
+
+        lax.fori_loop(0, quarter, one, 0)
+    for direction in range(ND - SLOTS, ND):
+        send(direction, direction % SLOTS).wait()
+
+
+def step_pairs(axis, step):
+    count = lax.axis_size(axis)
+    return [(i, i + step) for i in range(count) if 0 <= i + step < count]
+
+
+def neighbour(values, axis, step):
+    return lax.ppermute(values, axis, step_pairs(axis, step))
+
+
+def others_sum(values, axis):
+    count = lax.axis_size(axis)
+    total = None
+    for step in range(1, count):
+        part = lax.ppermute(values, axis, [(i, (i + step) % count) for i in range(count)])
+        total = part if total is None else total + part
+    return jnp.zeros_like(values) if total is None else total
+
+
+VMEM = pl.BlockSpec(memory_space=pltpu.VMEM)
+SMEM = pl.BlockSpec(memory_space=pltpu.SMEM)
+HBM = pl.BlockSpec(memory_space=pltpu.HBM)
+ANY = pl.BlockSpec(memory_space=pl.ANY)
+
+
+def in_vmem(*shape):
+    return pltpu.VMEM(shape, jnp.float32)
+
+
+def in_any(*shape):
+    return jax.ShapeDtypeStruct(shape, jnp.float32)
+
+
+def call(kernel, in_specs, out_shape, out_specs, flops, moved, scratch=(), aliases=None, limit=6):
+    return pl.pallas_call(
+        kernel,
+        in_specs=in_specs,
+        out_shape=out_shape,
+        out_specs=out_specs,
+        scratch_shapes=list(scratch),
+        input_output_aliases=aliases or {},
+        cost_estimate=pl.CostEstimate(flops=flops, bytes_accessed=moved, transcendentals=0),
+        compiler_params=pltpu.CompilerParams(vmem_limit_bytes=limit << 20),
+    )
+
+
+def resident(spectrum, land_mask, ice_mask, wind_u, wind_v, depth):
+    local_comp, rows, lanes = spectrum.shape
+    freqs = local_comp // ND
+    members = lax.axis_size("comp")
+    member = lax.axis_index("comp").astype(jnp.int32).reshape(1)
+    scalars, lane_table, row_table = numpy_tables(members, freqs)
+    scalars, lane_table, row_table = map(jnp.asarray, (scalars, lane_table, row_table))
+    cells = rows * lanes
+    row_message = 2 * 18 * freqs + CORNERS
+    block = (freqs, ND, rows, lanes)
+
+    kept, growth, wet, to_right, to_left, to_down, to_up = call(
+        functools.partial(pack_kernel, freqs),
+        [SMEM, SMEM, VMEM, VMEM, VMEM, VMEM, VMEM, HBM],
+        (
+            in_vmem(*block),
+            in_any(ND, rows, lanes),
+            in_any(rows, lanes),
+            in_any(GROUPS // 2, rows, lanes),
+            in_any(GROUPS // 2, rows, lanes),
+            in_any(row_message, lanes),
+            in_any(row_message, lanes),
+        ),
+        (VMEM,) * 7,
+        flops=local_comp * cells * 4,
+        moved=local_comp * cells * 4,
+        scratch=[pltpu.VMEM((rows, lanes), jnp.float32), pltpu.SemaphoreType.DMA((GROUPS,))],
+    )(member, scalars, lane_table, land_mask, ice_mask, wind_u, wind_v, pltpu.with_memory_space_constraint(spectrum.reshape(block), pltpu.HBM))
+
+    from_left = neighbour(to_right, "sect", 1)
+    from_right = neighbour(to_left, "sect", -1)
+    to_down, to_up = call(
+        functools.partial(corner_kernel, freqs),
+        [VMEM, VMEM, VMEM, ANY, ANY],
+        (in_any(row_message, lanes), in_any(row_message, lanes)),
+        (ANY, ANY),
+        flops=100,
+        moved=1 << 15,
+        scratch=[pltpu.VMEM((2, CORNERS, lanes), jnp.float32), pltpu.SemaphoreType.DMA((2,))],
+        aliases={3: 0, 4: 1},
+    )(wet, from_left, from_right, to_down, to_up)
+    from_above = neighbour(to_down, "slab", 1)
+    from_below = neighbour(to_up, "slab", -1)
+
+    kept, a_sums, b_sums, energy = call(
+        functools.partial(main_kernel, freqs, scalars.size - CLASSES),
+        [SMEM, SMEM, VMEM, VMEM, VMEM],
+        (
+            in_vmem(*block),
+            in_any(freqs * rows, lanes),
+            in_any(freqs * rows, lanes),
+            in_any(rows, lanes),
+        ),
+        (VMEM,) * 4,
+        flops=local_comp * cells * 16,
+        moved=local_comp * cells * 8,
+        scratch=[pltpu.VMEM((2, 4, rows, lanes), jnp.float32)],
+        aliases={4: 0},
+    )(member, scalars, wet, growth, kept)
+
+    a_sums, b_sums, energy, columns, edges = call(
+        functools.partial(border_kernel, freqs),
+        [SMEM] + [VMEM] * 14,
+        (
+            in_any(freqs * rows, lanes),
+            in_any(freqs * rows, lanes),
+            in_any(rows, lanes),
+            in_any(GROUPS, rows, lanes),
+            in_any(4, 18 * freqs, lanes),
+        ),
+        (VMEM,) * 5,
+        flops=cells * 1000,
+        moved=cells * 400,
+        aliases={12: 0, 13: 1, 14: 2},
+    )(
+        member, lane_table, row_table, wet, ice_mask, wind_u, wind_v, growth,
+        from_left, from_right, from_above, from_below, a_sums, b_sums, energy,
+    )
+
+    sums, square = call(
+        functools.partial(stress_kernel, freqs),
+        [SMEM, SMEM] + [VMEM] * 5,
+        (in_any(3, rows, lanes), in_any(rows, lanes)),
+        (VMEM, VMEM),
+        flops=cells * freqs * 12,
+        moved=cells * freqs * 8,
+    )(member, scalars, wet, a_sums, b_sums, energy, others_sum(energy, "comp"))
+    sums = sums + others_sum(sums, "comp")
+
+    stresses = sums[:2]
+    left = neighbour(stresses, "sect", 1)
+    right = neighbour(stresses, "sect", -1)
+    beside = jnp.where(jnp.arange(lanes) < lanes // 2, right, left)
+    strip = jnp.concatenate([stresses, beside], axis=2)
+    above = neighbour(strip[:, rows - SUB :], "slab", 1)
+    below = neighbour(strip[:, :SUB], "slab", -1)
+    slab, sect = lax.axis_index("slab"), lax.axis_index("sect")
+    inside = jnp.stack(
+        [
+            slab > 0,
+            slab < lax.axis_size("slab") - 1,
+            sect > 0,
+            sect < lax.axis_size("sect") - 1,
+        ]
+    ).astype(jnp.float32)
+
+    result, level = call(
+        functools.partial(final_kernel, freqs),
+        [SMEM, SMEM, SMEM] + [VMEM] * 12,
+        (in_any(*block), in_any(rows, lanes)),
+        (HBM, VMEM),
+        flops=local_comp * cells * 6,
+        moved=local_comp * cells * 8,
+        scratch=[
+            pltpu.VMEM((2, freqs, rows, lanes), jnp.float32),
+            pltpu.VMEM((SLOTS, freqs, 1, rows, lanes), jnp.float32),
+            pltpu.SemaphoreType.DMA((SLOTS,)),
+        ],
+    )(
+        member, scalars, inside, wet, depth, square, sums, left, right, above, below, growth, kept,
+        columns, edges,
+    )
+    return result.reshape(spectrum.shape), level
+
+
+def local(spectrum, *fields):
+    local_comp, rows, lanes = spectrum.shape
+    whole_rings = local_comp % ND == 0 and GROUP * 2 * (local_comp // ND) < LANES - 1
+    if whole_rings and lanes == LANES and rows % SUB == 0:
+        return resident(spectrum, *fields)
+    return general(spectrum, *fields)
+
+
 def solution(mesh):
     in_specs = (
         P("comp", "slab", "sect"),

time: 1020 us -> 117 us (0.11)
  waiting for transfers between devices: 266 us -> 14 us
  blocking collectives: 241 us -> 0 us
  other arithmetic: 217 us -> 0.12 us
  local copies, waits for them, and re-layouts: 165 us -> 19.3 us
  starting transfers between devices: 85.7 us -> 26 us
  Pallas kernels: 0 us -> 54.4 us
  matrix products: 33.6 us -> 0 us
    all_to_all x1 -> x0, blocking collectives: 236 us -> none  [local(): lax.all_to_all(damped, 'comp', split_axis=0, concat_axis=1, tiled=True)]
    all_to_all x1 -> x0, waiting for transfers between devices: 229 us -> none  [local(): lax.all_to_all(spectra, 'comp', split_axis=1, concat_axis=0, tiled=True)]
    mul x5 -> x0, other arithmetic: 134 us -> none  [the longest x2 114 us: advect(): return (spectra - change) * wet_cells]
    slice x18 -> x1, local copies, waits for them, and re-layouts: 83.7 us -> 0.01 us  [resident(): stresses = sums[:2]]
    pallas_call x0 -> x6, Pallas kernels: none -> 54.4 us  [the longest x1 24.3 us: resident(): call(functools.partial(main_kernel, freqs, scalars.size - CLASSES), [SMEM...]
    ppermute x28 -> x10, starting transfers between devices: 74.2 us -> 26 us  [the longest x8 22.8 us: neighbour(): return lax.ppermute(values, axis, step_pairs(axis, step))]
    ppermute x4 -> x0, local copies, waits for them, and re-layouts: 44.1 us -> none  [the longest x2 22.1 us: extended(): lax.ppermute(head, axis, [((i + 1) % count, i) for i in range(ends)])]
    div x7 -> x0, other arithmetic: 42.2 us -> none  [the longest x1 21.1 us: forcing(): spectra * (1.0 + growth) / (1.0 + 2.0 * high_ratio * jnp.square(energy))]
  transfers between devices with their start and end apart: 29 -> 10, of which waited for: 14 -> 6; matrix products, arithmetic and copies ran while one was open for 6% -> 0% of each run, Pallas kernels for 0% -> 21%
where the time goes in v1:
time: 117 us; the launch traced here: 115 us
  Pallas kernels  54.4 us (46%)
  starting transfers between devices  26 us (22%)
  local copies, waits for them, and re-layouts  19.3 us (16%)
  waiting for transfers between devices  14 us (12%)
    pallas_call x1, Pallas kernels, resident(): call(functools.partial(main_kernel, freqs, scalars.size - CLASSES), [SMEM...  24.3 us
    ppermute x8, starting transfers between devices, neighbour(): return lax.ppermute(values, axis, step_pairs(axis, step))  22.8 us
    unnamed x28, local copies, waits for them, and re-layouts  19.3 us
    pallas_call x1, Pallas kernels, resident(): call(functools.partial(final_kernel, freqs), [SMEM, SMEM, SMEM] + [VMEM]...  16.1 us
    pallas_call x1, Pallas kernels, resident(): call(functools.partial(pack_kernel, freqs), [SMEM, SMEM, VMEM, VMEM, VMEM...  10.4 us
    ppermute x8, waiting for transfers between devices, neighbour(): return lax.ppermute(values, axis, step_pairs(axis, step))  8.21 us
    ppermute x2, waiting for transfers between devices, others_sum(): lax.ppermute(values, axis, [(i, (i + step) % count) for i in range(count)])  5.76 us
    ppermute x2, starting transfers between devices, others_sum(): lax.ppermute(values, axis, [(i, (i + step) % count) for i in range(count)])  3.21 us
  transfers between devices with their start and end apart: 10, of which 6 were waited for; matrix products, arithmetic and copies ran while one was open for 0% of the time, Pallas kernels for 21%

profile of v1, /device:TPU:12, one launch (start us, length us, event | category | flops | bytes accessed | tf_op | source)
XLA Modules:
  0.0 114.7 jit_solution(5666681838388679531)
XLA Ops:
  0.6 0.0 copy-start.3
  0.6 0.9 copy-done.3
  1.5 0.0 copy-start.5
  1.5 0.7 copy-done.5
  2.2 0.0 copy-start.7
  2.2 0.8 copy-done.7
  3.0 0.0 copy-start.9
  3.0 0.8 copy-done.9
  3.8 0.8 copy-done.11
  4.5 0.8 copy-done.12
  5.3 0.0 copy-start.6
  5.3 0.0 copy-start.13
  5.3 10.4 %shard_map.104 = (f32[18,36,64,128]{3,2,1,0:T(8,128)S(1)}, f32[36,64,128]{2,1,0:T(8,128)S(1)}, f32[64,128]{1,0:T(8,128)S(1)}, f32[6,64,128]{2,1,0:T(8,128)S(1)},...) custom-call(s32[1]{0:T(128)} %bitcast.member_ref, f32[1810]{0:T(1024)S(1)} %copy-done.5, ...), custom_call_target="tpu_custom_call" | custom-call | flops 21233664 | bytes 21233664 | tf_op jit(solution)/shard_map/pallas_call | solution.py:800
  15.7 1.9 %collective-permute-start = (f32[6,64,128]{2,1,0:T(8,128)S(1)}, f32[6,64,128]{2,1,0:T(8,128)S(1)}, u32[]{:S(2)}, u32[]{:S(2)}) collective-permute-start(f32[6,64,128]{2,1,0:T(8,128)S(1)} %get-tuple-element.26), channel_id=1, source_target_pairs={{0,4},{4,8},{8,12},{1,5},{5,9},{9,13},{2,6},{6,10},{10,14},{3,7},{... | collective-permute-start | bytes 589832 | tf_op jit(solution)/shard_map/ppermute | solution.py:750
  17.7 3.6 %collective-permute-start.1 = (f32[6,64,128]{2,1,0:T(8,128)S(1)}, f32[6,64,128]{2,1,0:T(8,128)S(1)}, u32[]{:S(2)}, u32[]{:S(2)}) collective-permute-start(f32[6,64,128]{2,1,0:T(8,128)S(1)} %get-tuple-element.27), channel_id=1, source_target_pairs={{4,0},{8,4},{12,8},{5,1},{9,5},{13,9},{6,2},{10,6},{14,10},{7,3},{... | collective-permute-start | bytes 589832 | tf_op jit(solution)/shard_map/ppermute | solution.py:750
  21.3 1.4 %collective-permute-done.right_ref = f32[6,64,128]{2,1,0:T(8,128)S(1)} collective-permute-done((f32[6,64,128]{2,1,0:T(8,128)S(1)}, f32[6,64,128]{2,1,0:T(8,128)S(1)}, u32[]{:S(2)}, u32[]{:S(2)}) %collective-permute-start) | collective-permute-done | bytes 196640 | tf_op jit(solution)/shard_map/ppermute | solution.py:750
  22.7 1.8 %collective-permute-done.1.left_ref = f32[6,64,128]{2,1,0:T(8,128)S(1)} collective-permute-done((f32[6,64,128]{2,1,0:T(8,128)S(1)}, f32[6,64,128]{2,1,0:T(8,128)S(1)}, u32[]{:S(2)}, u32[]{:S(2)}) %collective-permute-start.1) | collective-permute-done | bytes 196640 | tf_op jit(solution)/shard_map/ppermute | solution.py:750
  24.5 0.1 shard_map.105
  24.6 3.5 %collective-permute-start.2 = (f32[656,128]{1,0:T(8,128)S(1)}, f32[656,128]{1,0:T(8,128)S(1)}, u32[]{:S(2)}, u32[]{:S(2)}) collective-permute-start(f32[656,128]{1,0:T(8,128)S(1)} %get-tuple-element.30), channel_id=1, source_target_pairs={{0,1},{1,2},{2,3},{4,5},{5,6},{6,7},{8,9},{9,10},{10,11},{12,13},{... | collective-permute-start | bytes 1007624 | tf_op jit(solution)/shard_map/ppermute | solution.py:750
  28.1 2.4 %collective-permute-start.3 = (f32[656,128]{1,0:T(8,128)S(1)}, f32[656,128]{1,0:T(8,128)S(1)}, u32[]{:S(2)}, u32[]{:S(2)}) collective-permute-start(f32[656,128]{1,0:T(8,128)S(1)} %get-tuple-element.31), channel_id=1, source_target_pairs={{1,0},{2,1},{3,2},{5,4},{6,5},{7,6},{9,8},{10,9},{11,10},{13,12},{... | collective-permute-start | bytes 1007624 | tf_op jit(solution)/shard_map/ppermute | solution.py:750
  30.5 24.3 %shard_map.106 = (f32[18,36,64,128]{3,2,1,0:T(8,128)S(1)}, f32[1152,128]{1,0:T(8,128)S(1)}, f32[1152,128]{1,0:T(8,128)S(1)}, f32[64,128]{1,0:T(8,128)S(1)}) custom-call(s32[1]{0:T(128)} %bitcast.member_ref, f32[1810]{0:T(1024)S(1)} %copy-done.5, f32[64,128]{1,0:T(8,128)S(1)} %get-tuple-element.24.wet_ref, ...), custom_call_target="tpu_custom_call", output_to_operand_aliasing={{0}: (4, {})} | custom-call | flops 84934656 | bytes 42467328 | tf_op jit(solution)/shard_map/pallas_call | solution.py:833
  54.8 0.0 copy-start
  54.8 7.6 %copy-done = f32[18,36,64,128]{3,2,1,0:T(8,128)} copy-done((f32[18,36,64,128]{3,2,1,0:T(8,128)}, f32[18,36,64,128]{3,2,1,0:T(8,128)S(1)}, u32[]{:S(2)}) %copy-start) | copy-done | bytes 21233688
  62.4 0.0 collective-permute-done.2.down_ref
  62.4 0.0 collective-permute-done.3.up_ref
  62.4 0.0 copy-done.2
  62.5 0.0 copy-done.4
  62.5 0.0 copy-done.8
  62.5 0.0 copy-done.10
  62.5 2.2 %shard_map.107 = (f32[1152,128]{1,0:T(8,128)S(1)}, f32[1152,128]{1,0:T(8,128)S(1)}, f32[64,128]{1,0:T(8,128)S(1)}, f32[12,64,128]{2,1,0:T(8,128)S(1)}, f32[4,324,128]{2,1,0:T(8,128)S(1)}) custom-call(s32[1]{0:T(128)} %bitcast.member_ref, f32[2,12,8,128]{3,2,1,0:T(8,128)S(1)} %copy-done.4, ...), custom_call_target="tpu_custom_call", output_to_operand_aliasing={{0}: (12, {}), {1}: (13, {}), {2}: (14, {})} | custom-call | flops 8192000 | bytes 3276800 | tf_op jit(solution)/shard_map/pallas_call | solution.py:849
  64.7 1.6 %collective-permute-start.4 = (f32[64,128]{1,0:T(8,128)S(1)}, f32[64,128]{1,0:T(8,128)S(1)}, u32[]{:S(2)}, u32[]{:S(2)}) collective-permute-start(f32[64,128]{1,0:T(8,128)S(1)} %get-tuple-element.38.own_ref), channel_id=1, source_target_pairs={{0,16},{16,0},{1,17},{17,1},{2,18},{18,2},{3,19},{19,3},{4,20},{20... | collective-permute-start | bytes 98312 | tf_op jit(solution)/shard_map/ppermute | solution.py:757
  66.3 2.7 %collective-permute-done.4.other_ref = f32[64,128]{1,0:T(8,128)S(1)} collective-permute-done((f32[64,128]{1,0:T(8,128)S(1)}, f32[64,128]{1,0:T(8,128)S(1)}, u32[]{:S(2)}, u32[]{:S(2)}) %collective-permute-start.4) | collective-permute-done | bytes 32800 | tf_op jit(solution)/shard_map/ppermute | solution.py:757
  68.9 1.3 %shard_map.108 = (f32[3,64,128]{2,1,0:T(8,128)S(1)}, f32[64,128]{1,0:T(8,128)S(1)}) custom-call(s32[1]{0:T(128)} %bitcast.member_ref, f32[1810]{0:T(1024)S(1)} %copy-done.5, f32[64,128]{1,0:T(8,128)S(1)} %get-tuple-element.24.wet_ref, f32[1152,128]{1,0:T(8,128)S(1)} %get-tuple-element.36.a_ref, f32[1152,128]{1,0:T(8,128)S(1)} %get-tuple-element.37.b_ref, ...), custom_call_target="tpu_custom_call" | custom-call | flops 1769472 | bytes 1179648 | tf_op jit(solution)/shard_map/pallas_call | solution.py:868
  70.2 1.6 %collective-permute-start.5 = (f32[3,64,128]{2,1,0:T(8,128)S(1)}, f32[3,64,128]{2,1,0:T(8,128)S(1)}, u32[]{:S(2)}, u32[]{:S(2)}) collective-permute-start(f32[3,64,128]{2,1,0:T(8,128)S(1)} %get-tuple-element.40), channel_id=1, source_target_pairs={{0,16},{16,0},{1,17},{17,1},{2,18},{18,2},{3,19},{19,3},{4,20},{20... | collective-permute-start | bytes 294920 | tf_op jit(solution)/shard_map/ppermute | solution.py:757
  71.8 3.1 %collective-permute-done.5 = f32[3,64,128]{2,1,0:T(8,128)S(1)} collective-permute-done((f32[3,64,128]{2,1,0:T(8,128)S(1)}, f32[3,64,128]{2,1,0:T(8,128)S(1)}, u32[]{:S(2)}, u32[]{:S(2)}) %collective-permute-start.5) | collective-permute-done | bytes 98336 | tf_op jit(solution)/shard_map/ppermute | solution.py:757
  74.9 1.9 %collective-permute-start.6 = (f32[2,64,128]{2,1,0:T(8,128)S(1)}, f32[2,64,128]{2,1,0:T(8,128)S(1)}, u32[]{:S(2)}, u32[]{:S(2)}) collective-permute-start(f32[2,64,128]{2,1,0:T(8,128)S(1)} %slice.12), channel_id=1, source_target_pairs={{0,4},{4,8},{8,12},{1,5},{5,9},{9,13},{2,6},{6,10},{10,14},{3,7},{... | collective-permute-start | bytes 196616 | tf_op jit(solution)/shard_map/ppermute | solution.py:750
  76.9 3.6 %collective-permute-start.7 = (f32[2,64,128]{2,1,0:T(8,128)S(1)}, f32[2,64,128]{2,1,0:T(8,128)S(1)}, u32[]{:S(2)}, u32[]{:S(2)}) collective-permute-start(f32[2,64,128]{2,1,0:T(8,128)S(1)} %slice.12), channel_id=1, source_target_pairs={{4,0},{8,4},{12,8},{5,1},{9,5},{13,9},{6,2},{10,6},{14,10},{7,3},{... | collective-permute-start | bytes 196616 | tf_op jit(solution)/shard_map/ppermute | solution.py:750
  80.5 0.0 collective-permute-done.6.left_ref
  80.5 1.9 %collective-permute-done.7.right_ref = f32[2,64,128]{2,1,0:T(8,128)S(1)} collective-permute-done((f32[2,64,128]{2,1,0:T(8,128)S(1)}, f32[2,64,128]{2,1,0:T(8,128)S(1)}, u32[]{:S(2)}, u32[]{:S(2)}) %collective-permute-start.7) | collective-permute-done | bytes 65568 | tf_op jit(solution)/shard_map/ppermute | solution.py:750
  82.4 3.5 %collective-permute-start.8 = (f32[2,8,256]{2,1,0:T(8,128)S(1)}, f32[2,8,256]{2,1,0:T(8,128)S(1)}, u32[]{:S(2)}, u32[]{:S(2)}) collective-permute-start(f32[2,8,256]{2,1,0:T(8,128)S(1)} %get-tuple-element.47), channel_id=1, source_target_pairs={{0,1},{1,2},{2,3},{4,5},{5,6},{6,7},{8,9},{9,10},{10,11},{12,13},{... | collective-permute-start | bytes 49160 | tf_op jit(solution)/shard_map/ppermute | solution.py:750
  85.9 2.4 %collective-permute-start.9 = (f32[2,8,256]{2,1,0:T(8,128)S(1)}, f32[2,8,256]{2,1,0:T(8,128)S(1)}, u32[]{:S(2)}, u32[]{:S(2)}) collective-permute-start(f32[2,8,256]{2,1,0:T(8,128)S(1)} %get-tuple-element.46), channel_id=1, source_target_pairs={{1,0},{2,1},{3,2},{5,4},{6,5},{7,6},{9,8},{10,9},{11,10},{13,12},{... | collective-permute-start | bytes 49160 | tf_op jit(solution)/shard_map/ppermute | solution.py:750
  88.3 0.1 add_convert_fusion.inside_ref
  88.4 0.0 collective-permute-done.8.above_ref
  88.4 3.2 %collective-permute-done.9.below_ref = f32[2,8,256]{2,1,0:T(8,128)S(1)} collective-permute-done((f32[2,8,256]{2,1,0:T(8,128)S(1)}, f32[2,8,256]{2,1,0:T(8,128)S(1)}, u32[]{:S(2)}, u32[]{:S(2)}) %collective-permute-start.9) | collective-permute-done | bytes 16416 | tf_op jit(solution)/shard_map/ppermute | solution.py:750
  91.5 0.0 copy-done.6
  91.5 0.0 copy-done.13
  91.5 7.0 %copy-done.1 = f32[18,36,64,128]{3,2,1,0:T(8,128)S(1)} copy-done((f32[18,36,64,128]{3,2,1,0:T(8,128)S(1)}, f32[18,36,64,128]{3,2,1,0:T(8,128)}, u32[]{:S(2)}) %copy-start.1) | copy-done | bytes 21233688
  98.6 16.1 %shard_map.109 = (f32[18,36,64,128]{3,2,1,0:T(8,128)}, f32[64,128]{1,0:T(8,128)}) custom-call(s32[1]{0:T(128)} %bitcast.member_ref, f32[1810]{0:T(1024)S(1)} %copy-done.6, f32[4]{0:T(128)S(1)} %add_convert_fusion.inside_ref, f32[64,128]{1,0:T(8,128)S(1)} %get-tuple-element.24.wet_ref, f32[64,128]{1,0:T(8,128)S(1)} %copy-done.13, ...), custom_call_target="tpu_custom_call" | custom-call | flops 31850496 | bytes 42467328 | tf_op jit(solution)/shard_map/pallas_call | solution.py:895
  (12 shorter events, 0.0 us)
Async XLA Ops:
  0.6 0.9 copy-start.3
  1.5 0.7 copy-start.5
  2.2 0.8 copy-start.7
  3.0 0.8 copy-start.9
  3.7 0.8 copy-start.11
  4.5 0.8 copy-start.12
  5.3 57.2 %copy-start.2 = (f32[2,10,5,18,128]{4,3,2,1,0:T(8,128)S(1)}, f32[2,10,5,18,128]{4,3,2,1,0:T(8,128)}, u32[]{:S(2)}) copy-start(f32[2,10,5,18,128]{4,3,2,1,0:T(8,128)} %constant.27.clone.table_ref) | copy-start | bytes 2764804
  5.3 57.2 %copy-start.4 = (f32[2,12,8,128]{3,2,1,0:T(8,128)S(1)}, f32[2,12,8,128]{3,2,1,0:T(8,128)}, u32[]{:S(2)}) copy-start(f32[2,12,8,128]{3,2,1,0:T(8,128)} %constant.26.clone.lanes_ref) | copy-start | bytes 294916
  5.3 57.2 %copy-start.8 = (s32[64,128]{1,0:T(8,128)S(1)}, s32[64,128]{1,0:T(8,128)}, u32[]{:S(2)}) copy-start(s32[64,128]{1,0:T(8,128)} %ice_ref.3) | copy-start | bytes 98308
  5.3 57.2 %copy-start.10 = (f32[64,128]{1,0:T(8,128)S(1)}, f32[64,128]{1,0:T(8,128)}, u32[]{:S(2)}) copy-start(f32[64,128]{1,0:T(8,128)} %east_ref.3) | copy-start | bytes 98308
  5.3 86.3 %copy-start.6 = (f32[1810]{0:T(1024)S(1)}, f32[1810]{0:T(1024)}, u32[]{:S(2)}) copy-start(f32[1810]{0:T(1024)} %constant.25.clone.scalar_ref) | copy-start | bytes 21724
  5.3 86.3 %copy-start.13 = (f32[64,128]{1,0:T(8,128)S(1)}, f32[64,128]{1,0:T(8,128)}, u32[]{:S(2)}) copy-start(f32[64,128]{1,0:T(8,128)} %depth_ref.1) | copy-start | bytes 98308
  15.7 7.0 %collective-permute-start = (f32[6,64,128]{2,1,0:T(8,128)S(1)}, f32[6,64,128]{2,1,0:T(8,128)S(1)}, u32[]{:S(2)}, u32[]{:S(2)}) collective-permute-start(f32[6,64,128]{2,1,0:T(8,128)S(1)} %get-tuple-element.26), channel_id=1, source_target_pairs={{0,4},{4,8},{8,12},{1,5},{5,9},{9,13},{2,6},{6,10},{10,14},{3,7},{... | collective-permute-start | bytes 589832 | tf_op jit(solution)/shard_map/ppermute | solution.py:750
  17.7 6.8 %collective-permute-start.1 = (f32[6,64,128]{2,1,0:T(8,128)S(1)}, f32[6,64,128]{2,1,0:T(8,128)S(1)}, u32[]{:S(2)}, u32[]{:S(2)}) collective-permute-start(f32[6,64,128]{2,1,0:T(8,128)S(1)} %get-tuple-element.27), channel_id=1, source_target_pairs={{4,0},{8,4},{12,8},{5,1},{9,5},{13,9},{6,2},{10,6},{14,10},{7,3},{... | collective-permute-start | bytes 589832 | tf_op jit(solution)/shard_map/ppermute | solution.py:750
  24.6 37.8 %collective-permute-start.2 = (f32[656,128]{1,0:T(8,128)S(1)}, f32[656,128]{1,0:T(8,128)S(1)}, u32[]{:S(2)}, u32[]{:S(2)}) collective-permute-start(f32[656,128]{1,0:T(8,128)S(1)} %get-tuple-element.30), channel_id=1, source_target_pairs={{0,1},{1,2},{2,3},{4,5},{5,6},{6,7},{8,9},{9,10},{10,11},{12,13},{... | collective-permute-start | bytes 1007624 | tf_op jit(solution)/shard_map/ppermute | solution.py:750
  28.1 34.4 %collective-permute-start.3 = (f32[656,128]{1,0:T(8,128)S(1)}, f32[656,128]{1,0:T(8,128)S(1)}, u32[]{:S(2)}, u32[]{:S(2)}) collective-permute-start(f32[656,128]{1,0:T(8,128)S(1)} %get-tuple-element.31), channel_id=1, source_target_pairs={{1,0},{2,1},{3,2},{5,4},{6,5},{7,6},{9,8},{10,9},{11,10},{13,12},{... | collective-permute-start | bytes 1007624 | tf_op jit(solution)/shard_map/ppermute | solution.py:750
  54.8 7.6 %copy-start = (f32[18,36,64,128]{3,2,1,0:T(8,128)}, f32[18,36,64,128]{3,2,1,0:T(8,128)S(1)}, u32[]{:S(2)}) copy-start(f32[18,36,64,128]{3,2,1,0:T(8,128)S(1)} %get-tuple-element.41.kept_ref) | copy-start | bytes 63700996
  64.7 4.3 %collective-permute-start.4 = (f32[64,128]{1,0:T(8,128)S(1)}, f32[64,128]{1,0:T(8,128)S(1)}, u32[]{:S(2)}, u32[]{:S(2)}) collective-permute-start(f32[64,128]{1,0:T(8,128)S(1)} %get-tuple-element.38.own_ref), channel_id=1, source_target_pairs={{0,16},{16,0},{1,17},{17,1},{2,18},{18,2},{3,19},{19,3},{4,20},{20... | collective-permute-start | bytes 98312 | tf_op jit(solution)/shard_map/ppermute | solution.py:757
  70.2 4.7 %collective-permute-start.5 = (f32[3,64,128]{2,1,0:T(8,128)S(1)}, f32[3,64,128]{2,1,0:T(8,128)S(1)}, u32[]{:S(2)}, u32[]{:S(2)}) collective-permute-start(f32[3,64,128]{2,1,0:T(8,128)S(1)} %get-tuple-element.40), channel_id=1, source_target_pairs={{0,16},{16,0},{1,17},{17,1},{2,18},{18,2},{3,19},{19,3},{4,20},{20... | collective-permute-start | bytes 294920 | tf_op jit(solution)/shard_map/ppermute | solution.py:757
  74.9 5.6 %collective-permute-start.6 = (f32[2,64,128]{2,1,0:T(8,128)S(1)}, f32[2,64,128]{2,1,0:T(8,128)S(1)}, u32[]{:S(2)}, u32[]{:S(2)}) collective-permute-start(f32[2,64,128]{2,1,0:T(8,128)S(1)} %slice.12), channel_id=1, source_target_pairs={{0,4},{4,8},{8,12},{1,5},{5,9},{9,13},{2,6},{6,10},{10,14},{3,7},{... | collective-permute-start | bytes 196616 | tf_op jit(solution)/shard_map/ppermute | solution.py:750
  76.9 5.5 %collective-permute-start.7 = (f32[2,64,128]{2,1,0:T(8,128)S(1)}, f32[2,64,128]{2,1,0:T(8,128)S(1)}, u32[]{:S(2)}, u32[]{:S(2)}) collective-permute-start(f32[2,64,128]{2,1,0:T(8,128)S(1)} %slice.12), channel_id=1, source_target_pairs={{4,0},{8,4},{12,8},{5,1},{9,5},{13,9},{6,2},{10,6},{14,10},{7,3},{... | collective-permute-start | bytes 196616 | tf_op jit(solution)/shard_map/ppermute | solution.py:750
  82.4 5.9 %collective-permute-start.8 = (f32[2,8,256]{2,1,0:T(8,128)S(1)}, f32[2,8,256]{2,1,0:T(8,128)S(1)}, u32[]{:S(2)}, u32[]{:S(2)}) collective-permute-start(f32[2,8,256]{2,1,0:T(8,128)S(1)} %get-tuple-element.47), channel_id=1, source_target_pairs={{0,1},{1,2},{2,3},{4,5},{5,6},{6,7},{8,9},{9,10},{10,11},{12,13},{... | collective-permute-start | bytes 49160 | tf_op jit(solution)/shard_map/ppermute | solution.py:750
  85.9 5.6 %collective-permute-start.9 = (f32[2,8,256]{2,1,0:T(8,128)S(1)}, f32[2,8,256]{2,1,0:T(8,128)S(1)}, u32[]{:S(2)}, u32[]{:S(2)}) collective-permute-start(f32[2,8,256]{2,1,0:T(8,128)S(1)} %get-tuple-element.46), channel_id=1, source_target_pairs={{1,0},{2,1},{3,2},{5,4},{6,5},{7,6},{9,8},{10,9},{11,10},{13,12},{... | collective-permute-start | bytes 49160 | tf_op jit(solution)/shard_map/ppermute | solution.py:750
  91.5 7.0 %copy-start.1 = (f32[18,36,64,128]{3,2,1,0:T(8,128)S(1)}, f32[18,36,64,128]{3,2,1,0:T(8,128)}, u32[]{:S(2)}) copy-start(f32[18,36,64,128]{3,2,1,0:T(8,128)} %copy-done) | copy-start | bytes 63700996

commit v2 on v1

v2 whole, which is shorter than its diff:
```python
import functools
import math

import jax
import jax.numpy as jnp
import numpy as np
from jax import lax
from jax.experimental import pallas as pl
from jax.experimental.pallas import tpu as pltpu
from jax.sharding import PartitionSpec as P

ND = 36
NF = 36
STEPS = 2
JAC = 4


def extended(cells, sides, width):
    for axis, dim in sides:
        count = lax.axis_size(axis)
        ends = count - 1
        head = lax.slice_in_dim(cells, 0, width, axis=dim)
        tail = lax.slice_in_dim(cells, cells.shape[dim] - width, cells.shape[dim], axis=dim)
        cells = jnp.concatenate(
            [
                lax.ppermute(tail, axis, [(i, (i + 1) % count) for i in range(ends)]),
                cells,
                lax.ppermute(head, axis, [((i + 1) % count, i) for i in range(ends)]),
            ],
            axis=dim,
        )
    return cells


def tables(index):
    freq_index = (index // ND).astype(jnp.float32)
    angle_index = (index % ND).astype(jnp.float32)
    heading = 2.0 * math.pi * angle_index / ND
    return (
        jnp.cos(heading),
        jnp.sin(heading),
        jnp.power(1.1, -freq_index),
        jnp.power(1.1, freq_index - (NF - 1)),
        0.5 + 0.5 * freq_index / (NF - 1),
    )


def column(values):
    return values[:, None, None]


def advect(spectra, wet_cells, speed_x, speed_y):
    padded = extended(spectra, (("slab", 1), ("sect", 2)), 1)
    upper_rows = padded[:, :-2, 1:-1]
    lower_rows = padded[:, 2:, 1:-1]
    left_cells = padded[:, 1:-1, :-2]
    right_cells = padded[:, 1:-1, 2:]
    change = (
        jnp.maximum(speed_x, 0.0) * (spectra - upper_rows)
        + jnp.minimum(speed_x, 0.0) * (lower_rows - spectra)
        + jnp.maximum(speed_y, 0.0) * (spectra - left_cells)
        + jnp.minimum(speed_y, 0.0) * (right_cells - spectra)
    )
    return (spectra - change) * wet_cells


def forcing(spectra, energy, wind_east, wind_north, ice_cover, cosine, sine, high_ratio):
    project = cosine * wind_east + sine * wind_north
    growth = 0.5 * high_ratio * jnp.square(jnp.maximum(project, 0.0)) * (1.0 - ice_cover)
    return spectra * (1.0 + growth) / (1.0 + 2.0 * high_ratio * jnp.square(energy))


def stress_weights(cosine, sine, shoaling):
    return jnp.stack(
        [shoaling * (cosine * cosine + 1.0) - 0.5, shoaling * (sine * sine + 1.0) - 0.5]
    )


def surge_solve(stress):
    padded = extended(stress, (("slab", 1), ("sect", 2)), 1)
    source_term = -(
        padded[0, 2:, 1:-1]
        + padded[0, :-2, 1:-1]
        - 2.0 * stress[0]
        + (padded[1, 1:-1, 2:] + padded[1, 1:-1, :-2] - 2.0 * stress[1])
    )
    surge_level = source_term / 4.5
    for _ in range(JAC):
        neighbours = extended(surge_level, (("slab", 0), ("sect", 1)), 1)
        surge_level = (
            source_term
            + neighbours[2:, 1:-1]
            + neighbours[:-2, 1:-1]
            + neighbours[1:-1, 2:]
            + neighbours[1:-1, :-2]
        ) / 4.5
    return surge_level


def general(spectrum, land_mask, ice_mask, wind_u, wind_v, depth):
    groups = lax.axis_size("comp")
    member = lax.axis_index("comp")
    local_comp, block_rows, block_cols = spectrum.shape
    point_rows = block_rows // groups
    total_comp = ND * NF
    wet_cells = (1 - land_mask).astype(jnp.float32)
    ice_cover = ice_mask.astype(jnp.float32)

    def own_rows(values):
        return lax.dynamic_slice_in_dim(values, member * point_rows, point_rows, values.ndim - 2)

    own_index = member * local_comp + jnp.arange(local_comp, dtype=jnp.int32)
    cosine, sine, low_ratio, high_ratio, shoaling = tables(own_index)
    spectra = spectrum * wet_cells
    for _ in range(STEPS):
        spectra = advect(
            spectra, wet_cells, column(0.7 * low_ratio * cosine), column(0.7 * low_ratio * sine)
        )
    points = lax.all_to_all(spectra, "comp", split_axis=1, concat_axis=0, tiled=True)
    cosine_full, sine_full, _, high_full, shoal_full = tables(
        jnp.arange(total_comp, dtype=jnp.int32)
    )
    energy = jnp.sum(points, axis=0) / total_comp
    sourced = forcing(
        points,
        energy,
        own_rows(wind_u),
        own_rows(wind_v),
        own_rows(ice_cover),
        column(cosine_full),
        column(sine_full),
        column(high_full),
    )
    stress = (
        jnp.einsum(
            "sk,krc->src",
            stress_weights(cosine_full, sine_full, shoal_full),
            sourced,
            precision=lax.Precision.HIGHEST,
        )
        / total_comp
    )
    stress_block = lax.all_gather(stress, "comp", axis=1, tiled=True)
    level_block = surge_solve(stress_block)
    final_energy = jnp.sum(sourced, axis=0) / total_comp
    damped = sourced / (
        1.0 + 4.0 * final_energy / (jnp.square(own_rows(depth) + own_rows(level_block)) + 1.0)
    )
    result = lax.all_to_all(damped, "comp", split_axis=0, concat_axis=1, tiled=True)
    return (result, level_block)


LANES = 128
SUB = 8
CLASSES = 10
KINDS = 5
GROUP = 3
GROUPS = ND // GROUP
CORNERS = 8


def class_of(direction):
    folded = direction % 18
    return folded if folded <= 9 else 18 - folded


def heads_down(direction):
    return direction < 9 or direction >= 27


def heads_right(direction):
    return direction < 18


def row_slot(direction):
    if direction < 9:
        return direction
    return direction - 18 if direction >= 27 else direction - 9


def numpy_tables(members, freqs):
    j = np.arange(members * freqs, dtype=np.float64)
    heading = 2.0 * np.pi * np.arange(ND) / ND
    cosine, sine = np.cos(heading), np.sin(heading)
    low = 1.1 ** (-j)
    high = 1.1 ** (j - (NF - 1))
    shoal = 0.5 + 0.5 * j / (NF - 1)
    step_x = 0.7 * low[:, None] * np.abs(cosine)
    step_y = 0.7 * low[:, None] * np.abs(sine)
    keep = 1.0 - step_x - step_y
    alpha, beta, scale = step_x / keep, step_y / keep, keep * keep
    classes = np.arange(CLASSES)
    square = np.broadcast_to(cosine * cosine, alpha.shape)
    scalars = np.stack(
        [
            alpha[:, classes],
            beta[:, classes],
            scale[:, classes],
            np.broadcast_to(high[:, None], (j.size, CLASSES)),
            np.broadcast_to(shoal[:, None], (j.size, CLASSES)),
        ],
        axis=-1,
    ).astype(np.float32)

    kinds = np.stack(
        [
            2.0 * beta,
            beta * beta,
            alpha * beta,
            scale,
            scale * square,
            np.broadcast_to(high[:, None], alpha.shape),
            np.broadcast_to(cosine, alpha.shape),
            np.broadcast_to(sine, alpha.shape),
        ]
    )
    lanes = np.zeros((members, GROUPS, 8, LANES), np.float32)
    packed = kinds.reshape(8, members, freqs, GROUPS, GROUP)
    packed = np.repeat(packed.transpose(1, 3, 0, 4, 2), 2, axis=-1)
    lanes[..., : GROUP * 2 * freqs] = packed.reshape(members, GROUPS, 8, -1)

    rows = np.stack(
        [2.0 * alpha, alpha * alpha, alpha * beta, scale, np.broadcast_to(high[:, None], alpha.shape)]
    )[:, :, classes]
    rows = rows.reshape(5, members, freqs, CLASSES).transpose(1, 3, 0, 2)
    rows = np.broadcast_to(rows[..., None], rows.shape + (LANES,)).astype(np.float32)
    return scalars.reshape(-1), lanes, rows


def iota(shape, axis):
    return lax.broadcasted_iota(jnp.int32, shape, axis)


def spread(values, column):
    return jnp.broadcast_to(values[:, column : column + 1], values.shape)


def shift_rows(values, step):
    rows = values.shape[0]
    edge = 0 if step > 0 else rows - 1
    moved = pltpu.roll(values, step % rows, 0)
    return jnp.where(iota(values.shape, 0) == edge, 0.0, moved)


def shift_lanes(values, step):
    lanes = values.shape[1]
    edge = 0 if step > 0 else lanes - 1
    moved = pltpu.roll(values, step % lanes, 1)
    return jnp.where(iota(values.shape, 1) == edge, 0.0, moved)


DEPTH = 3


def slot_base(quadrant):
    return (0, 9, 9, 18)[quadrant]


def class_index(direction):
    folded = lax.rem(direction, 18)
    return jnp.where(folded <= 9, folded, 18 - folded)


def pack_kernel(
    freqs, member_ref, lanes_hbm, table_hbm, land_hbm, ice_hbm, east_hbm, north_hbm, spectrum_ref,
    growth_ref, wet_ref, right_ref, left_ref, down_ref, up_ref, edges_ref,
    kept_ref, lanes_ref, table_ref, land_ref, ice_ref, east_ref, north_ref, small_sems, sems,
):
    member = member_ref[0]
    small = [
        pltpu.make_async_copy(source, target, small_sems.at[index])
        for index, (source, target) in enumerate(
            (
                (land_hbm, land_ref),
                (ice_hbm, ice_ref),
                (east_hbm, east_ref),
                (north_hbm, north_ref),
                (lanes_hbm.at[member], lanes_ref),
                (table_hbm.at[member], table_ref),
            )
        )
    ]
    for copy in small:
        copy.start()

    rows = land_ref.shape[0]
    blocks_ref = kept_ref.reshape(freqs, ND, rows, LANES)

    def fetch(group):
        part = (slice(None), pl.ds(group * GROUP, GROUP))
        return pltpu.make_async_copy(spectrum_ref.at[part], blocks_ref.at[part], sems.at[group])

    for group in range(DEPTH):
        fetch(group).start()
    edges_ref[...] = jnp.zeros_like(edges_ref)
    for copy in small:
        copy.wait()

    wet_cells = (1 - land_ref[...]).astype(jnp.float32)
    wet_ref[...] = wet_cells
    open_water = 0.5 * (1.0 - ice_ref[...].astype(jnp.float32))
    shape = wet_cells.shape
    tiles = rows // SUB
    for direction in range(ND):
        angle = 2.0 * math.pi * direction / ND
        project = math.cos(angle) * east_ref[...] + math.sin(angle) * north_ref[...]
        growth_ref[direction] = open_water * jnp.square(jnp.maximum(project, 0.0))

    lane = iota(shape, 1)
    even = lane % 2 == 0
    tile_lane = iota((SUB, LANES), 1)
    down_ref[pl.ds(2 * 18 * freqs, CORNERS), :] = jnp.zeros((CORNERS, LANES), jnp.float32)
    up_ref[pl.ds(2 * 18 * freqs, CORNERS), :] = jnp.zeros((CORNERS, LANES), jnp.float32)

    half = GROUPS // 2
    for to_right in (True, False):
        target_ref = right_ref if to_right else left_ref

        def gather(index, carry):
            group = index + (0 if to_right else half)
            fetch(group).wait()

            @pl.when(group + DEPTH < GROUPS)
            def _():
                fetch(group + DEPTH).start()

            packed = [jnp.zeros((SUB, LANES), jnp.float32) for _ in range(tiles)]
            for i in range(GROUP):
                for j in range(freqs):
                    place = i * 2 * freqs + 2 * j
                    here = (tile_lane >= place) & (tile_lane < place + 2)
                    turn = (place + 2 if to_right else place) % LANES
                    first = pl.multiple_of((j * ND + group * GROUP + i) * rows, SUB)
                    for tile in range(tiles):
                        cells = kept_ref[pl.ds(first + tile * SUB, SUB), :]
                        packed[tile] = jnp.where(here, pltpu.roll(cells, turn, 1), packed[tile])
            for tile in range(tiles):
                target_ref[index, tile * SUB : (tile + 1) * SUB, :] = packed[tile]
            return carry

        lax.fori_loop(0, half, gather, 0)

    pending = []
    for group in range(GROUPS):
        to_right, fore = group < half, 1 if heads_down(group * GROUP) else -1
        ahead, behind = (LANES - 1, LANES - 2) if to_right else (0, 1)
        wet_near, wet_far = spread(wet_cells, ahead), spread(wet_cells, behind)
        near_even = not to_right
        target_ref, index = (right_ref, group) if to_right else (left_ref, group - half)
        values = target_ref[index] * jnp.where(even == near_even, wet_near, wet_far)
        near = pltpu.roll(values, 1 if near_even else LANES - 1, 1)
        table = lanes_ref[group]
        follow = wet_near * (table[1:2] * values + table[2:3] * shift_rows(near, fore))
        message = jnp.where(even == near_even, values, follow)
        pending.append((target_ref, index, jnp.where(lane == LANES - 1, wet_near, message)))
        if group:
            place_ref, index, message = pending.pop(0)
            place_ref[index] = message
    place_ref, index, message = pending.pop()
    place_ref[index] = message

    pending = []
    for direction in range(ND):
        to_down = heads_down(direction)
        near_row, far_row = (rows - 1, rows - 2) if to_down else (0, 1)
        wet_near = wet_cells[near_row : near_row + 1, :]
        wet_far = wet_cells[far_row : far_row + 1, :]
        table = table_ref.at[class_of(direction)]
        near = kept_ref[pl.ds(direction * rows + near_row, freqs, stride=ND * rows), :] * wet_near
        far = kept_ref[pl.ds(direction * rows + far_row, freqs, stride=ND * rows), :] * wet_far
        beside = shift_lanes(near, 1 if heads_right(direction) else -1)
        follow = wet_near * (table[1] * far + table[2] * beside)
        slot = row_slot(direction) * freqs
        pending.append((down_ref if to_down else up_ref, slot, near, follow))
        if len(pending) > 2 or direction == ND - 1:
            for place_ref, slot, near, follow in pending:
                place_ref[slot : slot + freqs, :] = near
                place_ref[18 * freqs + slot : 18 * freqs + slot + freqs, :] = follow
            pending = []


def corner_kernel(
    freqs, wet_ref, right_ref, left_ref, down_in, up_in, _after, down_ref, up_ref, rows_ref, sems
):
    rows = wet_ref.shape[0]
    last = iota((1, LANES), 1) == LANES - 1
    rows_ref[...] = jnp.zeros_like(rows_ref)
    for which, row in ((0, rows - 1), (1, 0)):
        for i in range(6):
            source = right_ref if i < 3 else left_ref
            if which == 0:
                index = i if i < 3 else i
            else:
                index = i + 3 if i < 3 else i - 3
            column = 0 if i < 3 else LANES - 1
            own = jnp.broadcast_to(wet_ref[row : row + 1, column : column + 1], (1, LANES))
            rows_ref[which, i : i + 1, :] = jnp.where(last, own, source[index, row : row + 1, :])
    start = 2 * 18 * freqs
    copies = [
        pltpu.make_async_copy(
            rows_ref.at[which], ref.at[pl.ds(start, CORNERS), :], sems.at[which]
        )
        for which, ref in ((0, down_ref), (1, up_ref))
    ]
    for copy in copies:
        copy.start()
    for copy in copies:
        copy.wait()


AHEAD = 3


def main_kernel(
    freqs, start, stop, member_ref, scalar_ref, wet_ref, growth_ref, spectrum_ref, *refs
):
    if start:
        _after, _kept_in, a_in, b_in, energy_in, *refs = refs
    kept_ref, a_ref, b_ref, energy_ref, ring_ref, sems, *first_refs = refs
    member = member_ref[0]
    nought = jnp.minimum(member, 0)
    rows = wet_ref.shape[0]
    tiles = rows // SUB

    def fetch(j):
        slot = lax.rem(j, AHEAD)
        return pltpu.make_async_copy(spectrum_ref.at[j], ring_ref.at[slot], sems.at[slot])

    for j in range(start, min(start + AHEAD, stop)):
        fetch(jnp.int32(j)).start()

    lane = iota((SUB, LANES), 1)
    sub = iota((SUB, LANES), 0)
    not_first = jnp.where(lane == 0, 0.0, 1.0)
    not_last = jnp.where(lane == LANES - 1, 0.0, 1.0)
    top, bottom = sub == 0, sub == SUB - 1
    energy_ref[...] = energy_in[...] if start else jnp.zeros_like(energy_ref)
    for first_ref in first_refs:
        first_ref[...] = jnp.zeros_like(first_ref)

    def tile_at(tile):
        return pl.ds(tile * SUB, SUB)

    def row_shift(quadrant):
        return -1 if quadrant in (0, 3) else 1

    def parts_of(kind):
        if kind == 0:
            return ((0, 0, 0), (9, 1, 9), (18, 2, 0), (27, 3, 9))
        return ((kind, 0, kind), (18 - kind, 1, kind), (18 + kind, 2, kind), (36 - kind, 3, kind))

    def frequency(j, carry):
        fetch(j).wait()
        slot = lax.rem(j, AHEAD)
        base = (member * freqs + j) * CLASSES * KINDS
        at = [pl.ds(pl.multiple_of(j * rows, SUB) + t * SUB, SUB) for t in range(tiles)]

        def speeds(part):
            at_class = base + part[2] * KINDS
            beta = scalar_ref[at_class + 1]
            return scalar_ref[at_class], beta * (not_first if part[1] in (0, 1) else not_last)

        def beside(cells, quadrant):
            return pltpu.roll(cells, 1 if quadrant in (0, 1) else LANES - 1, 1)

        def first_step(kind):
            parts = parts_of(kind)
            speed = [speeds(part) for part in parts]
            wet = [wet_ref[tile_at(t), :] for t in range(tiles)]
            for (direction, quadrant, _), (alpha, across) in zip(parts, speed):
                shift = row_shift(quadrant)
                edge = top if shift < 0 else bottom
                target = first_refs[kind % 2 * 4 + quadrant]
                cells = [ring_ref[slot, direction, tile_at(t), :] * wet[t] for t in range(tiles)]
                turned = [pltpu.roll(cells[t], -shift % SUB, 0) for t in range(tiles)]
                for t in range(tiles):
                    before = turned[t + shift] if 0 <= t + shift < tiles else 0.0
                    ahead = jnp.where(edge, before, turned[t])
                    after = cells[t] + alpha * ahead + across * beside(cells[t], quadrant)
                    target[tile_at(t + 1), :] = wet[t] * after

        def second_step(kind):
            parts = parts_of(kind)
            scale, high = scalar_ref[base + kind * KINDS + 2], scalar_ref[base + 3]
            scaled_high = scale * high
            speed = [speeds(part) for part in parts]
            for t in range(tiles):
                moved, grown = [], []
                for (direction, quadrant, _), (alpha, across) in zip(parts, speed):
                    source = first_refs[kind % 2 * 4 + quadrant]
                    cells = source[tile_at(t + 1), :]
                    ahead = source[pl.ds((t + 1) * SUB + row_shift(quadrant) + nought, SUB), :]
                    after = cells + alpha * ahead + across * beside(cells, quadrant)
                    kept_ref[j, direction, tile_at(t), :] = after
                    moved.append(after)
                    grown.append(growth_ref[direction, tile_at(t), :] * after)
                if kind == 0:
                    plain_x, plain_y = scale * (moved[0] + moved[2]), scale * (moved[1] + moved[3])
                    grown_x = plain_x + scaled_high * (grown[0] + grown[2])
                    grown_y = plain_y + scaled_high * (grown[1] + grown[3])
                    square = math.cos(0.5 * math.pi) ** 2
                    energy_ref[tile_at(t), :] += plain_x + plain_y
                    a_ref[at[t], :] = grown_x + grown_y
                    b_ref[at[t], :] = grown_x + square * grown_y
                else:
                    plain = scale * ((moved[0] + moved[1]) + (moved[2] + moved[3]))
                    whole = plain + scaled_high * ((grown[0] + grown[1]) + (grown[2] + grown[3]))
                    square = math.cos(2.0 * math.pi * kind / ND) ** 2
                    energy_ref[tile_at(t), :] += plain
                    a_ref[at[t], :] += whole
                    b_ref[at[t], :] += square * whole

        first_step(0)
        for kind in range(CLASSES - 1):
            if kind + 1 < CLASSES - 1:
                first_step(kind + 1)
            second_step(kind)

        @pl.when(j + AHEAD < stop)
        def _():
            fetch(j + AHEAD).start()

        return carry

    lax.fori_loop(start, stop, frequency, 0)


def edge_rows(freqs, to_down, direction, at):
    first = ((0 if to_down else 18) + row_slot(direction)) * freqs * SUB
    return pl.ds(first + at, freqs, stride=SUB)


def enter_kernel(
    freqs, member_ref, lanes_ref, table_ref, wet_ref, right_ref, left_ref, down_ref, up_ref,
    _edges_in, energy_in, columns_ref, edges_ref, energy_ref,
):
    member = member_ref[0]
    wet_cells = wet_ref[...]
    shape = wet_cells.shape
    rows = shape[0]
    lane = iota(shape, 1)
    row = iota(shape, 0)
    even = lane % 2 == 0
    width = 2 * freqs
    used = lane < GROUP * width
    energy = energy_in[...]
    start = 2 * 18 * freqs

    for to_right in (True, False):
        near_column, far_column = (0, 1) if to_right else (LANES - 1, LANES - 2)
        near_even = to_right
        wet_near, wet_far = spread(wet_cells, near_column), spread(wet_cells, far_column)
        total = jnp.zeros(shape, jnp.float32)
        for index in range(GROUPS // 2):
            group = index if to_right else index + GROUPS // 2
            to_down = heads_down(group * GROUP)
            fore = 1 if to_down else -1
            message = (right_ref if to_right else left_ref)[index]
            table = lanes_ref[member, group]
            turn = LANES - 1 if near_even else 1
            entered = pltpu.roll(message, turn, 1)
            corner_index = index if to_down else (index - 3 if to_right else index + 3)
            corner = (down_ref if to_down else up_ref)[pl.ds(start + corner_index, 1), :]
            edge = 0 if to_down else rows - 1
            paths = corner[:, LANES - 1 :] + message[edge : edge + 1, LANES - 1 :]
            corner = pltpu.roll(jnp.broadcast_to(corner, (SUB, LANES)), turn, 1)[0:1]
            corner = jnp.broadcast_to(paths, (1, LANES)) * corner
            diagonal = shift_rows(wet_near * entered, fore)
            diagonal = jnp.where(row == edge, jnp.broadcast_to(corner, shape), diagonal)
            near = wet_near * (table[0:1] * entered + message + table[2:3] * diagonal)
            far = wet_near * wet_far * (table[1:2] * message)
            change = jnp.where(used, jnp.where(even == near_even, near, far), 0.0)
            columns_ref[group] = change
            total += table[3:4] * change
        total += pltpu.roll(total, LANES - width, 1) + pltpu.roll(total, LANES - 2 * width, 1)
        target = 0 if to_right else LANES - 2
        inside = (lane >= target) & (lane < target + 2)
        for j in range(freqs):
            turned = pltpu.roll(total, (target - 2 * j) % LANES, 1)
            energy += jnp.where(inside, turned, 0.0)
    energy_ref[...] = energy

    for to_down in (True, False):
        near_row, far_row = (0, 1) if to_down else (rows - 1, rows - 2)
        message_ref = down_ref if to_down else up_ref
        wet_near = wet_cells[near_row : near_row + 1, :]
        wet_both = wet_near * wet_cells[far_row : far_row + 1, :]
        totals = [jnp.zeros((freqs, LANES), jnp.float32) for _ in range(2)]
        for direction in range(ND):
            if heads_down(direction) != to_down:
                continue
            slot = row_slot(direction) * freqs
            entered = message_ref[slot : slot + freqs, :]
            follow = message_ref[18 * freqs + slot : 18 * freqs + slot + freqs, :]
            table = table_ref.at[member, class_of(direction)]
            side = 1 if heads_right(direction) else -1
            diagonal = shift_lanes(wet_near * entered, side)
            near = wet_near * (table[0] * entered + follow + table[2] * diagonal)
            far = wet_both * (table[1] * entered)
            for place, (change, at) in enumerate(((near, near_row), (far, far_row))):
                edges_ref[edge_rows(freqs, to_down, direction, at % SUB), :] = change
                totals[place] += table[3] * change
        for total, at in zip(totals, (near_row, far_row)):
            energy_ref[at : at + 1, :] += jnp.sum(total, axis=0, keepdims=True)


def entered_kernel(
    freqs, member_ref, lanes_ref, table_ref, ice_ref, east_ref, north_ref, growth_ref, columns_ref,
    edges_ref, a_in, b_in, a_ref, b_ref,
):
    member = member_ref[0]
    shape = ice_ref.shape
    rows = shape[0]
    lane = iota(shape, 1)
    even = lane % 2 == 0
    width = 2 * freqs
    a_ref[...] = a_in[...]
    b_ref[...] = b_in[...]

    for to_right in (True, False):
        near_column, far_column = (0, 1) if to_right else (LANES - 1, LANES - 2)

        def packed_field(values):
            return jnp.where(
                even == to_right, spread(values, near_column), spread(values, far_column)
            )

        east, north = packed_field(east_ref[...]), packed_field(north_ref[...])
        open_water = 0.5 * (1.0 - packed_field(ice_ref[...].astype(jnp.float32)))
        sums = [jnp.zeros(shape, jnp.float32) for _ in range(2)]
        for index in range(GROUPS // 2):
            group = index if to_right else index + GROUPS // 2
            table = lanes_ref[member, group]
            project = table[6:7] * east + table[7:8] * north
            growth = open_water * jnp.square(jnp.maximum(project, 0.0))
            grown = columns_ref[group] * (1.0 + table[5:6] * growth)
            sums[0] += table[3:4] * grown
            sums[1] += table[4:5] * grown
        sums = [
            part + pltpu.roll(part, LANES - width, 1) + pltpu.roll(part, LANES - 2 * width, 1)
            for part in sums
        ]
        target = 0 if to_right else LANES - 2
        inside = (lane >= target) & (lane < target + 2)
        for j in range(freqs):
            turn = (target - 2 * j) % LANES
            block = slice(j * rows, (j + 1) * rows)
            place = [jnp.where(inside, pltpu.roll(part, turn, 1), 0.0) for part in sums]
            a_ref[block, :] += place[0]
            b_ref[block, :] += place[1]

    for to_down in (True, False):
        near_row, far_row = (0, 1) if to_down else (rows - 1, rows - 2)
        totals = [jnp.zeros((freqs, LANES), jnp.float32) for _ in range(4)]
        for direction in range(ND):
            if heads_down(direction) != to_down:
                continue
            table = table_ref.at[member, class_of(direction)]
            square = math.cos(2.0 * math.pi * direction / ND) ** 2
            for place, at in enumerate((near_row, far_row)):
                change = edges_ref[edge_rows(freqs, to_down, direction, at % SUB), :]
                growth = growth_ref[direction, at : at + 1, :]
                grown = (table[3] * change) * (1.0 + table[4] * growth)
                totals[2 * place] += grown
                totals[2 * place + 1] += square * grown
        for place, at in enumerate((near_row, far_row)):
            picked = pl.ds(at, freqs, stride=rows)
            a_ref[picked, :] += totals[2 * place]
            b_ref[picked, :] += totals[2 * place + 1]


def stress_kernel(
    freqs, member_ref, scalar_ref, wet_ref, a_ref, b_ref, own_ref, other_ref, sums_ref, square_ref
):
    member = member_ref[0]
    wet_cells = wet_ref[...]
    rows = wet_cells.shape[0]
    energy = wet_cells * (own_ref[...] + other_ref[...]) / (ND * NF)
    square = jnp.square(energy)
    square_ref[...] = square

    sums = [jnp.zeros(wet_cells.shape, jnp.float32) for _ in range(3)]
    for j in range(freqs):
        base = (member * freqs + j) * CLASSES * KINDS
        high, shoal = scalar_ref[base + 3], scalar_ref[base + 4]
        block = slice(j * rows, (j + 1) * rows)
        ratio = wet_cells / (1.0 + (2.0 * high) * square)
        whole = ratio * a_ref[block, :]
        along = ratio * b_ref[block, :]
        sums[0] += shoal * along + (shoal - 0.5) * whole
        sums[1] += (2.0 * shoal - 0.5) * whole - shoal * along
        sums[2] += whole
    for index in range(3):
        sums_ref[index] = sums[index] / (ND * NF)


def total_kernel(own_ref, other_ref, sums_ref, stress_ref):
    sums_ref[...] = own_ref[...] + other_ref[...]
    stress_ref[...] = sums_ref[0:2]


def strip_kernel(stress_ref, left_ref, right_ref, beside_ref, top_ref, bottom_ref):
    rows = stress_ref.shape[1]
    low_half = iota((rows, LANES), 1) < LANES // 2
    for index in range(2):
        beside = jnp.where(low_half, right_ref[index], left_ref[index])
        beside_ref[index] = beside
        for target, first in ((top_ref, 0), (bottom_ref, rows - SUB)):
            target[index, :, 0:LANES] = stress_ref[index, first : first + SUB, :]
            target[index, :, LANES:] = beside[first : first + SUB, :]


SLOTS = 3


def final_kernel(
    freqs, member_ref, scalar_ref, wet_ref, depth_ref, square_ref, sums_ref, beside_ref, above_ref, below_ref,
    growth_ref, kept_ref, columns_ref, edges_ref,
    result_ref, level_ref, ratio_ref, ring_ref, sems,
):
    member = member_ref[0]
    wet_cells = wet_ref[...]
    rows = wet_cells.shape[0]
    slab, slabs = lax.axis_index("slab"), lax.axis_size("slab")
    sect, sects = lax.axis_index("sect"), lax.axis_size("sect")
    above_ok = jnp.where(slab > 0, 1.0, 0.0)
    below_ok = jnp.where(slab < slabs - 1, 1.0, 0.0)
    left_ok = jnp.where(sect > 0, 1.0, 0.0)
    right_ok = jnp.where(sect < sects - 1, 1.0, 0.0)

    def framed(index):
        middle = jnp.concatenate([sums_ref[index], beside_ref[index]], axis=1)
        return jnp.concatenate([middle, below_ref[index], above_ref[index]], axis=0)

    def around(values, axis):
        size = values.shape[axis]
        return pltpu.roll(values, 1, axis) + pltpu.roll(values, size - 1, axis)

    stress_x, stress_y = framed(0), framed(1)
    frame = stress_x.shape
    frame_row, frame_lane = iota(frame, 0), iota(frame, 1)
    row_ok = jnp.where(frame_row < rows, 1.0, jnp.where(frame_row < rows + SUB, below_ok, above_ok))
    lane_ok = jnp.where(
        frame_lane < LANES, 1.0, jnp.where(frame_lane < LANES + LANES // 2, right_ok, left_ok)
    )
    inside = row_ok * lane_ok / 4.5
    source = -((around(stress_x, 0) - 2.0 * stress_x) + (around(stress_y, 1) - 2.0 * stress_y))
    level = inside * source
    for _ in range(JAC):
        level = inside * (source + around(level, 0) + around(level, 1))
    level = level[:rows, :LANES]
    level_ref[...] = level
    damping = 1.0 + 4.0 * sums_ref[2] / (jnp.square(depth_ref[...] + level) + 1.0)
    square = square_ref[...]
    tiles = rows // SUB
    for j in range(freqs):
        high = scalar_ref[(member * freqs + j) * CLASSES * KINDS + 3]
        ratio = wet_cells / ((1.0 + (2.0 * high) * square) * damping)
        ratio_ref[0, j] = ratio
        ratio_ref[1, j] = high * ratio

    tile_lane = iota((SUB, LANES), 1)
    quarter = ND // 4

    def send(direction, slot):
        return pltpu.make_async_copy(
            ring_ref.at[slot], result_ref.at[:, pl.ds(direction, 1)], sems.at[slot]
        )

    for quadrant in range(4):
        to_right, to_down = quadrant in (0, 1), quadrant in (0, 3)
        target = 0 if to_right else LANES - 2
        at_side = (tile_lane >= target) & (tile_lane < target + 2)
        bank, edge_tile = (0, 0) if to_down else (1, tiles - 1)

        def one(index, carry):
            direction = quadrant * quarter + index
            slot = lax.rem(direction, SLOTS)

            @pl.when(direction >= SLOTS)
            def _():
                send(direction - SLOTS, slot).wait()

            kind = class_index(direction)
            group = lax.div(direction, GROUP)
            offset = 2 * freqs * lax.rem(direction, GROUP)
            row_at = (bank * 18 + direction - slot_base(quadrant)) * freqs
            aligned = [
                pltpu.roll(
                    columns_ref[group, t * SUB : (t + 1) * SUB, :],
                    lax.rem(target - offset + LANES, LANES),
                    1,
                )
                for t in range(tiles)
            ]
            growth = [growth_ref[direction, t * SUB : (t + 1) * SUB, :] for t in range(tiles)]
            def damped(j):
                scale = scalar_ref[((member * freqs + j) * CLASSES + kind) * KINDS + 2]
                result = []
                for t in range(tiles):
                    part = slice(t * SUB, (t + 1) * SUB)
                    entered = pltpu.roll(aligned[t], (LANES - 2 * j) % LANES, 1)
                    value = kept_ref[j, direction, part, :] + jnp.where(at_side, entered, 0.0)
                    if t == edge_tile:
                        edge_at = pl.ds(pl.multiple_of((row_at + j) * SUB, SUB), SUB)
                        value += edges_ref[edge_at, :]
                    factor = ratio_ref[0, j, part, :] + ratio_ref[1, j, part, :] * growth[t]
                    result.append(value * (scale * factor))
                return result

            pending = [damped(j) for j in range(min(2, freqs))]
            for j in range(freqs):
                if j + 2 < freqs:
                    pending.append(damped(j + 2))
                for t, value in enumerate(pending.pop(0)):
                    ring_ref[slot, j, 0, t * SUB : (t + 1) * SUB, :] = value
            send(direction, slot).start()
            return carry

        lax.fori_loop(0, quarter, one, 0)
    for direction in range(ND - SLOTS, ND):
        send(direction, direction % SLOTS).wait()


def step_pairs(axis, step):
    count = lax.axis_size(axis)
    return [(i, i + step) for i in range(count) if 0 <= i + step < count]


def neighbour(values, axis, step):
    return lax.ppermute(values, axis, step_pairs(axis, step))


def others_sum(values, axis):
    count = lax.axis_size(axis)
    total = None
    for step in range(1, count):
        part = lax.ppermute(values, axis, [(i, (i + step) % count) for i in range(count)])
        total = part if total is None else total + part
    return jnp.zeros_like(values) if total is None else total


VMEM = pl.BlockSpec(memory_space=pltpu.VMEM)
SMEM = pl.BlockSpec(memory_space=pltpu.SMEM)
HBM = pl.BlockSpec(memory_space=pltpu.HBM)
ANY = pl.BlockSpec(memory_space=pl.ANY)


def in_vmem(*shape):
    return pltpu.VMEM(shape, jnp.float32)


def in_any(*shape):
    return jax.ShapeDtypeStruct(shape, jnp.float32)


def in_hbm(values):
    return pltpu.with_memory_space_constraint(values, pltpu.HBM)


def call(kernel, in_specs, out_shape, out_specs, flops, moved, scratch=(), aliases=None, limit=6):
    return pl.pallas_call(
        kernel,
        in_specs=in_specs,
        out_shape=out_shape,
        out_specs=out_specs,
        scratch_shapes=list(scratch),
        input_output_aliases=aliases or {},
        cost_estimate=pl.CostEstimate(flops=flops, bytes_accessed=moved, transcendentals=0),
        compiler_params=pltpu.CompilerParams(vmem_limit_bytes=limit << 20),
    )


def resident(spectrum, land_mask, ice_mask, wind_u, wind_v, depth):
    local_comp, rows, lanes = spectrum.shape
    freqs = local_comp // ND
    members = lax.axis_size("comp")
    member = lax.axis_index("comp").astype(jnp.int32).reshape(1)
    scalars, lane_table, row_table = numpy_tables(members, freqs)
    scalars, lane_table, row_table = map(jnp.asarray, (scalars, lane_table, row_table))
    cells = rows * lanes
    row_message = 2 * 18 * freqs + CORNERS
    block = (freqs, ND, rows, lanes)
    spectrum = spectrum.reshape(block)

    growth, wet, to_right, to_left, to_down, to_up, edges = call(
        functools.partial(pack_kernel, freqs),
        [SMEM] + [HBM] * 7,
        (
            in_any(ND, rows, lanes),
            in_any(rows, lanes),
            in_any(GROUPS // 2, rows, lanes),
            in_any(GROUPS // 2, rows, lanes),
            in_any(row_message, lanes),
            in_any(row_message, lanes),
            in_any(2 * 18 * freqs * SUB, lanes),
        ),
        (VMEM,) * 7,
        flops=local_comp * cells * 4,
        moved=local_comp * cells * 4,
        scratch=[
            pltpu.VMEM((local_comp * rows, lanes), jnp.float32),
            pltpu.VMEM(lane_table.shape[1:], jnp.float32),
            pltpu.VMEM(row_table.shape[1:], jnp.float32),
            pltpu.VMEM((rows, lanes), jnp.int32),
            pltpu.VMEM((rows, lanes), jnp.int32),
            pltpu.VMEM((rows, lanes), jnp.float32),
            pltpu.VMEM((rows, lanes), jnp.float32),
            pltpu.SemaphoreType.DMA((6,)),
            pltpu.SemaphoreType.DMA((GROUPS,)),
        ],
        limit=30,
    )(
        member,
        *map(in_hbm, (lane_table, row_table, land_mask, ice_mask, wind_u, wind_v, spectrum)),
    )

    def main_part(start, stop, *before):
        return call(
            functools.partial(main_kernel, freqs, start, stop),
            [SMEM, SMEM, VMEM, VMEM, HBM] + ([ANY, VMEM, VMEM, VMEM, VMEM] if before else []),
            (
                in_vmem(*block),
                in_any(freqs * rows, lanes),
                in_any(freqs * rows, lanes),
                in_any(rows, lanes),
            ),
            (VMEM,) * 4,
            flops=local_comp * cells * 16 * (stop - start) // freqs,
            moved=local_comp * cells * 8 * (stop - start) // freqs,
            scratch=[
                pltpu.VMEM((AHEAD, ND, rows, lanes), jnp.float32),
                pltpu.SemaphoreType.DMA((AHEAD,)),
            ]
            + [pltpu.VMEM((rows + 2 * SUB, lanes), jnp.float32)] * 8,
            aliases={6 + index: index for index in range(4)} if before else {},
            limit=8,
        )(member, scalars, wet, growth, in_hbm(spectrum), *before)

    early = max(1, freqs // 3)
    from_left = neighbour(to_right, "sect", 1)
    from_right = neighbour(to_left, "sect", -1)
    kept, *partial = main_part(0, early)
    to_down, to_up = call(
        functools.partial(corner_kernel, freqs),
        [VMEM, VMEM, VMEM, ANY, ANY, ANY],
        (in_any(row_message, lanes), in_any(row_message, lanes)),
        (ANY, ANY),
        flops=100,
        moved=1 << 15,
        scratch=[pltpu.VMEM((2, CORNERS, lanes), jnp.float32), pltpu.SemaphoreType.DMA((2,))],
        aliases={3: 0, 4: 1},
    )(wet, from_left, from_right, to_down, to_up, partial[-1])
    from_above = neighbour(to_down, "slab", 1)
    from_below = neighbour(to_up, "slab", -1)
    kept, a_sums, b_sums, energy = main_part(early, freqs, to_down, kept, *partial)

    columns, edges, energy = call(
        functools.partial(enter_kernel, freqs),
        [SMEM] + [VMEM] * 9,
        (
            in_any(GROUPS, rows, lanes),
            in_any(2 * 18 * freqs * SUB, lanes),
            in_any(rows, lanes),
        ),
        (VMEM,) * 3,
        flops=cells * 600,
        moved=cells * 200,
        aliases={8: 1, 9: 2},
    )(
        member, lane_table, row_table, wet, from_left, from_right, from_above, from_below, edges,
        energy,
    )
    energy_there = others_sum(energy, "comp")
    a_sums, b_sums = call(
        functools.partial(entered_kernel, freqs),
        [SMEM] + [VMEM] * 10,
        (in_any(freqs * rows, lanes), in_any(freqs * rows, lanes)),
        (VMEM,) * 2,
        flops=cells * 600,
        moved=cells * 200,
        aliases={9: 0, 10: 1},
    )(
        member, lane_table, row_table, ice_mask, wind_u, wind_v, growth, columns, edges,
        a_sums, b_sums,
    )

    sums, square = call(
        functools.partial(stress_kernel, freqs),
        [SMEM, SMEM] + [VMEM] * 5,
        (in_any(3, rows, lanes), in_any(rows, lanes)),
        (VMEM, VMEM),
        flops=cells * freqs * 12,
        moved=cells * freqs * 8,
    )(member, scalars, wet, a_sums, b_sums, energy, energy_there)
    sums, stress = call(
        total_kernel,
        [VMEM, VMEM],
        (in_any(3, rows, lanes), in_any(2, rows, lanes)),
        (VMEM, VMEM),
        flops=cells * 3,
        moved=cells * 44,
    )(sums, others_sum(sums, "comp"))
    left = neighbour(stress, "sect", 1)
    right = neighbour(stress, "sect", -1)
    beside, top, bottom = call(
        strip_kernel,
        [VMEM, VMEM, VMEM],
        (in_any(2, rows, lanes), in_any(2, SUB, 2 * lanes), in_any(2, SUB, 2 * lanes)),
        (VMEM, VMEM, VMEM),
        flops=cells * 4,
        moved=cells * 36,
    )(stress, left, right)
    above = neighbour(bottom, "slab", 1)
    below = neighbour(top, "slab", -1)

    result, level = call(
        functools.partial(final_kernel, freqs),
        [SMEM, SMEM] + [VMEM] * 11,
        (in_any(*block), in_any(rows, lanes)),
        (HBM, VMEM),
        flops=local_comp * cells * 6,
        moved=local_comp * cells * 8,
        scratch=[
            pltpu.VMEM((2, freqs, rows, lanes), jnp.float32),
            pltpu.VMEM((SLOTS, freqs, 1, rows, lanes), jnp.float32),
            pltpu.SemaphoreType.DMA((SLOTS,)),
        ],
    )(
        member, scalars, wet, depth, square, sums, beside, above, below, growth, kept,
        columns, edges,
    )
    return result.reshape(local_comp, rows, lanes), level


def local(spectrum, *fields):
    local_comp, rows, lanes = spectrum.shape
    whole_rings = local_comp % ND == 0 and GROUP * 2 * (local_comp // ND) < LANES - 1
    if whole_rings and lanes == LANES and rows % SUB == 0:
        return resident(spectrum, *fields)
    return general(spectrum, *fields)


def solution(mesh):
    in_specs = (
        P("comp", "slab", "sect"),
        P("slab", "sect"),
        P("slab", "sect"),
        P("slab", "sect"),
        P("slab", "sect"),
        P("slab", "sect"),
    )
    out_specs = (P("comp", "slab", "sect"), P("slab", "sect"))
    return jax.shard_map(local, mesh=mesh, in_specs=in_specs, out_specs=out_specs, check_vma=False)
```

time: 117 us -> 86.6 us (0.74); the launches traced: 115 us -> 86.3 us
  local copies, waits for them, and re-layouts: 19.3 us -> 0.05 us
  Pallas kernels: 54.4 us -> 50.1 us
  waiting for transfers between devices: 14 us -> 10.6 us
  starting transfers between devices: 26 us -> 24.7 us
    unnamed x28 -> x14, local copies, waits for them, and re-layouts: 19.3 us -> 0.05 us
    pallas_call x4 -> x8, Pallas kernels: 53 us -> 49 us  [the longest x2 20.3 us: main_part(): call(functools.partial(main_kernel, freqs, start, stop), [SMEM, SMEM, VME...]
    ppermute x8, waiting for transfers between devices: 8.21 us -> 6.45 us  [neighbour(): return lax.ppermute(values, axis, step_pairs(axis, step))]
    ppermute x2, waiting for transfers between devices: 5.76 us -> 4.13 us  [others_sum(): lax.ppermute(values, axis, [(i, (i + step) % count) for i in range(count)])]
    ppermute x8, starting transfers between devices: 22.8 us -> 21.6 us  [neighbour(): return lax.ppermute(values, axis, step_pairs(axis, step))]
  transfers between devices with their start and end apart: 10 -> 10, of which waited for: 6 -> 4; matrix products, arithmetic and copies ran while one was open for 0% -> 0% of each run, Pallas kernels for 21% -> 25%
where the time goes in v2:
time: 86.6 us; the launch traced here: 86.3 us
  Pallas kernels  50.1 us (58%)
  starting transfers between devices  24.7 us (29%)
  waiting for transfers between devices  10.6 us (12%)
  between operations  0.88 us (1%)
    ppermute x8, starting transfers between devices, neighbour(): return lax.ppermute(values, axis, step_pairs(axis, step))  21.6 us
    pallas_call x2, Pallas kernels, main_part(): call(functools.partial(main_kernel, freqs, start, stop), [SMEM, SMEM, VME...  20.3 us
    pallas_call x1, Pallas kernels, resident(): call(functools.partial(final_kernel, freqs), [SMEM, SMEM] + [VMEM] * 11,...  16 us
    pallas_call x1, Pallas kernels, resident(): call(functools.partial(pack_kernel, freqs), [SMEM] + [HBM] * 7, (in_any(N...  10.2 us
    ppermute x8, waiting for transfers between devices, neighbour(): return lax.ppermute(values, axis, step_pairs(axis, step))  6.45 us
    ppermute x2, waiting for transfers between devices, others_sum(): lax.ppermute(values, axis, [(i, (i + step) % count) for i in range(count)])  4.13 us
    ppermute x2, starting transfers between devices, others_sum(): lax.ppermute(values, axis, [(i, (i + step) % count) for i in range(count)])  3.11 us
  transfers between devices with their start and end apart: 10, of which 4 were waited for; matrix products, arithmetic and copies ran while one was open for 0% of the time, Pallas kernels for 25%

profile of v2, /device:TPU:12, one launch (start us, length us, event | category | flops | bytes accessed | tf_op | source)
XLA Modules:
  0.0 86.3 jit_solution(1109317520028989452)
XLA Ops:
  0.6 0.0 copy-start.5
  0.6 10.2 %shard_map.104 = (f32[36,64,128]{2,1,0:T(8,128)S(1)}, f32[64,128]{1,0:T(8,128)S(1)}, f32[6,64,128]{2,1,0:T(8,128)S(1)}, f32[6,64,128]{2,1,0:T(8,128)S(1)}, f32[6...) custom-call(s32[1]{0:T(128)} %bitcast.member_ref, ...), custom_call_target="tpu_custom_call" | custom-call | flops 21233664 | bytes 21233664 | tf_op jit(solution)/shard_map/pallas_call | solution.py:886
  10.9 1.9 %collective-permute-start = (f32[6,64,128]{2,1,0:T(8,128)S(1)}, f32[6,64,128]{2,1,0:T(8,128)S(1)}, u32[]{:S(2)}, u32[]{:S(2)}) collective-permute-start(f32[6,64,128]{2,1,0:T(8,128)S(1)} %get-tuple-element.35), channel_id=1, source_target_pairs={{0,4},{4,8},{8,12},{1,5},{5,9},{9,13},{2,6},{6,10},{10,14},{3,7},{... | collective-permute-start | bytes 589832 | tf_op jit(solution)/shard_map/ppermute | solution.py:831
  12.8 3.6 %collective-permute-start.1 = (f32[6,64,128]{2,1,0:T(8,128)S(1)}, f32[6,64,128]{2,1,0:T(8,128)S(1)}, u32[]{:S(2)}, u32[]{:S(2)}) collective-permute-start(f32[6,64,128]{2,1,0:T(8,128)S(1)} %get-tuple-element.36), channel_id=1, source_target_pairs={{4,0},{8,4},{12,8},{5,1},{9,5},{13,9},{6,2},{10,6},{14,10},{7,3},{... | collective-permute-start | bytes 589832 | tf_op jit(solution)/shard_map/ppermute | solution.py:831
  16.4 0.0 copy-done.5
  16.4 7.4 %shard_map.105 = (f32[18,36,64,128]{3,2,1,0:T(8,128)S(1)}, f32[1152,128]{1,0:T(8,128)S(1)}, f32[1152,128]{1,0:T(8,128)S(1)}, f32[64,128]{1,0:T(8,128)S(1)}) custom-call(s32[1]{0:T(128)} %bitcast.member_ref, f32[1800]{0:T(1024)S(1)} %copy-done.5, f32[64,128]{1,0:T(8,128)S(1)} %get-tuple-element.33.wet_ref, f32[36,64,128]{2,1,0:T(8,128)S(1)} %get-tuple-element.34.growth_ref, ...), custom_call_target="tpu_custom_call" | custom-call | flops 28311552 | bytes 14155776 | tf_op jit(solution)/shard_map/pallas_call | solution.py:919
  23.9 0.0 collective-permute-done.right_ref
  23.9 0.0 collective-permute-done.1.left_ref
  23.9 0.1 shard_map.106
  24.0 2.4 %collective-permute-start.3 = (f32[656,128]{1,0:T(8,128)S(1)}, f32[656,128]{1,0:T(8,128)S(1)}, u32[]{:S(2)}, u32[]{:S(2)}) collective-permute-start(f32[656,128]{1,0:T(8,128)S(1)} %get-tuple-element.41), channel_id=1, source_target_pairs={{1,0},{2,1},{3,2},{5,4},{6,5},{7,6},{9,8},{10,9},{11,10},{13,12},{... | collective-permute-start | bytes 1007624 | tf_op jit(solution)/shard_map/ppermute | solution.py:831
  26.4 3.5 %collective-permute-start.2 = (f32[656,128]{1,0:T(8,128)S(1)}, f32[656,128]{1,0:T(8,128)S(1)}, u32[]{:S(2)}, u32[]{:S(2)}) collective-permute-start(f32[656,128]{1,0:T(8,128)S(1)} %get-tuple-element.40.refs_0_), channel_id=1, source_target_pairs={{0,1},{1,2},{2,3},{4,5},{5,6},{6,7},{8,9},{9,10},{10,11},{12,13},{... | collective-permute-start | bytes 1007624 | tf_op jit(solution)/shard_map/ppermute | solution.py:831
  29.9 0.0 copy-start
  29.9 0.0 copy-start.1
  29.9 0.0 copy-start.2
  29.9 0.0 copy-start.3
  29.9 0.0 copy-start.4
  29.9 0.0 copy-start.6
  30.0 12.9 %shard_map.107 = (f32[18,36,64,128]{3,2,1,0:T(8,128)S(1)}, f32[1152,128]{1,0:T(8,128)S(1)}, f32[1152,128]{1,0:T(8,128)S(1)}, f32[64,128]{1,0:T(8,128)S(1)}) custom-call(s32[1]{0:T(128)} %bitcast.member_ref, f32[1800]{0:T(1024)S(1)} %copy-done.5, ...), custom_call_target="tpu_custom_call", output_to_operand_aliasing={{0}: (6, {}), {1}: (7, {}), {2}: (8, {}), {3}: (9, {})} | custom-call | flops 56623104 | bytes 28311552 | tf_op jit(solution)/shard_map/pallas_call | solution.py:919
  42.9 0.0 collective-permute-done.3.up_ref
  42.9 0.0 collective-permute-done.2.down_ref
  42.9 0.0 copy-done
  42.9 0.0 copy-done.1
  42.9 1.1 %shard_map.108 = (f32[12,64,128]{2,1,0:T(8,128)S(1)}, f32[5184,128]{1,0:T(8,128)S(1)}, f32[64,128]{1,0:T(8,128)S(1)}) custom-call(s32[1]{0:T(128)} %bitcast.member_ref, f32[2,12,8,128]{3,2,1,0:T(8,128)S(1)} %copy-done.1, f32[2,10,5,18,128]{4,3,2,1,0:T(8,128)S(1)} %copy-done, ...), custom_call_target="tpu_custom_call", output_to_operand_aliasing={{1}: (8, {}), {2}: (9, {})} | custom-call | flops 4915200 | bytes 1638400 | tf_op jit(solution)/shard_map/pallas_call | solution.py:958
  44.0 1.6 %collective-permute-start.4 = (f32[64,128]{1,0:T(8,128)S(1)}, f32[64,128]{1,0:T(8,128)S(1)}, u32[]{:S(2)}, u32[]{:S(2)}) collective-permute-start(f32[64,128]{1,0:T(8,128)S(1)} %get-tuple-element.53.own_ref), channel_id=1, source_target_pairs={{0,16},{16,0},{1,17},{17,1},{2,18},{18,2},{3,19},{19,3},{4,20},{20... | collective-permute-start | bytes 98312 | tf_op jit(solution)/shard_map/ppermute | solution.py:838
  45.6 0.0 copy-done.2
  45.6 0.0 copy-done.3
  45.6 0.0 copy-done.4
  45.6 1.4 %shard_map.109 = (f32[1152,128]{1,0:T(8,128)S(1)}, f32[1152,128]{1,0:T(8,128)S(1)}) custom-call(s32[1]{0:T(128)} %bitcast.member_ref, f32[2,12,8,128]{3,2,1,0:T(8,128)S(1)} %copy-done.1, f32[2,10,5,18,128]{4,3,2,1,0:T(8,128)S(1)} %copy-done, s32[64,128]{1,0:T(8,128)S(1)} %copy-done.2, ...), custom_call_target="tpu_custom_call", output_to_operand_aliasing={{0}: (9, {}), {1}: (10, {})} | custom-call | flops 4915200 | bytes 1638400 | tf_op jit(solution)/shard_map/pallas_call | solution.py:975
  47.0 1.0 %collective-permute-done.4.other_ref = f32[64,128]{1,0:T(8,128)S(1)} collective-permute-done((f32[64,128]{1,0:T(8,128)S(1)}, f32[64,128]{1,0:T(8,128)S(1)}, u32[]{:S(2)}, u32[]{:S(2)}) %collective-permute-start.4) | collective-permute-done | bytes 32800 | tf_op jit(solution)/shard_map/ppermute | solution.py:838
  48.0 1.0 %shard_map.110 = (f32[3,64,128]{2,1,0:T(8,128)S(1)}, f32[64,128]{1,0:T(8,128)S(1)}) custom-call(s32[1]{0:T(128)} %bitcast.member_ref, f32[1800]{0:T(1024)S(1)} %copy-done.5, f32[64,128]{1,0:T(8,128)S(1)} %get-tuple-element.33.wet_ref, f32[1152,128]{1,0:T(8,128)S(1)} %get-tuple-element.51.a_ref, f32[1152,128]{1,0:T(8,128)S(1)} %get-tuple-element.52.b_ref, ...), custom_call_target="tpu_custom_call" | custom-call | flops 1769472 | bytes 1179648 | tf_op jit(solution)/shard_map/pallas_call | solution.py:988
  49.0 1.6 %collective-permute-start.5 = (f32[3,64,128]{2,1,0:T(8,128)S(1)}, f32[3,64,128]{2,1,0:T(8,128)S(1)}, u32[]{:S(2)}, u32[]{:S(2)}) collective-permute-start(f32[3,64,128]{2,1,0:T(8,128)S(1)} %get-tuple-element.55.own_ref), channel_id=1, source_target_pairs={{0,16},{16,0},{1,17},{17,1},{2,18},{18,2},{3,19},{19,3},{4,20},{20... | collective-permute-start | bytes 294920 | tf_op jit(solution)/shard_map/ppermute | solution.py:838
  50.5 3.1 %collective-permute-done.5.other_ref = f32[3,64,128]{2,1,0:T(8,128)S(1)} collective-permute-done((f32[3,64,128]{2,1,0:T(8,128)S(1)}, f32[3,64,128]{2,1,0:T(8,128)S(1)}, u32[]{:S(2)}, u32[]{:S(2)}) %collective-permute-start.5) | collective-permute-done | bytes 98336 | tf_op jit(solution)/shard_map/ppermute | solution.py:838
  53.7 1.9 %collective-permute-start.7 = (f32[2,64,128]{2,1,0:T(8,128)S(1)}, f32[2,64,128]{2,1,0:T(8,128)S(1)}, u32[]{:S(2)}, u32[]{:S(2)}) collective-permute-start(f32[2,64,128]{2,1,0:T(8,128)S(1)} %get-tuple-element.57.stress_ref), channel_id=1, source_target_pairs={{4,0},{8,4},{12,8},{5,1},{9,5},{13,9},{6,2},{10,6},{14,10},{7,3},{... | collective-permute-start | bytes 196616 | tf_op jit(solution)/shard_map/ppermute | solution.py:831
  55.6 2.4 %collective-permute-start.6 = (f32[2,64,128]{2,1,0:T(8,128)S(1)}, f32[2,64,128]{2,1,0:T(8,128)S(1)}, u32[]{:S(2)}, u32[]{:S(2)}) collective-permute-start(f32[2,64,128]{2,1,0:T(8,128)S(1)} %get-tuple-element.57.stress_ref), channel_id=1, source_target_pairs={{0,4},{4,8},{8,12},{1,5},{5,9},{9,13},{2,6},{6,10},{10,14},{3,7},{... | collective-permute-start | bytes 196616 | tf_op jit(solution)/shard_map/ppermute | solution.py:831
  58.0 0.0 collective-permute-done.7.right_ref
  58.0 3.2 %collective-permute-done.6.left_ref = f32[2,64,128]{2,1,0:T(8,128)S(1)} collective-permute-done((f32[2,64,128]{2,1,0:T(8,128)S(1)}, f32[2,64,128]{2,1,0:T(8,128)S(1)}, u32[]{:S(2)}, u32[]{:S(2)}) %collective-permute-start.6) | collective-permute-done | bytes 65568 | tf_op jit(solution)/shard_map/ppermute | solution.py:831
  61.2 3.5 %collective-permute-start.8 = (f32[2,8,256]{2,1,0:T(8,128)S(1)}, f32[2,8,256]{2,1,0:T(8,128)S(1)}, u32[]{:S(2)}, u32[]{:S(2)}) collective-permute-start(f32[2,8,256]{2,1,0:T(8,128)S(1)} %get-tuple-element.59), channel_id=1, source_target_pairs={{0,1},{1,2},{2,3},{4,5},{5,6},{6,7},{8,9},{9,10},{10,11},{12,13},{... | collective-permute-start | bytes 49160 | tf_op jit(solution)/shard_map/ppermute | solution.py:831
  64.7 2.3 %collective-permute-start.9 = (f32[2,8,256]{2,1,0:T(8,128)S(1)}, f32[2,8,256]{2,1,0:T(8,128)S(1)}, u32[]{:S(2)}, u32[]{:S(2)}) collective-permute-start(f32[2,8,256]{2,1,0:T(8,128)S(1)} %get-tuple-element.60), channel_id=1, source_target_pairs={{1,0},{2,1},{3,2},{5,4},{6,5},{7,6},{9,8},{10,9},{11,10},{13,12},{... | collective-permute-start | bytes 49160 | tf_op jit(solution)/shard_map/ppermute | solution.py:831
  67.1 0.0 collective-permute-done.8.above_ref
  67.1 3.3 %collective-permute-done.9.below_ref = f32[2,8,256]{2,1,0:T(8,128)S(1)} collective-permute-done((f32[2,8,256]{2,1,0:T(8,128)S(1)}, f32[2,8,256]{2,1,0:T(8,128)S(1)}, u32[]{:S(2)}, u32[]{:S(2)}) %collective-permute-start.9) | collective-permute-done | bytes 16416 | tf_op jit(solution)/shard_map/ppermute | solution.py:831
  70.3 0.0 copy-done.6
  70.3 16.0 %shard_map.113 = (f32[18,36,64,128]{3,2,1,0:T(8,128)}, f32[64,128]{1,0:T(8,128)}) custom-call(s32[1]{0:T(128)} %bitcast.member_ref, f32[1800]{0:T(1024)S(1)} %copy-done.5, f32[64,128]{1,0:T(8,128)S(1)} %get-tuple-element.33.wet_ref, f32[64,128]{1,0:T(8,128)S(1)} %copy-done.6, f32[64,128]{1,0:T(8,128)S(1)} %get-tuple-element.54.square_ref, ...), custom_call_target="tpu_custom_call" | custom-call | flops 31850496 | bytes 42467328 | tf_op jit(solution)/shard_map/pallas_call | solution.py:1017
  (2 shorter events, 0.0 us)
Async XLA Ops:
  0.6 15.8 %copy-start.5 = (f32[1800]{0:T(1024)S(1)}, f32[1800]{0:T(1024)}, u32[]{:S(2)}) copy-start(f32[1800]{0:T(1024)} %constant.12.clone.scalar_ref) | copy-start | bytes 21604
  10.9 13.0 %collective-permute-start = (f32[6,64,128]{2,1,0:T(8,128)S(1)}, f32[6,64,128]{2,1,0:T(8,128)S(1)}, u32[]{:S(2)}, u32[]{:S(2)}) collective-permute-start(f32[6,64,128]{2,1,0:T(8,128)S(1)} %get-tuple-element.35), channel_id=1, source_target_pairs={{0,4},{4,8},{8,12},{1,5},{5,9},{9,13},{2,6},{6,10},{10,14},{3,7},{... | collective-permute-start | bytes 589832 | tf_op jit(solution)/shard_map/ppermute | solution.py:831
  12.8 11.1 %collective-permute-start.1 = (f32[6,64,128]{2,1,0:T(8,128)S(1)}, f32[6,64,128]{2,1,0:T(8,128)S(1)}, u32[]{:S(2)}, u32[]{:S(2)}) collective-permute-start(f32[6,64,128]{2,1,0:T(8,128)S(1)} %get-tuple-element.36), channel_id=1, source_target_pairs={{4,0},{8,4},{12,8},{5,1},{9,5},{13,9},{6,2},{10,6},{14,10},{7,3},{... | collective-permute-start | bytes 589832 | tf_op jit(solution)/shard_map/ppermute | solution.py:831
  24.0 18.8 %collective-permute-start.3 = (f32[656,128]{1,0:T(8,128)S(1)}, f32[656,128]{1,0:T(8,128)S(1)}, u32[]{:S(2)}, u32[]{:S(2)}) collective-permute-start(f32[656,128]{1,0:T(8,128)S(1)} %get-tuple-element.41), channel_id=1, source_target_pairs={{1,0},{2,1},{3,2},{5,4},{6,5},{7,6},{9,8},{10,9},{11,10},{13,12},{... | collective-permute-start | bytes 1007624 | tf_op jit(solution)/shard_map/ppermute | solution.py:831
  26.4 16.5 %collective-permute-start.2 = (f32[656,128]{1,0:T(8,128)S(1)}, f32[656,128]{1,0:T(8,128)S(1)}, u32[]{:S(2)}, u32[]{:S(2)}) collective-permute-start(f32[656,128]{1,0:T(8,128)S(1)} %get-tuple-element.40.refs_0_), channel_id=1, source_target_pairs={{0,1},{1,2},{2,3},{4,5},{5,6},{6,7},{8,9},{9,10},{10,11},{12,13},{... | collective-permute-start | bytes 1007624 | tf_op jit(solution)/shard_map/ppermute | solution.py:831
  29.9 13.0 %copy-start = (f32[2,10,5,18,128]{4,3,2,1,0:T(8,128)S(1)}, f32[2,10,5,18,128]{4,3,2,1,0:T(8,128)}, u32[]{:S(2)}) copy-start(f32[2,10,5,18,128]{4,3,2,1,0:T(8,128)} %constant.14.clone.table_hbm.table_ref) | copy-start | bytes 2764804
  29.9 13.0 %copy-start.1 = (f32[2,12,8,128]{3,2,1,0:T(8,128)S(1)}, f32[2,12,8,128]{3,2,1,0:T(8,128)}, u32[]{:S(2)}) copy-start(f32[2,12,8,128]{3,2,1,0:T(8,128)} %constant.13.clone.lanes_hbm.lanes_ref) | copy-start | bytes 294916
  29.9 15.7 %copy-start.2 = (s32[64,128]{1,0:T(8,128)S(1)}, s32[64,128]{1,0:T(8,128)}, u32[]{:S(2)}) copy-start(s32[64,128]{1,0:T(8,128)} %ice_ref.1) | copy-start | bytes 98308
  29.9 15.6 %copy-start.3 = (f32[64,128]{1,0:T(8,128)S(1)}, f32[64,128]{1,0:T(8,128)}, u32[]{:S(2)}) copy-start(f32[64,128]{1,0:T(8,128)} %east_ref.1) | copy-start | bytes 98308
  29.9 15.6 %copy-start.4 = (f32[64,128]{1,0:T(8,128)S(1)}, f32[64,128]{1,0:T(8,128)}, u32[]{:S(2)}) copy-start(f32[64,128]{1,0:T(8,128)} %north_ref.1) | copy-start | bytes 98308
  29.9 40.4 %copy-start.6 = (f32[64,128]{1,0:T(8,128)S(1)}, f32[64,128]{1,0:T(8,128)}, u32[]{:S(2)}) copy-start(f32[64,128]{1,0:T(8,128)} %depth_ref.1) | copy-start | bytes 98308
  44.0 4.0 %collective-permute-start.4 = (f32[64,128]{1,0:T(8,128)S(1)}, f32[64,128]{1,0:T(8,128)S(1)}, u32[]{:S(2)}, u32[]{:S(2)}) collective-permute-start(f32[64,128]{1,0:T(8,128)S(1)} %get-tuple-element.53.own_ref), channel_id=1, source_target_pairs={{0,16},{16,0},{1,17},{17,1},{2,18},{18,2},{3,19},{19,3},{4,20},{20... | collective-permute-start | bytes 98312 | tf_op jit(solution)/shard_map/ppermute | solution.py:838
  49.0 4.7 %collective-permute-start.5 = (f32[3,64,128]{2,1,0:T(8,128)S(1)}, f32[3,64,128]{2,1,0:T(8,128)S(1)}, u32[]{:S(2)}, u32[]{:S(2)}) collective-permute-start(f32[3,64,128]{2,1,0:T(8,128)S(1)} %get-tuple-element.55.own_ref), channel_id=1, source_target_pairs={{0,16},{16,0},{1,17},{17,1},{2,18},{18,2},{3,19},{19,3},{4,20},{20... | collective-permute-start | bytes 294920 | tf_op jit(solution)/shard_map/ppermute | solution.py:838
  53.7 4.3 %collective-permute-start.7 = (f32[2,64,128]{2,1,0:T(8,128)S(1)}, f32[2,64,128]{2,1,0:T(8,128)S(1)}, u32[]{:S(2)}, u32[]{:S(2)}) collective-permute-start(f32[2,64,128]{2,1,0:T(8,128)S(1)} %get-tuple-element.57.stress_ref), channel_id=1, source_target_pairs={{4,0},{8,4},{12,8},{5,1},{9,5},{13,9},{6,2},{10,6},{14,10},{7,3},{... | collective-permute-start | bytes 196616 | tf_op jit(solution)/shard_map/ppermute | solution.py:831
  55.6 5.6 %collective-permute-start.6 = (f32[2,64,128]{2,1,0:T(8,128)S(1)}, f32[2,64,128]{2,1,0:T(8,128)S(1)}, u32[]{:S(2)}, u32[]{:S(2)}) collective-permute-start(f32[2,64,128]{2,1,0:T(8,128)S(1)} %get-tuple-element.57.stress_ref), channel_id=1, source_target_pairs={{0,4},{4,8},{8,12},{1,5},{5,9},{9,13},{2,6},{6,10},{10,14},{3,7},{... | collective-permute-start | bytes 196616 | tf_op jit(solution)/shard_map/ppermute | solution.py:831
  61.2 5.9 %collective-permute-start.8 = (f32[2,8,256]{2,1,0:T(8,128)S(1)}, f32[2,8,256]{2,1,0:T(8,128)S(1)}, u32[]{:S(2)}, u32[]{:S(2)}) collective-permute-start(f32[2,8,256]{2,1,0:T(8,128)S(1)} %get-tuple-element.59), channel_id=1, source_target_pairs={{0,1},{1,2},{2,3},{4,5},{5,6},{6,7},{8,9},{9,10},{10,11},{12,13},{... | collective-permute-start | bytes 49160 | tf_op jit(solution)/shard_map/ppermute | solution.py:831
  64.7 5.6 %collective-permute-start.9 = (f32[2,8,256]{2,1,0:T(8,128)S(1)}, f32[2,8,256]{2,1,0:T(8,128)S(1)}, u32[]{:S(2)}, u32[]{:S(2)}) collective-permute-start(f32[2,8,256]{2,1,0:T(8,128)S(1)} %get-tuple-element.60), channel_id=1, source_target_pairs={{1,0},{2,1},{3,2},{5,4},{6,5},{7,6},{9,8},{10,9},{11,10},{13,12},{... | collective-permute-start | bytes 49160 | tf_op jit(solution)/shard_map/ppermute | solution.py:831

commit v3 on v2

--- a/solution.py
+++ b/solution.py
@@ -249,24 +249,21 @@
     return jnp.where(iota(values.shape, 1) == edge, 0.0, moved)
 
 
-DEPTH = 3
-
-
-def slot_base(quadrant):
-    return (0, 9, 9, 18)[quadrant]
-
-
-def class_index(direction):
-    folded = lax.rem(direction, 18)
-    return jnp.where(folded <= 9, folded, 18 - folded)
+SLOTS = 4
+
+
+def sides(quadrant):
+    return 1 if quadrant in (0, 3) else -1, 1 if quadrant in (0, 1) else -1
 
 
 def pack_kernel(
-    freqs, member_ref, lanes_hbm, table_hbm, land_hbm, ice_hbm, east_hbm, north_hbm, spectrum_ref,
-    growth_ref, wet_ref, right_ref, left_ref, down_ref, up_ref, edges_ref,
-    kept_ref, lanes_ref, table_ref, land_ref, ice_ref, east_ref, north_ref, small_sems, sems,
+    freqs, member_ref, scalar_ref, lanes_hbm, table_hbm, land_hbm, ice_hbm, east_hbm, north_hbm,
+    spectrum_ref, kept_ref, growth_ref, wet_ref, right_ref, left_ref, down_ref, up_ref, edges_ref,
+    ring_ref, near_ref, far_ref, lanes_ref, table_ref, land_ref, ice_ref, east_ref, north_ref,
+    small_sems, sems, *masked_refs,
 ):
     member = member_ref[0]
+    nought = jnp.minimum(member, 0)
     small = [
         pltpu.make_async_copy(source, target, small_sems.at[index])
         for index, (source, target) in enumerate(
@@ -282,17 +279,21 @@
     ]
     for copy in small:
         copy.start()
-
     rows = land_ref.shape[0]
-    blocks_ref = kept_ref.reshape(freqs, ND, rows, LANES)
-
-    def fetch(group):
-        part = (slice(None), pl.ds(group * GROUP, GROUP))
-        return pltpu.make_async_copy(spectrum_ref.at[part], blocks_ref.at[part], sems.at[group])
-
-    for group in range(DEPTH):
-        fetch(group).start()
+
+    def fetch(j):
+        slot = lax.rem(j, SLOTS)
+        return pltpu.make_async_copy(spectrum_ref.at[j], ring_ref.at[slot], sems.at[slot])
+
+    for j in range(min(SLOTS, freqs)):
+        fetch(jnp.int32(j)).start()
     edges_ref[...] = jnp.zeros_like(edges_ref)
+    for masked_ref in masked_refs:
+        masked_ref[...] = jnp.zeros_like(masked_ref)
+    down_ref[pl.ds(2 * 18 * freqs, CORNERS), :] = jnp.zeros((CORNERS, LANES), jnp.float32)
+    up_ref[pl.ds(2 * 18 * freqs, CORNERS), :] = jnp.zeros((CORNERS, LANES), jnp.float32)
+    right_ref[...] = jnp.zeros_like(right_ref)
+    left_ref[...] = jnp.zeros_like(left_ref)
     for copy in small:
         copy.wait()
 
@@ -309,45 +310,87 @@
     lane = iota(shape, 1)
     even = lane % 2 == 0
     tile_lane = iota((SUB, LANES), 1)
-    down_ref[pl.ds(2 * 18 * freqs, CORNERS), :] = jnp.zeros((CORNERS, LANES), jnp.float32)
-    up_ref[pl.ds(2 * 18 * freqs, CORNERS), :] = jnp.zeros((CORNERS, LANES), jnp.float32)
-
+    not_first = jnp.where(tile_lane == 0, 0.0, 1.0)
+    not_last = jnp.where(tile_lane == LANES - 1, 0.0, 1.0)
+    quarter = ND // 4
     half = GROUPS // 2
-    for to_right in (True, False):
-        target_ref = right_ref if to_right else left_ref
-
-        def gather(index, carry):
-            group = index + (0 if to_right else half)
-            fetch(group).wait()
-
-            @pl.when(group + DEPTH < GROUPS)
-            def _():
-                fetch(group + DEPTH).start()
-
-            packed = [jnp.zeros((SUB, LANES), jnp.float32) for _ in range(tiles)]
-            for i in range(GROUP):
-                for j in range(freqs):
-                    place = i * 2 * freqs + 2 * j
-                    here = (tile_lane >= place) & (tile_lane < place + 2)
-                    turn = (place + 2 if to_right else place) % LANES
-                    first = pl.multiple_of((j * ND + group * GROUP + i) * rows, SUB)
-                    for tile in range(tiles):
-                        cells = kept_ref[pl.ds(first + tile * SUB, SUB), :]
-                        packed[tile] = jnp.where(here, pltpu.roll(cells, turn, 1), packed[tile])
-            for tile in range(tiles):
-                target_ref[index, tile * SUB : (tile + 1) * SUB, :] = packed[tile]
-            return carry
-
-        lax.fori_loop(0, half, gather, 0)
+
+    def tile_at(tile):
+        return slice(tile * SUB, (tile + 1) * SUB)
+
+    def mask_and_pack(j, quadrant):
+        slot = lax.rem(j, SLOTS)
+        to_down, to_right = sides(quadrant)
+        wet = [wet_ref[tile_at(t), :] for t in range(tiles)]
+        for i in range(quarter):
+            direction = quadrant * quarter + i
+            place = direction % GROUP * 2 * freqs + 2 * j
+            here = (tile_lane >= place) & (tile_lane < place + 2)
+            turn = lax.rem(place + 2, LANES) if to_right > 0 else place
+            side_ref = right_ref if to_right > 0 else left_ref
+            group = direction // GROUP % half
+            target = masked_refs[quadrant % 2 * quarter + i]
+            for t in range(tiles):
+                cells = ring_ref[slot, direction, tile_at(t), :] * wet[t]
+                target[tile_at(t + 1), :] = cells
+                pltpu.store(
+                    side_ref.at[group, tile_at(t), :], pltpu.roll(cells, turn, 1), mask=here
+                )
+
+    def first_step(j, quadrant):
+        to_down, to_right = sides(quadrant)
+        wet = [wet_ref[tile_at(t), :] for t in range(tiles)]
+        near_row, far_row = (rows - 1, rows - 2) if to_down > 0 else (0, 1)
+        for i in range(quarter):
+            direction = quadrant * quarter + i
+            base = ((member * freqs + j) * CLASSES + class_of(direction)) * KINDS
+            alpha = scalar_ref[base]
+            across = scalar_ref[base + 1] * (not_first if to_right > 0 else not_last)
+            source = masked_refs[quadrant % 2 * quarter + i]
+            near_ref[pl.ds(direction * freqs + j, 1), :] = source[
+                SUB + near_row : SUB + near_row + 1, :
+            ]
+            far_ref[pl.ds(direction * freqs + j, 1), :] = source[
+                SUB + far_row : SUB + far_row + 1, :
+            ]
+            for t in range(tiles):
+                cells = source[tile_at(t + 1), :]
+                ahead = source[pl.ds((t + 1) * SUB - to_down + nought, SUB), :]
+                beside = pltpu.roll(cells, to_right % LANES, 1)
+                kept_ref[j, direction, tile_at(t), :] = wet[t] * (
+                    cells + alpha * ahead + across * beside
+                )
+
+    fetch(jnp.int32(0)).wait()
+    mask_and_pack(jnp.int32(0), 0)
+
+    def frequency(j, carry):
+        fetch(j + 1).wait()
+        for quadrant in range(4):
+            mask_and_pack(j + quadrant // 3, (quadrant + 1) % 4)
+            first_step(j, quadrant)
+
+        @pl.when(j + SLOTS < freqs)
+        def _():
+            fetch(j + SLOTS).start()
+
+        return carry
+
+    lax.fori_loop(0, freqs - 1, frequency, 0)
+    last = jnp.int32(freqs - 1)
+    for quadrant in range(4):
+        if quadrant < 3:
+            mask_and_pack(last, quadrant + 1)
+        first_step(last, quadrant)
 
     pending = []
     for group in range(GROUPS):
         to_right, fore = group < half, 1 if heads_down(group * GROUP) else -1
         ahead, behind = (LANES - 1, LANES - 2) if to_right else (0, 1)
-        wet_near, wet_far = spread(wet_cells, ahead), spread(wet_cells, behind)
+        wet_near = spread(wet_cells, ahead)
         near_even = not to_right
         target_ref, index = (right_ref, group) if to_right else (left_ref, group - half)
-        values = target_ref[index] * jnp.where(even == near_even, wet_near, wet_far)
+        values = target_ref[index]
         near = pltpu.roll(values, 1 if near_even else LANES - 1, 1)
         table = lanes_ref[group]
         follow = wet_near * (table[1:2] * values + table[2:3] * shift_rows(near, fore))
@@ -362,12 +405,11 @@
     pending = []
     for direction in range(ND):
         to_down = heads_down(direction)
-        near_row, far_row = (rows - 1, rows - 2) if to_down else (0, 1)
+        near_row = rows - 1 if to_down else 0
         wet_near = wet_cells[near_row : near_row + 1, :]
-        wet_far = wet_cells[far_row : far_row + 1, :]
         table = table_ref.at[class_of(direction)]
-        near = kept_ref[pl.ds(direction * rows + near_row, freqs, stride=ND * rows), :] * wet_near
-        far = kept_ref[pl.ds(direction * rows + far_row, freqs, stride=ND * rows), :] * wet_far
+        near = near_ref[direction * freqs : (direction + 1) * freqs, :]
+        far = far_ref[direction * freqs : (direction + 1) * freqs, :]
         beside = shift_lanes(near, 1 if heads_right(direction) else -1)
         follow = wet_near * (table[1] * far + table[2] * beside)
         slot = row_slot(direction) * freqs
@@ -408,118 +450,93 @@
         copy.wait()
 
 
-AHEAD = 3
-
-
-def main_kernel(
-    freqs, start, stop, member_ref, scalar_ref, wet_ref, growth_ref, spectrum_ref, *refs
-):
+def main_kernel(freqs, start, stop, member_ref, scalar_ref, wet_ref, growth_ref, *refs):
     if start:
-        _after, _kept_in, a_in, b_in, energy_in, *refs = refs
-    kept_ref, a_ref, b_ref, energy_ref, ring_ref, sems, *first_refs = refs
+        _after, kept_in, a_in, b_in, energy_in, kept_ref, a_ref, b_ref, energy_ref = refs
+    else:
+        kept_in, kept_ref, a_ref, b_ref, energy_ref = refs
     member = member_ref[0]
     nought = jnp.minimum(member, 0)
     rows = wet_ref.shape[0]
     tiles = rows // SUB
-
-    def fetch(j):
-        slot = lax.rem(j, AHEAD)
-        return pltpu.make_async_copy(spectrum_ref.at[j], ring_ref.at[slot], sems.at[slot])
-
-    for j in range(start, min(start + AHEAD, stop)):
-        fetch(jnp.int32(j)).start()
-
     lane = iota((SUB, LANES), 1)
     sub = iota((SUB, LANES), 0)
     not_first = jnp.where(lane == 0, 0.0, 1.0)
     not_last = jnp.where(lane == LANES - 1, 0.0, 1.0)
     top, bottom = sub == 0, sub == SUB - 1
     energy_ref[...] = energy_in[...] if start else jnp.zeros_like(energy_ref)
-    for first_ref in first_refs:
-        first_ref[...] = jnp.zeros_like(first_ref)
 
     def tile_at(tile):
         return pl.ds(tile * SUB, SUB)
 
-    def row_shift(quadrant):
-        return -1 if quadrant in (0, 3) else 1
-
     def parts_of(kind):
         if kind == 0:
-            return ((0, 0, 0), (9, 1, 9), (18, 2, 0), (27, 3, 9))
-        return ((kind, 0, kind), (18 - kind, 1, kind), (18 + kind, 2, kind), (36 - kind, 3, kind))
+            return ((0, 0, 0), (18, 2, 0), (9, 1, 9), (27, 3, 9))
+        return ((kind, 0, kind), (18 + kind, 2, kind), (18 - kind, 1, kind), (36 - kind, 3, kind))
 
     def frequency(j, carry):
-        fetch(j).wait()
-        slot = lax.rem(j, AHEAD)
         base = (member * freqs + j) * CLASSES * KINDS
         at = [pl.ds(pl.multiple_of(j * rows, SUB) + t * SUB, SUB) for t in range(tiles)]
 
-        def speeds(part):
-            at_class = base + part[2] * KINDS
-            beta = scalar_ref[at_class + 1]
-            return scalar_ref[at_class], beta * (not_first if part[1] in (0, 1) else not_last)
-
-        def beside(cells, quadrant):
-            return pltpu.roll(cells, 1 if quadrant in (0, 1) else LANES - 1, 1)
-
-        def first_step(kind):
-            parts = parts_of(kind)
-            speed = [speeds(part) for part in parts]
-            wet = [wet_ref[tile_at(t), :] for t in range(tiles)]
-            for (direction, quadrant, _), (alpha, across) in zip(parts, speed):
-                shift = row_shift(quadrant)
-                edge = top if shift < 0 else bottom
-                target = first_refs[kind % 2 * 4 + quadrant]
-                cells = [ring_ref[slot, direction, tile_at(t), :] * wet[t] for t in range(tiles)]
-                turned = [pltpu.roll(cells[t], -shift % SUB, 0) for t in range(tiles)]
+        def second_step(part):
+            direction, quadrant, kind = part
+            to_down, to_right = sides(quadrant)
+            alpha = scalar_ref[base + kind * KINDS]
+            across = scalar_ref[base + kind * KINDS + 1] * (not_first if to_right > 0 else not_last)
+            result = []
+            for t in range(tiles):
+                cells = kept_in[j, direction, tile_at(t), :]
+                if 0 <= t * SUB - to_down <= rows - SUB:
+                    ahead = kept_in[j, direction, pl.ds(t * SUB - to_down + nought, SUB), :]
+                else:
+                    ahead = pltpu.roll(cells, to_down % SUB, 0)
+                    ahead = jnp.where(top if to_down > 0 else bottom, 0.0, ahead)
+                beside = pltpu.roll(cells, to_right % LANES, 1)
+                result.append(cells + alpha * ahead + across * beside)
+            return result
+
+        def put(parts, results):
+            for (direction, _, _), result in zip(parts, results):
                 for t in range(tiles):
-                    before = turned[t + shift] if 0 <= t + shift < tiles else 0.0
-                    ahead = jnp.where(edge, before, turned[t])
-                    after = cells[t] + alpha * ahead + across * beside(cells[t], quadrant)
-                    target[tile_at(t + 1), :] = wet[t] * after
-
-        def second_step(kind):
+                    kept_ref[j, direction, tile_at(t), :] = result[t]
+
+        pending = None
+        for kind in range(CLASSES - 1):
             parts = parts_of(kind)
             scale, high = scalar_ref[base + kind * KINDS + 2], scalar_ref[base + 3]
             scaled_high = scale * high
-            speed = [speeds(part) for part in parts]
+            pairs = []
+            for pair in (parts[:2], parts[2:]):
+                results = [second_step(part) for part in pair]
+                plain = [x + y for x, y in zip(*results)]
+                grown = [
+                    growth_ref[pair[0][0], tile_at(t), :] * results[0][t]
+                    + growth_ref[pair[1][0], tile_at(t), :] * results[1][t]
+                    for t in range(tiles)
+                ]
+                pairs.append((plain, grown))
+                if pending is not None:
+                    put(*pending)
+                pending = pair, results
+            (plain_x, grown_x), (plain_y, grown_y) = pairs
             for t in range(tiles):
-                moved, grown = [], []
-                for (direction, quadrant, _), (alpha, across) in zip(parts, speed):
-                    source = first_refs[kind % 2 * 4 + quadrant]
-                    cells = source[tile_at(t + 1), :]
-                    ahead = source[pl.ds((t + 1) * SUB + row_shift(quadrant) + nought, SUB), :]
-                    after = cells + alpha * ahead + across * beside(cells, quadrant)
-                    kept_ref[j, direction, tile_at(t), :] = after
-                    moved.append(after)
-                    grown.append(growth_ref[direction, tile_at(t), :] * after)
                 if kind == 0:
-                    plain_x, plain_y = scale * (moved[0] + moved[2]), scale * (moved[1] + moved[3])
-                    grown_x = plain_x + scaled_high * (grown[0] + grown[2])
-                    grown_y = plain_y + scaled_high * (grown[1] + grown[3])
+                    plain = scale * plain_x[t], scale * plain_y[t]
+                    whole = [
+                        p + scaled_high * g for p, g in zip(plain, (grown_x[t], grown_y[t]))
+                    ]
                     square = math.cos(0.5 * math.pi) ** 2
-                    energy_ref[tile_at(t), :] += plain_x + plain_y
-                    a_ref[at[t], :] = grown_x + grown_y
-                    b_ref[at[t], :] = grown_x + square * grown_y
+                    energy_ref[tile_at(t), :] += plain[0] + plain[1]
+                    a_ref[at[t], :] = whole[0] + whole[1]
+                    b_ref[at[t], :] = whole[0] + square * whole[1]
                 else:
-                    plain = scale * ((moved[0] + moved[1]) + (moved[2] + moved[3]))
-                    whole = plain + scaled_high * ((grown[0] + grown[1]) + (grown[2] + grown[3]))
+                    plain = scale * (plain_x[t] + plain_y[t])
+                    whole = plain + scaled_high * (grown_x[t] + grown_y[t])
                     square = math.cos(2.0 * math.pi * kind / ND) ** 2
                     energy_ref[tile_at(t), :] += plain
                     a_ref[at[t], :] += whole
                     b_ref[at[t], :] += square * whole
-
-        first_step(0)
-        for kind in range(CLASSES - 1):
-            if kind + 1 < CLASSES - 1:
-                first_step(kind + 1)
-            second_step(kind)
-
-        @pl.when(j + AHEAD < stop)
-        def _():
-            fetch(j + AHEAD).start()
-
+        put(*pending)
         return carry
 
     lax.fori_loop(start, stop, frequency, 0)
@@ -710,9 +727,6 @@
             target[index, :, LANES:] = beside[first : first + SUB, :]
 
 
-SLOTS = 3
-
-
 def final_kernel(
     freqs, member_ref, scalar_ref, wet_ref, depth_ref, square_ref, sums_ref, beside_ref, above_ref, below_ref,
     growth_ref, kept_ref, columns_ref, edges_ref,
@@ -762,64 +776,61 @@
     tile_lane = iota((SUB, LANES), 1)
     quarter = ND // 4
 
-    def send(direction, slot):
+    def send(j, quadrant):
+        slot = lax.rem(j, 2)
         return pltpu.make_async_copy(
-            ring_ref.at[slot], result_ref.at[:, pl.ds(direction, 1)], sems.at[slot]
+            ring_ref.at[slot, quadrant],
+            result_ref.at[j, pl.ds(quadrant * quarter, quarter)],
+            sems.at[slot, quadrant],
         )
 
-    for quadrant in range(4):
-        to_right, to_down = quadrant in (0, 1), quadrant in (0, 3)
-        target = 0 if to_right else LANES - 2
-        at_side = (tile_lane >= target) & (tile_lane < target + 2)
-        bank, edge_tile = (0, 0) if to_down else (1, tiles - 1)
-
-        def one(index, carry):
-            direction = quadrant * quarter + index
-            slot = lax.rem(direction, SLOTS)
-
-            @pl.when(direction >= SLOTS)
-            def _():
-                send(direction - SLOTS, slot).wait()
-
-            kind = class_index(direction)
-            group = lax.div(direction, GROUP)
-            offset = 2 * freqs * lax.rem(direction, GROUP)
-            row_at = (bank * 18 + direction - slot_base(quadrant)) * freqs
-            aligned = [
-                pltpu.roll(
-                    columns_ref[group, t * SUB : (t + 1) * SUB, :],
-                    lax.rem(target - offset + LANES, LANES),
-                    1,
-                )
-                for t in range(tiles)
-            ]
-            growth = [growth_ref[direction, t * SUB : (t + 1) * SUB, :] for t in range(tiles)]
-            def damped(j):
-                scale = scalar_ref[((member * freqs + j) * CLASSES + kind) * KINDS + 2]
-                result = []
-                for t in range(tiles):
-                    part = slice(t * SUB, (t + 1) * SUB)
-                    entered = pltpu.roll(aligned[t], (LANES - 2 * j) % LANES, 1)
-                    value = kept_ref[j, direction, part, :] + jnp.where(at_side, entered, 0.0)
-                    if t == edge_tile:
-                        edge_at = pl.ds(pl.multiple_of((row_at + j) * SUB, SUB), SUB)
-                        value += edges_ref[edge_at, :]
-                    factor = ratio_ref[0, j, part, :] + ratio_ref[1, j, part, :] * growth[t]
-                    result.append(value * (scale * factor))
-                return result
-
-            pending = [damped(j) for j in range(min(2, freqs))]
-            for j in range(freqs):
-                if j + 2 < freqs:
-                    pending.append(damped(j + 2))
+    def frequency(j, carry):
+        slot = lax.rem(j, 2)
+
+        @pl.when(j >= 2)
+        def _():
+            for quadrant in range(4):
+                send(j - 2, quadrant).wait()
+
+        def damped(quadrant, i):
+            direction = quadrant * quarter + i
+            to_down, to_right = sides(quadrant)
+            base = ((member * freqs + j) * CLASSES + class_of(direction)) * KINDS
+            scale = scalar_ref[base + 2]
+            target = 0 if to_right > 0 else LANES - 2
+            at_side = (tile_lane >= target) & (tile_lane < target + 2)
+            turn = target - direction % GROUP * 2 * freqs + LANES - 2 * j
+            turn = lax.rem(turn + LANES, LANES)
+            edge_tile = 0 if to_down > 0 else tiles - 1
+            edge = ((0 if to_down > 0 else 18) + row_slot(direction)) * freqs + j
+            result = []
+            for t in range(tiles):
+                part = slice(t * SUB, (t + 1) * SUB)
+                entered = pltpu.roll(columns_ref[direction // GROUP, part, :], turn, 1)
+                value = kept_ref[j, direction, part, :] + jnp.where(at_side, entered, 0.0)
+                if t == edge_tile:
+                    value += edges_ref[pl.ds(pl.multiple_of(edge * SUB, SUB), SUB), :]
+                growth = growth_ref[direction, part, :]
+                factor = ratio_ref[0, j, part, :] + ratio_ref[1, j, part, :] * growth
+                result.append(value * (scale * factor))
+            return result
+
+        pending = []
+        for direction in range(ND + 2):
+            if direction < ND:
+                pending.append(damped(*divmod(direction, quarter)))
+            if direction >= 2:
+                quadrant, i = divmod(direction - 2, quarter)
                 for t, value in enumerate(pending.pop(0)):
-                    ring_ref[slot, j, 0, t * SUB : (t + 1) * SUB, :] = value
-            send(direction, slot).start()
-            return carry
-
-        lax.fori_loop(0, quarter, one, 0)
-    for direction in range(ND - SLOTS, ND):
-        send(direction, direction % SLOTS).wait()
+                    ring_ref[slot, quadrant, i, t * SUB : (t + 1) * SUB, :] = value
+                if i == quarter - 1:
+                    send(j, quadrant).start()
+        return carry
+
+    lax.fori_loop(0, freqs, frequency, 0)
+    for j in range(max(0, freqs - 2), freqs):
+        for quadrant in range(4):
+            send(jnp.int32(j), quadrant).wait()
 
 
 def step_pairs(axis, step):
@@ -883,10 +894,11 @@
     block = (freqs, ND, rows, lanes)
     spectrum = spectrum.reshape(block)
 
-    growth, wet, to_right, to_left, to_down, to_up, edges = call(
+    kept, growth, wet, to_right, to_left, to_down, to_up, edges = call(
         functools.partial(pack_kernel, freqs),
-        [SMEM] + [HBM] * 7,
+        [SMEM, SMEM] + [HBM] * 7,
         (
+            in_vmem(*block),
             in_any(ND, rows, lanes),
             in_any(rows, lanes),
             in_any(GROUPS // 2, rows, lanes),
@@ -895,11 +907,13 @@
             in_any(row_message, lanes),
             in_any(2 * 18 * freqs * SUB, lanes),
         ),
-        (VMEM,) * 7,
-        flops=local_comp * cells * 4,
-        moved=local_comp * cells * 4,
+        (VMEM,) * 8,
+        flops=local_comp * cells * 8,
+        moved=local_comp * cells * 8,
         scratch=[
-            pltpu.VMEM((local_comp * rows, lanes), jnp.float32),
+            pltpu.VMEM((SLOTS, ND, rows, lanes), jnp.float32),
+            pltpu.VMEM((ND * freqs, lanes), jnp.float32),
+            pltpu.VMEM((ND * freqs, lanes), jnp.float32),
             pltpu.VMEM(lane_table.shape[1:], jnp.float32),
             pltpu.VMEM(row_table.shape[1:], jnp.float32),
             pltpu.VMEM((rows, lanes), jnp.int32),
@@ -907,18 +921,20 @@
             pltpu.VMEM((rows, lanes), jnp.float32),
             pltpu.VMEM((rows, lanes), jnp.float32),
             pltpu.SemaphoreType.DMA((6,)),
-            pltpu.SemaphoreType.DMA((GROUPS,)),
-        ],
-        limit=30,
+            pltpu.SemaphoreType.DMA((SLOTS,)),
+        ]
+        + [pltpu.VMEM((rows + 2 * SUB, lanes), jnp.float32)] * (ND // 2),
+        limit=12,
     )(
         member,
+        scalars,
         *map(in_hbm, (lane_table, row_table, land_mask, ice_mask, wind_u, wind_v, spectrum)),
     )
 
     def main_part(start, stop, *before):
         return call(
             functools.partial(main_kernel, freqs, start, stop),
-            [SMEM, SMEM, VMEM, VMEM, HBM] + ([ANY, VMEM, VMEM, VMEM, VMEM] if before else []),
+            [SMEM, SMEM, VMEM, VMEM] + ([ANY] + [VMEM] * 4 if start else [VMEM]),
             (
                 in_vmem(*block),
                 in_any(freqs * rows, lanes),
@@ -926,21 +942,15 @@
                 in_any(rows, lanes),
             ),
             (VMEM,) * 4,
-            flops=local_comp * cells * 16 * (stop - start) // freqs,
+            flops=local_comp * cells * 9 * (stop - start) // freqs,
             moved=local_comp * cells * 8 * (stop - start) // freqs,
-            scratch=[
-                pltpu.VMEM((AHEAD, ND, rows, lanes), jnp.float32),
-                pltpu.SemaphoreType.DMA((AHEAD,)),
-            ]
-            + [pltpu.VMEM((rows + 2 * SUB, lanes), jnp.float32)] * 8,
-            aliases={6 + index: index for index in range(4)} if before else {},
-            limit=8,
-        )(member, scalars, wet, growth, in_hbm(spectrum), *before)
+            aliases={5 + index: index for index in range(4)} if start else {4: 0},
+        )(member, scalars, wet, growth, *before)
 
     early = max(1, freqs // 3)
     from_left = neighbour(to_right, "sect", 1)
     from_right = neighbour(to_left, "sect", -1)
-    kept, *partial = main_part(0, early)
+    kept, *partial = main_part(0, early, kept)
     to_down, to_up = call(
         functools.partial(corner_kernel, freqs),
         [VMEM, VMEM, VMEM, ANY, ANY, ANY],
@@ -1023,8 +1033,8 @@
         moved=local_comp * cells * 8,
         scratch=[
             pltpu.VMEM((2, freqs, rows, lanes), jnp.float32),
-            pltpu.VMEM((SLOTS, freqs, 1, rows, lanes), jnp.float32),
-            pltpu.SemaphoreType.DMA((SLOTS,)),
+            pltpu.VMEM((2, 4, ND // 4, rows, lanes), jnp.float32),
+            pltpu.SemaphoreType.DMA((2, 4)),
         ],
     )(
         member, scalars, wet, depth, square, sums, beside, above, below, growth, kept,

time: 86.6 us -> 87.5 us (1.010)
    pallas_call x1, Pallas kernels: 10.2 us -> 16.8 us  [resident(): call(functools.partial(pack_kernel, freqs), [SMEM, SMEM] + [HBM] * 7, (in...]
    pallas_call x1, Pallas kernels: 16 us -> 12.7 us  [resident(): call(functools.partial(final_kernel, freqs), [SMEM, SMEM] + [VMEM] * 11,...]
    pallas_call x2, Pallas kernels: 20.3 us -> 17.1 us  [main_part(): call(functools.partial(main_kernel, freqs, start, stop), [SMEM, SMEM, VME...]
  transfers between devices with their start and end apart: 10 -> 10, of which waited for: 4 -> 4; matrix products, arithmetic and copies ran while one was open for 0% -> 0% of each run, Pallas kernels for 25% -> 21%
where the time goes in v3:
time: 87.5 us; the launch traced here: 87.1 us
  Pallas kernels  50.3 us (57%)
  starting transfers between devices  24.7 us (28%)
  waiting for transfers between devices  10.6 us (12%)
    ppermute x8, starting transfers between devices, neighbour(): return lax.ppermute(values, axis, step_pairs(axis, step))  21.6 us
    pallas_call x2, Pallas kernels, main_part(): call(functools.partial(main_kernel, freqs, start, stop), [SMEM, SMEM, VME...  17.1 us
    pallas_call x1, Pallas kernels, resident(): call(functools.partial(pack_kernel, freqs), [SMEM, SMEM] + [HBM] * 7, (in...  16.8 us
    pallas_call x1, Pallas kernels, resident(): call(functools.partial(final_kernel, freqs), [SMEM, SMEM] + [VMEM] * 11,...  12.7 us
    ppermute x8, waiting for transfers between devices, neighbour(): return lax.ppermute(values, axis, step_pairs(axis, step))  6.45 us
    ppermute x2, waiting for transfers between devices, others_sum(): lax.ppermute(values, axis, [(i, (i + step) % count) for i in range(count)])  4.11 us
    ppermute x2, starting transfers between devices, others_sum(): lax.ppermute(values, axis, [(i, (i + step) % count) for i in range(count)])  3.11 us
  transfers between devices with their start and end apart: 10, of which 4 were waited for; matrix products, arithmetic and copies ran while one was open for 0% of the time, Pallas kernels for 21%

profile of v3, /device:TPU:12, one launch (start us, length us, event | category | flops | bytes accessed | tf_op | source)
XLA Modules:
  0.0 87.1 jit_solution(16903366071393986993)
XLA Ops:
  0.6 0.0 copy-start.2
  0.6 0.7 copy-done.2
  1.3 16.8 %shard_map.104 = (f32[18,36,64,128]{3,2,1,0:T(8,128)S(1)}, f32[36,64,128]{2,1,0:T(8,128)S(1)}, f32[64,128]{1,0:T(8,128)S(1)}, f32[6,64,128]{2,1,0:T(8,128)S(1)},...) custom-call(s32[1]{0:T(128)} %bitcast.member_ref, ...), custom_call_target="tpu_custom_call" | custom-call | flops 42467328 | bytes 42467328 | tf_op jit(solution)/shard_map/pallas_call | solution.py:897
  18.1 1.9 %collective-permute-start = (f32[6,64,128]{2,1,0:T(8,128)S(1)}, f32[6,64,128]{2,1,0:T(8,128)S(1)}, u32[]{:S(2)}, u32[]{:S(2)}) collective-permute-start(f32[6,64,128]{2,1,0:T(8,128)S(1)} %get-tuple-element.36), channel_id=1, source_target_pairs={{0,4},{4,8},{8,12},{1,5},{5,9},{9,13},{2,6},{6,10},{10,14},{3,7},{... | collective-permute-start | bytes 589832 | tf_op jit(solution)/shard_map/ppermute | solution.py:842
  20.1 3.6 %collective-permute-start.1 = (f32[6,64,128]{2,1,0:T(8,128)S(1)}, f32[6,64,128]{2,1,0:T(8,128)S(1)}, u32[]{:S(2)}, u32[]{:S(2)}) collective-permute-start(f32[6,64,128]{2,1,0:T(8,128)S(1)} %get-tuple-element.37), channel_id=1, source_target_pairs={{4,0},{8,4},{12,8},{5,1},{9,5},{13,9},{6,2},{10,6},{14,10},{7,3},{... | collective-permute-start | bytes 589832 | tf_op jit(solution)/shard_map/ppermute | solution.py:842
  23.7 0.0 copy-start
  23.7 0.0 copy-start.1
  23.7 0.0 copy-start.3
  23.7 0.0 copy-start.4
  23.8 0.0 copy-start.5
  23.8 5.9 %shard_map.105 = (f32[18,36,64,128]{3,2,1,0:T(8,128)S(1)}, f32[1152,128]{1,0:T(8,128)S(1)}, f32[1152,128]{1,0:T(8,128)S(1)}, f32[64,128]{1,0:T(8,128)S(1)}) custom-call(s32[1]{0:T(128)} %bitcast.member_ref, f32[1800]{0:T(1024)S(1)} %copy-done.2, f32[64,128]{1,0:T(8,128)S(1)} %get-tuple-element.34.wet_ref, ...), custom_call_target="tpu_custom_call", output_to_operand_aliasing={{0}: (4, {})} | custom-call | flops 15925248 | bytes 14155776 | tf_op jit(solution)/shard_map/pallas_call | solution.py:935
  29.7 0.0 copy-start.6
  29.7 0.0 collective-permute-done.right_ref
  29.7 0.0 collective-permute-done.1.left_ref
  29.7 0.1 shard_map.106
  29.8 2.4 %collective-permute-start.3 = (f32[656,128]{1,0:T(8,128)S(1)}, f32[656,128]{1,0:T(8,128)S(1)}, u32[]{:S(2)}, u32[]{:S(2)}) collective-permute-start(f32[656,128]{1,0:T(8,128)S(1)} %get-tuple-element.43), channel_id=1, source_target_pairs={{1,0},{2,1},{3,2},{5,4},{6,5},{7,6},{9,8},{10,9},{11,10},{13,12},{... | collective-permute-start | bytes 1007624 | tf_op jit(solution)/shard_map/ppermute | solution.py:842
  32.2 3.5 %collective-permute-start.2 = (f32[656,128]{1,0:T(8,128)S(1)}, f32[656,128]{1,0:T(8,128)S(1)}, u32[]{:S(2)}, u32[]{:S(2)}) collective-permute-start(f32[656,128]{1,0:T(8,128)S(1)} %get-tuple-element.42.refs_0_), channel_id=1, source_target_pairs={{0,1},{1,2},{2,3},{4,5},{5,6},{6,7},{8,9},{9,10},{10,11},{12,13},{... | collective-permute-start | bytes 1007624 | tf_op jit(solution)/shard_map/ppermute | solution.py:842
  35.7 11.2 %shard_map.107 = (f32[18,36,64,128]{3,2,1,0:T(8,128)S(1)}, f32[1152,128]{1,0:T(8,128)S(1)}, f32[1152,128]{1,0:T(8,128)S(1)}, f32[64,128]{1,0:T(8,128)S(1)}) custom-call(s32[1]{0:T(128)} %bitcast.member_ref, f32[1800]{0:T(1024)S(1)} %copy-done.2, ...), custom_call_target="tpu_custom_call", output_to_operand_aliasing={{0}: (5, {}), {1}: (6, {}), {2}: (7, {}), {3}: (8, {})} | custom-call | flops 31850496 | bytes 28311552 | tf_op jit(solution)/shard_map/pallas_call | solution.py:935
  46.9 0.0 collective-permute-done.3.up_ref
  46.9 0.0 collective-permute-done.2.down_ref
  46.9 0.0 copy-done
  46.9 0.0 copy-done.1
  46.9 1.1 %shard_map.108 = (f32[12,64,128]{2,1,0:T(8,128)S(1)}, f32[5184,128]{1,0:T(8,128)S(1)}, f32[64,128]{1,0:T(8,128)S(1)}) custom-call(s32[1]{0:T(128)} %bitcast.member_ref, f32[2,12,8,128]{3,2,1,0:T(8,128)S(1)} %copy-done.1, f32[2,10,5,18,128]{4,3,2,1,0:T(8,128)S(1)} %copy-done, ...), custom_call_target="tpu_custom_call", output_to_operand_aliasing={{1}: (8, {}), {2}: (9, {})} | custom-call | flops 4915200 | bytes 1638400 | tf_op jit(solution)/shard_map/pallas_call | solution.py:968
  48.0 1.6 %collective-permute-start.4 = (f32[64,128]{1,0:T(8,128)S(1)}, f32[64,128]{1,0:T(8,128)S(1)}, u32[]{:S(2)}, u32[]{:S(2)}) collective-permute-start(f32[64,128]{1,0:T(8,128)S(1)} %get-tuple-element.55.own_ref), channel_id=1, source_target_pairs={{0,16},{16,0},{1,17},{17,1},{2,18},{18,2},{3,19},{19,3},{4,20},{20... | collective-permute-start | bytes 98312 | tf_op jit(solution)/shard_map/ppermute | solution.py:849
  49.6 0.0 copy-done.3
  49.6 0.0 copy-done.4
  49.6 0.0 copy-done.5
  49.6 1.4 %shard_map.109 = (f32[1152,128]{1,0:T(8,128)S(1)}, f32[1152,128]{1,0:T(8,128)S(1)}) custom-call(s32[1]{0:T(128)} %bitcast.member_ref, f32[2,12,8,128]{3,2,1,0:T(8,128)S(1)} %copy-done.1, f32[2,10,5,18,128]{4,3,2,1,0:T(8,128)S(1)} %copy-done, s32[64,128]{1,0:T(8,128)S(1)} %copy-done.3, ...), custom_call_target="tpu_custom_call", output_to_operand_aliasing={{0}: (9, {}), {1}: (10, {})} | custom-call | flops 4915200 | bytes 1638400 | tf_op jit(solution)/shard_map/pallas_call | solution.py:985
  51.0 1.0 %collective-permute-done.4.other_ref = f32[64,128]{1,0:T(8,128)S(1)} collective-permute-done((f32[64,128]{1,0:T(8,128)S(1)}, f32[64,128]{1,0:T(8,128)S(1)}, u32[]{:S(2)}, u32[]{:S(2)}) %collective-permute-start.4) | collective-permute-done | bytes 32800 | tf_op jit(solution)/shard_map/ppermute | solution.py:849
  52.0 1.0 %shard_map.110 = (f32[3,64,128]{2,1,0:T(8,128)S(1)}, f32[64,128]{1,0:T(8,128)S(1)}) custom-call(s32[1]{0:T(128)} %bitcast.member_ref, f32[1800]{0:T(1024)S(1)} %copy-done.2, f32[64,128]{1,0:T(8,128)S(1)} %get-tuple-element.34.wet_ref, f32[1152,128]{1,0:T(8,128)S(1)} %get-tuple-element.53.a_ref, f32[1152,128]{1,0:T(8,128)S(1)} %get-tuple-element.54.b_ref, ...), custom_call_target="tpu_custom_call" | custom-call | flops 1769472 | bytes 1179648 | tf_op jit(solution)/shard_map/pallas_call | solution.py:998
  53.0 1.6 %collective-permute-start.5 = (f32[3,64,128]{2,1,0:T(8,128)S(1)}, f32[3,64,128]{2,1,0:T(8,128)S(1)}, u32[]{:S(2)}, u32[]{:S(2)}) collective-permute-start(f32[3,64,128]{2,1,0:T(8,128)S(1)} %get-tuple-element.57.own_ref), channel_id=1, source_target_pairs={{0,16},{16,0},{1,17},{17,1},{2,18},{18,2},{3,19},{19,3},{4,20},{20... | collective-permute-start | bytes 294920 | tf_op jit(solution)/shard_map/ppermute | solution.py:849
  54.6 3.1 %collective-permute-done.5.other_ref = f32[3,64,128]{2,1,0:T(8,128)S(1)} collective-permute-done((f32[3,64,128]{2,1,0:T(8,128)S(1)}, f32[3,64,128]{2,1,0:T(8,128)S(1)}, u32[]{:S(2)}, u32[]{:S(2)}) %collective-permute-start.5) | collective-permute-done | bytes 98336 | tf_op jit(solution)/shard_map/ppermute | solution.py:849
  57.7 1.9 %collective-permute-start.7 = (f32[2,64,128]{2,1,0:T(8,128)S(1)}, f32[2,64,128]{2,1,0:T(8,128)S(1)}, u32[]{:S(2)}, u32[]{:S(2)}) collective-permute-start(f32[2,64,128]{2,1,0:T(8,128)S(1)} %get-tuple-element.59.stress_ref), channel_id=1, source_target_pairs={{4,0},{8,4},{12,8},{5,1},{9,5},{13,9},{6,2},{10,6},{14,10},{7,3},{... | collective-permute-start | bytes 196616 | tf_op jit(solution)/shard_map/ppermute | solution.py:842
  59.6 2.4 %collective-permute-start.6 = (f32[2,64,128]{2,1,0:T(8,128)S(1)}, f32[2,64,128]{2,1,0:T(8,128)S(1)}, u32[]{:S(2)}, u32[]{:S(2)}) collective-permute-start(f32[2,64,128]{2,1,0:T(8,128)S(1)} %get-tuple-element.59.stress_ref), channel_id=1, source_target_pairs={{0,4},{4,8},{8,12},{1,5},{5,9},{9,13},{2,6},{6,10},{10,14},{3,7},{... | collective-permute-start | bytes 196616 | tf_op jit(solution)/shard_map/ppermute | solution.py:842
  62.1 0.0 collective-permute-done.7.right_ref
  62.1 3.2 %collective-permute-done.6.left_ref = f32[2,64,128]{2,1,0:T(8,128)S(1)} collective-permute-done((f32[2,64,128]{2,1,0:T(8,128)S(1)}, f32[2,64,128]{2,1,0:T(8,128)S(1)}, u32[]{:S(2)}, u32[]{:S(2)}) %collective-permute-start.6) | collective-permute-done | bytes 65568 | tf_op jit(solution)/shard_map/ppermute | solution.py:842
  65.2 3.5 %collective-permute-start.8 = (f32[2,8,256]{2,1,0:T(8,128)S(1)}, f32[2,8,256]{2,1,0:T(8,128)S(1)}, u32[]{:S(2)}, u32[]{:S(2)}) collective-permute-start(f32[2,8,256]{2,1,0:T(8,128)S(1)} %get-tuple-element.61), channel_id=1, source_target_pairs={{0,1},{1,2},{2,3},{4,5},{5,6},{6,7},{8,9},{9,10},{10,11},{12,13},{... | collective-permute-start | bytes 49160 | tf_op jit(solution)/shard_map/ppermute | solution.py:842
  68.8 2.3 %collective-permute-start.9 = (f32[2,8,256]{2,1,0:T(8,128)S(1)}, f32[2,8,256]{2,1,0:T(8,128)S(1)}, u32[]{:S(2)}, u32[]{:S(2)}) collective-permute-start(f32[2,8,256]{2,1,0:T(8,128)S(1)} %get-tuple-element.62), channel_id=1, source_target_pairs={{1,0},{2,1},{3,2},{5,4},{6,5},{7,6},{9,8},{10,9},{11,10},{13,12},{... | collective-permute-start | bytes 49160 | tf_op jit(solution)/shard_map/ppermute | solution.py:842
  71.1 0.0 collective-permute-done.8.above_ref
  71.1 3.3 %collective-permute-done.9.below_ref = f32[2,8,256]{2,1,0:T(8,128)S(1)} collective-permute-done((f32[2,8,256]{2,1,0:T(8,128)S(1)}, f32[2,8,256]{2,1,0:T(8,128)S(1)}, u32[]{:S(2)}, u32[]{:S(2)}) %collective-permute-start.9) | collective-permute-done | bytes 16416 | tf_op jit(solution)/shard_map/ppermute | solution.py:842
  74.4 0.0 copy-done.6
  74.4 12.7 %shard_map.113 = (f32[18,36,64,128]{3,2,1,0:T(8,128)}, f32[64,128]{1,0:T(8,128)}) custom-call(s32[1]{0:T(128)} %bitcast.member_ref, f32[1800]{0:T(1024)S(1)} %copy-done.2, f32[64,128]{1,0:T(8,128)S(1)} %get-tuple-element.34.wet_ref, f32[64,128]{1,0:T(8,128)S(1)} %copy-done.6, f32[64,128]{1,0:T(8,128)S(1)} %get-tuple-element.56.square_ref, ...), custom_call_target="tpu_custom_call" | custom-call | flops 31850496 | bytes 42467328 | tf_op jit(solution)/shard_map/pallas_call | solution.py:1027
  (2 shorter events, 0.0 us)
Async XLA Ops:
  0.6 0.7 copy-start.2
  18.1 11.6 %collective-permute-start = (f32[6,64,128]{2,1,0:T(8,128)S(1)}, f32[6,64,128]{2,1,0:T(8,128)S(1)}, u32[]{:S(2)}, u32[]{:S(2)}) collective-permute-start(f32[6,64,128]{2,1,0:T(8,128)S(1)} %get-tuple-element.36), channel_id=1, source_target_pairs={{0,4},{4,8},{8,12},{1,5},{5,9},{9,13},{2,6},{6,10},{10,14},{3,7},{... | collective-permute-start | bytes 589832 | tf_op jit(solution)/shard_map/ppermute | solution.py:842
  20.1 9.7 %collective-permute-start.1 = (f32[6,64,128]{2,1,0:T(8,128)S(1)}, f32[6,64,128]{2,1,0:T(8,128)S(1)}, u32[]{:S(2)}, u32[]{:S(2)}) collective-permute-start(f32[6,64,128]{2,1,0:T(8,128)S(1)} %get-tuple-element.37), channel_id=1, source_target_pairs={{4,0},{8,4},{12,8},{5,1},{9,5},{13,9},{6,2},{10,6},{14,10},{7,3},{... | collective-permute-start | bytes 589832 | tf_op jit(solution)/shard_map/ppermute | solution.py:842
  23.7 23.2 %copy-start = (f32[2,10,5,18,128]{4,3,2,1,0:T(8,128)S(1)}, f32[2,10,5,18,128]{4,3,2,1,0:T(8,128)}, u32[]{:S(2)}) copy-start(f32[2,10,5,18,128]{4,3,2,1,0:T(8,128)} %constant.14.clone.table_hbm.table_ref) | copy-start | bytes 2764804
  23.7 23.2 %copy-start.1 = (f32[2,12,8,128]{3,2,1,0:T(8,128)S(1)}, f32[2,12,8,128]{3,2,1,0:T(8,128)}, u32[]{:S(2)}) copy-start(f32[2,12,8,128]{3,2,1,0:T(8,128)} %constant.13.clone.lanes_hbm.lanes_ref) | copy-start | bytes 294916
  23.7 25.9 %copy-start.3 = (s32[64,128]{1,0:T(8,128)S(1)}, s32[64,128]{1,0:T(8,128)}, u32[]{:S(2)}) copy-start(s32[64,128]{1,0:T(8,128)} %ice_ref.1) | copy-start | bytes 98308
  23.7 25.9 %copy-start.4 = (f32[64,128]{1,0:T(8,128)S(1)}, f32[64,128]{1,0:T(8,128)}, u32[]{:S(2)}) copy-start(f32[64,128]{1,0:T(8,128)} %east_ref.1) | copy-start | bytes 98308
  23.8 25.9 %copy-start.5 = (f32[64,128]{1,0:T(8,128)S(1)}, f32[64,128]{1,0:T(8,128)}, u32[]{:S(2)}) copy-start(f32[64,128]{1,0:T(8,128)} %north_ref.1) | copy-start | bytes 98308
  29.7 44.7 %copy-start.6 = (f32[64,128]{1,0:T(8,128)S(1)}, f32[64,128]{1,0:T(8,128)}, u32[]{:S(2)}) copy-start(f32[64,128]{1,0:T(8,128)} %depth_ref.1) | copy-start | bytes 98308
  29.8 17.1 %collective-permute-start.3 = (f32[656,128]{1,0:T(8,128)S(1)}, f32[656,128]{1,0:T(8,128)S(1)}, u32[]{:S(2)}, u32[]{:S(2)}) collective-permute-start(f32[656,128]{1,0:T(8,128)S(1)} %get-tuple-element.43), channel_id=1, source_target_pairs={{1,0},{2,1},{3,2},{5,4},{6,5},{7,6},{9,8},{10,9},{11,10},{13,12},{... | collective-permute-start | bytes 1007624 | tf_op jit(solution)/shard_map/ppermute | solution.py:842
  32.2 14.7 %collective-permute-start.2 = (f32[656,128]{1,0:T(8,128)S(1)}, f32[656,128]{1,0:T(8,128)S(1)}, u32[]{:S(2)}, u32[]{:S(2)}) collective-permute-start(f32[656,128]{1,0:T(8,128)S(1)} %get-tuple-element.42.refs_0_), channel_id=1, source_target_pairs={{0,1},{1,2},{2,3},{4,5},{5,6},{6,7},{8,9},{9,10},{10,11},{12,13},{... | collective-permute-start | bytes 1007624 | tf_op jit(solution)/shard_map/ppermute | solution.py:842
  48.0 4.0 %collective-permute-start.4 = (f32[64,128]{1,0:T(8,128)S(1)}, f32[64,128]{1,0:T(8,128)S(1)}, u32[]{:S(2)}, u32[]{:S(2)}) collective-permute-start(f32[64,128]{1,0:T(8,128)S(1)} %get-tuple-element.55.own_ref), channel_id=1, source_target_pairs={{0,16},{16,0},{1,17},{17,1},{2,18},{18,2},{3,19},{19,3},{4,20},{20... | collective-permute-start | bytes 98312 | tf_op jit(solution)/shard_map/ppermute | solution.py:849
  53.0 4.7 %collective-permute-start.5 = (f32[3,64,128]{2,1,0:T(8,128)S(1)}, f32[3,64,128]{2,1,0:T(8,128)S(1)}, u32[]{:S(2)}, u32[]{:S(2)}) collective-permute-start(f32[3,64,128]{2,1,0:T(8,128)S(1)} %get-tuple-element.57.own_ref), channel_id=1, source_target_pairs={{0,16},{16,0},{1,17},{17,1},{2,18},{18,2},{3,19},{19,3},{4,20},{20... | collective-permute-start | bytes 294920 | tf_op jit(solution)/shard_map/ppermute | solution.py:849
  57.7 4.3 %collective-permute-start.7 = (f32[2,64,128]{2,1,0:T(8,128)S(1)}, f32[2,64,128]{2,1,0:T(8,128)S(1)}, u32[]{:S(2)}, u32[]{:S(2)}) collective-permute-start(f32[2,64,128]{2,1,0:T(8,128)S(1)} %get-tuple-element.59.stress_ref), channel_id=1, source_target_pairs={{4,0},{8,4},{12,8},{5,1},{9,5},{13,9},{6,2},{10,6},{14,10},{7,3},{... | collective-permute-start | bytes 196616 | tf_op jit(solution)/shard_map/ppermute | solution.py:842
  59.6 5.6 %collective-permute-start.6 = (f32[2,64,128]{2,1,0:T(8,128)S(1)}, f32[2,64,128]{2,1,0:T(8,128)S(1)}, u32[]{:S(2)}, u32[]{:S(2)}) collective-permute-start(f32[2,64,128]{2,1,0:T(8,128)S(1)} %get-tuple-element.59.stress_ref), channel_id=1, source_target_pairs={{0,4},{4,8},{8,12},{1,5},{5,9},{9,13},{2,6},{6,10},{10,14},{3,7},{... | collective-permute-start | bytes 196616 | tf_op jit(solution)/shard_map/ppermute | solution.py:842
  65.2 5.9 %collective-permute-start.8 = (f32[2,8,256]{2,1,0:T(8,128)S(1)}, f32[2,8,256]{2,1,0:T(8,128)S(1)}, u32[]{:S(2)}, u32[]{:S(2)}) collective-permute-start(f32[2,8,256]{2,1,0:T(8,128)S(1)} %get-tuple-element.61), channel_id=1, source_target_pairs={{0,1},{1,2},{2,3},{4,5},{5,6},{6,7},{8,9},{9,10},{10,11},{12,13},{... | collective-permute-start | bytes 49160 | tf_op jit(solution)/shard_map/ppermute | solution.py:842
  68.8 5.6 %collective-permute-start.9 = (f32[2,8,256]{2,1,0:T(8,128)S(1)}, f32[2,8,256]{2,1,0:T(8,128)S(1)}, u32[]{:S(2)}, u32[]{:S(2)}) collective-permute-start(f32[2,8,256]{2,1,0:T(8,128)S(1)} %get-tuple-element.62), channel_id=1, source_target_pairs={{1,0},{2,1},{3,2},{5,4},{6,5},{7,6},{9,8},{10,9},{11,10},{13,12},{... | collective-permute-start | bytes 49160 | tf_op jit(solution)/shard_map/ppermute | solution.py:842

commit v4 on v2

--- a/solution.py
+++ b/solution.py
@@ -227,6 +227,10 @@
     return scalars.reshape(-1), lanes, rows
 
 
+def odd_position(axis):
+    return lax.rem(lax.axis_index(axis), 2) == 1
+
+
 def iota(shape, axis):
     return lax.broadcasted_iota(jnp.int32, shape, axis)
 
@@ -252,19 +256,14 @@
 DEPTH = 3
 
 
-def slot_base(quadrant):
-    return (0, 9, 9, 18)[quadrant]
-
-
-def class_index(direction):
-    folded = lax.rem(direction, 18)
-    return jnp.where(folded <= 9, folded, 18 - folded)
+def sides(quadrant):
+    return 1 if quadrant in (0, 3) else -1, 1 if quadrant in (0, 1) else -1
 
 
 def pack_kernel(
     freqs, member_ref, lanes_hbm, table_hbm, land_hbm, ice_hbm, east_hbm, north_hbm, spectrum_ref,
-    growth_ref, wet_ref, right_ref, left_ref, down_ref, up_ref, edges_ref,
-    kept_ref, lanes_ref, table_ref, land_ref, ice_ref, east_ref, north_ref, small_sems, sems,
+    growth_ref, wet_ref, swap_side_ref, other_side_ref, swap_row_ref, other_row_ref, edges_ref,
+    kept_ref, right_ref, left_ref, lanes_ref, table_ref, land_ref, ice_ref, east_ref, north_ref, small_sems, sems,
 ):
     member = member_ref[0]
     small = [
@@ -309,8 +308,9 @@
     lane = iota(shape, 1)
     even = lane % 2 == 0
     tile_lane = iota((SUB, LANES), 1)
-    down_ref[pl.ds(2 * 18 * freqs, CORNERS), :] = jnp.zeros((CORNERS, LANES), jnp.float32)
-    up_ref[pl.ds(2 * 18 * freqs, CORNERS), :] = jnp.zeros((CORNERS, LANES), jnp.float32)
+    for row_ref in (swap_row_ref, other_row_ref):
+        row_ref[pl.ds(2 * 18 * freqs, CORNERS), :] = jnp.zeros((CORNERS, LANES), jnp.float32)
+    odd_sect, odd_slab = odd_position("sect"), odd_position("slab")
 
     half = GROUPS // 2
     for to_right in (True, False):
@@ -340,27 +340,20 @@
 
         lax.fori_loop(0, half, gather, 0)
 
-    pending = []
-    for group in range(GROUPS):
+    def side_message(group):
         to_right, fore = group < half, 1 if heads_down(group * GROUP) else -1
         ahead, behind = (LANES - 1, LANES - 2) if to_right else (0, 1)
         wet_near, wet_far = spread(wet_cells, ahead), spread(wet_cells, behind)
         near_even = not to_right
-        target_ref, index = (right_ref, group) if to_right else (left_ref, group - half)
-        values = target_ref[index] * jnp.where(even == near_even, wet_near, wet_far)
+        packed = right_ref[group] if to_right else left_ref[group - half]
+        values = packed * jnp.where(even == near_even, wet_near, wet_far)
         near = pltpu.roll(values, 1 if near_even else LANES - 1, 1)
         table = lanes_ref[group]
         follow = wet_near * (table[1:2] * values + table[2:3] * shift_rows(near, fore))
         message = jnp.where(even == near_even, values, follow)
-        pending.append((target_ref, index, jnp.where(lane == LANES - 1, wet_near, message)))
-        if group:
-            place_ref, index, message = pending.pop(0)
-            place_ref[index] = message
-    place_ref, index, message = pending.pop()
-    place_ref[index] = message
-
-    pending = []
-    for direction in range(ND):
+        return jnp.where(lane == LANES - 1, wet_near, message)
+
+    def row_message(direction):
         to_down = heads_down(direction)
         near_row, far_row = (rows - 1, rows - 2) if to_down else (0, 1)
         wet_near = wet_cells[near_row : near_row + 1, :]
@@ -369,38 +362,47 @@
         near = kept_ref[pl.ds(direction * rows + near_row, freqs, stride=ND * rows), :] * wet_near
         far = kept_ref[pl.ds(direction * rows + far_row, freqs, stride=ND * rows), :] * wet_far
         beside = shift_lanes(near, 1 if heads_right(direction) else -1)
-        follow = wet_near * (table[1] * far + table[2] * beside)
-        slot = row_slot(direction) * freqs
-        pending.append((down_ref if to_down else up_ref, slot, near, follow))
-        if len(pending) > 2 or direction == ND - 1:
-            for place_ref, slot, near, follow in pending:
-                place_ref[slot : slot + freqs, :] = near
-                place_ref[18 * freqs + slot : 18 * freqs + slot + freqs, :] = follow
-            pending = []
+        return near, wet_near * (table[1] * far + table[2] * beside)
+
+    for index in range(half):
+        right, left = side_message(index), side_message(index + half)
+        swap_side_ref[index] = jnp.where(odd_sect, left, right)
+        other_side_ref[index] = jnp.where(odd_sect, right, left)
+    by_slot = {(heads_down(d), row_slot(d)): d for d in range(ND)}
+    for slot in range(18):
+        pairs = zip(row_message(by_slot[True, slot]), row_message(by_slot[False, slot]))
+        for which, (down, up) in enumerate(pairs):
+            first = (which * 18 + slot) * freqs
+            swap_row_ref[first : first + freqs, :] = jnp.where(odd_slab, up, down)
+            other_row_ref[first : first + freqs, :] = jnp.where(odd_slab, down, up)
 
 
 def corner_kernel(
-    freqs, wet_ref, right_ref, left_ref, down_in, up_in, _after, down_ref, up_ref, rows_ref, sems
+    freqs, wet_ref, swapped_ref, other_ref, swap_in, other_in, _after, swap_row_ref, other_row_ref,
+    rows_ref, sems,
 ):
     rows = wet_ref.shape[0]
+    odd_sect, odd_slab = odd_position("sect"), odd_position("slab")
     last = iota((1, LANES), 1) == LANES - 1
     rows_ref[...] = jnp.zeros_like(rows_ref)
-    for which, row in ((0, rows - 1), (1, 0)):
-        for i in range(6):
-            source = right_ref if i < 3 else left_ref
-            if which == 0:
-                index = i if i < 3 else i
-            else:
-                index = i + 3 if i < 3 else i - 3
-            column = 0 if i < 3 else LANES - 1
+    for i in range(6):
+        from_left = i < 3
+        column = 0 if from_left else LANES - 1
+        ends = []
+        for row, index in ((rows - 1, i), (0, i + 3 if from_left else i - 3)):
+            swapped = swapped_ref[index, row : row + 1, :]
+            other = other_ref[index, row : row + 1, :]
+            came = jnp.where(odd_sect == from_left, swapped, other)
             own = jnp.broadcast_to(wet_ref[row : row + 1, column : column + 1], (1, LANES))
-            rows_ref[which, i : i + 1, :] = jnp.where(last, own, source[index, row : row + 1, :])
+            ends.append(jnp.where(last, own, came))
+        rows_ref[0, i : i + 1, :] = jnp.where(odd_slab, *ends[::-1])
+        rows_ref[1, i : i + 1, :] = jnp.where(odd_slab, *ends)
     start = 2 * 18 * freqs
     copies = [
         pltpu.make_async_copy(
             rows_ref.at[which], ref.at[pl.ds(start, CORNERS), :], sems.at[which]
         )
-        for which, ref in ((0, down_ref), (1, up_ref))
+        for which, ref in ((0, swap_row_ref), (1, other_row_ref))
     ]
     for copy in copies:
         copy.start()
@@ -408,26 +410,23 @@
         copy.wait()
 
 
-AHEAD = 3
-
-
 def main_kernel(
     freqs, start, stop, member_ref, scalar_ref, wet_ref, growth_ref, spectrum_ref, *refs
 ):
     if start:
         _after, _kept_in, a_in, b_in, energy_in, *refs = refs
-    kept_ref, a_ref, b_ref, energy_ref, ring_ref, sems, *first_refs = refs
+    kept_ref, a_ref, b_ref, energy_ref, ring0, ring1, sums_ref, sems, *first_refs = refs
+    rings = (ring0, ring1)
     member = member_ref[0]
     nought = jnp.minimum(member, 0)
     rows = wet_ref.shape[0]
     tiles = rows // SUB
 
-    def fetch(j):
-        slot = lax.rem(j, AHEAD)
-        return pltpu.make_async_copy(spectrum_ref.at[j], ring_ref.at[slot], sems.at[slot])
-
-    for j in range(start, min(start + AHEAD, stop)):
-        fetch(jnp.int32(j)).start()
+    def fetch(j, which):
+        return pltpu.make_async_copy(spectrum_ref.at[j], rings[which], sems.at[which])
+
+    for which in range(min(2, stop - start)):
+        fetch(start + which, which).start()
 
     lane = iota((SUB, LANES), 1)
     sub = iota((SUB, LANES), 0)
@@ -439,90 +438,124 @@
         first_ref[...] = jnp.zeros_like(first_ref)
 
     def tile_at(tile):
-        return pl.ds(tile * SUB, SUB)
-
-    def row_shift(quadrant):
-        return -1 if quadrant in (0, 3) else 1
+        return slice(tile * SUB, (tile + 1) * SUB)
 
     def parts_of(kind):
         if kind == 0:
             return ((0, 0, 0), (9, 1, 9), (18, 2, 0), (27, 3, 9))
         return ((kind, 0, kind), (18 - kind, 1, kind), (18 + kind, 2, kind), (36 - kind, 3, kind))
 
-    def frequency(j, carry):
-        fetch(j).wait()
-        slot = lax.rem(j, AHEAD)
+    def frequency(j, which):
+        fetch(j, which).wait()
+        ring_ref = rings[which]
         base = (member * freqs + j) * CLASSES * KINDS
-        at = [pl.ds(pl.multiple_of(j * rows, SUB) + t * SUB, SUB) for t in range(tiles)]
 
         def speeds(part):
-            at_class = base + part[2] * KINDS
-            beta = scalar_ref[at_class + 1]
-            return scalar_ref[at_class], beta * (not_first if part[1] in (0, 1) else not_last)
-
-        def beside(cells, quadrant):
-            return pltpu.roll(cells, 1 if quadrant in (0, 1) else LANES - 1, 1)
-
-        def first_step(kind):
-            parts = parts_of(kind)
-            speed = [speeds(part) for part in parts]
-            wet = [wet_ref[tile_at(t), :] for t in range(tiles)]
-            for (direction, quadrant, _), (alpha, across) in zip(parts, speed):
-                shift = row_shift(quadrant)
-                edge = top if shift < 0 else bottom
-                target = first_refs[kind % 2 * 4 + quadrant]
-                cells = [ring_ref[slot, direction, tile_at(t), :] * wet[t] for t in range(tiles)]
-                turned = [pltpu.roll(cells[t], -shift % SUB, 0) for t in range(tiles)]
-                for t in range(tiles):
-                    before = turned[t + shift] if 0 <= t + shift < tiles else 0.0
-                    ahead = jnp.where(edge, before, turned[t])
-                    after = cells[t] + alpha * ahead + across * beside(cells[t], quadrant)
-                    target[tile_at(t + 1), :] = wet[t] * after
-
-        def second_step(kind):
-            parts = parts_of(kind)
+            _, quadrant, kind = part
+            across = scalar_ref[base + kind * KINDS + 1]
+            across = across * (not_first if quadrant in (0, 1) else not_last)
+            return scalar_ref[base + kind * KINDS], across
+
+        walks = [(kind, part) for kind in range(CLASSES - 1) for part in parts_of(kind)]
+        wet = [wet_ref[tile_at(t), :] for t in range(tiles)]
+        held = {}
+
+        def mask(walk):
+            direction = walks[walk][1][0]
+            target = first_refs[walk % 4]
+            cells = [ring_ref[direction, tile_at(t), :] * wet[t] for t in range(tiles)]
+            for t in range(tiles):
+                target[tile_at(t + 1), :] = cells[t]
+            held[walk] = cells
+
+        def step(walk, source, cells):
+            _, quadrant, _ = walks[walk][1]
+            alpha, across = speeds(walks[walk][1])
+            to_down, to_right = sides(quadrant)
+            ahead = [source[pl.ds((t + 1) * SUB - to_down + nought, SUB), :] for t in range(tiles)]
+            return [
+                cells[t] + alpha * ahead[t] + across * pltpu.roll(cells[t], to_right % LANES, 1)
+                for t in range(tiles)
+            ]
+
+        def first_step(walk):
+            after = step(walk, first_refs[walk % 4], held[walk])
+            cells = [wet[t] * after[t] for t in range(tiles)]
+            target = first_refs[4 + walk % 4]
+            for t in range(tiles):
+                target[tile_at(t + 1), :] = cells[t]
+            held[walk] = cells
+
+        def second_step(walk):
+            direction = walks[walk][1][0]
+            after = step(walk, first_refs[4 + walk % 4], held.pop(walk))
+            for t in range(tiles):
+                kept_ref[j, direction, tile_at(t), :] = after[t]
+            return after, [growth_ref[direction, tile_at(t), :] * after[t] for t in range(tiles)]
+
+        def plus(one, other):
+            return [x + y for x, y in zip(one, other)]
+
+        def add_up(kind, moved, grown):
             scale, high = scalar_ref[base + kind * KINDS + 2], scalar_ref[base + 3]
             scaled_high = scale * high
-            speed = [speeds(part) for part in parts]
-            for t in range(tiles):
-                moved, grown = [], []
-                for (direction, quadrant, _), (alpha, across) in zip(parts, speed):
-                    source = first_refs[kind % 2 * 4 + quadrant]
-                    cells = source[tile_at(t + 1), :]
-                    ahead = source[pl.ds((t + 1) * SUB + row_shift(quadrant) + nought, SUB), :]
-                    after = cells + alpha * ahead + across * beside(cells, quadrant)
-                    kept_ref[j, direction, tile_at(t), :] = after
+            if kind == 0:
+                plain_x, plain_y = plus(moved[0], moved[2]), plus(moved[1], moved[3])
+                grown_x, grown_y = plus(grown[0], grown[2]), plus(grown[1], grown[3])
+                square = math.cos(0.5 * math.pi) ** 2
+                for t in range(tiles):
+                    plain = scale * plain_x[t], scale * plain_y[t]
+                    whole_x = plain[0] + scaled_high * grown_x[t]
+                    whole_y = plain[1] + scaled_high * grown_y[t]
+                    energy_ref[tile_at(t), :] += plain[0] + plain[1]
+                    sums_ref[0, tile_at(t), :] = whole_x + whole_y
+                    sums_ref[1, tile_at(t), :] = whole_x + square * whole_y
+            else:
+                square = math.cos(2.0 * math.pi * kind / ND) ** 2
+                for t in range(tiles):
+                    plain = scale * moved[t]
+                    whole = plain + scaled_high * grown[t]
+                    energy_ref[tile_at(t), :] += plain
+                    sums_ref[0, tile_at(t), :] += whole
+                    sums_ref[1, tile_at(t), :] += square * whole
+
+        moved, grown = [], []
+        for walk in range(len(walks) + 2):
+            if walk < len(walks):
+                mask(walk)
+            if 1 <= walk <= len(walks):
+                first_step(walk - 1)
+            if walk >= 2:
+                kind = walks[walk - 2][0]
+                after, with_growth = second_step(walk - 2)
+                if kind and moved:
+                    moved, grown = plus(moved, after), plus(grown, with_growth)
+                elif kind:
+                    moved, grown = after, with_growth
+                else:
                     moved.append(after)
-                    grown.append(growth_ref[direction, tile_at(t), :] * after)
-                if kind == 0:
-                    plain_x, plain_y = scale * (moved[0] + moved[2]), scale * (moved[1] + moved[3])
-                    grown_x = plain_x + scaled_high * (grown[0] + grown[2])
-                    grown_y = plain_y + scaled_high * (grown[1] + grown[3])
-                    square = math.cos(0.5 * math.pi) ** 2
-                    energy_ref[tile_at(t), :] += plain_x + plain_y
-                    a_ref[at[t], :] = grown_x + grown_y
-                    b_ref[at[t], :] = grown_x + square * grown_y
-                else:
-                    plain = scale * ((moved[0] + moved[1]) + (moved[2] + moved[3]))
-                    whole = plain + scaled_high * ((grown[0] + grown[1]) + (grown[2] + grown[3]))
-                    square = math.cos(2.0 * math.pi * kind / ND) ** 2
-                    energy_ref[tile_at(t), :] += plain
-                    a_ref[at[t], :] += whole
-                    b_ref[at[t], :] += square * whole
-
-        first_step(0)
-        for kind in range(CLASSES - 1):
-            if kind + 1 < CLASSES - 1:
-                first_step(kind + 1)
-            second_step(kind)
-
-        @pl.when(j + AHEAD < stop)
-        def _():
-            fetch(j + AHEAD).start()
+                    grown.append(with_growth)
+                if walk % 4 == 1:
+                    add_up(kind, moved, grown)
+                    moved, grown = [], []
+        at = pl.ds(pl.multiple_of(j * rows, SUB), rows)
+        a_ref[at, :] = sums_ref[0]
+        b_ref[at, :] = sums_ref[1]
+
+    def pair(index, carry):
+        for which in range(2):
+            j = start + 2 * index + which
+            frequency(j, which)
+
+            @pl.when(j + 2 < stop)
+            def _():
+                fetch(j + 2, which).start()
 
         return carry
 
-    lax.fori_loop(start, stop, frequency, 0)
+    lax.fori_loop(0, (stop - start) // 2, pair, 0)
+    if (stop - start) % 2:
+        frequency(jnp.int32(stop - 1), 0)
 
 
 def edge_rows(freqs, to_down, direction, at):
@@ -531,8 +564,8 @@
 
 
 def enter_kernel(
-    freqs, member_ref, lanes_ref, table_ref, wet_ref, right_ref, left_ref, down_ref, up_ref,
-    _edges_in, energy_in, columns_ref, edges_ref, energy_ref,
+    freqs, member_ref, lanes_ref, table_ref, wet_ref, swap_side_ref, other_side_ref, swap_row_ref,
+    other_row_ref, _edges_in, energy_in, columns_ref, edges_ref, energy_ref,
 ):
     member = member_ref[0]
     wet_cells = wet_ref[...]
@@ -545,6 +578,10 @@
     used = lane < GROUP * width
     energy = energy_in[...]
     start = 2 * 18 * freqs
+    odd_sect, odd_slab = odd_position("sect"), odd_position("slab")
+
+    def from_rows(to_down, part):
+        return jnp.where(odd_slab == to_down, swap_row_ref[part, :], other_row_ref[part, :])
 
     for to_right in (True, False):
         near_column, far_column = (0, 1) if to_right else (LANES - 1, LANES - 2)
@@ -555,12 +592,12 @@
             group = index if to_right else index + GROUPS // 2
             to_down = heads_down(group * GROUP)
             fore = 1 if to_down else -1
-            message = (right_ref if to_right else left_ref)[index]
+            message = jnp.where(odd_sect == to_right, swap_side_ref[index], other_side_ref[index])
             table = lanes_ref[member, group]
             turn = LANES - 1 if near_even else 1
             entered = pltpu.roll(message, turn, 1)
             corner_index = index if to_down else (index - 3 if to_right else index + 3)
-            corner = (down_ref if to_down else up_ref)[pl.ds(start + corner_index, 1), :]
+            corner = from_rows(to_down, slice(start + corner_index, start + corner_index + 1))
             edge = 0 if to_down else rows - 1
             paths = corner[:, LANES - 1 :] + message[edge : edge + 1, LANES - 1 :]
             corner = pltpu.roll(jnp.broadcast_to(corner, (SUB, LANES)), turn, 1)[0:1]
@@ -582,7 +619,6 @@
 
     for to_down in (True, False):
         near_row, far_row = (0, 1) if to_down else (rows - 1, rows - 2)
-        message_ref = down_ref if to_down else up_ref
         wet_near = wet_cells[near_row : near_row + 1, :]
         wet_both = wet_near * wet_cells[far_row : far_row + 1, :]
         totals = [jnp.zeros((freqs, LANES), jnp.float32) for _ in range(2)]
@@ -590,8 +626,8 @@
             if heads_down(direction) != to_down:
                 continue
             slot = row_slot(direction) * freqs
-            entered = message_ref[slot : slot + freqs, :]
-            follow = message_ref[18 * freqs + slot : 18 * freqs + slot + freqs, :]
+            entered = from_rows(to_down, slice(slot, slot + freqs))
+            follow = from_rows(to_down, slice(18 * freqs + slot, 18 * freqs + slot + freqs))
             table = table_ref.at[member, class_of(direction)]
             side = 1 if heads_right(direction) else -1
             diagonal = shift_lanes(wet_near * entered, side)
@@ -670,14 +706,13 @@
 
 
 def stress_kernel(
-    freqs, member_ref, scalar_ref, wet_ref, a_ref, b_ref, own_ref, other_ref, sums_ref, square_ref
+    freqs, member_ref, scalar_ref, wet_ref, a_ref, b_ref, own_ref, other_ref, sums_ref, ratio_ref
 ):
     member = member_ref[0]
     wet_cells = wet_ref[...]
     rows = wet_cells.shape[0]
     energy = wet_cells * (own_ref[...] + other_ref[...]) / (ND * NF)
     square = jnp.square(energy)
-    square_ref[...] = square
 
     sums = [jnp.zeros(wet_cells.shape, jnp.float32) for _ in range(3)]
     for j in range(freqs):
@@ -685,6 +720,7 @@
         high, shoal = scalar_ref[base + 3], scalar_ref[base + 4]
         block = slice(j * rows, (j + 1) * rows)
         ratio = wet_cells / (1.0 + (2.0 * high) * square)
+        ratio_ref[j] = ratio
         whole = ratio * a_ref[block, :]
         along = ratio * b_ref[block, :]
         sums[0] += shoal * along + (shoal - 0.5) * whole
@@ -699,28 +735,34 @@
     stress_ref[...] = sums_ref[0:2]
 
 
-def strip_kernel(stress_ref, left_ref, right_ref, beside_ref, top_ref, bottom_ref):
+def strip_kernel(stress_ref, swapped_ref, other_ref, beside_ref, first_ref, second_ref):
     rows = stress_ref.shape[1]
     low_half = iota((rows, LANES), 1) < LANES // 2
+    odd_sect = lax.rem(lax.axis_index("sect"), 2) == 1
+    odd_slab = lax.rem(lax.axis_index("slab"), 2) == 1
     for index in range(2):
-        beside = jnp.where(low_half, right_ref[index], left_ref[index])
+        swapped, other = swapped_ref[index], other_ref[index]
+        beside = jnp.where(low_half != odd_sect, swapped, other)
         beside_ref[index] = beside
-        for target, first in ((top_ref, 0), (bottom_ref, rows - SUB)):
-            target[index, :, 0:LANES] = stress_ref[index, first : first + SUB, :]
-            target[index, :, LANES:] = beside[first : first + SUB, :]
-
-
-SLOTS = 3
+        ends = [
+            jnp.concatenate([values[first : first + SUB] for values in (stress_ref[index], beside)], 1)
+            for first in (0, rows - SUB)
+        ]
+        first_ref[index] = jnp.where(odd_slab, *ends)
+        second_ref[index] = jnp.where(odd_slab, *ends[::-1])
+
+
+BEHIND = 8
 
 
 def final_kernel(
-    freqs, member_ref, scalar_ref, wet_ref, depth_ref, square_ref, sums_ref, beside_ref, above_ref, below_ref,
-    growth_ref, kept_ref, columns_ref, edges_ref,
-    result_ref, level_ref, ratio_ref, ring_ref, sems,
+    freqs, member_ref, scalar_ref, depth_ref, ratios_ref, sums_ref, beside_ref, swapped_ref,
+    other_ref, growth_ref, kept_ref, columns_ref, edges_ref,
+    result_ref, level_ref, damping_ref, ring0, ring1, sems,
 ):
     member = member_ref[0]
-    wet_cells = wet_ref[...]
-    rows = wet_cells.shape[0]
+    rings = (ring0, ring1)
+    rows = depth_ref.shape[0]
     slab, slabs = lax.axis_index("slab"), lax.axis_size("slab")
     sect, sects = lax.axis_index("sect"), lax.axis_size("sect")
     above_ok = jnp.where(slab > 0, 1.0, 0.0)
@@ -728,9 +770,14 @@
     left_ok = jnp.where(sect > 0, 1.0, 0.0)
     right_ok = jnp.where(sect < sects - 1, 1.0, 0.0)
 
+    odd = lax.rem(slab, 2) == 1
+
     def framed(index):
         middle = jnp.concatenate([sums_ref[index], beside_ref[index]], axis=1)
-        return jnp.concatenate([middle, below_ref[index], above_ref[index]], axis=0)
+        swapped, other = swapped_ref[index], other_ref[index]
+        below = jnp.where(odd, other, swapped)
+        above = jnp.where(odd, swapped, other)
+        return jnp.concatenate([middle, below, above], axis=0)
 
     def around(values, axis):
         size = values.shape[axis]
@@ -750,85 +797,67 @@
         level = inside * (source + around(level, 0) + around(level, 1))
     level = level[:rows, :LANES]
     level_ref[...] = level
-    damping = 1.0 + 4.0 * sums_ref[2] / (jnp.square(depth_ref[...] + level) + 1.0)
-    square = square_ref[...]
+    damping = 1.0 / (1.0 + 4.0 * sums_ref[2] / (jnp.square(depth_ref[...] + level) + 1.0))
     tiles = rows // SUB
-    for j in range(freqs):
-        high = scalar_ref[(member * freqs + j) * CLASSES * KINDS + 3]
-        ratio = wet_cells / ((1.0 + (2.0 * high) * square) * damping)
-        ratio_ref[0, j] = ratio
-        ratio_ref[1, j] = high * ratio
-
+    damping_ref[...] = damping
     tile_lane = iota((SUB, LANES), 1)
-    quarter = ND // 4
-
-    def send(direction, slot):
-        return pltpu.make_async_copy(
-            ring_ref.at[slot], result_ref.at[:, pl.ds(direction, 1)], sems.at[slot]
-        )
-
-    for quadrant in range(4):
-        to_right, to_down = quadrant in (0, 1), quadrant in (0, 3)
-        target = 0 if to_right else LANES - 2
-        at_side = (tile_lane >= target) & (tile_lane < target + 2)
-        bank, edge_tile = (0, 0) if to_down else (1, tiles - 1)
-
-        def one(index, carry):
-            direction = quadrant * quarter + index
-            slot = lax.rem(direction, SLOTS)
-
-            @pl.when(direction >= SLOTS)
-            def _():
-                send(direction - SLOTS, slot).wait()
-
-            kind = class_index(direction)
-            group = lax.div(direction, GROUP)
-            offset = 2 * freqs * lax.rem(direction, GROUP)
-            row_at = (bank * 18 + direction - slot_base(quadrant)) * freqs
-            aligned = [
-                pltpu.roll(
-                    columns_ref[group, t * SUB : (t + 1) * SUB, :],
-                    lax.rem(target - offset + LANES, LANES),
-                    1,
-                )
-                for t in range(tiles)
-            ]
-            growth = [growth_ref[direction, t * SUB : (t + 1) * SUB, :] for t in range(tiles)]
-            def damped(j):
-                scale = scalar_ref[((member * freqs + j) * CLASSES + kind) * KINDS + 2]
-                result = []
-                for t in range(tiles):
-                    part = slice(t * SUB, (t + 1) * SUB)
-                    entered = pltpu.roll(aligned[t], (LANES - 2 * j) % LANES, 1)
-                    value = kept_ref[j, direction, part, :] + jnp.where(at_side, entered, 0.0)
-                    if t == edge_tile:
-                        edge_at = pl.ds(pl.multiple_of((row_at + j) * SUB, SUB), SUB)
-                        value += edges_ref[edge_at, :]
-                    factor = ratio_ref[0, j, part, :] + ratio_ref[1, j, part, :] * growth[t]
-                    result.append(value * (scale * factor))
-                return result
-
-            pending = [damped(j) for j in range(min(2, freqs))]
-            for j in range(freqs):
-                if j + 2 < freqs:
-                    pending.append(damped(j + 2))
-                for t, value in enumerate(pending.pop(0)):
-                    ring_ref[slot, j, 0, t * SUB : (t + 1) * SUB, :] = value
-            send(direction, slot).start()
-            return carry
-
-        lax.fori_loop(0, quarter, one, 0)
-    for direction in range(ND - SLOTS, ND):
-        send(direction, direction % SLOTS).wait()
-
-
-def step_pairs(axis, step):
+
+    def send(j, which):
+        return pltpu.make_async_copy(rings[which], result_ref.at[j], sems.at[which])
+
+    def frequency(j, which):
+        @pl.when(j >= 2)
+        def _():
+            send(j - 2, which).wait()
+
+        base = (member * freqs + j) * CLASSES * KINDS
+        high = scalar_ref[base + 3]
+        scales = [scalar_ref[base + kind * KINDS + 2] for kind in range(CLASSES)]
+
+        def damped(direction, t, ratio, high_ratio):
+            to_down, to_right = sides(direction // (ND // 4))
+            part = slice(t * SUB, (t + 1) * SUB)
+            target = 0 if to_right > 0 else LANES - 2
+            at_side = (tile_lane >= target) & (tile_lane < target + 2)
+            turn = target - direction % GROUP * 2 * freqs + 2 * LANES - 2 * j
+            entered = pltpu.roll(columns_ref[direction // GROUP, part, :], lax.rem(turn, LANES), 1)
+            value = kept_ref[j, direction, part, :] + jnp.where(at_side, entered, 0.0)
+            if t == (0 if to_down > 0 else tiles - 1):
+                edge = ((0 if to_down > 0 else 18) + row_slot(direction)) * freqs + j
+                value += edges_ref[pl.ds(pl.multiple_of(edge * SUB, SUB), SUB), :]
+            factor = ratio + high_ratio * growth_ref[direction, part, :]
+            return value * (scales[class_of(direction)] * factor)
+
+        pending = []
+        for t in range(tiles):
+            part = slice(t * SUB, (t + 1) * SUB)
+            ratio = ratios_ref[j, part, :] * damping_ref[part, :]
+            high_ratio = high * ratio
+            for direction in range(ND):
+                pending.append((direction, part, damped(direction, t, ratio, high_ratio)))
+                if len(pending) > BEHIND:
+                    target, place, value = pending.pop(0)
+                    rings[which][target, place, :] = value
+        for target, place, value in pending:
+            rings[which][target, place, :] = value
+        send(j, which).start()
+
+    def pair(index, carry):
+        for which in range(2):
+            frequency(2 * index + which, which)
+        return carry
+
+    lax.fori_loop(0, freqs // 2, pair, 0)
+    if freqs % 2:
+        frequency(jnp.int32(freqs - 1), 0)
+    for j in range(max(0, freqs - 2), freqs):
+        send(j, j % 2).wait()
+
+
+def swap(values, axis, first):
     count = lax.axis_size(axis)
-    return [(i, i + step) for i in range(count) if 0 <= i + step < count]
-
-
-def neighbour(values, axis, step):
-    return lax.ppermute(values, axis, step_pairs(axis, step))
+    pairs = [(i, i + 1) for i in range(first, count - 1, 2)]
+    return lax.ppermute(values, axis, pairs + [(b, a) for a, b in pairs])
 
 
 def others_sum(values, axis):
@@ -883,7 +912,7 @@
     block = (freqs, ND, rows, lanes)
     spectrum = spectrum.reshape(block)
 
-    growth, wet, to_right, to_left, to_down, to_up, edges = call(
+    growth, wet, swap_side, other_side, swap_row, other_row, edges = call(
         functools.partial(pack_kernel, freqs),
         [SMEM] + [HBM] * 7,
         (
@@ -900,6 +929,8 @@
         moved=local_comp * cells * 4,
         scratch=[
             pltpu.VMEM((local_comp * rows, lanes), jnp.float32),
+            pltpu.VMEM((GROUPS // 2, rows, lanes), jnp.float32),
+            pltpu.VMEM((GROUPS // 2, rows, lanes), jnp.float32),
             pltpu.VMEM(lane_table.shape[1:], jnp.float32),
             pltpu.VMEM(row_table.shape[1:], jnp.float32),
             pltpu.VMEM((rows, lanes), jnp.int32),
@@ -929,19 +960,19 @@
             flops=local_comp * cells * 16 * (stop - start) // freqs,
             moved=local_comp * cells * 8 * (stop - start) // freqs,
             scratch=[
-                pltpu.VMEM((AHEAD, ND, rows, lanes), jnp.float32),
-                pltpu.SemaphoreType.DMA((AHEAD,)),
+                pltpu.VMEM((ND, rows, lanes), jnp.float32),
+                pltpu.VMEM((ND, rows, lanes), jnp.float32),
+                pltpu.VMEM((2, rows, lanes), jnp.float32),
+                pltpu.SemaphoreType.DMA((2,)),
             ]
             + [pltpu.VMEM((rows + 2 * SUB, lanes), jnp.float32)] * 8,
             aliases={6 + index: index for index in range(4)} if before else {},
-            limit=8,
         )(member, scalars, wet, growth, in_hbm(spectrum), *before)
 
     early = max(1, freqs // 3)
-    from_left = neighbour(to_right, "sect", 1)
-    from_right = neighbour(to_left, "sect", -1)
+    swap_side, other_side = swap(swap_side, "sect", 0), swap(other_side, "sect", 1)
     kept, *partial = main_part(0, early)
-    to_down, to_up = call(
+    swap_row, other_row = call(
         functools.partial(corner_kernel, freqs),
         [VMEM, VMEM, VMEM, ANY, ANY, ANY],
         (in_any(row_message, lanes), in_any(row_message, lanes)),
@@ -950,10 +981,10 @@
         moved=1 << 15,
         scratch=[pltpu.VMEM((2, CORNERS, lanes), jnp.float32), pltpu.SemaphoreType.DMA((2,))],
         aliases={3: 0, 4: 1},
-    )(wet, from_left, from_right, to_down, to_up, partial[-1])
-    from_above = neighbour(to_down, "slab", 1)
-    from_below = neighbour(to_up, "slab", -1)
-    kept, a_sums, b_sums, energy = main_part(early, freqs, to_down, kept, *partial)
+    )(wet, swap_side, other_side, swap_row, other_row, partial[-1])
+    swapped_row = swap(swap_row, "slab", 0)
+    other_row = swap(other_row, "slab", 1)
+    kept, a_sums, b_sums, energy = main_part(early, freqs, swap_row, kept, *partial)
 
     columns, edges, energy = call(
         functools.partial(enter_kernel, freqs),
@@ -968,7 +999,7 @@
         moved=cells * 200,
         aliases={8: 1, 9: 2},
     )(
-        member, lane_table, row_table, wet, from_left, from_right, from_above, from_below, edges,
+        member, lane_table, row_table, wet, swap_side, other_side, swapped_row, other_row, edges,
         energy,
     )
     energy_there = others_sum(energy, "comp")
@@ -985,10 +1016,10 @@
         a_sums, b_sums,
     )
 
-    sums, square = call(
+    sums, ratios = call(
         functools.partial(stress_kernel, freqs),
         [SMEM, SMEM] + [VMEM] * 5,
-        (in_any(3, rows, lanes), in_any(rows, lanes)),
+        (in_any(3, rows, lanes), in_any(freqs, rows, lanes)),
         (VMEM, VMEM),
         flops=cells * freqs * 12,
         moved=cells * freqs * 8,
@@ -1001,33 +1032,31 @@
         flops=cells * 3,
         moved=cells * 44,
     )(sums, others_sum(sums, "comp"))
-    left = neighbour(stress, "sect", 1)
-    right = neighbour(stress, "sect", -1)
-    beside, top, bottom = call(
+    beside, first, second = call(
         strip_kernel,
         [VMEM, VMEM, VMEM],
         (in_any(2, rows, lanes), in_any(2, SUB, 2 * lanes), in_any(2, SUB, 2 * lanes)),
         (VMEM, VMEM, VMEM),
         flops=cells * 4,
         moved=cells * 36,
-    )(stress, left, right)
-    above = neighbour(bottom, "slab", 1)
-    below = neighbour(top, "slab", -1)
+    )(stress, swap(stress, "sect", 0), swap(stress, "sect", 1))
+    aside, beyond = swap(first, "slab", 0), swap(second, "slab", 1)
 
     result, level = call(
         functools.partial(final_kernel, freqs),
-        [SMEM, SMEM] + [VMEM] * 11,
+        [SMEM, SMEM] + [VMEM] * 10,
         (in_any(*block), in_any(rows, lanes)),
         (HBM, VMEM),
         flops=local_comp * cells * 6,
         moved=local_comp * cells * 8,
         scratch=[
-            pltpu.VMEM((2, freqs, rows, lanes), jnp.float32),
-            pltpu.VMEM((SLOTS, freqs, 1, rows, lanes), jnp.float32),
-            pltpu.SemaphoreType.DMA((SLOTS,)),
+            pltpu.VMEM((rows, lanes), jnp.float32),
+            pltpu.VMEM((ND, rows, lanes), jnp.float32),
+            pltpu.VMEM((ND, rows, lanes), jnp.float32),
+            pltpu.SemaphoreType.DMA((2,)),
         ],
     )(
-        member, scalars, wet, depth, square, sums, beside, above, below, growth, kept,
+        member, scalars, depth, ratios, sums, beside, aside, beyond, growth, kept,
         columns, edges,
     )
     return result.reshape(local_comp, rows, lanes), level

time: 86.6 us -> 85.5 us (0.987)
  starting transfers between devices: 24.7 us -> 15.6 us
  Pallas kernels: 50.1 us -> 57.8 us
    ppermute x8, starting transfers between devices: 21.6 us -> 12.5 us  [swap(): return lax.ppermute(values, axis, pairs + [(b, a) for a, b in pairs])]
    pallas_call x2, Pallas kernels: 20.3 us -> 29.3 us  [main_part(): call(functools.partial(main_kernel, freqs, start, stop), [SMEM, SMEM, VME...]
    pallas_call x1, Pallas kernels: 16 us -> 14.7 us  [resident(): call(functools.partial(final_kernel, freqs), [SMEM, SMEM] + [VMEM] * 10,...]
  transfers between devices with their start and end apart: 10 -> 10, of which waited for: 4 -> 4; matrix products, arithmetic and copies ran while one was open for 0% -> 0% of each run, Pallas kernels for 25% -> 36%
where the time goes in v4:
time: 85.5 us; the launch traced here: 85.3 us
  Pallas kernels  57.8 us (68%)
  starting transfers between devices  15.6 us (18%)
  waiting for transfers between devices  10.9 us (13%)
  between operations  0.87 us (1%)
    pallas_call x2, Pallas kernels, main_part(): call(functools.partial(main_kernel, freqs, start, stop), [SMEM, SMEM, VME...  29.3 us
    pallas_call x1, Pallas kernels, resident(): call(functools.partial(final_kernel, freqs), [SMEM, SMEM] + [VMEM] * 10,...  14.7 us
    ppermute x8, starting transfers between devices, swap(): return lax.ppermute(values, axis, pairs + [(b, a) for a, b in pairs])  12.5 us
    pallas_call x1, Pallas kernels, resident(): call(functools.partial(pack_kernel, freqs), [SMEM] + [HBM] * 7, (in_any(N...  10.1 us
    ppermute x8, waiting for transfers between devices, swap(): return lax.ppermute(values, axis, pairs + [(b, a) for a, b in pairs])  6.85 us
    ppermute x2, waiting for transfers between devices, others_sum(): lax.ppermute(values, axis, [(i, (i + step) % count) for i in range(count)])  4.09 us
    ppermute x2, starting transfers between devices, others_sum(): lax.ppermute(values, axis, [(i, (i + step) % count) for i in range(count)])  3.14 us
  transfers between devices with their start and end apart: 10, of which 4 were waited for; matrix products, arithmetic and copies ran while one was open for 0% of the time, Pallas kernels for 36%

profile of v4, /device:TPU:12, one launch (start us, length us, event | category | flops | bytes accessed | tf_op | source)
XLA Modules:
  0.0 85.3 jit_solution(9509131825792334855)
XLA Ops:
  0.6 0.0 copy-start.5
  0.6 10.1 %shard_map.104 = (f32[36,64,128]{2,1,0:T(8,128)S(1)}, f32[64,128]{1,0:T(8,128)S(1)}, f32[6,64,128]{2,1,0:T(8,128)S(1)}, f32[6,64,128]{2,1,0:T(8,128)S(1)}, f32[6...) custom-call(s32[1]{0:T(128)} %bitcast.member_ref, ...), custom_call_target="tpu_custom_call" | custom-call | flops 21233664 | bytes 21233664 | tf_op jit(solution)/shard_map/pallas_call | solution.py:915
  10.7 0.1 collective-permute-start
  10.8 2.5 %collective-permute-start.1 = (f32[6,64,128]{2,1,0:T(8,128)S(1)}, f32[6,64,128]{2,1,0:T(8,128)S(1)}, u32[]{:S(2)}, u32[]{:S(2)}) collective-permute-start(f32[6,64,128]{2,1,0:T(8,128)S(1)} %get-tuple-element.36), channel_id=1, source_target_pairs={{4,8},{8,4},{5,9},{9,5},{6,10},{10,6},{7,11},{11,7},{20,24},{24,20... | collective-permute-start | bytes 589832 | tf_op jit(solution)/shard_map/ppermute | solution.py:860
  13.3 0.0 copy-done.5
  13.3 10.4 %shard_map.105 = (f32[18,36,64,128]{3,2,1,0:T(8,128)S(1)}, f32[1152,128]{1,0:T(8,128)S(1)}, f32[1152,128]{1,0:T(8,128)S(1)}, f32[64,128]{1,0:T(8,128)S(1)}) custom-call(s32[1]{0:T(128)} %bitcast.member_ref, f32[1800]{0:T(1024)S(1)} %copy-done.5, f32[64,128]{1,0:T(8,128)S(1)} %get-tuple-element.33.wet_ref, f32[36,64,128]{2,1,0:T(8,128)S(1)} %get-tuple-element.34.growth_ref, ...), custom_call_target="tpu_custom_call" | custom-call | flops 28311552 | bytes 14155776 | tf_op jit(solution)/shard_map/pallas_call | solution.py:950
  23.7 0.0 collective-permute-done.swapped_ref.swap_side_ref
  23.7 0.0 collective-permute-done.1.other_ref.other_side_ref
  23.8 0.1 shard_map.106
  23.9 3.5 %collective-permute-start.3 = (f32[656,128]{1,0:T(8,128)S(1)}, f32[656,128]{1,0:T(8,128)S(1)}, u32[]{:S(2)}, u32[]{:S(2)}) collective-permute-start(f32[656,128]{1,0:T(8,128)S(1)} %get-tuple-element.41), channel_id=1, source_target_pairs={{1,2},{2,1},{5,6},{6,5},{9,10},{10,9},{13,14},{14,13},{17,18},{18,... | collective-permute-start | bytes 1007624 | tf_op jit(solution)/shard_map/ppermute | solution.py:860
  27.4 0.1 collective-permute-start.2
  27.4 0.0 copy-start
  27.5 0.0 copy-start.1
  27.5 0.0 copy-start.2
  27.5 0.0 copy-start.3
  27.5 0.0 copy-start.4
  27.5 0.0 copy-start.6
  27.5 18.9 %shard_map.107 = (f32[18,36,64,128]{3,2,1,0:T(8,128)S(1)}, f32[1152,128]{1,0:T(8,128)S(1)}, f32[1152,128]{1,0:T(8,128)S(1)}, f32[64,128]{1,0:T(8,128)S(1)}) custom-call(s32[1]{0:T(128)} %bitcast.member_ref, f32[1800]{0:T(1024)S(1)} %copy-done.5, ...), custom_call_target="tpu_custom_call", output_to_operand_aliasing={{0}: (6, {}), {1}: (7, {}), {2}: (8, {}), {3}: (9, {})} | custom-call | flops 56623104 | bytes 28311552 | tf_op jit(solution)/shard_map/pallas_call | solution.py:950
  46.4 0.0 collective-permute-done.3.other_row_ref
  46.4 0.0 collective-permute-done.2.swap_row_ref
  46.4 0.0 copy-done
  46.5 0.0 copy-done.1
  46.5 1.1 %shard_map.108 = (f32[12,64,128]{2,1,0:T(8,128)S(1)}, f32[5184,128]{1,0:T(8,128)S(1)}, f32[64,128]{1,0:T(8,128)S(1)}) custom-call(s32[1]{0:T(128)} %bitcast.member_ref, f32[2,12,8,128]{3,2,1,0:T(8,128)S(1)} %copy-done.1, f32[2,10,5,18,128]{4,3,2,1,0:T(8,128)S(1)} %copy-done, ...), custom_call_target="tpu_custom_call", output_to_operand_aliasing={{1}: (8, {}), {2}: (9, {})} | custom-call | flops 4915200 | bytes 1638400 | tf_op jit(solution)/shard_map/pallas_call | solution.py:989
  47.6 1.6 %collective-permute-start.4 = (f32[64,128]{1,0:T(8,128)S(1)}, f32[64,128]{1,0:T(8,128)S(1)}, u32[]{:S(2)}, u32[]{:S(2)}) collective-permute-start(f32[64,128]{1,0:T(8,128)S(1)} %get-tuple-element.53.own_ref), channel_id=1, source_target_pairs={{0,16},{16,0},{1,17},{17,1},{2,18},{18,2},{3,19},{19,3},{4,20},{20... | collective-permute-start | bytes 98312 | tf_op jit(solution)/shard_map/ppermute | solution.py:867
  49.1 0.0 copy-done.2
  49.1 0.0 copy-done.3
  49.1 0.0 copy-done.4
  49.1 1.4 %shard_map.109 = (f32[1152,128]{1,0:T(8,128)S(1)}, f32[1152,128]{1,0:T(8,128)S(1)}) custom-call(s32[1]{0:T(128)} %bitcast.member_ref, f32[2,12,8,128]{3,2,1,0:T(8,128)S(1)} %copy-done.1, f32[2,10,5,18,128]{4,3,2,1,0:T(8,128)S(1)} %copy-done, s32[64,128]{1,0:T(8,128)S(1)} %copy-done.2, ...), custom_call_target="tpu_custom_call", output_to_operand_aliasing={{0}: (9, {}), {1}: (10, {})} | custom-call | flops 4915200 | bytes 1638400 | tf_op jit(solution)/shard_map/pallas_call | solution.py:1006
  50.6 1.0 %collective-permute-done.4.other_ref = f32[64,128]{1,0:T(8,128)S(1)} collective-permute-done((f32[64,128]{1,0:T(8,128)S(1)}, f32[64,128]{1,0:T(8,128)S(1)}, u32[]{:S(2)}, u32[]{:S(2)}) %collective-permute-start.4) | collective-permute-done | bytes 32800 | tf_op jit(solution)/shard_map/ppermute | solution.py:867
  51.6 1.0 %shard_map.110 = (f32[3,64,128]{2,1,0:T(8,128)S(1)}, f32[18,64,128]{2,1,0:T(8,128)S(1)}) custom-call(s32[1]{0:T(128)} %bitcast.member_ref, f32[1800]{0:T(1024)S(1)} %copy-done.5, f32[64,128]{1,0:T(8,128)S(1)} %get-tuple-element.33.wet_ref, f32[1152,128]{1,0:T(8,128)S(1)} %get-tuple-element.51.a_ref, f32[1152,128]{1,0:T(8,128)S(1)} %get-tuple-element.52.b_ref, ...), custom_call_target="tpu_custom_call" | custom-call | flops 1769472 | bytes 1179648 | tf_op jit(solution)/shard_map/pallas_call | solution.py:1019
  52.5 1.6 %collective-permute-start.5 = (f32[3,64,128]{2,1,0:T(8,128)S(1)}, f32[3,64,128]{2,1,0:T(8,128)S(1)}, u32[]{:S(2)}, u32[]{:S(2)}) collective-permute-start(f32[3,64,128]{2,1,0:T(8,128)S(1)} %get-tuple-element.55.own_ref), channel_id=1, source_target_pairs={{0,16},{16,0},{1,17},{17,1},{2,18},{18,2},{3,19},{19,3},{4,20},{20... | collective-permute-start | bytes 294920 | tf_op jit(solution)/shard_map/ppermute | solution.py:867
  54.1 3.1 %collective-permute-done.5.other_ref = f32[3,64,128]{2,1,0:T(8,128)S(1)} collective-permute-done((f32[3,64,128]{2,1,0:T(8,128)S(1)}, f32[3,64,128]{2,1,0:T(8,128)S(1)}, u32[]{:S(2)}, u32[]{:S(2)}) %collective-permute-start.5) | collective-permute-done | bytes 98336 | tf_op jit(solution)/shard_map/ppermute | solution.py:867
  57.2 1.9 %collective-permute-start.7 = (f32[2,64,128]{2,1,0:T(8,128)S(1)}, f32[2,64,128]{2,1,0:T(8,128)S(1)}, u32[]{:S(2)}, u32[]{:S(2)}) collective-permute-start(f32[2,64,128]{2,1,0:T(8,128)S(1)} %get-tuple-element.57.stress_ref), channel_id=1, source_target_pairs={{4,8},{8,4},{5,9},{9,5},{6,10},{10,6},{7,11},{11,7},{20,24},{24,20... | collective-permute-start | bytes 196616 | tf_op jit(solution)/shard_map/ppermute | solution.py:860
  59.2 0.1 collective-permute-start.6
  59.2 3.6 %collective-permute-done.7.other_ref = f32[2,64,128]{2,1,0:T(8,128)S(1)} collective-permute-done((f32[2,64,128]{2,1,0:T(8,128)S(1)}, f32[2,64,128]{2,1,0:T(8,128)S(1)}, u32[]{:S(2)}, u32[]{:S(2)}) %collective-permute-start.7) | collective-permute-done | bytes 65568 | tf_op jit(solution)/shard_map/ppermute | solution.py:860
  62.8 0.0 collective-permute-done.6.swapped_ref
  62.9 2.0 %collective-permute-start.8 = (f32[2,8,256]{2,1,0:T(8,128)S(1)}, f32[2,8,256]{2,1,0:T(8,128)S(1)}, u32[]{:S(2)}, u32[]{:S(2)}) collective-permute-start(f32[2,8,256]{2,1,0:T(8,128)S(1)} %get-tuple-element.59), channel_id=1, source_target_pairs={{0,1},{2,3},{1,0},{3,2},{4,5},{6,7},{5,4},{7,6},{8,9},{10,11},{9,8... | collective-permute-start | bytes 49160 | tf_op jit(solution)/shard_map/ppermute | solution.py:860
  64.9 2.3 %collective-permute-start.9 = (f32[2,8,256]{2,1,0:T(8,128)S(1)}, f32[2,8,256]{2,1,0:T(8,128)S(1)}, u32[]{:S(2)}, u32[]{:S(2)}) collective-permute-start(f32[2,8,256]{2,1,0:T(8,128)S(1)} %get-tuple-element.60), channel_id=1, source_target_pairs={{1,2},{2,1},{5,6},{6,5},{9,10},{10,9},{13,14},{14,13},{17,18},{18,... | collective-permute-start | bytes 49160 | tf_op jit(solution)/shard_map/ppermute | solution.py:860
  67.2 0.0 collective-permute-done.8.swapped_ref
  67.3 3.3 %collective-permute-done.9.other_ref = f32[2,8,256]{2,1,0:T(8,128)S(1)} collective-permute-done((f32[2,8,256]{2,1,0:T(8,128)S(1)}, f32[2,8,256]{2,1,0:T(8,128)S(1)}, u32[]{:S(2)}, u32[]{:S(2)}) %collective-permute-start.9) | collective-permute-done | bytes 16416 | tf_op jit(solution)/shard_map/ppermute | solution.py:860
  70.5 0.0 copy-done.6
  70.5 14.7 %shard_map.113 = (f32[18,36,64,128]{3,2,1,0:T(8,128)}, f32[64,128]{1,0:T(8,128)}) custom-call(s32[1]{0:T(128)} %bitcast.member_ref, f32[1800]{0:T(1024)S(1)} %copy-done.5, f32[64,128]{1,0:T(8,128)S(1)} %copy-done.6, f32[18,64,128]{2,1,0:T(8,128)S(1)} %get-tuple-element.54.ratios_ref, f32[3,64,128]{2,1,0:T(8,128)S(1)} %get-tuple-element.56.sums_ref, ...), custom_call_target="tpu_custom_call" | custom-call | flops 31850496 | bytes 42467328 | tf_op jit(solution)/shard_map/pallas_call | solution.py:1045
  (2 shorter events, 0.0 us)
Async XLA Ops:
  0.6 12.7 %copy-start.5 = (f32[1800]{0:T(1024)S(1)}, f32[1800]{0:T(1024)}, u32[]{:S(2)}) copy-start(f32[1800]{0:T(1024)} %constant.12.clone.scalar_ref) | copy-start | bytes 21604
  10.7 13.0 %collective-permute-start = (f32[6,64,128]{2,1,0:T(8,128)S(1)}, f32[6,64,128]{2,1,0:T(8,128)S(1)}, u32[]{:S(2)}, u32[]{:S(2)}) collective-permute-start(f32[6,64,128]{2,1,0:T(8,128)S(1)} %get-tuple-element.35), channel_id=1, source_target_pairs={{0,4},{8,12},{4,0},{12,8},{1,5},{9,13},{5,1},{13,9},{2,6},{10,14},... | collective-permute-start | bytes 589832 | tf_op jit(solution)/shard_map/ppermute | solution.py:860
  10.8 13.0 %collective-permute-start.1 = (f32[6,64,128]{2,1,0:T(8,128)S(1)}, f32[6,64,128]{2,1,0:T(8,128)S(1)}, u32[]{:S(2)}, u32[]{:S(2)}) collective-permute-start(f32[6,64,128]{2,1,0:T(8,128)S(1)} %get-tuple-element.36), channel_id=1, source_target_pairs={{4,8},{8,4},{5,9},{9,5},{6,10},{10,6},{7,11},{11,7},{20,24},{24,20... | collective-permute-start | bytes 589832 | tf_op jit(solution)/shard_map/ppermute | solution.py:860
  23.9 22.6 %collective-permute-start.3 = (f32[656,128]{1,0:T(8,128)S(1)}, f32[656,128]{1,0:T(8,128)S(1)}, u32[]{:S(2)}, u32[]{:S(2)}) collective-permute-start(f32[656,128]{1,0:T(8,128)S(1)} %get-tuple-element.41), channel_id=1, source_target_pairs={{1,2},{2,1},{5,6},{6,5},{9,10},{10,9},{13,14},{14,13},{17,18},{18,... | collective-permute-start | bytes 1007624 | tf_op jit(solution)/shard_map/ppermute | solution.py:860
  27.4 19.1 %collective-permute-start.2 = (f32[656,128]{1,0:T(8,128)S(1)}, f32[656,128]{1,0:T(8,128)S(1)}, u32[]{:S(2)}, u32[]{:S(2)}) collective-permute-start(f32[656,128]{1,0:T(8,128)S(1)} %get-tuple-element.40.refs_0_), channel_id=1, source_target_pairs={{0,1},{2,3},{1,0},{3,2},{4,5},{6,7},{5,4},{7,6},{8,9},{10,11},{9,8... | collective-permute-start | bytes 1007624 | tf_op jit(solution)/shard_map/ppermute | solution.py:860
  27.4 19.0 %copy-start = (f32[2,10,5,18,128]{4,3,2,1,0:T(8,128)S(1)}, f32[2,10,5,18,128]{4,3,2,1,0:T(8,128)}, u32[]{:S(2)}) copy-start(f32[2,10,5,18,128]{4,3,2,1,0:T(8,128)} %constant.14.clone.table_hbm.table_ref) | copy-start | bytes 2764804
  27.5 19.0 %copy-start.1 = (f32[2,12,8,128]{3,2,1,0:T(8,128)S(1)}, f32[2,12,8,128]{3,2,1,0:T(8,128)}, u32[]{:S(2)}) copy-start(f32[2,12,8,128]{3,2,1,0:T(8,128)} %constant.13.clone.lanes_hbm.lanes_ref) | copy-start | bytes 294916
  27.5 21.7 %copy-start.2 = (s32[64,128]{1,0:T(8,128)S(1)}, s32[64,128]{1,0:T(8,128)}, u32[]{:S(2)}) copy-start(s32[64,128]{1,0:T(8,128)} %ice_ref.1) | copy-start | bytes 98308
  27.5 21.7 %copy-start.3 = (f32[64,128]{1,0:T(8,128)S(1)}, f32[64,128]{1,0:T(8,128)}, u32[]{:S(2)}) copy-start(f32[64,128]{1,0:T(8,128)} %east_ref.1) | copy-start | bytes 98308
  27.5 21.7 %copy-start.4 = (f32[64,128]{1,0:T(8,128)S(1)}, f32[64,128]{1,0:T(8,128)}, u32[]{:S(2)}) copy-start(f32[64,128]{1,0:T(8,128)} %north_ref.1) | copy-start | bytes 98308
  27.5 43.0 %copy-start.6 = (f32[64,128]{1,0:T(8,128)S(1)}, f32[64,128]{1,0:T(8,128)}, u32[]{:S(2)}) copy-start(f32[64,128]{1,0:T(8,128)} %depth_ref.1) | copy-start | bytes 98308
  47.6 4.0 %collective-permute-start.4 = (f32[64,128]{1,0:T(8,128)S(1)}, f32[64,128]{1,0:T(8,128)S(1)}, u32[]{:S(2)}, u32[]{:S(2)}) collective-permute-start(f32[64,128]{1,0:T(8,128)S(1)} %get-tuple-element.53.own_ref), channel_id=1, source_target_pairs={{0,16},{16,0},{1,17},{17,1},{2,18},{18,2},{3,19},{19,3},{4,20},{20... | collective-permute-start | bytes 98312 | tf_op jit(solution)/shard_map/ppermute | solution.py:867
  52.5 4.7 %collective-permute-start.5 = (f32[3,64,128]{2,1,0:T(8,128)S(1)}, f32[3,64,128]{2,1,0:T(8,128)S(1)}, u32[]{:S(2)}, u32[]{:S(2)}) collective-permute-start(f32[3,64,128]{2,1,0:T(8,128)S(1)} %get-tuple-element.55.own_ref), channel_id=1, source_target_pairs={{0,16},{16,0},{1,17},{17,1},{2,18},{18,2},{3,19},{19,3},{4,20},{20... | collective-permute-start | bytes 294920 | tf_op jit(solution)/shard_map/ppermute | solution.py:867
  57.2 5.6 %collective-permute-start.7 = (f32[2,64,128]{2,1,0:T(8,128)S(1)}, f32[2,64,128]{2,1,0:T(8,128)S(1)}, u32[]{:S(2)}, u32[]{:S(2)}) collective-permute-start(f32[2,64,128]{2,1,0:T(8,128)S(1)} %get-tuple-element.57.stress_ref), channel_id=1, source_target_pairs={{4,8},{8,4},{5,9},{9,5},{6,10},{10,6},{7,11},{11,7},{20,24},{24,20... | collective-permute-start | bytes 196616 | tf_op jit(solution)/shard_map/ppermute | solution.py:860
  59.2 3.7 %collective-permute-start.6 = (f32[2,64,128]{2,1,0:T(8,128)S(1)}, f32[2,64,128]{2,1,0:T(8,128)S(1)}, u32[]{:S(2)}, u32[]{:S(2)}) collective-permute-start(f32[2,64,128]{2,1,0:T(8,128)S(1)} %get-tuple-element.57.stress_ref), channel_id=1, source_target_pairs={{0,4},{8,12},{4,0},{12,8},{1,5},{9,13},{5,1},{13,9},{2,6},{10,14},... | collective-permute-start | bytes 196616 | tf_op jit(solution)/shard_map/ppermute | solution.py:860
  62.9 4.4 %collective-permute-start.8 = (f32[2,8,256]{2,1,0:T(8,128)S(1)}, f32[2,8,256]{2,1,0:T(8,128)S(1)}, u32[]{:S(2)}, u32[]{:S(2)}) collective-permute-start(f32[2,8,256]{2,1,0:T(8,128)S(1)} %get-tuple-element.59), channel_id=1, source_target_pairs={{0,1},{2,3},{1,0},{3,2},{4,5},{6,7},{5,4},{7,6},{8,9},{10,11},{9,8... | collective-permute-start | bytes 49160 | tf_op jit(solution)/shard_map/ppermute | solution.py:860
  64.9 5.6 %collective-permute-start.9 = (f32[2,8,256]{2,1,0:T(8,128)S(1)}, f32[2,8,256]{2,1,0:T(8,128)S(1)}, u32[]{:S(2)}, u32[]{:S(2)}) collective-permute-start(f32[2,8,256]{2,1,0:T(8,128)S(1)} %get-tuple-element.60), channel_id=1, source_target_pairs={{1,2},{2,1},{5,6},{6,5},{9,10},{10,9},{13,14},{14,13},{17,18},{18,... | collective-permute-start | bytes 49160 | tf_op jit(solution)/shard_map/ppermute | solution.py:860

commit v5 on v4

--- a/solution.py
+++ b/solution.py
@@ -418,7 +418,6 @@
     kept_ref, a_ref, b_ref, energy_ref, ring0, ring1, sums_ref, sems, *first_refs = refs
     rings = (ring0, ring1)
     member = member_ref[0]
-    nought = jnp.minimum(member, 0)
     rows = wet_ref.shape[0]
     tiles = rows // SUB
 
@@ -434,8 +433,6 @@
     not_last = jnp.where(lane == LANES - 1, 0.0, 1.0)
     top, bottom = sub == 0, sub == SUB - 1
     energy_ref[...] = energy_in[...] if start else jnp.zeros_like(energy_ref)
-    for first_ref in first_refs:
-        first_ref[...] = jnp.zeros_like(first_ref)
 
     def tile_at(tile):
         return slice(tile * SUB, (tile + 1) * SUB)
@@ -456,88 +453,77 @@
             across = across * (not_first if quadrant in (0, 1) else not_last)
             return scalar_ref[base + kind * KINDS], across
 
-        walks = [(kind, part) for kind in range(CLASSES - 1) for part in parts_of(kind)]
-        wet = [wet_ref[tile_at(t), :] for t in range(tiles)]
-        held = {}
-
-        def mask(walk):
-            direction = walks[walk][1][0]
-            target = first_refs[walk % 4]
-            cells = [ring_ref[direction, tile_at(t), :] * wet[t] for t in range(tiles)]
-            for t in range(tiles):
-                target[tile_at(t + 1), :] = cells[t]
-            held[walk] = cells
-
-        def step(walk, source, cells):
-            _, quadrant, _ = walks[walk][1]
-            alpha, across = speeds(walks[walk][1])
+        def step(load, part, speed):
+            _, quadrant, _ = part
+            alpha, across = speed
             to_down, to_right = sides(quadrant)
-            ahead = [source[pl.ds((t + 1) * SUB - to_down + nought, SUB), :] for t in range(tiles)]
-            return [
-                cells[t] + alpha * ahead[t] + across * pltpu.roll(cells[t], to_right % LANES, 1)
-                for t in range(tiles)
-            ]
-
-        def first_step(walk):
-            after = step(walk, first_refs[walk % 4], held[walk])
-            cells = [wet[t] * after[t] for t in range(tiles)]
-            target = first_refs[4 + walk % 4]
-            for t in range(tiles):
-                target[tile_at(t + 1), :] = cells[t]
-            held[walk] = cells
-
-        def second_step(walk):
-            direction = walks[walk][1][0]
-            after = step(walk, first_refs[4 + walk % 4], held.pop(walk))
-            for t in range(tiles):
-                kept_ref[j, direction, tile_at(t), :] = after[t]
-            return after, [growth_ref[direction, tile_at(t), :] * after[t] for t in range(tiles)]
-
-        def plus(one, other):
-            return [x + y for x, y in zip(one, other)]
-
-        def add_up(kind, moved, grown):
+            edge = top if to_down > 0 else bottom
+            cells, turned = {}, {}
+
+            def get(t):
+                if t not in cells:
+                    cells[t] = load(t)
+                    turned[t] = pltpu.roll(cells[t], to_down % SUB, 0)
+                return turned[t]
+
+            def at(t):
+                ahead = jnp.where(
+                    edge, get(t - to_down) if 0 <= t - to_down < tiles else 0.0, get(t)
+                )
+                beside = pltpu.roll(cells[t], to_right % LANES, 1)
+                return cells[t] + alpha * ahead + across * beside
+
+            return at
+
+        def first_step(kind):
+            for part in parts_of(kind):
+                direction, quadrant, _ = part
+                target = first_refs[kind % 2 * 4 + quadrant]
+                after = step(
+                    lambda t: ring_ref[direction, tile_at(t), :] * wet_ref[tile_at(t), :],
+                    part,
+                    speeds(part),
+                )
+                for t in range(tiles):
+                    target[tile_at(t), :] = wet_ref[tile_at(t), :] * after(t)
+
+        def second_step(kind):
+            parts = parts_of(kind)
             scale, high = scalar_ref[base + kind * KINDS + 2], scalar_ref[base + 3]
             scaled_high = scale * high
-            if kind == 0:
-                plain_x, plain_y = plus(moved[0], moved[2]), plus(moved[1], moved[3])
-                grown_x, grown_y = plus(grown[0], grown[2]), plus(grown[1], grown[3])
-                square = math.cos(0.5 * math.pi) ** 2
-                for t in range(tiles):
-                    plain = scale * plain_x[t], scale * plain_y[t]
-                    whole_x = plain[0] + scaled_high * grown_x[t]
-                    whole_y = plain[1] + scaled_high * grown_y[t]
-                    energy_ref[tile_at(t), :] += plain[0] + plain[1]
-                    sums_ref[0, tile_at(t), :] = whole_x + whole_y
-                    sums_ref[1, tile_at(t), :] = whole_x + square * whole_y
-            else:
-                square = math.cos(2.0 * math.pi * kind / ND) ** 2
-                for t in range(tiles):
-                    plain = scale * moved[t]
-                    whole = plain + scaled_high * grown[t]
+            sources = [first_refs[kind % 2 * 4 + quadrant] for _, quadrant, _ in parts]
+            steps = [
+                step(lambda t, source=source: source[tile_at(t), :], part, speeds(part))
+                for part, source in zip(parts, sources)
+            ]
+            for t in range(tiles):
+                moved, grown = [], []
+                for (direction, _, _), after_at in zip(parts, steps):
+                    after = after_at(t)
+                    kept_ref[j, direction, tile_at(t), :] = after
+                    moved.append(after)
+                    grown.append(growth_ref[direction, tile_at(t), :] * after)
+                if kind == 0:
+                    plain_x, plain_y = scale * (moved[0] + moved[2]), scale * (moved[1] + moved[3])
+                    grown_x = plain_x + scaled_high * (grown[0] + grown[2])
+                    grown_y = plain_y + scaled_high * (grown[1] + grown[3])
+                    square = math.cos(0.5 * math.pi) ** 2
+                    energy_ref[tile_at(t), :] += plain_x + plain_y
+                    sums_ref[0, tile_at(t), :] = grown_x + grown_y
+                    sums_ref[1, tile_at(t), :] = grown_x + square * grown_y
+                else:
+                    plain = scale * ((moved[0] + moved[1]) + (moved[2] + moved[3]))
+                    whole = plain + scaled_high * ((grown[0] + grown[1]) + (grown[2] + grown[3]))
+                    square = math.cos(2.0 * math.pi * kind / ND) ** 2
                     energy_ref[tile_at(t), :] += plain
                     sums_ref[0, tile_at(t), :] += whole
                     sums_ref[1, tile_at(t), :] += square * whole
 
-        moved, grown = [], []
-        for walk in range(len(walks) + 2):
-            if walk < len(walks):
-                mask(walk)
-            if 1 <= walk <= len(walks):
-                first_step(walk - 1)
-            if walk >= 2:
-                kind = walks[walk - 2][0]
-                after, with_growth = second_step(walk - 2)
-                if kind and moved:
-                    moved, grown = plus(moved, after), plus(grown, with_growth)
-                elif kind:
-                    moved, grown = after, with_growth
-                else:
-                    moved.append(after)
-                    grown.append(with_growth)
-                if walk % 4 == 1:
-                    add_up(kind, moved, grown)
-                    moved, grown = [], []
+        first_step(0)
+        for kind in range(CLASSES - 1):
+            if kind + 1 < CLASSES - 1:
+                first_step(kind + 1)
+            second_step(kind)
         at = pl.ds(pl.multiple_of(j * rows, SUB), rows)
         a_ref[at, :] = sums_ref[0]
         b_ref[at, :] = sums_ref[1]
@@ -752,13 +738,13 @@
         second_ref[index] = jnp.where(odd_slab, *ends[::-1])
 
 
-BEHIND = 8
+BEHIND = 16
 
 
 def final_kernel(
     freqs, member_ref, scalar_ref, depth_ref, ratios_ref, sums_ref, beside_ref, swapped_ref,
     other_ref, growth_ref, kept_ref, columns_ref, edges_ref,
-    result_ref, level_ref, damping_ref, ring0, ring1, sems,
+    result_ref, level_ref, damping_ref, turning_ref, ring0, ring1, sems,
 ):
     member = member_ref[0]
     rings = (ring0, ring1)
@@ -800,6 +786,7 @@
     damping = 1.0 / (1.0 + 4.0 * sums_ref[2] / (jnp.square(depth_ref[...] + level) + 1.0))
     tiles = rows // SUB
     damping_ref[...] = damping
+    turning_ref[...] = columns_ref[...]
     tile_lane = iota((SUB, LANES), 1)
 
     def send(j, which):
@@ -819,8 +806,10 @@
             part = slice(t * SUB, (t + 1) * SUB)
             target = 0 if to_right > 0 else LANES - 2
             at_side = (tile_lane >= target) & (tile_lane < target + 2)
-            turn = target - direction % GROUP * 2 * freqs + 2 * LANES - 2 * j
-            entered = pltpu.roll(columns_ref[direction // GROUP, part, :], lax.rem(turn, LANES), 1)
+            turn = (target - direction % GROUP * 2 * freqs) % LANES
+            entered = turning_ref[direction // GROUP, part, :]
+            if turn:
+                entered = pltpu.roll(entered, turn, 1)
             value = kept_ref[j, direction, part, :] + jnp.where(at_side, entered, 0.0)
             if t == (0 if to_down > 0 else tiles - 1):
                 edge = ((0 if to_down > 0 else 18) + row_slot(direction)) * freqs + j
@@ -841,6 +830,9 @@
         for target, place, value in pending:
             rings[which][target, place, :] = value
         send(j, which).start()
+        turned = [pltpu.roll(turning_ref[group], LANES - 2, 1) for group in range(GROUPS)]
+        for group in range(GROUPS):
+            turning_ref[group] = turned[group]
 
     def pair(index, carry):
         for which in range(2):
@@ -965,7 +957,7 @@
                 pltpu.VMEM((2, rows, lanes), jnp.float32),
                 pltpu.SemaphoreType.DMA((2,)),
             ]
-            + [pltpu.VMEM((rows + 2 * SUB, lanes), jnp.float32)] * 8,
+            + [pltpu.VMEM((rows, lanes), jnp.float32)] * 8,
             aliases={6 + index: index for index in range(4)} if before else {},
         )(member, scalars, wet, growth, in_hbm(spectrum), *before)
 
@@ -1051,6 +1043,7 @@
         moved=local_comp * cells * 8,
         scratch=[
             pltpu.VMEM((rows, lanes), jnp.float32),
+            pltpu.VMEM((GROUPS, rows, lanes), jnp.float32),
             pltpu.VMEM((ND, rows, lanes), jnp.float32),
             pltpu.VMEM((ND, rows, lanes), jnp.float32),
             pltpu.SemaphoreType.DMA((2,)),

time: 85.5 us -> 79.2 us (0.926)
  Pallas kernels: 57.8 us -> 51.1 us
    pallas_call x2, Pallas kernels: 29.3 us -> 22.7 us  [main_part(): call(functools.partial(main_kernel, freqs, start, stop), [SMEM, SMEM, VME...]
  transfers between devices with their start and end apart: 10 -> 10, of which waited for: 4 -> 4; matrix products, arithmetic and copies ran while one was open for 0% -> 0% of each run, Pallas kernels for 36% -> 31%
where the time goes in v5:
time: 79.2 us; the launch traced here: 78.6 us
  Pallas kernels  51.1 us (65%)
  starting transfers between devices  15.6 us (20%)
  waiting for transfers between devices  10.9 us (14%)
  between operations  0.87 us (1%)
    pallas_call x2, Pallas kernels, main_part(): call(functools.partial(main_kernel, freqs, start, stop), [SMEM, SMEM, VME...  22.7 us
    pallas_call x1, Pallas kernels, resident(): call(functools.partial(final_kernel, freqs), [SMEM, SMEM] + [VMEM] * 10,...  14.7 us
    ppermute x8, starting transfers between devices, swap(): return lax.ppermute(values, axis, pairs + [(b, a) for a, b in pairs])  12.5 us
    pallas_call x1, Pallas kernels, resident(): call(functools.partial(pack_kernel, freqs), [SMEM] + [HBM] * 7, (in_any(N...  10.1 us
    ppermute x8, waiting for transfers between devices, swap(): return lax.ppermute(values, axis, pairs + [(b, a) for a, b in pairs])  6.85 us
    ppermute x2, waiting for transfers between devices, others_sum(): lax.ppermute(values, axis, [(i, (i + step) % count) for i in range(count)])  4.09 us
    ppermute x2, starting transfers between devices, others_sum(): lax.ppermute(values, axis, [(i, (i + step) % count) for i in range(count)])  3.14 us
  transfers between devices with their start and end apart: 10, of which 4 were waited for; matrix products, arithmetic and copies ran while one was open for 0% of the time, Pallas kernels for 31%

profile of v5, /device:TPU:12, one launch (start us, length us, event | category | flops | bytes accessed | tf_op | source)
XLA Modules:
  0.0 78.6 jit_solution(11439038137053184347)
XLA Ops:
  0.6 0.0 copy-start.5
  0.6 10.1 %shard_map.104 = (f32[36,64,128]{2,1,0:T(8,128)S(1)}, f32[64,128]{1,0:T(8,128)S(1)}, f32[6,64,128]{2,1,0:T(8,128)S(1)}, f32[6,64,128]{2,1,0:T(8,128)S(1)}, f32[6...) custom-call(s32[1]{0:T(128)} %bitcast.member_ref, ...), custom_call_target="tpu_custom_call" | custom-call | flops 21233664 | bytes 21233664 | tf_op jit(solution)/shard_map/pallas_call | solution.py:907
  10.7 0.1 collective-permute-start
  10.8 2.5 %collective-permute-start.1 = (f32[6,64,128]{2,1,0:T(8,128)S(1)}, f32[6,64,128]{2,1,0:T(8,128)S(1)}, u32[]{:S(2)}, u32[]{:S(2)}) collective-permute-start(f32[6,64,128]{2,1,0:T(8,128)S(1)} %get-tuple-element.36), channel_id=1, source_target_pairs={{4,8},{8,4},{5,9},{9,5},{6,10},{10,6},{7,11},{11,7},{20,24},{24,20... | collective-permute-start | bytes 589832 | tf_op jit(solution)/shard_map/ppermute | solution.py:852
  13.3 0.0 copy-done.5
  13.3 8.1 %shard_map.105 = (f32[18,36,64,128]{3,2,1,0:T(8,128)S(1)}, f32[1152,128]{1,0:T(8,128)S(1)}, f32[1152,128]{1,0:T(8,128)S(1)}, f32[64,128]{1,0:T(8,128)S(1)}) custom-call(s32[1]{0:T(128)} %bitcast.member_ref, f32[1800]{0:T(1024)S(1)} %copy-done.5, f32[64,128]{1,0:T(8,128)S(1)} %get-tuple-element.33.wet_ref, f32[36,64,128]{2,1,0:T(8,128)S(1)} %get-tuple-element.34.growth_ref, ...), custom_call_target="tpu_custom_call" | custom-call | flops 28311552 | bytes 14155776 | tf_op jit(solution)/shard_map/pallas_call | solution.py:942
  21.5 0.0 collective-permute-done.swapped_ref.swap_side_ref
  21.5 0.0 collective-permute-done.1.other_ref.other_side_ref
  21.5 0.1 shard_map.106
  21.6 3.5 %collective-permute-start.3 = (f32[656,128]{1,0:T(8,128)S(1)}, f32[656,128]{1,0:T(8,128)S(1)}, u32[]{:S(2)}, u32[]{:S(2)}) collective-permute-start(f32[656,128]{1,0:T(8,128)S(1)} %get-tuple-element.41), channel_id=1, source_target_pairs={{1,2},{2,1},{5,6},{6,5},{9,10},{10,9},{13,14},{14,13},{17,18},{18,... | collective-permute-start | bytes 1007624 | tf_op jit(solution)/shard_map/ppermute | solution.py:852
  25.1 0.1 collective-permute-start.2
  25.2 0.0 copy-start
  25.2 0.0 copy-start.1
  25.2 0.0 copy-start.2
  25.2 0.0 copy-start.3
  25.2 0.0 copy-start.4
  25.2 0.0 copy-start.6
  25.2 14.6 %shard_map.107 = (f32[18,36,64,128]{3,2,1,0:T(8,128)S(1)}, f32[1152,128]{1,0:T(8,128)S(1)}, f32[1152,128]{1,0:T(8,128)S(1)}, f32[64,128]{1,0:T(8,128)S(1)}) custom-call(s32[1]{0:T(128)} %bitcast.member_ref, f32[1800]{0:T(1024)S(1)} %copy-done.5, ...), custom_call_target="tpu_custom_call", output_to_operand_aliasing={{0}: (6, {}), {1}: (7, {}), {2}: (8, {}), {3}: (9, {})} | custom-call | flops 56623104 | bytes 28311552 | tf_op jit(solution)/shard_map/pallas_call | solution.py:942
  39.8 0.0 collective-permute-done.3.other_row_ref
  39.9 0.0 collective-permute-done.2.swap_row_ref
  39.9 0.0 copy-done
  39.9 0.0 copy-done.1
  39.9 1.1 %shard_map.108 = (f32[12,64,128]{2,1,0:T(8,128)S(1)}, f32[5184,128]{1,0:T(8,128)S(1)}, f32[64,128]{1,0:T(8,128)S(1)}) custom-call(s32[1]{0:T(128)} %bitcast.member_ref, f32[2,12,8,128]{3,2,1,0:T(8,128)S(1)} %copy-done.1, f32[2,10,5,18,128]{4,3,2,1,0:T(8,128)S(1)} %copy-done, ...), custom_call_target="tpu_custom_call", output_to_operand_aliasing={{1}: (8, {}), {2}: (9, {})} | custom-call | flops 4915200 | bytes 1638400 | tf_op jit(solution)/shard_map/pallas_call | solution.py:981
  41.0 1.6 %collective-permute-start.4 = (f32[64,128]{1,0:T(8,128)S(1)}, f32[64,128]{1,0:T(8,128)S(1)}, u32[]{:S(2)}, u32[]{:S(2)}) collective-permute-start(f32[64,128]{1,0:T(8,128)S(1)} %get-tuple-element.53.own_ref), channel_id=1, source_target_pairs={{0,16},{16,0},{1,17},{17,1},{2,18},{18,2},{3,19},{19,3},{4,20},{20... | collective-permute-start | bytes 98312 | tf_op jit(solution)/shard_map/ppermute | solution.py:859
  42.6 0.0 copy-done.2
  42.6 0.0 copy-done.3
  42.6 0.0 copy-done.4
  42.6 1.4 %shard_map.109 = (f32[1152,128]{1,0:T(8,128)S(1)}, f32[1152,128]{1,0:T(8,128)S(1)}) custom-call(s32[1]{0:T(128)} %bitcast.member_ref, f32[2,12,8,128]{3,2,1,0:T(8,128)S(1)} %copy-done.1, f32[2,10,5,18,128]{4,3,2,1,0:T(8,128)S(1)} %copy-done, s32[64,128]{1,0:T(8,128)S(1)} %copy-done.2, ...), custom_call_target="tpu_custom_call", output_to_operand_aliasing={{0}: (9, {}), {1}: (10, {})} | custom-call | flops 4915200 | bytes 1638400 | tf_op jit(solution)/shard_map/pallas_call | solution.py:998
  44.0 1.0 %collective-permute-done.4.other_ref = f32[64,128]{1,0:T(8,128)S(1)} collective-permute-done((f32[64,128]{1,0:T(8,128)S(1)}, f32[64,128]{1,0:T(8,128)S(1)}, u32[]{:S(2)}, u32[]{:S(2)}) %collective-permute-start.4) | collective-permute-done | bytes 32800 | tf_op jit(solution)/shard_map/ppermute | solution.py:859
  45.0 1.0 %shard_map.110 = (f32[3,64,128]{2,1,0:T(8,128)S(1)}, f32[18,64,128]{2,1,0:T(8,128)S(1)}) custom-call(s32[1]{0:T(128)} %bitcast.member_ref, f32[1800]{0:T(1024)S(1)} %copy-done.5, f32[64,128]{1,0:T(8,128)S(1)} %get-tuple-element.33.wet_ref, f32[1152,128]{1,0:T(8,128)S(1)} %get-tuple-element.51.a_ref, f32[1152,128]{1,0:T(8,128)S(1)} %get-tuple-element.52.b_ref, ...), custom_call_target="tpu_custom_call" | custom-call | flops 1769472 | bytes 1179648 | tf_op jit(solution)/shard_map/pallas_call | solution.py:1011
  46.0 1.6 %collective-permute-start.5 = (f32[3,64,128]{2,1,0:T(8,128)S(1)}, f32[3,64,128]{2,1,0:T(8,128)S(1)}, u32[]{:S(2)}, u32[]{:S(2)}) collective-permute-start(f32[3,64,128]{2,1,0:T(8,128)S(1)} %get-tuple-element.55.own_ref), channel_id=1, source_target_pairs={{0,16},{16,0},{1,17},{17,1},{2,18},{18,2},{3,19},{19,3},{4,20},{20... | collective-permute-start | bytes 294920 | tf_op jit(solution)/shard_map/ppermute | solution.py:859
  47.5 3.1 %collective-permute-done.5.other_ref = f32[3,64,128]{2,1,0:T(8,128)S(1)} collective-permute-done((f32[3,64,128]{2,1,0:T(8,128)S(1)}, f32[3,64,128]{2,1,0:T(8,128)S(1)}, u32[]{:S(2)}, u32[]{:S(2)}) %collective-permute-start.5) | collective-permute-done | bytes 98336 | tf_op jit(solution)/shard_map/ppermute | solution.py:859
  50.7 1.9 %collective-permute-start.7 = (f32[2,64,128]{2,1,0:T(8,128)S(1)}, f32[2,64,128]{2,1,0:T(8,128)S(1)}, u32[]{:S(2)}, u32[]{:S(2)}) collective-permute-start(f32[2,64,128]{2,1,0:T(8,128)S(1)} %get-tuple-element.57.stress_ref), channel_id=1, source_target_pairs={{4,8},{8,4},{5,9},{9,5},{6,10},{10,6},{7,11},{11,7},{20,24},{24,20... | collective-permute-start | bytes 196616 | tf_op jit(solution)/shard_map/ppermute | solution.py:852
  52.6 0.1 collective-permute-start.6
  52.7 3.6 %collective-permute-done.7.other_ref = f32[2,64,128]{2,1,0:T(8,128)S(1)} collective-permute-done((f32[2,64,128]{2,1,0:T(8,128)S(1)}, f32[2,64,128]{2,1,0:T(8,128)S(1)}, u32[]{:S(2)}, u32[]{:S(2)}) %collective-permute-start.7) | collective-permute-done | bytes 65568 | tf_op jit(solution)/shard_map/ppermute | solution.py:852
  56.2 0.0 collective-permute-done.6.swapped_ref
  56.3 2.0 %collective-permute-start.8 = (f32[2,8,256]{2,1,0:T(8,128)S(1)}, f32[2,8,256]{2,1,0:T(8,128)S(1)}, u32[]{:S(2)}, u32[]{:S(2)}) collective-permute-start(f32[2,8,256]{2,1,0:T(8,128)S(1)} %get-tuple-element.59), channel_id=1, source_target_pairs={{0,1},{2,3},{1,0},{3,2},{4,5},{6,7},{5,4},{7,6},{8,9},{10,11},{9,8... | collective-permute-start | bytes 49160 | tf_op jit(solution)/shard_map/ppermute | solution.py:852
  58.3 2.3 %collective-permute-start.9 = (f32[2,8,256]{2,1,0:T(8,128)S(1)}, f32[2,8,256]{2,1,0:T(8,128)S(1)}, u32[]{:S(2)}, u32[]{:S(2)}) collective-permute-start(f32[2,8,256]{2,1,0:T(8,128)S(1)} %get-tuple-element.60), channel_id=1, source_target_pairs={{1,2},{2,1},{5,6},{6,5},{9,10},{10,9},{13,14},{14,13},{17,18},{18,... | collective-permute-start | bytes 49160 | tf_op jit(solution)/shard_map/ppermute | solution.py:852
  60.7 0.0 collective-permute-done.8.swapped_ref
  60.7 3.3 %collective-permute-done.9.other_ref = f32[2,8,256]{2,1,0:T(8,128)S(1)} collective-permute-done((f32[2,8,256]{2,1,0:T(8,128)S(1)}, f32[2,8,256]{2,1,0:T(8,128)S(1)}, u32[]{:S(2)}, u32[]{:S(2)}) %collective-permute-start.9) | collective-permute-done | bytes 16416 | tf_op jit(solution)/shard_map/ppermute | solution.py:852
  63.9 0.0 copy-done.6
  63.9 14.7 %shard_map.113 = (f32[18,36,64,128]{3,2,1,0:T(8,128)}, f32[64,128]{1,0:T(8,128)}) custom-call(s32[1]{0:T(128)} %bitcast.member_ref, f32[1800]{0:T(1024)S(1)} %copy-done.5, f32[64,128]{1,0:T(8,128)S(1)} %copy-done.6, f32[18,64,128]{2,1,0:T(8,128)S(1)} %get-tuple-element.54.ratios_ref, f32[3,64,128]{2,1,0:T(8,128)S(1)} %get-tuple-element.56.sums_ref, ...), custom_call_target="tpu_custom_call" | custom-call | flops 31850496 | bytes 42467328 | tf_op jit(solution)/shard_map/pallas_call | solution.py:1037
  (2 shorter events, 0.0 us)
Async XLA Ops:
  0.6 12.7 %copy-start.5 = (f32[1800]{0:T(1024)S(1)}, f32[1800]{0:T(1024)}, u32[]{:S(2)}) copy-start(f32[1800]{0:T(1024)} %constant.12.clone.scalar_ref) | copy-start | bytes 21604
  10.7 10.8 %collective-permute-start = (f32[6,64,128]{2,1,0:T(8,128)S(1)}, f32[6,64,128]{2,1,0:T(8,128)S(1)}, u32[]{:S(2)}, u32[]{:S(2)}) collective-permute-start(f32[6,64,128]{2,1,0:T(8,128)S(1)} %get-tuple-element.35), channel_id=1, source_target_pairs={{0,4},{8,12},{4,0},{12,8},{1,5},{9,13},{5,1},{13,9},{2,6},{10,14},... | collective-permute-start | bytes 589832 | tf_op jit(solution)/shard_map/ppermute | solution.py:852
  10.8 10.7 %collective-permute-start.1 = (f32[6,64,128]{2,1,0:T(8,128)S(1)}, f32[6,64,128]{2,1,0:T(8,128)S(1)}, u32[]{:S(2)}, u32[]{:S(2)}) collective-permute-start(f32[6,64,128]{2,1,0:T(8,128)S(1)} %get-tuple-element.36), channel_id=1, source_target_pairs={{4,8},{8,4},{5,9},{9,5},{6,10},{10,6},{7,11},{11,7},{20,24},{24,20... | collective-permute-start | bytes 589832 | tf_op jit(solution)/shard_map/ppermute | solution.py:852
  21.6 18.3 %collective-permute-start.3 = (f32[656,128]{1,0:T(8,128)S(1)}, f32[656,128]{1,0:T(8,128)S(1)}, u32[]{:S(2)}, u32[]{:S(2)}) collective-permute-start(f32[656,128]{1,0:T(8,128)S(1)} %get-tuple-element.41), channel_id=1, source_target_pairs={{1,2},{2,1},{5,6},{6,5},{9,10},{10,9},{13,14},{14,13},{17,18},{18,... | collective-permute-start | bytes 1007624 | tf_op jit(solution)/shard_map/ppermute | solution.py:852
  25.1 14.8 %collective-permute-start.2 = (f32[656,128]{1,0:T(8,128)S(1)}, f32[656,128]{1,0:T(8,128)S(1)}, u32[]{:S(2)}, u32[]{:S(2)}) collective-permute-start(f32[656,128]{1,0:T(8,128)S(1)} %get-tuple-element.40.refs_0_), channel_id=1, source_target_pairs={{0,1},{2,3},{1,0},{3,2},{4,5},{6,7},{5,4},{7,6},{8,9},{10,11},{9,8... | collective-permute-start | bytes 1007624 | tf_op jit(solution)/shard_map/ppermute | solution.py:852
  25.2 14.7 %copy-start = (f32[2,10,5,18,128]{4,3,2,1,0:T(8,128)S(1)}, f32[2,10,5,18,128]{4,3,2,1,0:T(8,128)}, u32[]{:S(2)}) copy-start(f32[2,10,5,18,128]{4,3,2,1,0:T(8,128)} %constant.14.clone.table_hbm.table_ref) | copy-start | bytes 2764804
  25.2 14.7 %copy-start.1 = (f32[2,12,8,128]{3,2,1,0:T(8,128)S(1)}, f32[2,12,8,128]{3,2,1,0:T(8,128)}, u32[]{:S(2)}) copy-start(f32[2,12,8,128]{3,2,1,0:T(8,128)} %constant.13.clone.lanes_hbm.lanes_ref) | copy-start | bytes 294916
  25.2 17.4 %copy-start.2 = (s32[64,128]{1,0:T(8,128)S(1)}, s32[64,128]{1,0:T(8,128)}, u32[]{:S(2)}) copy-start(s32[64,128]{1,0:T(8,128)} %ice_ref.1) | copy-start | bytes 98308
  25.2 17.4 %copy-start.3 = (f32[64,128]{1,0:T(8,128)S(1)}, f32[64,128]{1,0:T(8,128)}, u32[]{:S(2)}) copy-start(f32[64,128]{1,0:T(8,128)} %east_ref.1) | copy-start | bytes 98308
  25.2 17.4 %copy-start.4 = (f32[64,128]{1,0:T(8,128)S(1)}, f32[64,128]{1,0:T(8,128)}, u32[]{:S(2)}) copy-start(f32[64,128]{1,0:T(8,128)} %north_ref.1) | copy-start | bytes 98308
  25.2 38.7 %copy-start.6 = (f32[64,128]{1,0:T(8,128)S(1)}, f32[64,128]{1,0:T(8,128)}, u32[]{:S(2)}) copy-start(f32[64,128]{1,0:T(8,128)} %depth_ref.1) | copy-start | bytes 98308
  41.0 4.0 %collective-permute-start.4 = (f32[64,128]{1,0:T(8,128)S(1)}, f32[64,128]{1,0:T(8,128)S(1)}, u32[]{:S(2)}, u32[]{:S(2)}) collective-permute-start(f32[64,128]{1,0:T(8,128)S(1)} %get-tuple-element.53.own_ref), channel_id=1, source_target_pairs={{0,16},{16,0},{1,17},{17,1},{2,18},{18,2},{3,19},{19,3},{4,20},{20... | collective-permute-start | bytes 98312 | tf_op jit(solution)/shard_map/ppermute | solution.py:859
  46.0 4.7 %collective-permute-start.5 = (f32[3,64,128]{2,1,0:T(8,128)S(1)}, f32[3,64,128]{2,1,0:T(8,128)S(1)}, u32[]{:S(2)}, u32[]{:S(2)}) collective-permute-start(f32[3,64,128]{2,1,0:T(8,128)S(1)} %get-tuple-element.55.own_ref), channel_id=1, source_target_pairs={{0,16},{16,0},{1,17},{17,1},{2,18},{18,2},{3,19},{19,3},{4,20},{20... | collective-permute-start | bytes 294920 | tf_op jit(solution)/shard_map/ppermute | solution.py:859
  50.7 5.6 %collective-permute-start.7 = (f32[2,64,128]{2,1,0:T(8,128)S(1)}, f32[2,64,128]{2,1,0:T(8,128)S(1)}, u32[]{:S(2)}, u32[]{:S(2)}) collective-permute-start(f32[2,64,128]{2,1,0:T(8,128)S(1)} %get-tuple-element.57.stress_ref), channel_id=1, source_target_pairs={{4,8},{8,4},{5,9},{9,5},{6,10},{10,6},{7,11},{11,7},{20,24},{24,20... | collective-permute-start | bytes 196616 | tf_op jit(solution)/shard_map/ppermute | solution.py:852
  52.6 3.7 %collective-permute-start.6 = (f32[2,64,128]{2,1,0:T(8,128)S(1)}, f32[2,64,128]{2,1,0:T(8,128)S(1)}, u32[]{:S(2)}, u32[]{:S(2)}) collective-permute-start(f32[2,64,128]{2,1,0:T(8,128)S(1)} %get-tuple-element.57.stress_ref), channel_id=1, source_target_pairs={{0,4},{8,12},{4,0},{12,8},{1,5},{9,13},{5,1},{13,9},{2,6},{10,14},... | collective-permute-start | bytes 196616 | tf_op jit(solution)/shard_map/ppermute | solution.py:852
  56.3 4.4 %collective-permute-start.8 = (f32[2,8,256]{2,1,0:T(8,128)S(1)}, f32[2,8,256]{2,1,0:T(8,128)S(1)}, u32[]{:S(2)}, u32[]{:S(2)}) collective-permute-start(f32[2,8,256]{2,1,0:T(8,128)S(1)} %get-tuple-element.59), channel_id=1, source_target_pairs={{0,1},{2,3},{1,0},{3,2},{4,5},{6,7},{5,4},{7,6},{8,9},{10,11},{9,8... | collective-permute-start | bytes 49160 | tf_op jit(solution)/shard_map/ppermute | solution.py:852
  58.3 5.6 %collective-permute-start.9 = (f32[2,8,256]{2,1,0:T(8,128)S(1)}, f32[2,8,256]{2,1,0:T(8,128)S(1)}, u32[]{:S(2)}, u32[]{:S(2)}) collective-permute-start(f32[2,8,256]{2,1,0:T(8,128)S(1)} %get-tuple-element.60), channel_id=1, source_target_pairs={{1,2},{2,1},{5,6},{6,5},{9,10},{10,9},{13,14},{14,13},{17,18},{18,... | collective-permute-start | bytes 49160 | tf_op jit(solution)/shard_map/ppermute | solution.py:852

commit v6 on v5

--- a/solution.py
+++ b/solution.py
@@ -313,7 +313,8 @@
     odd_sect, odd_slab = odd_position("sect"), odd_position("slab")
 
     half = GROUPS // 2
-    for to_right in (True, False):
+
+    def gather_all(to_right):
         target_ref = right_ref if to_right else left_ref
 
         def gather(index, carry):
@@ -364,17 +365,26 @@
         beside = shift_lanes(near, 1 if heads_right(direction) else -1)
         return near, wet_near * (table[1] * far + table[2] * beside)
 
+    def row_messages(slots):
+        for slot in slots:
+            pairs = zip(row_message(by_slot[True, slot]), row_message(by_slot[False, slot]))
+            for which, (down, up) in enumerate(pairs):
+                first = (which * 18 + slot) * freqs
+                swap_row_ref[first : first + freqs, :] = jnp.where(odd_slab, up, down)
+                other_row_ref[first : first + freqs, :] = jnp.where(odd_slab, down, up)
+
+    by_slot = {(heads_down(d), row_slot(d)): d for d in range(ND)}
+    gather_all(True)
+    rights = [side_message(index) for index in range(half)]
     for index in range(half):
-        right, left = side_message(index), side_message(index + half)
+        right_ref[index] = rights[index]
+    row_messages(range(9))
+    gather_all(False)
+    for index in range(half):
+        right, left = right_ref[index], side_message(index + half)
         swap_side_ref[index] = jnp.where(odd_sect, left, right)
         other_side_ref[index] = jnp.where(odd_sect, right, left)
-    by_slot = {(heads_down(d), row_slot(d)): d for d in range(ND)}
-    for slot in range(18):
-        pairs = zip(row_message(by_slot[True, slot]), row_message(by_slot[False, slot]))
-        for which, (down, up) in enumerate(pairs):
-            first = (which * 18 + slot) * freqs
-            swap_row_ref[first : first + freqs, :] = jnp.where(odd_slab, up, down)
-            other_row_ref[first : first + freqs, :] = jnp.where(odd_slab, down, up)
+    row_messages(range(9, 18))
 
 
 def corner_kernel(
@@ -410,22 +420,26 @@
         copy.wait()
 
 
+AHEAD = 3
+
+
 def main_kernel(
     freqs, start, stop, member_ref, scalar_ref, wet_ref, growth_ref, spectrum_ref, *refs
 ):
     if start:
         _after, _kept_in, a_in, b_in, energy_in, *refs = refs
-    kept_ref, a_ref, b_ref, energy_ref, ring0, ring1, sums_ref, sems, *first_refs = refs
-    rings = (ring0, ring1)
+    kept_ref, a_ref, b_ref, energy_ref, ring_ref, sems, *first_refs = refs
     member = member_ref[0]
+    nought = jnp.minimum(member, 0)
     rows = wet_ref.shape[0]
     tiles = rows // SUB
 
-    def fetch(j, which):
-        return pltpu.make_async_copy(spectrum_ref.at[j], rings[which], sems.at[which])
-
-    for which in range(min(2, stop - start)):
-        fetch(start + which, which).start()
+    def fetch(j):
+        slot = lax.rem(j, AHEAD)
+        return pltpu.make_async_copy(spectrum_ref.at[j], ring_ref.at[slot], sems.at[slot])
+
+    for j in range(start, min(start + AHEAD, stop)):
+        fetch(jnp.int32(j)).start()
 
     lane = iota((SUB, LANES), 1)
     sub = iota((SUB, LANES), 0)
@@ -433,73 +447,62 @@
     not_last = jnp.where(lane == LANES - 1, 0.0, 1.0)
     top, bottom = sub == 0, sub == SUB - 1
     energy_ref[...] = energy_in[...] if start else jnp.zeros_like(energy_ref)
+    for first_ref in first_refs:
+        first_ref[...] = jnp.zeros_like(first_ref)
 
     def tile_at(tile):
-        return slice(tile * SUB, (tile + 1) * SUB)
+        return pl.ds(tile * SUB, SUB)
+
+    def row_shift(quadrant):
+        return -1 if quadrant in (0, 3) else 1
 
     def parts_of(kind):
         if kind == 0:
             return ((0, 0, 0), (9, 1, 9), (18, 2, 0), (27, 3, 9))
         return ((kind, 0, kind), (18 - kind, 1, kind), (18 + kind, 2, kind), (36 - kind, 3, kind))
 
-    def frequency(j, which):
-        fetch(j, which).wait()
-        ring_ref = rings[which]
+    def frequency(j, carry):
+        fetch(j).wait()
+        slot = lax.rem(j, AHEAD)
         base = (member * freqs + j) * CLASSES * KINDS
+        at = [pl.ds(pl.multiple_of(j * rows, SUB) + t * SUB, SUB) for t in range(tiles)]
 
         def speeds(part):
-            _, quadrant, kind = part
-            across = scalar_ref[base + kind * KINDS + 1]
-            across = across * (not_first if quadrant in (0, 1) else not_last)
-            return scalar_ref[base + kind * KINDS], across
-
-        def step(load, part, speed):
-            _, quadrant, _ = part
-            alpha, across = speed
-            to_down, to_right = sides(quadrant)
-            edge = top if to_down > 0 else bottom
-            cells, turned = {}, {}
-
-            def get(t):
-                if t not in cells:
-                    cells[t] = load(t)
-                    turned[t] = pltpu.roll(cells[t], to_down % SUB, 0)
-                return turned[t]
-
-            def at(t):
-                ahead = jnp.where(
-                    edge, get(t - to_down) if 0 <= t - to_down < tiles else 0.0, get(t)
-                )
-                beside = pltpu.roll(cells[t], to_right % LANES, 1)
-                return cells[t] + alpha * ahead + across * beside
-
-            return at
+            at_class = base + part[2] * KINDS
+            beta = scalar_ref[at_class + 1]
+            return scalar_ref[at_class], beta * (not_first if part[1] in (0, 1) else not_last)
+
+        def beside(cells, quadrant):
+            return pltpu.roll(cells, 1 if quadrant in (0, 1) else LANES - 1, 1)
 
         def first_step(kind):
-            for part in parts_of(kind):
-                direction, quadrant, _ = part
+            parts = parts_of(kind)
+            speed = [speeds(part) for part in parts]
+            wet = [wet_ref[tile_at(t), :] for t in range(tiles)]
+            for (direction, quadrant, _), (alpha, across) in zip(parts, speed):
+                shift = row_shift(quadrant)
+                edge = top if shift < 0 else bottom
                 target = first_refs[kind % 2 * 4 + quadrant]
-                after = step(
-                    lambda t: ring_ref[direction, tile_at(t), :] * wet_ref[tile_at(t), :],
-                    part,
-                    speeds(part),
-                )
+                cells = [ring_ref[slot, direction, tile_at(t), :] * wet[t] for t in range(tiles)]
+                turned = [pltpu.roll(cells[t], -shift % SUB, 0) for t in range(tiles)]
                 for t in range(tiles):
-                    target[tile_at(t), :] = wet_ref[tile_at(t), :] * after(t)
+                    before = turned[t + shift] if 0 <= t + shift < tiles else 0.0
+                    ahead = jnp.where(edge, before, turned[t])
+                    after = cells[t] + alpha * ahead + across * beside(cells[t], quadrant)
+                    target[tile_at(t + 1), :] = wet[t] * after
 
         def second_step(kind):
             parts = parts_of(kind)
             scale, high = scalar_ref[base + kind * KINDS + 2], scalar_ref[base + 3]
             scaled_high = scale * high
-            sources = [first_refs[kind % 2 * 4 + quadrant] for _, quadrant, _ in parts]
-            steps = [
-                step(lambda t, source=source: source[tile_at(t), :], part, speeds(part))
-                for part, source in zip(parts, sources)
-            ]
+            speed = [speeds(part) for part in parts]
             for t in range(tiles):
                 moved, grown = [], []
-                for (direction, _, _), after_at in zip(parts, steps):
-                    after = after_at(t)
+                for (direction, quadrant, _), (alpha, across) in zip(parts, speed):
+                    source = first_refs[kind % 2 * 4 + quadrant]
+                    cells = source[tile_at(t + 1), :]
+                    ahead = source[pl.ds((t + 1) * SUB + row_shift(quadrant) + nought, SUB), :]
+                    after = cells + alpha * ahead + across * beside(cells, quadrant)
                     kept_ref[j, direction, tile_at(t), :] = after
                     moved.append(after)
                     grown.append(growth_ref[direction, tile_at(t), :] * after)
@@ -509,39 +512,29 @@
                     grown_y = plain_y + scaled_high * (grown[1] + grown[3])
                     square = math.cos(0.5 * math.pi) ** 2
                     energy_ref[tile_at(t), :] += plain_x + plain_y
-                    sums_ref[0, tile_at(t), :] = grown_x + grown_y
-                    sums_ref[1, tile_at(t), :] = grown_x + square * grown_y
+                    a_ref[at[t], :] = grown_x + grown_y
+                    b_ref[at[t], :] = grown_x + square * grown_y
                 else:
                     plain = scale * ((moved[0] + moved[1]) + (moved[2] + moved[3]))
                     whole = plain + scaled_high * ((grown[0] + grown[1]) + (grown[2] + grown[3]))
                     square = math.cos(2.0 * math.pi * kind / ND) ** 2
                     energy_ref[tile_at(t), :] += plain
-                    sums_ref[0, tile_at(t), :] += whole
-                    sums_ref[1, tile_at(t), :] += square * whole
+                    a_ref[at[t], :] += whole
+                    b_ref[at[t], :] += square * whole
 
         first_step(0)
         for kind in range(CLASSES - 1):
             if kind + 1 < CLASSES - 1:
                 first_step(kind + 1)
             second_step(kind)
-        at = pl.ds(pl.multiple_of(j * rows, SUB), rows)
-        a_ref[at, :] = sums_ref[0]
-        b_ref[at, :] = sums_ref[1]
-
-    def pair(index, carry):
-        for which in range(2):
-            j = start + 2 * index + which
-            frequency(j, which)
-
-            @pl.when(j + 2 < stop)
-            def _():
-                fetch(j + 2, which).start()
+
+        @pl.when(j + AHEAD < stop)
+        def _():
+            fetch(j + AHEAD).start()
 
         return carry
 
-    lax.fori_loop(0, (stop - start) // 2, pair, 0)
-    if (stop - start) % 2:
-        frequency(jnp.int32(stop - 1), 0)
+    lax.fori_loop(start, stop, frequency, 0)
 
 
 def edge_rows(freqs, to_down, direction, at):
@@ -738,7 +731,7 @@
         second_ref[index] = jnp.where(odd_slab, *ends[::-1])
 
 
-BEHIND = 16
+BEHIND = 12
 
 
 def final_kernel(
@@ -789,17 +782,20 @@
     turning_ref[...] = columns_ref[...]
     tile_lane = iota((SUB, LANES), 1)
 
-    def send(j, which):
-        return pltpu.make_async_copy(rings[which], result_ref.at[j], sems.at[which])
+    def send(j, which, piece):
+        part = pl.ds(piece * ND // 4, ND // 4)
+        return pltpu.make_async_copy(
+            rings[which].at[part], result_ref.at[j, part], sems.at[which, piece]
+        )
 
     def frequency(j, which):
         @pl.when(j >= 2)
         def _():
-            send(j - 2, which).wait()
+            for piece in range(4):
+                send(j - 2, which, piece).wait()
 
         base = (member * freqs + j) * CLASSES * KINDS
         high = scalar_ref[base + 3]
-        scales = [scalar_ref[base + kind * KINDS + 2] for kind in range(CLASSES)]
 
         def damped(direction, t, ratio, high_ratio):
             to_down, to_right = sides(direction // (ND // 4))
@@ -814,22 +810,25 @@
             if t == (0 if to_down > 0 else tiles - 1):
                 edge = ((0 if to_down > 0 else 18) + row_slot(direction)) * freqs + j
                 value += edges_ref[pl.ds(pl.multiple_of(edge * SUB, SUB), SUB), :]
-            factor = ratio + high_ratio * growth_ref[direction, part, :]
-            return value * (scales[class_of(direction)] * factor)
+            return value * (ratio + high_ratio * growth_ref[direction, part, :])
 
         pending = []
-        for t in range(tiles):
-            part = slice(t * SUB, (t + 1) * SUB)
-            ratio = ratios_ref[j, part, :] * damping_ref[part, :]
-            high_ratio = high * ratio
-            for direction in range(ND):
-                pending.append((direction, part, damped(direction, t, ratio, high_ratio)))
-                if len(pending) > BEHIND:
+        for kind in range(CLASSES - 1):
+            together = (0, 9, 18, 27) if kind == 0 else (kind, 18 - kind, 18 + kind, 36 - kind)
+            scale = scalar_ref[base + kind * KINDS + 2]
+            for t in range(tiles):
+                part = slice(t * SUB, (t + 1) * SUB)
+                ratio = scale * (ratios_ref[j, part, :] * damping_ref[part, :])
+                high_ratio = high * ratio
+                for direction in together:
+                    pending.append((direction, part, damped(direction, t, ratio, high_ratio)))
+                while len(pending) > BEHIND:
                     target, place, value = pending.pop(0)
                     rings[which][target, place, :] = value
         for target, place, value in pending:
             rings[which][target, place, :] = value
-        send(j, which).start()
+        for piece in range(4):
+            send(j, which, piece).start()
         turned = [pltpu.roll(turning_ref[group], LANES - 2, 1) for group in range(GROUPS)]
         for group in range(GROUPS):
             turning_ref[group] = turned[group]
@@ -843,7 +842,8 @@
     if freqs % 2:
         frequency(jnp.int32(freqs - 1), 0)
     for j in range(max(0, freqs - 2), freqs):
-        send(j, j % 2).wait()
+        for piece in range(4):
+            send(j, j % 2, piece).wait()
 
 
 def swap(values, axis, first):
@@ -952,13 +952,12 @@
             flops=local_comp * cells * 16 * (stop - start) // freqs,
             moved=local_comp * cells * 8 * (stop - start) // freqs,
             scratch=[
-                pltpu.VMEM((ND, rows, lanes), jnp.float32),
-                pltpu.VMEM((ND, rows, lanes), jnp.float32),
-                pltpu.VMEM((2, rows, lanes), jnp.float32),
-                pltpu.SemaphoreType.DMA((2,)),
+                pltpu.VMEM((AHEAD, ND, rows, lanes), jnp.float32),
+                pltpu.SemaphoreType.DMA((AHEAD,)),
             ]
-            + [pltpu.VMEM((rows, lanes), jnp.float32)] * 8,
+            + [pltpu.VMEM((rows + 2 * SUB, lanes), jnp.float32)] * 8,
             aliases={6 + index: index for index in range(4)} if before else {},
+            limit=8,
         )(member, scalars, wet, growth, in_hbm(spectrum), *before)
 
     early = max(1, freqs // 3)
@@ -1046,7 +1045,7 @@
             pltpu.VMEM((GROUPS, rows, lanes), jnp.float32),
             pltpu.VMEM((ND, rows, lanes), jnp.float32),
             pltpu.VMEM((ND, rows, lanes), jnp.float32),
-            pltpu.SemaphoreType.DMA((2,)),
+            pltpu.SemaphoreType.DMA((2, 4)),
         ],
     )(
         member, scalars, depth, ratios, sums, beside, aside, beyond, growth, kept,

time: 79.2 us -> 76.9 us (0.971)
  Pallas kernels: 51.1 us -> 49.2 us
    pallas_call x2, Pallas kernels: 22.7 us -> 20.7 us  [main_part(): call(functools.partial(main_kernel, freqs, start, stop), [SMEM, SMEM, VME...]
  transfers between devices with their start and end apart: 10 -> 10, of which waited for: 4 -> 4; matrix products, arithmetic and copies ran while one was open for 0% -> 0% of each run, Pallas kernels for 31% -> 29%
where the time goes in v6:
time: 76.9 us; the launch traced here: 76.7 us
  Pallas kernels  49.2 us (64%)
  starting transfers between devices  15.6 us (20%)
  waiting for transfers between devices  11 us (14%)
  between operations  0.87 us (1%)
    pallas_call x2, Pallas kernels, main_part(): call(functools.partial(main_kernel, freqs, start, stop), [SMEM, SMEM, VME...  20.7 us
    pallas_call x1, Pallas kernels, resident(): call(functools.partial(final_kernel, freqs), [SMEM, SMEM] + [VMEM] * 10,...  14.8 us
    ppermute x8, starting transfers between devices, swap(): return lax.ppermute(values, axis, pairs + [(b, a) for a, b in pairs])  12.5 us
    pallas_call x1, Pallas kernels, resident(): call(functools.partial(pack_kernel, freqs), [SMEM] + [HBM] * 7, (in_any(N...  9.98 us
    ppermute x8, waiting for transfers between devices, swap(): return lax.ppermute(values, axis, pairs + [(b, a) for a, b in pairs])  6.85 us
    ppermute x2, waiting for transfers between devices, others_sum(): lax.ppermute(values, axis, [(i, (i + step) % count) for i in range(count)])  4.12 us
    ppermute x2, starting transfers between devices, others_sum(): lax.ppermute(values, axis, [(i, (i + step) % count) for i in range(count)])  3.11 us
  transfers between devices with their start and end apart: 10, of which 4 were waited for; matrix products, arithmetic and copies ran while one was open for 0% of the time, Pallas kernels for 29%

profile of v6, /device:TPU:12, one launch (start us, length us, event | category | flops | bytes accessed | tf_op | source)
XLA Modules:
  0.0 76.7 jit_solution(9126496373932307925)
XLA Ops:
  0.6 0.0 copy-start.5
  0.6 10.0 %shard_map.104 = (f32[36,64,128]{2,1,0:T(8,128)S(1)}, f32[64,128]{1,0:T(8,128)S(1)}, f32[6,64,128]{2,1,0:T(8,128)S(1)}, f32[6,64,128]{2,1,0:T(8,128)S(1)}, f32[6...) custom-call(s32[1]{0:T(128)} %bitcast.member_ref, ...), custom_call_target="tpu_custom_call" | custom-call | flops 21233664 | bytes 21233664 | tf_op jit(solution)/shard_map/pallas_call | solution.py:907
  10.6 0.1 collective-permute-start
  10.7 2.5 %collective-permute-start.1 = (f32[6,64,128]{2,1,0:T(8,128)S(1)}, f32[6,64,128]{2,1,0:T(8,128)S(1)}, u32[]{:S(2)}, u32[]{:S(2)}) collective-permute-start(f32[6,64,128]{2,1,0:T(8,128)S(1)} %get-tuple-element.36), channel_id=1, source_target_pairs={{4,8},{8,4},{5,9},{9,5},{6,10},{10,6},{7,11},{11,7},{20,24},{24,20... | collective-permute-start | bytes 589832 | tf_op jit(solution)/shard_map/ppermute | solution.py:852
  13.2 0.0 copy-done.5
  13.2 7.5 %shard_map.105 = (f32[18,36,64,128]{3,2,1,0:T(8,128)S(1)}, f32[1152,128]{1,0:T(8,128)S(1)}, f32[1152,128]{1,0:T(8,128)S(1)}, f32[64,128]{1,0:T(8,128)S(1)}) custom-call(s32[1]{0:T(128)} %bitcast.member_ref, f32[1800]{0:T(1024)S(1)} %copy-done.5, f32[64,128]{1,0:T(8,128)S(1)} %get-tuple-element.33.wet_ref, f32[36,64,128]{2,1,0:T(8,128)S(1)} %get-tuple-element.34.growth_ref, ...), custom_call_target="tpu_custom_call" | custom-call | flops 28311552 | bytes 14155776 | tf_op jit(solution)/shard_map/pallas_call | solution.py:942
  20.8 0.0 collective-permute-done.swapped_ref.swap_side_ref
  20.8 0.0 collective-permute-done.1.other_ref.other_side_ref
  20.8 0.1 shard_map.106
  20.9 3.5 %collective-permute-start.3 = (f32[656,128]{1,0:T(8,128)S(1)}, f32[656,128]{1,0:T(8,128)S(1)}, u32[]{:S(2)}, u32[]{:S(2)}) collective-permute-start(f32[656,128]{1,0:T(8,128)S(1)} %get-tuple-element.41), channel_id=1, source_target_pairs={{1,2},{2,1},{5,6},{6,5},{9,10},{10,9},{13,14},{14,13},{17,18},{18,... | collective-permute-start | bytes 1007624 | tf_op jit(solution)/shard_map/ppermute | solution.py:852
  24.4 0.1 collective-permute-start.2
  24.5 0.0 copy-start
  24.5 0.0 copy-start.1
  24.5 0.0 copy-start.2
  24.5 0.0 copy-start.3
  24.5 0.0 copy-start.4
  24.6 0.0 copy-start.6
  24.6 13.1 %shard_map.107 = (f32[18,36,64,128]{3,2,1,0:T(8,128)S(1)}, f32[1152,128]{1,0:T(8,128)S(1)}, f32[1152,128]{1,0:T(8,128)S(1)}, f32[64,128]{1,0:T(8,128)S(1)}) custom-call(s32[1]{0:T(128)} %bitcast.member_ref, f32[1800]{0:T(1024)S(1)} %copy-done.5, ...), custom_call_target="tpu_custom_call", output_to_operand_aliasing={{0}: (6, {}), {1}: (7, {}), {2}: (8, {}), {3}: (9, {})} | custom-call | flops 56623104 | bytes 28311552 | tf_op jit(solution)/shard_map/pallas_call | solution.py:942
  37.7 0.0 collective-permute-done.3.other_row_ref
  37.7 0.0 collective-permute-done.2.swap_row_ref
  37.7 0.0 copy-done
  37.8 0.0 copy-done.1
  37.8 1.1 %shard_map.108 = (f32[12,64,128]{2,1,0:T(8,128)S(1)}, f32[5184,128]{1,0:T(8,128)S(1)}, f32[64,128]{1,0:T(8,128)S(1)}) custom-call(s32[1]{0:T(128)} %bitcast.member_ref, f32[2,12,8,128]{3,2,1,0:T(8,128)S(1)} %copy-done.1, f32[2,10,5,18,128]{4,3,2,1,0:T(8,128)S(1)} %copy-done, ...), custom_call_target="tpu_custom_call", output_to_operand_aliasing={{1}: (8, {}), {2}: (9, {})} | custom-call | flops 4915200 | bytes 1638400 | tf_op jit(solution)/shard_map/pallas_call | solution.py:980
  38.9 1.6 %collective-permute-start.4 = (f32[64,128]{1,0:T(8,128)S(1)}, f32[64,128]{1,0:T(8,128)S(1)}, u32[]{:S(2)}, u32[]{:S(2)}) collective-permute-start(f32[64,128]{1,0:T(8,128)S(1)} %get-tuple-element.53.own_ref), channel_id=1, source_target_pairs={{0,16},{16,0},{1,17},{17,1},{2,18},{18,2},{3,19},{19,3},{4,20},{20... | collective-permute-start | bytes 98312 | tf_op jit(solution)/shard_map/ppermute | solution.py:859
  40.5 0.0 copy-done.2
  40.5 0.0 copy-done.3
  40.5 0.0 copy-done.4
  40.5 1.4 %shard_map.109 = (f32[1152,128]{1,0:T(8,128)S(1)}, f32[1152,128]{1,0:T(8,128)S(1)}) custom-call(s32[1]{0:T(128)} %bitcast.member_ref, f32[2,12,8,128]{3,2,1,0:T(8,128)S(1)} %copy-done.1, f32[2,10,5,18,128]{4,3,2,1,0:T(8,128)S(1)} %copy-done, s32[64,128]{1,0:T(8,128)S(1)} %copy-done.2, ...), custom_call_target="tpu_custom_call", output_to_operand_aliasing={{0}: (9, {}), {1}: (10, {})} | custom-call | flops 4915200 | bytes 1638400 | tf_op jit(solution)/shard_map/pallas_call | solution.py:997
  41.9 1.0 %collective-permute-done.4.other_ref = f32[64,128]{1,0:T(8,128)S(1)} collective-permute-done((f32[64,128]{1,0:T(8,128)S(1)}, f32[64,128]{1,0:T(8,128)S(1)}, u32[]{:S(2)}, u32[]{:S(2)}) %collective-permute-start.4) | collective-permute-done | bytes 32800 | tf_op jit(solution)/shard_map/ppermute | solution.py:859
  42.9 1.0 %shard_map.110 = (f32[3,64,128]{2,1,0:T(8,128)S(1)}, f32[18,64,128]{2,1,0:T(8,128)S(1)}) custom-call(s32[1]{0:T(128)} %bitcast.member_ref, f32[1800]{0:T(1024)S(1)} %copy-done.5, f32[64,128]{1,0:T(8,128)S(1)} %get-tuple-element.33.wet_ref, f32[1152,128]{1,0:T(8,128)S(1)} %get-tuple-element.51.a_ref, f32[1152,128]{1,0:T(8,128)S(1)} %get-tuple-element.52.b_ref, ...), custom_call_target="tpu_custom_call" | custom-call | flops 1769472 | bytes 1179648 | tf_op jit(solution)/shard_map/pallas_call | solution.py:1010
  43.9 1.6 %collective-permute-start.5 = (f32[3,64,128]{2,1,0:T(8,128)S(1)}, f32[3,64,128]{2,1,0:T(8,128)S(1)}, u32[]{:S(2)}, u32[]{:S(2)}) collective-permute-start(f32[3,64,128]{2,1,0:T(8,128)S(1)} %get-tuple-element.55.own_ref), channel_id=1, source_target_pairs={{0,16},{16,0},{1,17},{17,1},{2,18},{18,2},{3,19},{19,3},{4,20},{20... | collective-permute-start | bytes 294920 | tf_op jit(solution)/shard_map/ppermute | solution.py:859
  45.4 3.1 %collective-permute-done.5.other_ref = f32[3,64,128]{2,1,0:T(8,128)S(1)} collective-permute-done((f32[3,64,128]{2,1,0:T(8,128)S(1)}, f32[3,64,128]{2,1,0:T(8,128)S(1)}, u32[]{:S(2)}, u32[]{:S(2)}) %collective-permute-start.5) | collective-permute-done | bytes 98336 | tf_op jit(solution)/shard_map/ppermute | solution.py:859
  48.6 1.9 %collective-permute-start.7 = (f32[2,64,128]{2,1,0:T(8,128)S(1)}, f32[2,64,128]{2,1,0:T(8,128)S(1)}, u32[]{:S(2)}, u32[]{:S(2)}) collective-permute-start(f32[2,64,128]{2,1,0:T(8,128)S(1)} %get-tuple-element.57.stress_ref), channel_id=1, source_target_pairs={{4,8},{8,4},{5,9},{9,5},{6,10},{10,6},{7,11},{11,7},{20,24},{24,20... | collective-permute-start | bytes 196616 | tf_op jit(solution)/shard_map/ppermute | solution.py:852
  50.5 0.1 collective-permute-start.6
  50.6 3.6 %collective-permute-done.7.other_ref = f32[2,64,128]{2,1,0:T(8,128)S(1)} collective-permute-done((f32[2,64,128]{2,1,0:T(8,128)S(1)}, f32[2,64,128]{2,1,0:T(8,128)S(1)}, u32[]{:S(2)}, u32[]{:S(2)}) %collective-permute-start.7) | collective-permute-done | bytes 65568 | tf_op jit(solution)/shard_map/ppermute | solution.py:852
  54.1 0.0 collective-permute-done.6.swapped_ref
  54.2 2.0 %collective-permute-start.8 = (f32[2,8,256]{2,1,0:T(8,128)S(1)}, f32[2,8,256]{2,1,0:T(8,128)S(1)}, u32[]{:S(2)}, u32[]{:S(2)}) collective-permute-start(f32[2,8,256]{2,1,0:T(8,128)S(1)} %get-tuple-element.59), channel_id=1, source_target_pairs={{0,1},{2,3},{1,0},{3,2},{4,5},{6,7},{5,4},{7,6},{8,9},{10,11},{9,8... | collective-permute-start | bytes 49160 | tf_op jit(solution)/shard_map/ppermute | solution.py:852
  56.2 2.3 %collective-permute-start.9 = (f32[2,8,256]{2,1,0:T(8,128)S(1)}, f32[2,8,256]{2,1,0:T(8,128)S(1)}, u32[]{:S(2)}, u32[]{:S(2)}) collective-permute-start(f32[2,8,256]{2,1,0:T(8,128)S(1)} %get-tuple-element.60), channel_id=1, source_target_pairs={{1,2},{2,1},{5,6},{6,5},{9,10},{10,9},{13,14},{14,13},{17,18},{18,... | collective-permute-start | bytes 49160 | tf_op jit(solution)/shard_map/ppermute | solution.py:852
  58.6 0.0 collective-permute-done.8.swapped_ref
  58.6 3.3 %collective-permute-done.9.other_ref = f32[2,8,256]{2,1,0:T(8,128)S(1)} collective-permute-done((f32[2,8,256]{2,1,0:T(8,128)S(1)}, f32[2,8,256]{2,1,0:T(8,128)S(1)}, u32[]{:S(2)}, u32[]{:S(2)}) %collective-permute-start.9) | collective-permute-done | bytes 16416 | tf_op jit(solution)/shard_map/ppermute | solution.py:852
  61.8 0.0 copy-done.6
  61.8 14.8 %shard_map.113 = (f32[18,36,64,128]{3,2,1,0:T(8,128)}, f32[64,128]{1,0:T(8,128)}) custom-call(s32[1]{0:T(128)} %bitcast.member_ref, f32[1800]{0:T(1024)S(1)} %copy-done.5, f32[64,128]{1,0:T(8,128)S(1)} %copy-done.6, f32[18,64,128]{2,1,0:T(8,128)S(1)} %get-tuple-element.54.ratios_ref, f32[3,64,128]{2,1,0:T(8,128)S(1)} %get-tuple-element.56.sums_ref, ...), custom_call_target="tpu_custom_call" | custom-call | flops 31850496 | bytes 42467328 | tf_op jit(solution)/shard_map/pallas_call | solution.py:1036
  (2 shorter events, 0.0 us)
Async XLA Ops:
  0.6 12.6 %copy-start.5 = (f32[1800]{0:T(1024)S(1)}, f32[1800]{0:T(1024)}, u32[]{:S(2)}) copy-start(f32[1800]{0:T(1024)} %constant.12.clone.scalar_ref) | copy-start | bytes 21604
  10.6 10.2 %collective-permute-start = (f32[6,64,128]{2,1,0:T(8,128)S(1)}, f32[6,64,128]{2,1,0:T(8,128)S(1)}, u32[]{:S(2)}, u32[]{:S(2)}) collective-permute-start(f32[6,64,128]{2,1,0:T(8,128)S(1)} %get-tuple-element.35), channel_id=1, source_target_pairs={{0,4},{8,12},{4,0},{12,8},{1,5},{9,13},{5,1},{13,9},{2,6},{10,14},... | collective-permute-start | bytes 589832 | tf_op jit(solution)/shard_map/ppermute | solution.py:852
  10.7 10.1 %collective-permute-start.1 = (f32[6,64,128]{2,1,0:T(8,128)S(1)}, f32[6,64,128]{2,1,0:T(8,128)S(1)}, u32[]{:S(2)}, u32[]{:S(2)}) collective-permute-start(f32[6,64,128]{2,1,0:T(8,128)S(1)} %get-tuple-element.36), channel_id=1, source_target_pairs={{4,8},{8,4},{5,9},{9,5},{6,10},{10,6},{7,11},{11,7},{20,24},{24,20... | collective-permute-start | bytes 589832 | tf_op jit(solution)/shard_map/ppermute | solution.py:852
  20.9 16.8 %collective-permute-start.3 = (f32[656,128]{1,0:T(8,128)S(1)}, f32[656,128]{1,0:T(8,128)S(1)}, u32[]{:S(2)}, u32[]{:S(2)}) collective-permute-start(f32[656,128]{1,0:T(8,128)S(1)} %get-tuple-element.41), channel_id=1, source_target_pairs={{1,2},{2,1},{5,6},{6,5},{9,10},{10,9},{13,14},{14,13},{17,18},{18,... | collective-permute-start | bytes 1007624 | tf_op jit(solution)/shard_map/ppermute | solution.py:852
  24.4 13.3 %collective-permute-start.2 = (f32[656,128]{1,0:T(8,128)S(1)}, f32[656,128]{1,0:T(8,128)S(1)}, u32[]{:S(2)}, u32[]{:S(2)}) collective-permute-start(f32[656,128]{1,0:T(8,128)S(1)} %get-tuple-element.40.refs_0_), channel_id=1, source_target_pairs={{0,1},{2,3},{1,0},{3,2},{4,5},{6,7},{5,4},{7,6},{8,9},{10,11},{9,8... | collective-permute-start | bytes 1007624 | tf_op jit(solution)/shard_map/ppermute | solution.py:852
  24.5 13.2 %copy-start = (f32[2,10,5,18,128]{4,3,2,1,0:T(8,128)S(1)}, f32[2,10,5,18,128]{4,3,2,1,0:T(8,128)}, u32[]{:S(2)}) copy-start(f32[2,10,5,18,128]{4,3,2,1,0:T(8,128)} %constant.14.clone.table_hbm.table_ref) | copy-start | bytes 2764804
  24.5 13.2 %copy-start.1 = (f32[2,12,8,128]{3,2,1,0:T(8,128)S(1)}, f32[2,12,8,128]{3,2,1,0:T(8,128)}, u32[]{:S(2)}) copy-start(f32[2,12,8,128]{3,2,1,0:T(8,128)} %constant.13.clone.lanes_hbm.lanes_ref) | copy-start | bytes 294916
  24.5 15.9 %copy-start.2 = (s32[64,128]{1,0:T(8,128)S(1)}, s32[64,128]{1,0:T(8,128)}, u32[]{:S(2)}) copy-start(s32[64,128]{1,0:T(8,128)} %ice_ref.1) | copy-start | bytes 98308
  24.5 15.9 %copy-start.3 = (f32[64,128]{1,0:T(8,128)S(1)}, f32[64,128]{1,0:T(8,128)}, u32[]{:S(2)}) copy-start(f32[64,128]{1,0:T(8,128)} %east_ref.1) | copy-start | bytes 98308
  24.5 15.9 %copy-start.4 = (f32[64,128]{1,0:T(8,128)S(1)}, f32[64,128]{1,0:T(8,128)}, u32[]{:S(2)}) copy-start(f32[64,128]{1,0:T(8,128)} %north_ref.1) | copy-start | bytes 98308
  24.6 37.3 %copy-start.6 = (f32[64,128]{1,0:T(8,128)S(1)}, f32[64,128]{1,0:T(8,128)}, u32[]{:S(2)}) copy-start(f32[64,128]{1,0:T(8,128)} %depth_ref.1) | copy-start | bytes 98308
  38.9 4.0 %collective-permute-start.4 = (f32[64,128]{1,0:T(8,128)S(1)}, f32[64,128]{1,0:T(8,128)S(1)}, u32[]{:S(2)}, u32[]{:S(2)}) collective-permute-start(f32[64,128]{1,0:T(8,128)S(1)} %get-tuple-element.53.own_ref), channel_id=1, source_target_pairs={{0,16},{16,0},{1,17},{17,1},{2,18},{18,2},{3,19},{19,3},{4,20},{20... | collective-permute-start | bytes 98312 | tf_op jit(solution)/shard_map/ppermute | solution.py:859
  43.9 4.7 %collective-permute-start.5 = (f32[3,64,128]{2,1,0:T(8,128)S(1)}, f32[3,64,128]{2,1,0:T(8,128)S(1)}, u32[]{:S(2)}, u32[]{:S(2)}) collective-permute-start(f32[3,64,128]{2,1,0:T(8,128)S(1)} %get-tuple-element.55.own_ref), channel_id=1, source_target_pairs={{0,16},{16,0},{1,17},{17,1},{2,18},{18,2},{3,19},{19,3},{4,20},{20... | collective-permute-start | bytes 294920 | tf_op jit(solution)/shard_map/ppermute | solution.py:859
  48.6 5.6 %collective-permute-start.7 = (f32[2,64,128]{2,1,0:T(8,128)S(1)}, f32[2,64,128]{2,1,0:T(8,128)S(1)}, u32[]{:S(2)}, u32[]{:S(2)}) collective-permute-start(f32[2,64,128]{2,1,0:T(8,128)S(1)} %get-tuple-element.57.stress_ref), channel_id=1, source_target_pairs={{4,8},{8,4},{5,9},{9,5},{6,10},{10,6},{7,11},{11,7},{20,24},{24,20... | collective-permute-start | bytes 196616 | tf_op jit(solution)/shard_map/ppermute | solution.py:852
  50.5 3.7 %collective-permute-start.6 = (f32[2,64,128]{2,1,0:T(8,128)S(1)}, f32[2,64,128]{2,1,0:T(8,128)S(1)}, u32[]{:S(2)}, u32[]{:S(2)}) collective-permute-start(f32[2,64,128]{2,1,0:T(8,128)S(1)} %get-tuple-element.57.stress_ref), channel_id=1, source_target_pairs={{0,4},{8,12},{4,0},{12,8},{1,5},{9,13},{5,1},{13,9},{2,6},{10,14},... | collective-permute-start | bytes 196616 | tf_op jit(solution)/shard_map/ppermute | solution.py:852
  54.2 4.4 %collective-permute-start.8 = (f32[2,8,256]{2,1,0:T(8,128)S(1)}, f32[2,8,256]{2,1,0:T(8,128)S(1)}, u32[]{:S(2)}, u32[]{:S(2)}) collective-permute-start(f32[2,8,256]{2,1,0:T(8,128)S(1)} %get-tuple-element.59), channel_id=1, source_target_pairs={{0,1},{2,3},{1,0},{3,2},{4,5},{6,7},{5,4},{7,6},{8,9},{10,11},{9,8... | collective-permute-start | bytes 49160 | tf_op jit(solution)/shard_map/ppermute | solution.py:852
  56.2 5.6 %collective-permute-start.9 = (f32[2,8,256]{2,1,0:T(8,128)S(1)}, f32[2,8,256]{2,1,0:T(8,128)S(1)}, u32[]{:S(2)}, u32[]{:S(2)}) collective-permute-start(f32[2,8,256]{2,1,0:T(8,128)S(1)} %get-tuple-element.60), channel_id=1, source_target_pairs={{1,2},{2,1},{5,6},{6,5},{9,10},{10,9},{13,14},{14,13},{17,18},{18,... | collective-permute-start | bytes 49160 | tf_op jit(solution)/shard_map/ppermute | solution.py:852

commit v7 on v6

--- a/solution.py
+++ b/solution.py
@@ -253,7 +253,7 @@
     return jnp.where(iota(values.shape, 1) == edge, 0.0, moved)
 
 
-DEPTH = 3
+DEPTH = 5
 
 
 def sides(quadrant):
@@ -685,7 +685,8 @@
 
 
 def stress_kernel(
-    freqs, member_ref, scalar_ref, wet_ref, a_ref, b_ref, own_ref, other_ref, sums_ref, ratio_ref
+    freqs, member_ref, scalar_ref, wet_ref, a_ref, b_ref, own_ref, other_ref, sums_ref, final_ref,
+    ratio_ref,
 ):
     member = member_ref[0]
     wet_cells = wet_ref[...]
@@ -705,13 +706,13 @@
         sums[0] += shoal * along + (shoal - 0.5) * whole
         sums[1] += (2.0 * shoal - 0.5) * whole - shoal * along
         sums[2] += whole
-    for index in range(3):
+    for index in range(2):
         sums_ref[index] = sums[index] / (ND * NF)
-
-
-def total_kernel(own_ref, other_ref, sums_ref, stress_ref):
-    sums_ref[...] = own_ref[...] + other_ref[...]
-    stress_ref[...] = sums_ref[0:2]
+    final_ref[...] = sums[2] / (ND * NF)
+
+
+def total_kernel(own_ref, other_ref, sum_ref):
+    sum_ref[...] = own_ref[...] + other_ref[...]
 
 
 def strip_kernel(stress_ref, swapped_ref, other_ref, beside_ref, first_ref, second_ref):
@@ -732,15 +733,15 @@
 
 
 BEHIND = 12
+RINGS = 6
 
 
 def final_kernel(
-    freqs, member_ref, scalar_ref, depth_ref, ratios_ref, sums_ref, beside_ref, swapped_ref,
-    other_ref, growth_ref, kept_ref, columns_ref, edges_ref,
-    result_ref, level_ref, damping_ref, turning_ref, ring0, ring1, sems,
+    freqs, member_ref, scalar_ref, depth_ref, ratios_ref, sums_ref, own_ref, there_ref, beside_ref,
+    swapped_ref, other_ref, growth_ref, kept_ref, columns_ref, edges_ref,
+    result_ref, level_ref, damping_ref, turning_ref, sems, *rings,
 ):
     member = member_ref[0]
-    rings = (ring0, ring1)
     rows = depth_ref.shape[0]
     slab, slabs = lax.axis_index("slab"), lax.axis_size("slab")
     sect, sects = lax.axis_index("sect"), lax.axis_size("sect")
@@ -776,7 +777,8 @@
         level = inside * (source + around(level, 0) + around(level, 1))
     level = level[:rows, :LANES]
     level_ref[...] = level
-    damping = 1.0 / (1.0 + 4.0 * sums_ref[2] / (jnp.square(depth_ref[...] + level) + 1.0))
+    final = own_ref[...] + there_ref[...]
+    damping = 1.0 / (1.0 + 4.0 * final / (jnp.square(depth_ref[...] + level) + 1.0))
     tiles = rows // SUB
     damping_ref[...] = damping
     turning_ref[...] = columns_ref[...]
@@ -789,10 +791,10 @@
         )
 
     def frequency(j, which):
-        @pl.when(j >= 2)
+        @pl.when(j >= RINGS)
         def _():
             for piece in range(4):
-                send(j - 2, which, piece).wait()
+                send(j - RINGS, which, piece).wait()
 
         base = (member * freqs + j) * CLASSES * KINDS
         high = scalar_ref[base + 3]
@@ -833,17 +835,18 @@
         for group in range(GROUPS):
             turning_ref[group] = turned[group]
 
-    def pair(index, carry):
-        for which in range(2):
-            frequency(2 * index + which, which)
+    def turn(index, carry):
+        for which in range(RINGS):
+            frequency(RINGS * index + which, which)
         return carry
 
-    lax.fori_loop(0, freqs // 2, pair, 0)
-    if freqs % 2:
-        frequency(jnp.int32(freqs - 1), 0)
-    for j in range(max(0, freqs - 2), freqs):
+    whole_turns = freqs // RINGS
+    lax.fori_loop(0, whole_turns, turn, 0)
+    for j in range(whole_turns * RINGS, freqs):
+        frequency(jnp.int32(j), j % RINGS)
+    for j in range(max(0, freqs - RINGS), freqs):
         for piece in range(4):
-            send(j, j % 2, piece).wait()
+            send(j, j % RINGS, piece).wait()
 
 
 def swap(values, axis, first):
@@ -1007,22 +1010,23 @@
         a_sums, b_sums,
     )
 
-    sums, ratios = call(
+    stress, final, ratios = call(
         functools.partial(stress_kernel, freqs),
         [SMEM, SMEM] + [VMEM] * 5,
-        (in_any(3, rows, lanes), in_any(freqs, rows, lanes)),
-        (VMEM, VMEM),
+        (in_any(2, rows, lanes), in_any(rows, lanes), in_any(freqs, rows, lanes)),
+        (VMEM, VMEM, VMEM),
         flops=cells * freqs * 12,
         moved=cells * freqs * 8,
     )(member, scalars, wet, a_sums, b_sums, energy, energy_there)
-    sums, stress = call(
+    stress = call(
         total_kernel,
         [VMEM, VMEM],
-        (in_any(3, rows, lanes), in_any(2, rows, lanes)),
-        (VMEM, VMEM),
-        flops=cells * 3,
-        moved=cells * 44,
-    )(sums, others_sum(sums, "comp"))
+        in_any(2, rows, lanes),
+        VMEM,
+        flops=cells * 2,
+        moved=cells * 24,
+    )(stress, others_sum(stress, "comp"))
+    final_there = others_sum(final, "comp")
     beside, first, second = call(
         strip_kernel,
         [VMEM, VMEM, VMEM],
@@ -1035,7 +1039,7 @@
 
     result, level = call(
         functools.partial(final_kernel, freqs),
-        [SMEM, SMEM] + [VMEM] * 10,
+        [SMEM, SMEM] + [VMEM] * 12,
         (in_any(*block), in_any(rows, lanes)),
         (HBM, VMEM),
         flops=local_comp * cells * 6,
@@ -1043,12 +1047,12 @@
         scratch=[
             pltpu.VMEM((rows, lanes), jnp.float32),
             pltpu.VMEM((GROUPS, rows, lanes), jnp.float32),
-            pltpu.VMEM((ND, rows, lanes), jnp.float32),
-            pltpu.VMEM((ND, rows, lanes), jnp.float32),
-            pltpu.SemaphoreType.DMA((2, 4)),
-        ],
+            pltpu.SemaphoreType.DMA((RINGS, 4)),
+        ]
+        + [pltpu.VMEM((ND, rows, lanes), jnp.float32)] * RINGS,
+        limit=12,
     )(
-        member, scalars, depth, ratios, sums, beside, aside, beyond, growth, kept,
+        member, scalars, depth, ratios, stress, final, final_there, beside, aside, beyond, growth, kept,
         columns, edges,
     )
     return result.reshape(local_comp, rows, lanes), level

time: 76.9 us -> 74.3 us (0.966)
  Pallas kernels: 49.2 us -> 46.9 us
  waiting for transfers between devices: 11 us -> 8.94 us
  starting transfers between devices: 15.6 us -> 17.3 us
    pallas_call x2, Pallas kernels: 14.9 us -> 12.2 us  [the longest x1 12.2 us: resident(): call(functools.partial(final_kernel, freqs), [SMEM, SMEM] + [VMEM] * 12,...]
    ppermute x2 -> x3, starting transfers between devices: 3.11 us -> 4.79 us  [others_sum(): lax.ppermute(values, axis, [(i, (i + step) % count) for i in range(count)])]
    ppermute x8, waiting for transfers between devices: 6.85 us -> 5.24 us  [swap(): return lax.ppermute(values, axis, pairs + [(b, a) for a, b in pairs])]
    pallas_call x1, Pallas kernels: 9.98 us -> 10.8 us  [resident(): call(functools.partial(pack_kernel, freqs), [SMEM] + [HBM] * 7, (in_any(N...]
    ppermute x2 -> x3, waiting for transfers between devices: 4.12 us -> 3.7 us  [others_sum(): lax.ppermute(values, axis, [(i, (i + step) % count) for i in range(count)])]
  transfers between devices with their start and end apart: 10 -> 11, of which waited for: 4 -> 4; matrix products, arithmetic and copies ran while one was open for 0% -> 0% of each run, Pallas kernels for 29% -> 29%
where the time goes in v7:
time: 74.3 us; the launch traced here: 74.1 us
  Pallas kernels  46.9 us (63%)
  starting transfers between devices  17.3 us (23%)
  waiting for transfers between devices  8.94 us (12%)
  between operations  0.88 us (1%)
    pallas_call x2, Pallas kernels, main_part(): call(functools.partial(main_kernel, freqs, start, stop), [SMEM, SMEM, VME...  20.3 us
    ppermute x8, starting transfers between devices, swap(): return lax.ppermute(values, axis, pairs + [(b, a) for a, b in pairs])  12.5 us
    pallas_call x1, Pallas kernels, resident(): call(functools.partial(final_kernel, freqs), [SMEM, SMEM] + [VMEM] * 12,...  12.2 us
    pallas_call x1, Pallas kernels, resident(): call(functools.partial(pack_kernel, freqs), [SMEM] + [HBM] * 7, (in_any(N...  10.8 us
    ppermute x8, waiting for transfers between devices, swap(): return lax.ppermute(values, axis, pairs + [(b, a) for a, b in pairs])  5.24 us
    ppermute x3, starting transfers between devices, others_sum(): lax.ppermute(values, axis, [(i, (i + step) % count) for i in range(count)])  4.79 us
    ppermute x3, waiting for transfers between devices, others_sum(): lax.ppermute(values, axis, [(i, (i + step) % count) for i in range(count)])  3.7 us
  transfers between devices with their start and end apart: 11, of which 4 were waited for; matrix products, arithmetic and copies ran while one was open for 0% of the time, Pallas kernels for 29%

profile of v7, /device:TPU:12, one launch (start us, length us, event | category | flops | bytes accessed | tf_op | source)
XLA Modules:
  0.0 74.1 jit_solution(2754254316717886617)
XLA Ops:
  0.6 0.0 copy-start.5
  0.6 10.8 %shard_map.104 = (f32[36,64,128]{2,1,0:T(8,128)S(1)}, f32[64,128]{1,0:T(8,128)S(1)}, f32[6,64,128]{2,1,0:T(8,128)S(1)}, f32[6,64,128]{2,1,0:T(8,128)S(1)}, f32[6...) custom-call(s32[1]{0:T(128)} %bitcast.member_ref, ...), custom_call_target="tpu_custom_call" | custom-call | flops 21233664 | bytes 21233664 | tf_op jit(solution)/shard_map/pallas_call | solution.py:910
  11.5 0.1 collective-permute-start
  11.6 2.5 %collective-permute-start.1 = (f32[6,64,128]{2,1,0:T(8,128)S(1)}, f32[6,64,128]{2,1,0:T(8,128)S(1)}, u32[]{:S(2)}, u32[]{:S(2)}) collective-permute-start(f32[6,64,128]{2,1,0:T(8,128)S(1)} %get-tuple-element.35), channel_id=1, source_target_pairs={{4,8},{8,4},{5,9},{9,5},{6,10},{10,6},{7,11},{11,7},{20,24},{24,20... | collective-permute-start | bytes 589832 | tf_op jit(solution)/shard_map/ppermute | solution.py:855
  14.1 0.0 copy-done.5
  14.1 7.4 %shard_map.105 = (f32[18,36,64,128]{3,2,1,0:T(8,128)S(1)}, f32[1152,128]{1,0:T(8,128)S(1)}, f32[1152,128]{1,0:T(8,128)S(1)}, f32[64,128]{1,0:T(8,128)S(1)}) custom-call(s32[1]{0:T(128)} %bitcast.member_ref, f32[1800]{0:T(1024)S(1)} %copy-done.5, f32[64,128]{1,0:T(8,128)S(1)} %get-tuple-element.32.wet_ref, f32[36,64,128]{2,1,0:T(8,128)S(1)} %get-tuple-element.33.growth_ref, ...), custom_call_target="tpu_custom_call" | custom-call | flops 28311552 | bytes 14155776 | tf_op jit(solution)/shard_map/pallas_call | solution.py:945
  21.5 0.0 collective-permute-done.swapped_ref.swap_side_ref
  21.5 0.0 collective-permute-done.1.other_ref.other_side_ref
  21.5 0.1 shard_map.106
  21.6 3.5 %collective-permute-start.3 = (f32[656,128]{1,0:T(8,128)S(1)}, f32[656,128]{1,0:T(8,128)S(1)}, u32[]{:S(2)}, u32[]{:S(2)}) collective-permute-start(f32[656,128]{1,0:T(8,128)S(1)} %get-tuple-element.40), channel_id=1, source_target_pairs={{1,2},{2,1},{5,6},{6,5},{9,10},{10,9},{13,14},{14,13},{17,18},{18,... | collective-permute-start | bytes 1007624 | tf_op jit(solution)/shard_map/ppermute | solution.py:855
  25.1 0.1 collective-permute-start.2
  25.2 0.0 copy-start
  25.2 0.0 copy-start.1
  25.2 0.0 copy-start.2
  25.3 0.0 copy-start.3
  25.3 0.0 copy-start.4
  25.3 0.0 copy-start.6
  25.3 12.9 %shard_map.107 = (f32[18,36,64,128]{3,2,1,0:T(8,128)S(1)}, f32[1152,128]{1,0:T(8,128)S(1)}, f32[1152,128]{1,0:T(8,128)S(1)}, f32[64,128]{1,0:T(8,128)S(1)}) custom-call(s32[1]{0:T(128)} %bitcast.member_ref, f32[1800]{0:T(1024)S(1)} %copy-done.5, ...), custom_call_target="tpu_custom_call", output_to_operand_aliasing={{0}: (6, {}), {1}: (7, {}), {2}: (8, {}), {3}: (9, {})} | custom-call | flops 56623104 | bytes 28311552 | tf_op jit(solution)/shard_map/pallas_call | solution.py:945
  38.2 0.0 collective-permute-done.3.other_row_ref
  38.2 0.0 collective-permute-done.2.swap_row_ref
  38.2 0.0 copy-done
  38.2 0.0 copy-done.1
  38.2 1.1 %shard_map.108 = (f32[12,64,128]{2,1,0:T(8,128)S(1)}, f32[5184,128]{1,0:T(8,128)S(1)}, f32[64,128]{1,0:T(8,128)S(1)}) custom-call(s32[1]{0:T(128)} %bitcast.member_ref, f32[2,12,8,128]{3,2,1,0:T(8,128)S(1)} %copy-done.1, f32[2,10,5,18,128]{4,3,2,1,0:T(8,128)S(1)} %copy-done, ...), custom_call_target="tpu_custom_call", output_to_operand_aliasing={{1}: (8, {}), {2}: (9, {})} | custom-call | flops 4915200 | bytes 1638400 | tf_op jit(solution)/shard_map/pallas_call | solution.py:983
  39.3 1.6 %collective-permute-start.4 = (f32[64,128]{1,0:T(8,128)S(1)}, f32[64,128]{1,0:T(8,128)S(1)}, u32[]{:S(2)}, u32[]{:S(2)}) collective-permute-start(f32[64,128]{1,0:T(8,128)S(1)} %get-tuple-element.52.own_ref), channel_id=1, source_target_pairs={{0,16},{16,0},{1,17},{17,1},{2,18},{18,2},{3,19},{19,3},{4,20},{20... | collective-permute-start | bytes 98312 | tf_op jit(solution)/shard_map/ppermute | solution.py:862
  40.9 0.0 copy-done.2
  40.9 0.0 copy-done.3
  40.9 0.0 copy-done.4
  40.9 1.4 %shard_map.109 = (f32[1152,128]{1,0:T(8,128)S(1)}, f32[1152,128]{1,0:T(8,128)S(1)}) custom-call(s32[1]{0:T(128)} %bitcast.member_ref, f32[2,12,8,128]{3,2,1,0:T(8,128)S(1)} %copy-done.1, f32[2,10,5,18,128]{4,3,2,1,0:T(8,128)S(1)} %copy-done, s32[64,128]{1,0:T(8,128)S(1)} %copy-done.2, ...), custom_call_target="tpu_custom_call", output_to_operand_aliasing={{0}: (9, {}), {1}: (10, {})} | custom-call | flops 4915200 | bytes 1638400 | tf_op jit(solution)/shard_map/pallas_call | solution.py:1000
  42.3 1.0 %collective-permute-done.4.other_ref = f32[64,128]{1,0:T(8,128)S(1)} collective-permute-done((f32[64,128]{1,0:T(8,128)S(1)}, f32[64,128]{1,0:T(8,128)S(1)}, u32[]{:S(2)}, u32[]{:S(2)}) %collective-permute-start.4) | collective-permute-done | bytes 32800 | tf_op jit(solution)/shard_map/ppermute | solution.py:862
  43.3 1.0 %shard_map.110 = (f32[2,64,128]{2,1,0:T(8,128)S(1)}, f32[64,128]{1,0:T(8,128)S(1)}, f32[18,64,128]{2,1,0:T(8,128)S(1)}) custom-call(s32[1]{0:T(128)} %bitcast.member_ref, f32[1800]{0:T(1024)S(1)} %copy-done.5, f32[64,128]{1,0:T(8,128)S(1)} %get-tuple-element.32.wet_ref, f32[1152,128]{1,0:T(8,128)S(1)} %get-tuple-element.50.a_ref, ...), custom_call_target="tpu_custom_call" | custom-call | flops 1769472 | bytes 1179648 | tf_op jit(solution)/shard_map/pallas_call | solution.py:1013
  44.3 1.6 %collective-permute-start.5 = (f32[2,64,128]{2,1,0:T(8,128)S(1)}, f32[2,64,128]{2,1,0:T(8,128)S(1)}, u32[]{:S(2)}, u32[]{:S(2)}) collective-permute-start(f32[2,64,128]{2,1,0:T(8,128)S(1)} %get-tuple-element.54.own_ref), channel_id=1, source_target_pairs={{0,16},{16,0},{1,17},{17,1},{2,18},{18,2},{3,19},{19,3},{4,20},{20... | collective-permute-start | bytes 196616 | tf_op jit(solution)/shard_map/ppermute | solution.py:862
  45.9 2.7 %collective-permute-done.5.other_ref = f32[2,64,128]{2,1,0:T(8,128)S(1)} collective-permute-done((f32[2,64,128]{2,1,0:T(8,128)S(1)}, f32[2,64,128]{2,1,0:T(8,128)S(1)}, u32[]{:S(2)}, u32[]{:S(2)}) %collective-permute-start.5) | collective-permute-done | bytes 65568 | tf_op jit(solution)/shard_map/ppermute | solution.py:862
  48.6 1.9 %collective-permute-start.8 = (f32[2,64,128]{2,1,0:T(8,128)S(1)}, f32[2,64,128]{2,1,0:T(8,128)S(1)}, u32[]{:S(2)}, u32[]{:S(2)}) collective-permute-start(f32[2,64,128]{2,1,0:T(8,128)S(1)} %shard_map.111.stress_ref.sums_ref), channel_id=1, source_target_pairs={{4,8},{8,4},{5,9},{9,5},{6,10},{10,6},{7,11},{11,7},{20,24},{24,20... | collective-permute-start | bytes 196616 | tf_op jit(solution)/shard_map/ppermute | solution.py:855
  50.5 0.1 collective-permute-start.7
  50.6 1.6 %collective-permute-start.6 = (f32[64,128]{1,0:T(8,128)S(1)}, f32[64,128]{1,0:T(8,128)S(1)}, u32[]{:S(2)}, u32[]{:S(2)}) collective-permute-start(f32[64,128]{1,0:T(8,128)S(1)} %get-tuple-element.55.own_ref), channel_id=1, source_target_pairs={{0,16},{16,0},{1,17},{17,1},{2,18},{18,2},{3,19},{19,3},{4,20},{20... | collective-permute-start | bytes 98312 | tf_op jit(solution)/shard_map/ppermute | solution.py:862
  52.2 2.0 %collective-permute-done.8.other_ref = f32[2,64,128]{2,1,0:T(8,128)S(1)} collective-permute-done((f32[2,64,128]{2,1,0:T(8,128)S(1)}, f32[2,64,128]{2,1,0:T(8,128)S(1)}, u32[]{:S(2)}, u32[]{:S(2)}) %collective-permute-start.8) | collective-permute-done | bytes 65568 | tf_op jit(solution)/shard_map/ppermute | solution.py:855
  54.2 0.0 collective-permute-done.7.swapped_ref
  54.2 2.0 %collective-permute-start.9 = (f32[2,8,256]{2,1,0:T(8,128)S(1)}, f32[2,8,256]{2,1,0:T(8,128)S(1)}, u32[]{:S(2)}, u32[]{:S(2)}) collective-permute-start(f32[2,8,256]{2,1,0:T(8,128)S(1)} %get-tuple-element.57), channel_id=1, source_target_pairs={{0,1},{2,3},{1,0},{3,2},{4,5},{6,7},{5,4},{7,6},{8,9},{10,11},{9,8... | collective-permute-start | bytes 49160 | tf_op jit(solution)/shard_map/ppermute | solution.py:855
  56.3 2.3 %collective-permute-start.10 = (f32[2,8,256]{2,1,0:T(8,128)S(1)}, f32[2,8,256]{2,1,0:T(8,128)S(1)}, u32[]{:S(2)}, u32[]{:S(2)}) collective-permute-start(f32[2,8,256]{2,1,0:T(8,128)S(1)} %get-tuple-element.58), channel_id=1, source_target_pairs={{1,2},{2,1},{5,6},{6,5},{9,10},{10,9},{13,14},{14,13},{17,18},{18,... | collective-permute-start | bytes 49160 | tf_op jit(solution)/shard_map/ppermute | solution.py:855
  58.6 0.0 collective-permute-done.6.there_ref
  58.6 0.0 collective-permute-done.9.swapped_ref
  58.6 3.2 %collective-permute-done.10.other_ref = f32[2,8,256]{2,1,0:T(8,128)S(1)} collective-permute-done((f32[2,8,256]{2,1,0:T(8,128)S(1)}, f32[2,8,256]{2,1,0:T(8,128)S(1)}, u32[]{:S(2)}, u32[]{:S(2)}) %collective-permute-start.10) | collective-permute-done | bytes 16416 | tf_op jit(solution)/shard_map/ppermute | solution.py:855
  61.9 0.0 copy-done.6
  61.9 12.2 %shard_map.113 = (f32[18,36,64,128]{3,2,1,0:T(8,128)}, f32[64,128]{1,0:T(8,128)}) custom-call(s32[1]{0:T(128)} %bitcast.member_ref, f32[1800]{0:T(1024)S(1)} %copy-done.5, f32[64,128]{1,0:T(8,128)S(1)} %copy-done.6, f32[18,64,128]{2,1,0:T(8,128)S(1)} %get-tuple-element.53.ratios_ref, f32[2,64,128]{2,1,0:T(8,128)S(1)} %shard_map.111.stress_ref.sums_ref, ...), custom_call_target="tpu_custom_call" | custom-call | flops 31850496 | bytes 42467328 | tf_op jit(solution)/shard_map/pallas_call | solution.py:1040
  (2 shorter events, 0.0 us)
Async XLA Ops:
  0.6 13.5 %copy-start.5 = (f32[1800]{0:T(1024)S(1)}, f32[1800]{0:T(1024)}, u32[]{:S(2)}) copy-start(f32[1800]{0:T(1024)} %constant.12.clone.scalar_ref) | copy-start | bytes 21604
  11.5 10.0 %collective-permute-start = (f32[6,64,128]{2,1,0:T(8,128)S(1)}, f32[6,64,128]{2,1,0:T(8,128)S(1)}, u32[]{:S(2)}, u32[]{:S(2)}) collective-permute-start(f32[6,64,128]{2,1,0:T(8,128)S(1)} %get-tuple-element.34), channel_id=1, source_target_pairs={{0,4},{8,12},{4,0},{12,8},{1,5},{9,13},{5,1},{13,9},{2,6},{10,14},... | collective-permute-start | bytes 589832 | tf_op jit(solution)/shard_map/ppermute | solution.py:855
  11.6 9.9 %collective-permute-start.1 = (f32[6,64,128]{2,1,0:T(8,128)S(1)}, f32[6,64,128]{2,1,0:T(8,128)S(1)}, u32[]{:S(2)}, u32[]{:S(2)}) collective-permute-start(f32[6,64,128]{2,1,0:T(8,128)S(1)} %get-tuple-element.35), channel_id=1, source_target_pairs={{4,8},{8,4},{5,9},{9,5},{6,10},{10,6},{7,11},{11,7},{20,24},{24,20... | collective-permute-start | bytes 589832 | tf_op jit(solution)/shard_map/ppermute | solution.py:855
  21.6 16.5 %collective-permute-start.3 = (f32[656,128]{1,0:T(8,128)S(1)}, f32[656,128]{1,0:T(8,128)S(1)}, u32[]{:S(2)}, u32[]{:S(2)}) collective-permute-start(f32[656,128]{1,0:T(8,128)S(1)} %get-tuple-element.40), channel_id=1, source_target_pairs={{1,2},{2,1},{5,6},{6,5},{9,10},{10,9},{13,14},{14,13},{17,18},{18,... | collective-permute-start | bytes 1007624 | tf_op jit(solution)/shard_map/ppermute | solution.py:855
  25.1 13.0 %collective-permute-start.2 = (f32[656,128]{1,0:T(8,128)S(1)}, f32[656,128]{1,0:T(8,128)S(1)}, u32[]{:S(2)}, u32[]{:S(2)}) collective-permute-start(f32[656,128]{1,0:T(8,128)S(1)} %get-tuple-element.39.refs_0_), channel_id=1, source_target_pairs={{0,1},{2,3},{1,0},{3,2},{4,5},{6,7},{5,4},{7,6},{8,9},{10,11},{9,8... | collective-permute-start | bytes 1007624 | tf_op jit(solution)/shard_map/ppermute | solution.py:855
  25.2 13.0 %copy-start = (f32[2,10,5,18,128]{4,3,2,1,0:T(8,128)S(1)}, f32[2,10,5,18,128]{4,3,2,1,0:T(8,128)}, u32[]{:S(2)}) copy-start(f32[2,10,5,18,128]{4,3,2,1,0:T(8,128)} %constant.14.clone.table_hbm.table_ref) | copy-start | bytes 2764804
  25.2 13.0 %copy-start.1 = (f32[2,12,8,128]{3,2,1,0:T(8,128)S(1)}, f32[2,12,8,128]{3,2,1,0:T(8,128)}, u32[]{:S(2)}) copy-start(f32[2,12,8,128]{3,2,1,0:T(8,128)} %constant.13.clone.lanes_hbm.lanes_ref) | copy-start | bytes 294916
  25.2 15.7 %copy-start.2 = (s32[64,128]{1,0:T(8,128)S(1)}, s32[64,128]{1,0:T(8,128)}, u32[]{:S(2)}) copy-start(s32[64,128]{1,0:T(8,128)} %ice_ref.1) | copy-start | bytes 98308
  25.3 15.7 %copy-start.3 = (f32[64,128]{1,0:T(8,128)S(1)}, f32[64,128]{1,0:T(8,128)}, u32[]{:S(2)}) copy-start(f32[64,128]{1,0:T(8,128)} %east_ref.1) | copy-start | bytes 98308
  25.3 15.6 %copy-start.4 = (f32[64,128]{1,0:T(8,128)S(1)}, f32[64,128]{1,0:T(8,128)}, u32[]{:S(2)}) copy-start(f32[64,128]{1,0:T(8,128)} %north_ref.1) | copy-start | bytes 98308
  25.3 36.6 %copy-start.6 = (f32[64,128]{1,0:T(8,128)S(1)}, f32[64,128]{1,0:T(8,128)}, u32[]{:S(2)}) copy-start(f32[64,128]{1,0:T(8,128)} %depth_ref.1) | copy-start | bytes 98308
  39.3 4.0 %collective-permute-start.4 = (f32[64,128]{1,0:T(8,128)S(1)}, f32[64,128]{1,0:T(8,128)S(1)}, u32[]{:S(2)}, u32[]{:S(2)}) collective-permute-start(f32[64,128]{1,0:T(8,128)S(1)} %get-tuple-element.52.own_ref), channel_id=1, source_target_pairs={{0,16},{16,0},{1,17},{17,1},{2,18},{18,2},{3,19},{19,3},{4,20},{20... | collective-permute-start | bytes 98312 | tf_op jit(solution)/shard_map/ppermute | solution.py:862
  44.3 4.3 %collective-permute-start.5 = (f32[2,64,128]{2,1,0:T(8,128)S(1)}, f32[2,64,128]{2,1,0:T(8,128)S(1)}, u32[]{:S(2)}, u32[]{:S(2)}) collective-permute-start(f32[2,64,128]{2,1,0:T(8,128)S(1)} %get-tuple-element.54.own_ref), channel_id=1, source_target_pairs={{0,16},{16,0},{1,17},{17,1},{2,18},{18,2},{3,19},{19,3},{4,20},{20... | collective-permute-start | bytes 196616 | tf_op jit(solution)/shard_map/ppermute | solution.py:862
  48.6 5.6 %collective-permute-start.8 = (f32[2,64,128]{2,1,0:T(8,128)S(1)}, f32[2,64,128]{2,1,0:T(8,128)S(1)}, u32[]{:S(2)}, u32[]{:S(2)}) collective-permute-start(f32[2,64,128]{2,1,0:T(8,128)S(1)} %shard_map.111.stress_ref.sums_ref), channel_id=1, source_target_pairs={{4,8},{8,4},{5,9},{9,5},{6,10},{10,6},{7,11},{11,7},{20,24},{24,20... | collective-permute-start | bytes 196616 | tf_op jit(solution)/shard_map/ppermute | solution.py:855
  50.5 3.7 %collective-permute-start.7 = (f32[2,64,128]{2,1,0:T(8,128)S(1)}, f32[2,64,128]{2,1,0:T(8,128)S(1)}, u32[]{:S(2)}, u32[]{:S(2)}) collective-permute-start(f32[2,64,128]{2,1,0:T(8,128)S(1)} %shard_map.111.stress_ref.sums_ref), channel_id=1, source_target_pairs={{0,4},{8,12},{4,0},{12,8},{1,5},{9,13},{5,1},{13,9},{2,6},{10,14},... | collective-permute-start | bytes 196616 | tf_op jit(solution)/shard_map/ppermute | solution.py:855
  50.6 8.0 %collective-permute-start.6 = (f32[64,128]{1,0:T(8,128)S(1)}, f32[64,128]{1,0:T(8,128)S(1)}, u32[]{:S(2)}, u32[]{:S(2)}) collective-permute-start(f32[64,128]{1,0:T(8,128)S(1)} %get-tuple-element.55.own_ref), channel_id=1, source_target_pairs={{0,16},{16,0},{1,17},{17,1},{2,18},{18,2},{3,19},{19,3},{4,20},{20... | collective-permute-start | bytes 98312 | tf_op jit(solution)/shard_map/ppermute | solution.py:862
  54.2 4.4 %collective-permute-start.9 = (f32[2,8,256]{2,1,0:T(8,128)S(1)}, f32[2,8,256]{2,1,0:T(8,128)S(1)}, u32[]{:S(2)}, u32[]{:S(2)}) collective-permute-start(f32[2,8,256]{2,1,0:T(8,128)S(1)} %get-tuple-element.57), channel_id=1, source_target_pairs={{0,1},{2,3},{1,0},{3,2},{4,5},{6,7},{5,4},{7,6},{8,9},{10,11},{9,8... | collective-permute-start | bytes 49160 | tf_op jit(solution)/shard_map/ppermute | solution.py:855
  56.3 5.6 %collective-permute-start.10 = (f32[2,8,256]{2,1,0:T(8,128)S(1)}, f32[2,8,256]{2,1,0:T(8,128)S(1)}, u32[]{:S(2)}, u32[]{:S(2)}) collective-permute-start(f32[2,8,256]{2,1,0:T(8,128)S(1)} %get-tuple-element.58), channel_id=1, source_target_pairs={{1,2},{2,1},{5,6},{6,5},{9,10},{10,9},{13,14},{14,13},{17,18},{18,... | collective-permute-start | bytes 49160 | tf_op jit(solution)/shard_map/ppermute | solution.py:855

commit v8 on v6

--- a/solution.py
+++ b/solution.py
@@ -253,7 +253,7 @@
     return jnp.where(iota(values.shape, 1) == edge, 0.0, moved)
 
 
-DEPTH = 3
+DEPTH = 2
 
 
 def sides(quadrant):
@@ -262,8 +262,8 @@
 
 def pack_kernel(
     freqs, member_ref, lanes_hbm, table_hbm, land_hbm, ice_hbm, east_hbm, north_hbm, spectrum_ref,
-    growth_ref, wet_ref, swap_side_ref, other_side_ref, swap_row_ref, other_row_ref, edges_ref,
-    kept_ref, right_ref, left_ref, lanes_ref, table_ref, land_ref, ice_ref, east_ref, north_ref, small_sems, sems,
+    kept_ref, growth_ref, wet_ref, swap_side_ref, other_side_ref, swap_row_ref, other_row_ref,
+    edges_ref, ring_ref, right_ref, left_ref, lanes_ref, table_ref, land_ref, ice_ref, east_ref, north_ref, small_sems, sems,
 ):
     member = member_ref[0]
     small = [
@@ -283,14 +283,15 @@
         copy.start()
 
     rows = land_ref.shape[0]
-    blocks_ref = kept_ref.reshape(freqs, ND, rows, LANES)
+    flat_ref = kept_ref.reshape(freqs * ND * rows, LANES)
 
     def fetch(group):
+        slot = lax.rem(group, DEPTH + 1)
         part = (slice(None), pl.ds(group * GROUP, GROUP))
-        return pltpu.make_async_copy(spectrum_ref.at[part], blocks_ref.at[part], sems.at[group])
+        return pltpu.make_async_copy(spectrum_ref.at[part], ring_ref.at[slot], sems.at[slot])
 
     for group in range(DEPTH):
-        fetch(group).start()
+        fetch(jnp.int32(group)).start()
     edges_ref[...] = jnp.zeros_like(edges_ref)
     for copy in small:
         copy.wait()
@@ -325,7 +326,16 @@
             def _():
                 fetch(group + DEPTH).start()
 
+            slot = lax.rem(group, DEPTH + 1)
             packed = [jnp.zeros((SUB, LANES), jnp.float32) for _ in range(tiles)]
+            wet = [wet_ref[tile * SUB : (tile + 1) * SUB, :] for tile in range(tiles)]
+            pending = []
+
+            def put(count):
+                while len(pending) > count:
+                    at, cells = pending.pop(0)
+                    flat_ref[pl.ds(at, SUB), :] = cells
+
             for i in range(GROUP):
                 for j in range(freqs):
                     place = i * 2 * freqs + 2 * j
@@ -333,8 +343,11 @@
                     turn = (place + 2 if to_right else place) % LANES
                     first = pl.multiple_of((j * ND + group * GROUP + i) * rows, SUB)
                     for tile in range(tiles):
-                        cells = kept_ref[pl.ds(first + tile * SUB, SUB), :]
+                        cells = ring_ref[slot, j, i, tile * SUB : (tile + 1) * SUB, :] * wet[tile]
                         packed[tile] = jnp.where(here, pltpu.roll(cells, turn, 1), packed[tile])
+                        pending.append((first + tile * SUB, cells))
+                    put(2 * tiles)
+            put(0)
             for tile in range(tiles):
                 target_ref[index, tile * SUB : (tile + 1) * SUB, :] = packed[tile]
             return carry
@@ -343,11 +356,9 @@
 
     def side_message(group):
         to_right, fore = group < half, 1 if heads_down(group * GROUP) else -1
-        ahead, behind = (LANES - 1, LANES - 2) if to_right else (0, 1)
-        wet_near, wet_far = spread(wet_cells, ahead), spread(wet_cells, behind)
+        wet_near = spread(wet_cells, LANES - 1 if to_right else 0)
         near_even = not to_right
-        packed = right_ref[group] if to_right else left_ref[group - half]
-        values = packed * jnp.where(even == near_even, wet_near, wet_far)
+        values = right_ref[group] if to_right else left_ref[group - half]
         near = pltpu.roll(values, 1 if near_even else LANES - 1, 1)
         table = lanes_ref[group]
         follow = wet_near * (table[1:2] * values + table[2:3] * shift_rows(near, fore))
@@ -358,10 +369,9 @@
         to_down = heads_down(direction)
         near_row, far_row = (rows - 1, rows - 2) if to_down else (0, 1)
         wet_near = wet_cells[near_row : near_row + 1, :]
-        wet_far = wet_cells[far_row : far_row + 1, :]
         table = table_ref.at[class_of(direction)]
-        near = kept_ref[pl.ds(direction * rows + near_row, freqs, stride=ND * rows), :] * wet_near
-        far = kept_ref[pl.ds(direction * rows + far_row, freqs, stride=ND * rows), :] * wet_far
+        near = flat_ref[pl.ds(direction * rows + near_row, freqs, stride=ND * rows), :]
+        far = flat_ref[pl.ds(direction * rows + far_row, freqs, stride=ND * rows), :]
         beside = shift_lanes(near, 1 if heads_right(direction) else -1)
         return near, wet_near * (table[1] * far + table[2] * beside)
 
@@ -424,10 +434,10 @@
 
 
 def main_kernel(
-    freqs, start, stop, member_ref, scalar_ref, wet_ref, growth_ref, spectrum_ref, *refs
+    freqs, start, stop, member_ref, scalar_ref, wet_ref, growth_ref, masked_ref, *refs
 ):
     if start:
-        _after, _kept_in, a_in, b_in, energy_in, *refs = refs
+        _after, a_in, b_in, energy_in, *refs = refs
     kept_ref, a_ref, b_ref, energy_ref, ring_ref, sems, *first_refs = refs
     member = member_ref[0]
     nought = jnp.minimum(member, 0)
@@ -436,7 +446,7 @@
 
     def fetch(j):
         slot = lax.rem(j, AHEAD)
-        return pltpu.make_async_copy(spectrum_ref.at[j], ring_ref.at[slot], sems.at[slot])
+        return pltpu.make_async_copy(masked_ref.at[j], ring_ref.at[slot], sems.at[slot])
 
     for j in range(start, min(start + AHEAD, stop)):
         fetch(jnp.int32(j)).start()
@@ -483,12 +493,13 @@
                 shift = row_shift(quadrant)
                 edge = top if shift < 0 else bottom
                 target = first_refs[kind % 2 * 4 + quadrant]
-                cells = [ring_ref[slot, direction, tile_at(t), :] * wet[t] for t in range(tiles)]
-                turned = [pltpu.roll(cells[t], -shift % SUB, 0) for t in range(tiles)]
                 for t in range(tiles):
-                    before = turned[t + shift] if 0 <= t + shift < tiles else 0.0
-                    ahead = jnp.where(edge, before, turned[t])
-                    after = cells[t] + alpha * ahead + across * beside(cells[t], quadrant)
+                    cells = ring_ref[slot, direction, tile_at(t), :]
+                    if 0 <= t * SUB + shift <= rows - SUB:
+                        ahead = ring_ref[slot, direction, pl.ds(t * SUB + shift + nought, SUB), :]
+                    else:
+                        ahead = jnp.where(edge, 0.0, pltpu.roll(cells, -shift % SUB, 0))
+                    after = cells + alpha * ahead + across * beside(cells, quadrant)
                     target[tile_at(t + 1), :] = wet[t] * after
 
         def second_step(kind):
@@ -732,15 +743,15 @@
 
 
 BEHIND = 12
+RINGS = 6
 
 
 def final_kernel(
     freqs, member_ref, scalar_ref, depth_ref, ratios_ref, sums_ref, beside_ref, swapped_ref,
     other_ref, growth_ref, kept_ref, columns_ref, edges_ref,
-    result_ref, level_ref, damping_ref, turning_ref, ring0, ring1, sems,
+    result_ref, level_ref, damping_ref, turning_ref, sems, *rings,
 ):
     member = member_ref[0]
-    rings = (ring0, ring1)
     rows = depth_ref.shape[0]
     slab, slabs = lax.axis_index("slab"), lax.axis_size("slab")
     sect, sects = lax.axis_index("sect"), lax.axis_size("sect")
@@ -789,10 +800,10 @@
         )
 
     def frequency(j, which):
-        @pl.when(j >= 2)
+        @pl.when(j >= RINGS)
         def _():
             for piece in range(4):
-                send(j - 2, which, piece).wait()
+                send(j - RINGS, which, piece).wait()
 
         base = (member * freqs + j) * CLASSES * KINDS
         high = scalar_ref[base + 3]
@@ -833,17 +844,18 @@
         for group in range(GROUPS):
             turning_ref[group] = turned[group]
 
-    def pair(index, carry):
-        for which in range(2):
-            frequency(2 * index + which, which)
+    def turn(index, carry):
+        for which in range(RINGS):
+            frequency(RINGS * index + which, which)
         return carry
 
-    lax.fori_loop(0, freqs // 2, pair, 0)
-    if freqs % 2:
-        frequency(jnp.int32(freqs - 1), 0)
-    for j in range(max(0, freqs - 2), freqs):
+    whole_turns = freqs // RINGS
+    lax.fori_loop(0, whole_turns, turn, 0)
+    for j in range(whole_turns * RINGS, freqs):
+        frequency(jnp.int32(j), j % RINGS)
+    for j in range(max(0, freqs - RINGS), freqs):
         for piece in range(4):
-            send(j, j % 2, piece).wait()
+            send(j, j % RINGS, piece).wait()
 
 
 def swap(values, axis, first):
@@ -904,10 +916,11 @@
     block = (freqs, ND, rows, lanes)
     spectrum = spectrum.reshape(block)
 
-    growth, wet, swap_side, other_side, swap_row, other_row, edges = call(
+    kept, growth, wet, swap_side, other_side, swap_row, other_row, edges = call(
         functools.partial(pack_kernel, freqs),
         [SMEM] + [HBM] * 7,
         (
+            in_vmem(*block),
             in_any(ND, rows, lanes),
             in_any(rows, lanes),
             in_any(GROUPS // 2, rows, lanes),
@@ -916,11 +929,11 @@
             in_any(row_message, lanes),
             in_any(2 * 18 * freqs * SUB, lanes),
         ),
-        (VMEM,) * 7,
+        (VMEM,) * 8,
         flops=local_comp * cells * 4,
         moved=local_comp * cells * 4,
         scratch=[
-            pltpu.VMEM((local_comp * rows, lanes), jnp.float32),
+            pltpu.VMEM((DEPTH + 1, freqs, GROUP, rows, lanes), jnp.float32),
             pltpu.VMEM((GROUPS // 2, rows, lanes), jnp.float32),
             pltpu.VMEM((GROUPS // 2, rows, lanes), jnp.float32),
             pltpu.VMEM(lane_table.shape[1:], jnp.float32),
@@ -930,18 +943,18 @@
             pltpu.VMEM((rows, lanes), jnp.float32),
             pltpu.VMEM((rows, lanes), jnp.float32),
             pltpu.SemaphoreType.DMA((6,)),
-            pltpu.SemaphoreType.DMA((GROUPS,)),
+            pltpu.SemaphoreType.DMA((DEPTH + 1,)),
         ],
-        limit=30,
+        limit=10,
     )(
         member,
         *map(in_hbm, (lane_table, row_table, land_mask, ice_mask, wind_u, wind_v, spectrum)),
     )
 
-    def main_part(start, stop, *before):
+    def main_part(start, stop, masked, *before):
         return call(
             functools.partial(main_kernel, freqs, start, stop),
-            [SMEM, SMEM, VMEM, VMEM, HBM] + ([ANY, VMEM, VMEM, VMEM, VMEM] if before else []),
+            [SMEM, SMEM, VMEM, VMEM, ANY] + ([ANY, VMEM, VMEM, VMEM] if before else []),
             (
                 in_vmem(*block),
                 in_any(freqs * rows, lanes),
@@ -956,13 +969,13 @@
                 pltpu.SemaphoreType.DMA((AHEAD,)),
             ]
             + [pltpu.VMEM((rows + 2 * SUB, lanes), jnp.float32)] * 8,
-            aliases={6 + index: index for index in range(4)} if before else {},
+            aliases={4: 0, **({6 + index: 1 + index for index in range(3)} if before else {})},
             limit=8,
-        )(member, scalars, wet, growth, in_hbm(spectrum), *before)
+        )(member, scalars, wet, growth, masked, *before)
 
     early = max(1, freqs // 3)
     swap_side, other_side = swap(swap_side, "sect", 0), swap(other_side, "sect", 1)
-    kept, *partial = main_part(0, early)
+    kept, *partial = main_part(0, early, kept)
     swap_row, other_row = call(
         functools.partial(corner_kernel, freqs),
         [VMEM, VMEM, VMEM, ANY, ANY, ANY],
@@ -975,7 +988,7 @@
     )(wet, swap_side, other_side, swap_row, other_row, partial[-1])
     swapped_row = swap(swap_row, "slab", 0)
     other_row = swap(other_row, "slab", 1)
-    kept, a_sums, b_sums, energy = main_part(early, freqs, swap_row, kept, *partial)
+    kept, a_sums, b_sums, energy = main_part(early, freqs, kept, swap_row, *partial)
 
     columns, edges, energy = call(
         functools.partial(enter_kernel, freqs),
@@ -1043,10 +1056,10 @@
         scratch=[
             pltpu.VMEM((rows, lanes), jnp.float32),
             pltpu.VMEM((GROUPS, rows, lanes), jnp.float32),
-            pltpu.VMEM((ND, rows, lanes), jnp.float32),
-            pltpu.VMEM((ND, rows, lanes), jnp.float32),
-            pltpu.SemaphoreType.DMA((2, 4)),
-        ],
+            pltpu.SemaphoreType.DMA((RINGS, 4)),
+        ]
+        + [pltpu.VMEM((ND, rows, lanes), jnp.float32)] * RINGS,
+        limit=12,
     )(
         member, scalars, depth, ratios, sums, beside, aside, beyond, growth, kept,
         columns, edges,

time: 76.9 us -> 76.2 us (level)
  Pallas kernels: 49.2 us -> 48.3 us
    pallas_call x1, Pallas kernels: 14.8 us -> 12.2 us  [resident(): call(functools.partial(final_kernel, freqs), [SMEM, SMEM] + [VMEM] * 10,...]
    pallas_call x1, Pallas kernels: 9.98 us -> 11.5 us  [resident(): call(functools.partial(pack_kernel, freqs), [SMEM] + [HBM] * 7, (in_vmem(...]
  transfers between devices with their start and end apart: 10 -> 10, of which waited for: 4 -> 4; matrix products, arithmetic and copies ran while one was open for 0% -> 0% of each run, Pallas kernels for 29% -> 30%
where the time goes in v8:
time: 76.2 us; the launch traced here: 75.9 us
  Pallas kernels  48.3 us (63%)
  starting transfers between devices  15.7 us (21%)
  waiting for transfers between devices  11 us (14%)
  between operations  0.87 us (1%)
    pallas_call x2, Pallas kernels, main_part(): call(functools.partial(main_kernel, freqs, start, stop), [SMEM, SMEM, VME...  21 us
    ppermute x8, starting transfers between devices, swap(): return lax.ppermute(values, axis, pairs + [(b, a) for a, b in pairs])  12.5 us
    pallas_call x1, Pallas kernels, resident(): call(functools.partial(final_kernel, freqs), [SMEM, SMEM] + [VMEM] * 10,...  12.2 us
    pallas_call x1, Pallas kernels, resident(): call(functools.partial(pack_kernel, freqs), [SMEM] + [HBM] * 7, (in_vmem(...  11.5 us
    ppermute x8, waiting for transfers between devices, swap(): return lax.ppermute(values, axis, pairs + [(b, a) for a, b in pairs])  6.85 us
    ppermute x2, waiting for transfers between devices, others_sum(): lax.ppermute(values, axis, [(i, (i + step) % count) for i in range(count)])  4.1 us
    ppermute x2, starting transfers between devices, others_sum(): lax.ppermute(values, axis, [(i, (i + step) % count) for i in range(count)])  3.14 us
  transfers between devices with their start and end apart: 10, of which 4 were waited for; matrix products, arithmetic and copies ran while one was open for 0% of the time, Pallas kernels for 30%

profile of v8, /device:TPU:12, one launch (start us, length us, event | category | flops | bytes accessed | tf_op | source)
XLA Modules:
  0.0 75.9 jit_solution(15216540816085733303)
XLA Ops:
  0.6 0.0 copy-start.5
  0.6 11.5 %shard_map.104 = (f32[18,36,64,128]{3,2,1,0:T(8,128)S(1)}, f32[36,64,128]{2,1,0:T(8,128)S(1)}, f32[64,128]{1,0:T(8,128)S(1)}, f32[6,64,128]{2,1,0:T(8,128)S(1)},...) custom-call(s32[1]{0:T(128)} %bitcast.member_ref, ...), custom_call_target="tpu_custom_call" | custom-call | flops 21233664 | bytes 21233664 | tf_op jit(solution)/shard_map/pallas_call | solution.py:919
  12.1 0.1 collective-permute-start
  12.2 2.5 %collective-permute-start.1 = (f32[6,64,128]{2,1,0:T(8,128)S(1)}, f32[6,64,128]{2,1,0:T(8,128)S(1)}, u32[]{:S(2)}, u32[]{:S(2)}) collective-permute-start(f32[6,64,128]{2,1,0:T(8,128)S(1)} %get-tuple-element.37), channel_id=1, source_target_pairs={{4,8},{8,4},{5,9},{9,5},{6,10},{10,6},{7,11},{11,7},{20,24},{24,20... | collective-permute-start | bytes 589832 | tf_op jit(solution)/shard_map/ppermute | solution.py:864
  14.7 0.0 copy-done.5
  14.7 0.0 copy-start
  14.8 0.0 copy-start.1
  14.8 0.0 copy-start.2
  14.8 0.0 copy-start.3
  14.8 0.0 copy-start.4
  14.8 7.2 %shard_map.105 = (f32[18,36,64,128]{3,2,1,0:T(8,128)S(1)}, f32[1152,128]{1,0:T(8,128)S(1)}, f32[1152,128]{1,0:T(8,128)S(1)}, f32[64,128]{1,0:T(8,128)S(1)}) custom-call(s32[1]{0:T(128)} %bitcast.member_ref, f32[1800]{0:T(1024)S(1)} %copy-done.5, f32[64,128]{1,0:T(8,128)S(1)} %get-tuple-element.34.wet_ref, ...), custom_call_target="tpu_custom_call", output_to_operand_aliasing={{0}: (4, {})} | custom-call | flops 28311552 | bytes 14155776 | tf_op jit(solution)/shard_map/pallas_call | solution.py:955
  22.1 0.0 copy-start.6
  22.1 0.0 collective-permute-done.swapped_ref.swap_side_ref
  22.1 0.0 collective-permute-done.1.other_ref.other_side_ref
  22.1 0.1 shard_map.106
  22.2 3.5 %collective-permute-start.3 = (f32[656,128]{1,0:T(8,128)S(1)}, f32[656,128]{1,0:T(8,128)S(1)}, u32[]{:S(2)}, u32[]{:S(2)}) collective-permute-start(f32[656,128]{1,0:T(8,128)S(1)} %get-tuple-element.43), channel_id=1, source_target_pairs={{1,2},{2,1},{5,6},{6,5},{9,10},{10,9},{13,14},{14,13},{17,18},{18,... | collective-permute-start | bytes 1007624 | tf_op jit(solution)/shard_map/ppermute | solution.py:864
  25.7 0.1 collective-permute-start.2
  25.8 13.8 %shard_map.107 = (f32[18,36,64,128]{3,2,1,0:T(8,128)S(1)}, f32[1152,128]{1,0:T(8,128)S(1)}, f32[1152,128]{1,0:T(8,128)S(1)}, f32[64,128]{1,0:T(8,128)S(1)}) custom-call(s32[1]{0:T(128)} %bitcast.member_ref, f32[1800]{0:T(1024)S(1)} %copy-done.5, ...), custom_call_target="tpu_custom_call", output_to_operand_aliasing={{0}: (4, {}), {1}: (6, {}), {2}: (7, {}), {3}: (8, {})} | custom-call | flops 56623104 | bytes 28311552 | tf_op jit(solution)/shard_map/pallas_call | solution.py:955
  39.5 0.0 collective-permute-done.3.other_row_ref
  39.6 0.0 collective-permute-done.2.swap_row_ref
  39.6 0.0 copy-done
  39.6 0.0 copy-done.1
  39.6 1.1 %shard_map.108 = (f32[12,64,128]{2,1,0:T(8,128)S(1)}, f32[5184,128]{1,0:T(8,128)S(1)}, f32[64,128]{1,0:T(8,128)S(1)}) custom-call(s32[1]{0:T(128)} %bitcast.member_ref, f32[2,12,8,128]{3,2,1,0:T(8,128)S(1)} %copy-done.1, f32[2,10,5,18,128]{4,3,2,1,0:T(8,128)S(1)} %copy-done, ...), custom_call_target="tpu_custom_call", output_to_operand_aliasing={{1}: (8, {}), {2}: (9, {})} | custom-call | flops 4915200 | bytes 1638400 | tf_op jit(solution)/shard_map/pallas_call | solution.py:993
  40.7 1.6 %collective-permute-start.4 = (f32[64,128]{1,0:T(8,128)S(1)}, f32[64,128]{1,0:T(8,128)S(1)}, u32[]{:S(2)}, u32[]{:S(2)}) collective-permute-start(f32[64,128]{1,0:T(8,128)S(1)} %get-tuple-element.55.own_ref), channel_id=1, source_target_pairs={{0,16},{16,0},{1,17},{17,1},{2,18},{18,2},{3,19},{19,3},{4,20},{20... | collective-permute-start | bytes 98312 | tf_op jit(solution)/shard_map/ppermute | solution.py:871
  42.3 0.0 copy-done.2
  42.3 0.0 copy-done.3
  42.3 0.0 copy-done.4
  42.3 1.4 %shard_map.109 = (f32[1152,128]{1,0:T(8,128)S(1)}, f32[1152,128]{1,0:T(8,128)S(1)}) custom-call(s32[1]{0:T(128)} %bitcast.member_ref, f32[2,12,8,128]{3,2,1,0:T(8,128)S(1)} %copy-done.1, f32[2,10,5,18,128]{4,3,2,1,0:T(8,128)S(1)} %copy-done, s32[64,128]{1,0:T(8,128)S(1)} %copy-done.2, ...), custom_call_target="tpu_custom_call", output_to_operand_aliasing={{0}: (9, {}), {1}: (10, {})} | custom-call | flops 4915200 | bytes 1638400 | tf_op jit(solution)/shard_map/pallas_call | solution.py:1010
  43.7 1.0 %collective-permute-done.4.other_ref = f32[64,128]{1,0:T(8,128)S(1)} collective-permute-done((f32[64,128]{1,0:T(8,128)S(1)}, f32[64,128]{1,0:T(8,128)S(1)}, u32[]{:S(2)}, u32[]{:S(2)}) %collective-permute-start.4) | collective-permute-done | bytes 32800 | tf_op jit(solution)/shard_map/ppermute | solution.py:871
  44.7 1.0 %shard_map.110 = (f32[3,64,128]{2,1,0:T(8,128)S(1)}, f32[18,64,128]{2,1,0:T(8,128)S(1)}) custom-call(s32[1]{0:T(128)} %bitcast.member_ref, f32[1800]{0:T(1024)S(1)} %copy-done.5, f32[64,128]{1,0:T(8,128)S(1)} %get-tuple-element.34.wet_ref, f32[1152,128]{1,0:T(8,128)S(1)} %get-tuple-element.53.a_ref, f32[1152,128]{1,0:T(8,128)S(1)} %get-tuple-element.54.b_ref, ...), custom_call_target="tpu_custom_call" | custom-call | flops 1769472 | bytes 1179648 | tf_op jit(solution)/shard_map/pallas_call | solution.py:1023
  45.7 1.6 %collective-permute-start.5 = (f32[3,64,128]{2,1,0:T(8,128)S(1)}, f32[3,64,128]{2,1,0:T(8,128)S(1)}, u32[]{:S(2)}, u32[]{:S(2)}) collective-permute-start(f32[3,64,128]{2,1,0:T(8,128)S(1)} %get-tuple-element.57.own_ref), channel_id=1, source_target_pairs={{0,16},{16,0},{1,17},{17,1},{2,18},{18,2},{3,19},{19,3},{4,20},{20... | collective-permute-start | bytes 294920 | tf_op jit(solution)/shard_map/ppermute | solution.py:871
  47.2 3.1 %collective-permute-done.5.other_ref = f32[3,64,128]{2,1,0:T(8,128)S(1)} collective-permute-done((f32[3,64,128]{2,1,0:T(8,128)S(1)}, f32[3,64,128]{2,1,0:T(8,128)S(1)}, u32[]{:S(2)}, u32[]{:S(2)}) %collective-permute-start.5) | collective-permute-done | bytes 98336 | tf_op jit(solution)/shard_map/ppermute | solution.py:871
  50.4 1.9 %collective-permute-start.7 = (f32[2,64,128]{2,1,0:T(8,128)S(1)}, f32[2,64,128]{2,1,0:T(8,128)S(1)}, u32[]{:S(2)}, u32[]{:S(2)}) collective-permute-start(f32[2,64,128]{2,1,0:T(8,128)S(1)} %get-tuple-element.59.stress_ref), channel_id=1, source_target_pairs={{4,8},{8,4},{5,9},{9,5},{6,10},{10,6},{7,11},{11,7},{20,24},{24,20... | collective-permute-start | bytes 196616 | tf_op jit(solution)/shard_map/ppermute | solution.py:864
  52.3 0.1 collective-permute-start.6
  52.4 3.6 %collective-permute-done.7.other_ref = f32[2,64,128]{2,1,0:T(8,128)S(1)} collective-permute-done((f32[2,64,128]{2,1,0:T(8,128)S(1)}, f32[2,64,128]{2,1,0:T(8,128)S(1)}, u32[]{:S(2)}, u32[]{:S(2)}) %collective-permute-start.7) | collective-permute-done | bytes 65568 | tf_op jit(solution)/shard_map/ppermute | solution.py:864
  56.0 0.0 collective-permute-done.6.swapped_ref
  56.0 2.1 %collective-permute-start.8 = (f32[2,8,256]{2,1,0:T(8,128)S(1)}, f32[2,8,256]{2,1,0:T(8,128)S(1)}, u32[]{:S(2)}, u32[]{:S(2)}) collective-permute-start(f32[2,8,256]{2,1,0:T(8,128)S(1)} %get-tuple-element.61), channel_id=1, source_target_pairs={{0,1},{2,3},{1,0},{3,2},{4,5},{6,7},{5,4},{7,6},{8,9},{10,11},{9,8... | collective-permute-start | bytes 49160 | tf_op jit(solution)/shard_map/ppermute | solution.py:864
  58.1 2.3 %collective-permute-start.9 = (f32[2,8,256]{2,1,0:T(8,128)S(1)}, f32[2,8,256]{2,1,0:T(8,128)S(1)}, u32[]{:S(2)}, u32[]{:S(2)}) collective-permute-start(f32[2,8,256]{2,1,0:T(8,128)S(1)} %get-tuple-element.62), channel_id=1, source_target_pairs={{1,2},{2,1},{5,6},{6,5},{9,10},{10,9},{13,14},{14,13},{17,18},{18,... | collective-permute-start | bytes 49160 | tf_op jit(solution)/shard_map/ppermute | solution.py:864
  60.4 0.0 collective-permute-done.8.swapped_ref
  60.4 3.3 %collective-permute-done.9.other_ref = f32[2,8,256]{2,1,0:T(8,128)S(1)} collective-permute-done((f32[2,8,256]{2,1,0:T(8,128)S(1)}, f32[2,8,256]{2,1,0:T(8,128)S(1)}, u32[]{:S(2)}, u32[]{:S(2)}) %collective-permute-start.9) | collective-permute-done | bytes 16416 | tf_op jit(solution)/shard_map/ppermute | solution.py:864
  63.7 0.0 copy-done.6
  63.7 12.2 %shard_map.113 = (f32[18,36,64,128]{3,2,1,0:T(8,128)}, f32[64,128]{1,0:T(8,128)}) custom-call(s32[1]{0:T(128)} %bitcast.member_ref, f32[1800]{0:T(1024)S(1)} %copy-done.5, f32[64,128]{1,0:T(8,128)S(1)} %copy-done.6, f32[18,64,128]{2,1,0:T(8,128)S(1)} %get-tuple-element.56.ratios_ref, f32[3,64,128]{2,1,0:T(8,128)S(1)} %get-tuple-element.58.sums_ref, ...), custom_call_target="tpu_custom_call" | custom-call | flops 31850496 | bytes 42467328 | tf_op jit(solution)/shard_map/pallas_call | solution.py:1049
  (2 shorter events, 0.0 us)
Async XLA Ops:
  0.6 14.1 %copy-start.5 = (f32[1800]{0:T(1024)S(1)}, f32[1800]{0:T(1024)}, u32[]{:S(2)}) copy-start(f32[1800]{0:T(1024)} %constant.12.clone.scalar_ref) | copy-start | bytes 21604
  12.1 9.9 %collective-permute-start = (f32[6,64,128]{2,1,0:T(8,128)S(1)}, f32[6,64,128]{2,1,0:T(8,128)S(1)}, u32[]{:S(2)}, u32[]{:S(2)}) collective-permute-start(f32[6,64,128]{2,1,0:T(8,128)S(1)} %get-tuple-element.36), channel_id=1, source_target_pairs={{0,4},{8,12},{4,0},{12,8},{1,5},{9,13},{5,1},{13,9},{2,6},{10,14},... | collective-permute-start | bytes 589832 | tf_op jit(solution)/shard_map/ppermute | solution.py:864
  12.2 9.9 %collective-permute-start.1 = (f32[6,64,128]{2,1,0:T(8,128)S(1)}, f32[6,64,128]{2,1,0:T(8,128)S(1)}, u32[]{:S(2)}, u32[]{:S(2)}) collective-permute-start(f32[6,64,128]{2,1,0:T(8,128)S(1)} %get-tuple-element.37), channel_id=1, source_target_pairs={{4,8},{8,4},{5,9},{9,5},{6,10},{10,6},{7,11},{11,7},{20,24},{24,20... | collective-permute-start | bytes 589832 | tf_op jit(solution)/shard_map/ppermute | solution.py:864
  14.7 24.8 %copy-start = (f32[2,10,5,18,128]{4,3,2,1,0:T(8,128)S(1)}, f32[2,10,5,18,128]{4,3,2,1,0:T(8,128)}, u32[]{:S(2)}) copy-start(f32[2,10,5,18,128]{4,3,2,1,0:T(8,128)} %constant.14.clone.table_hbm.table_ref) | copy-start | bytes 2764804
  14.8 24.8 %copy-start.1 = (f32[2,12,8,128]{3,2,1,0:T(8,128)S(1)}, f32[2,12,8,128]{3,2,1,0:T(8,128)}, u32[]{:S(2)}) copy-start(f32[2,12,8,128]{3,2,1,0:T(8,128)} %constant.13.clone.lanes_hbm.lanes_ref) | copy-start | bytes 294916
  14.8 27.5 %copy-start.2 = (s32[64,128]{1,0:T(8,128)S(1)}, s32[64,128]{1,0:T(8,128)}, u32[]{:S(2)}) copy-start(s32[64,128]{1,0:T(8,128)} %ice_ref.1) | copy-start | bytes 98308
  14.8 27.5 %copy-start.3 = (f32[64,128]{1,0:T(8,128)S(1)}, f32[64,128]{1,0:T(8,128)}, u32[]{:S(2)}) copy-start(f32[64,128]{1,0:T(8,128)} %east_ref.1) | copy-start | bytes 98308
  14.8 27.5 %copy-start.4 = (f32[64,128]{1,0:T(8,128)S(1)}, f32[64,128]{1,0:T(8,128)}, u32[]{:S(2)}) copy-start(f32[64,128]{1,0:T(8,128)} %north_ref.1) | copy-start | bytes 98308
  22.1 41.6 %copy-start.6 = (f32[64,128]{1,0:T(8,128)S(1)}, f32[64,128]{1,0:T(8,128)}, u32[]{:S(2)}) copy-start(f32[64,128]{1,0:T(8,128)} %depth_ref.1) | copy-start | bytes 98308
  22.2 17.3 %collective-permute-start.3 = (f32[656,128]{1,0:T(8,128)S(1)}, f32[656,128]{1,0:T(8,128)S(1)}, u32[]{:S(2)}, u32[]{:S(2)}) collective-permute-start(f32[656,128]{1,0:T(8,128)S(1)} %get-tuple-element.43), channel_id=1, source_target_pairs={{1,2},{2,1},{5,6},{6,5},{9,10},{10,9},{13,14},{14,13},{17,18},{18,... | collective-permute-start | bytes 1007624 | tf_op jit(solution)/shard_map/ppermute | solution.py:864
  25.7 13.9 %collective-permute-start.2 = (f32[656,128]{1,0:T(8,128)S(1)}, f32[656,128]{1,0:T(8,128)S(1)}, u32[]{:S(2)}, u32[]{:S(2)}) collective-permute-start(f32[656,128]{1,0:T(8,128)S(1)} %get-tuple-element.42.refs_0_), channel_id=1, source_target_pairs={{0,1},{2,3},{1,0},{3,2},{4,5},{6,7},{5,4},{7,6},{8,9},{10,11},{9,8... | collective-permute-start | bytes 1007624 | tf_op jit(solution)/shard_map/ppermute | solution.py:864
  40.7 4.0 %collective-permute-start.4 = (f32[64,128]{1,0:T(8,128)S(1)}, f32[64,128]{1,0:T(8,128)S(1)}, u32[]{:S(2)}, u32[]{:S(2)}) collective-permute-start(f32[64,128]{1,0:T(8,128)S(1)} %get-tuple-element.55.own_ref), channel_id=1, source_target_pairs={{0,16},{16,0},{1,17},{17,1},{2,18},{18,2},{3,19},{19,3},{4,20},{20... | collective-permute-start | bytes 98312 | tf_op jit(solution)/shard_map/ppermute | solution.py:871
  45.7 4.7 %collective-permute-start.5 = (f32[3,64,128]{2,1,0:T(8,128)S(1)}, f32[3,64,128]{2,1,0:T(8,128)S(1)}, u32[]{:S(2)}, u32[]{:S(2)}) collective-permute-start(f32[3,64,128]{2,1,0:T(8,128)S(1)} %get-tuple-element.57.own_ref), channel_id=1, source_target_pairs={{0,16},{16,0},{1,17},{17,1},{2,18},{18,2},{3,19},{19,3},{4,20},{20... | collective-permute-start | bytes 294920 | tf_op jit(solution)/shard_map/ppermute | solution.py:871
  50.4 5.6 %collective-permute-start.7 = (f32[2,64,128]{2,1,0:T(8,128)S(1)}, f32[2,64,128]{2,1,0:T(8,128)S(1)}, u32[]{:S(2)}, u32[]{:S(2)}) collective-permute-start(f32[2,64,128]{2,1,0:T(8,128)S(1)} %get-tuple-element.59.stress_ref), channel_id=1, source_target_pairs={{4,8},{8,4},{5,9},{9,5},{6,10},{10,6},{7,11},{11,7},{20,24},{24,20... | collective-permute-start | bytes 196616 | tf_op jit(solution)/shard_map/ppermute | solution.py:864
  52.3 3.7 %collective-permute-start.6 = (f32[2,64,128]{2,1,0:T(8,128)S(1)}, f32[2,64,128]{2,1,0:T(8,128)S(1)}, u32[]{:S(2)}, u32[]{:S(2)}) collective-permute-start(f32[2,64,128]{2,1,0:T(8,128)S(1)} %get-tuple-element.59.stress_ref), channel_id=1, source_target_pairs={{0,4},{8,12},{4,0},{12,8},{1,5},{9,13},{5,1},{13,9},{2,6},{10,14},... | collective-permute-start | bytes 196616 | tf_op jit(solution)/shard_map/ppermute | solution.py:864
  56.0 4.4 %collective-permute-start.8 = (f32[2,8,256]{2,1,0:T(8,128)S(1)}, f32[2,8,256]{2,1,0:T(8,128)S(1)}, u32[]{:S(2)}, u32[]{:S(2)}) collective-permute-start(f32[2,8,256]{2,1,0:T(8,128)S(1)} %get-tuple-element.61), channel_id=1, source_target_pairs={{0,1},{2,3},{1,0},{3,2},{4,5},{6,7},{5,4},{7,6},{8,9},{10,11},{9,8... | collective-permute-start | bytes 49160 | tf_op jit(solution)/shard_map/ppermute | solution.py:864
  58.1 5.6 %collective-permute-start.9 = (f32[2,8,256]{2,1,0:T(8,128)S(1)}, f32[2,8,256]{2,1,0:T(8,128)S(1)}, u32[]{:S(2)}, u32[]{:S(2)}) collective-permute-start(f32[2,8,256]{2,1,0:T(8,128)S(1)} %get-tuple-element.62), channel_id=1, source_target_pairs={{1,2},{2,1},{5,6},{6,5},{9,10},{10,9},{13,14},{14,13},{17,18},{18,... | collective-permute-start | bytes 49160 | tf_op jit(solution)/shard_map/ppermute | solution.py:864

commit v9 on v6

--- a/solution.py
+++ b/solution.py
@@ -253,7 +253,7 @@
     return jnp.where(iota(values.shape, 1) == edge, 0.0, moved)
 
 
-DEPTH = 3
+DEPTH = 2
 
 
 def sides(quadrant):
@@ -289,8 +289,7 @@
         part = (slice(None), pl.ds(group * GROUP, GROUP))
         return pltpu.make_async_copy(spectrum_ref.at[part], blocks_ref.at[part], sems.at[group])
 
-    for group in range(DEPTH):
-        fetch(group).start()
+    fetch(0).start()
     edges_ref[...] = jnp.zeros_like(edges_ref)
     for copy in small:
         copy.wait()
@@ -305,6 +304,8 @@
         project = math.cos(angle) * east_ref[...] + math.sin(angle) * north_ref[...]
         growth_ref[direction] = open_water * jnp.square(jnp.maximum(project, 0.0))
 
+    for group in range(1, DEPTH):
+        fetch(group).start()
     lane = iota(shape, 1)
     even = lane % 2 == 0
     tile_lane = iota((SUB, LANES), 1)
@@ -438,8 +439,7 @@
         slot = lax.rem(j, AHEAD)
         return pltpu.make_async_copy(spectrum_ref.at[j], ring_ref.at[slot], sems.at[slot])
 
-    for j in range(start, min(start + AHEAD, stop)):
-        fetch(jnp.int32(j)).start()
+    fetch(jnp.int32(start)).start()
 
     lane = iota((SUB, LANES), 1)
     sub = iota((SUB, LANES), 0)
@@ -463,7 +463,18 @@
 
     def frequency(j, carry):
         fetch(j).wait()
+
+        @pl.when(j == start)
+        def _():
+            for later in range(start + 1, min(start + AHEAD, stop)):
+                fetch(jnp.int32(later)).start()
+
         slot = lax.rem(j, AHEAD)
+        sums = [[None] * tiles for _ in range(3)]
+
+        def add(which, t, value):
+            have = sums[which][t]
+            sums[which][t] = value if have is None else have + value
         base = (member * freqs + j) * CLASSES * KINDS
         at = [pl.ds(pl.multiple_of(j * rows, SUB) + t * SUB, SUB) for t in range(tiles)]
 
@@ -511,22 +522,26 @@
                     grown_x = plain_x + scaled_high * (grown[0] + grown[2])
                     grown_y = plain_y + scaled_high * (grown[1] + grown[3])
                     square = math.cos(0.5 * math.pi) ** 2
-                    energy_ref[tile_at(t), :] += plain_x + plain_y
-                    a_ref[at[t], :] = grown_x + grown_y
-                    b_ref[at[t], :] = grown_x + square * grown_y
+                    add(0, t, plain_x + plain_y)
+                    add(1, t, grown_x + grown_y)
+                    add(2, t, grown_x + square * grown_y)
                 else:
                     plain = scale * ((moved[0] + moved[1]) + (moved[2] + moved[3]))
                     whole = plain + scaled_high * ((grown[0] + grown[1]) + (grown[2] + grown[3]))
                     square = math.cos(2.0 * math.pi * kind / ND) ** 2
-                    energy_ref[tile_at(t), :] += plain
-                    a_ref[at[t], :] += whole
-                    b_ref[at[t], :] += square * whole
+                    add(0, t, plain)
+                    add(1, t, whole)
+                    add(2, t, square * whole)
 
         first_step(0)
         for kind in range(CLASSES - 1):
             if kind + 1 < CLASSES - 1:
                 first_step(kind + 1)
             second_step(kind)
+        for t in range(tiles):
+            energy_ref[tile_at(t), :] += sums[0][t]
+            a_ref[at[t], :] = sums[1][t]
+            b_ref[at[t], :] = sums[2][t]
 
         @pl.when(j + AHEAD < stop)
         def _():
@@ -732,15 +747,15 @@
 
 
 BEHIND = 12
+RINGS = 6
 
 
 def final_kernel(
     freqs, member_ref, scalar_ref, depth_ref, ratios_ref, sums_ref, beside_ref, swapped_ref,
     other_ref, growth_ref, kept_ref, columns_ref, edges_ref,
-    result_ref, level_ref, damping_ref, turning_ref, ring0, ring1, sems,
+    result_ref, level_ref, damping_ref, turning_ref, sems, *rings,
 ):
     member = member_ref[0]
-    rings = (ring0, ring1)
     rows = depth_ref.shape[0]
     slab, slabs = lax.axis_index("slab"), lax.axis_size("slab")
     sect, sects = lax.axis_index("sect"), lax.axis_size("sect")
@@ -789,10 +804,10 @@
         )
 
     def frequency(j, which):
-        @pl.when(j >= 2)
+        @pl.when(j >= RINGS)
         def _():
             for piece in range(4):
-                send(j - 2, which, piece).wait()
+                send(j - RINGS, which, piece).wait()
 
         base = (member * freqs + j) * CLASSES * KINDS
         high = scalar_ref[base + 3]
@@ -833,17 +848,18 @@
         for group in range(GROUPS):
             turning_ref[group] = turned[group]
 
-    def pair(index, carry):
-        for which in range(2):
-            frequency(2 * index + which, which)
+    def turn(index, carry):
+        for which in range(RINGS):
+            frequency(RINGS * index + which, which)
         return carry
 
-    lax.fori_loop(0, freqs // 2, pair, 0)
-    if freqs % 2:
-        frequency(jnp.int32(freqs - 1), 0)
-    for j in range(max(0, freqs - 2), freqs):
+    whole_turns = freqs // RINGS
+    lax.fori_loop(0, whole_turns, turn, 0)
+    for j in range(whole_turns * RINGS, freqs):
+        frequency(jnp.int32(j), j % RINGS)
+    for j in range(max(0, freqs - RINGS), freqs):
         for piece in range(4):
-            send(j, j % 2, piece).wait()
+            send(j, j % RINGS, piece).wait()
 
 
 def swap(values, axis, first):
@@ -1043,10 +1059,10 @@
         scratch=[
             pltpu.VMEM((rows, lanes), jnp.float32),
             pltpu.VMEM((GROUPS, rows, lanes), jnp.float32),
-            pltpu.VMEM((ND, rows, lanes), jnp.float32),
-            pltpu.VMEM((ND, rows, lanes), jnp.float32),
-            pltpu.SemaphoreType.DMA((2, 4)),
-        ],
+            pltpu.SemaphoreType.DMA((RINGS, 4)),
+        ]
+        + [pltpu.VMEM((ND, rows, lanes), jnp.float32)] * RINGS,
+        limit=12,
     )(
         member, scalars, depth, ratios, sums, beside, aside, beyond, growth, kept,
         columns, edges,

time: 76.9 us -> 76.4 us (level)
    pallas_call x1, Pallas kernels: 14.8 us -> 12.2 us  [resident(): call(functools.partial(final_kernel, freqs), [SMEM, SMEM] + [VMEM] * 10,...]
    pallas_call x1, Pallas kernels: 9.98 us -> 11.9 us  [resident(): call(functools.partial(pack_kernel, freqs), [SMEM] + [HBM] * 7, (in_any(N...]
where the time goes in v9:
time: 76.4 us; the launch traced here: 76.1 us
  Pallas kernels  48.6 us (64%)
  starting transfers between devices  15.6 us (20%)
  waiting for transfers between devices  11 us (14%)
  between operations  0.87 us (1%)
    pallas_call x2, Pallas kernels, main_part(): call(functools.partial(main_kernel, freqs, start, stop), [SMEM, SMEM, VME...  20.9 us
    ppermute x8, starting transfers between devices, swap(): return lax.ppermute(values, axis, pairs + [(b, a) for a, b in pairs])  12.5 us
    pallas_call x1, Pallas kernels, resident(): call(functools.partial(final_kernel, freqs), [SMEM, SMEM] + [VMEM] * 10,...  12.2 us
    pallas_call x1, Pallas kernels, resident(): call(functools.partial(pack_kernel, freqs), [SMEM] + [HBM] * 7, (in_any(N...  11.9 us
    ppermute x8, waiting for transfers between devices, swap(): return lax.ppermute(values, axis, pairs + [(b, a) for a, b in pairs])  6.85 us
    ppermute x2, waiting for transfers between devices, others_sum(): lax.ppermute(values, axis, [(i, (i + step) % count) for i in range(count)])  4.14 us
    ppermute x2, starting transfers between devices, others_sum(): lax.ppermute(values, axis, [(i, (i + step) % count) for i in range(count)])  3.11 us
  transfers between devices with their start and end apart: 10, of which 4 were waited for; matrix products, arithmetic and copies ran while one was open for 0% of the time, Pallas kernels for 29%

profile of v9, /device:TPU:12, one launch (start us, length us, event | category | flops | bytes accessed | tf_op | source)
XLA Modules:
  0.0 76.1 jit_solution(8321965482611285746)
XLA Ops:
  0.6 0.0 copy-start.5
  0.6 11.9 %shard_map.104 = (f32[36,64,128]{2,1,0:T(8,128)S(1)}, f32[64,128]{1,0:T(8,128)S(1)}, f32[6,64,128]{2,1,0:T(8,128)S(1)}, f32[6,64,128]{2,1,0:T(8,128)S(1)}, f32[6...) custom-call(s32[1]{0:T(128)} %bitcast.member_ref, ...), custom_call_target="tpu_custom_call" | custom-call | flops 21233664 | bytes 21233664 | tf_op jit(solution)/shard_map/pallas_call | solution.py:923
  12.6 0.1 collective-permute-start
  12.6 2.5 %collective-permute-start.1 = (f32[6,64,128]{2,1,0:T(8,128)S(1)}, f32[6,64,128]{2,1,0:T(8,128)S(1)}, u32[]{:S(2)}, u32[]{:S(2)}) collective-permute-start(f32[6,64,128]{2,1,0:T(8,128)S(1)} %get-tuple-element.36), channel_id=1, source_target_pairs={{4,8},{8,4},{5,9},{9,5},{6,10},{10,6},{7,11},{11,7},{20,24},{24,20... | collective-permute-start | bytes 589832 | tf_op jit(solution)/shard_map/ppermute | solution.py:868
  15.2 0.0 copy-done.5
  15.2 7.7 %shard_map.105 = (f32[18,36,64,128]{3,2,1,0:T(8,128)S(1)}, f32[1152,128]{1,0:T(8,128)S(1)}, f32[1152,128]{1,0:T(8,128)S(1)}, f32[64,128]{1,0:T(8,128)S(1)}) custom-call(s32[1]{0:T(128)} %bitcast.member_ref, f32[1800]{0:T(1024)S(1)} %copy-done.5, f32[64,128]{1,0:T(8,128)S(1)} %get-tuple-element.33.wet_ref, f32[36,64,128]{2,1,0:T(8,128)S(1)} %get-tuple-element.34.growth_ref, ...), custom_call_target="tpu_custom_call" | custom-call | flops 28311552 | bytes 14155776 | tf_op jit(solution)/shard_map/pallas_call | solution.py:958
  22.9 0.0 collective-permute-done.swapped_ref.swap_side_ref
  22.9 0.0 collective-permute-done.1.other_ref.other_side_ref
  22.9 0.1 shard_map.106
  23.0 3.5 %collective-permute-start.3 = (f32[656,128]{1,0:T(8,128)S(1)}, f32[656,128]{1,0:T(8,128)S(1)}, u32[]{:S(2)}, u32[]{:S(2)}) collective-permute-start(f32[656,128]{1,0:T(8,128)S(1)} %get-tuple-element.41), channel_id=1, source_target_pairs={{1,2},{2,1},{5,6},{6,5},{9,10},{10,9},{13,14},{14,13},{17,18},{18,... | collective-permute-start | bytes 1007624 | tf_op jit(solution)/shard_map/ppermute | solution.py:868
  26.5 0.1 collective-permute-start.2
  26.6 0.0 copy-start
  26.6 0.0 copy-start.1
  26.6 0.0 copy-start.2
  26.7 0.0 copy-start.3
  26.7 0.0 copy-start.4
  26.7 0.0 copy-start.6
  26.7 13.1 %shard_map.107 = (f32[18,36,64,128]{3,2,1,0:T(8,128)S(1)}, f32[1152,128]{1,0:T(8,128)S(1)}, f32[1152,128]{1,0:T(8,128)S(1)}, f32[64,128]{1,0:T(8,128)S(1)}) custom-call(s32[1]{0:T(128)} %bitcast.member_ref, f32[1800]{0:T(1024)S(1)} %copy-done.5, ...), custom_call_target="tpu_custom_call", output_to_operand_aliasing={{0}: (6, {}), {1}: (7, {}), {2}: (8, {}), {3}: (9, {})} | custom-call | flops 56623104 | bytes 28311552 | tf_op jit(solution)/shard_map/pallas_call | solution.py:958
  39.8 0.0 collective-permute-done.3.other_row_ref
  39.8 0.0 collective-permute-done.2.swap_row_ref
  39.9 0.0 copy-done
  39.9 0.0 copy-done.1
  39.9 1.1 %shard_map.108 = (f32[12,64,128]{2,1,0:T(8,128)S(1)}, f32[5184,128]{1,0:T(8,128)S(1)}, f32[64,128]{1,0:T(8,128)S(1)}) custom-call(s32[1]{0:T(128)} %bitcast.member_ref, f32[2,12,8,128]{3,2,1,0:T(8,128)S(1)} %copy-done.1, f32[2,10,5,18,128]{4,3,2,1,0:T(8,128)S(1)} %copy-done, ...), custom_call_target="tpu_custom_call", output_to_operand_aliasing={{1}: (8, {}), {2}: (9, {})} | custom-call | flops 4915200 | bytes 1638400 | tf_op jit(solution)/shard_map/pallas_call | solution.py:996
  41.0 1.6 %collective-permute-start.4 = (f32[64,128]{1,0:T(8,128)S(1)}, f32[64,128]{1,0:T(8,128)S(1)}, u32[]{:S(2)}, u32[]{:S(2)}) collective-permute-start(f32[64,128]{1,0:T(8,128)S(1)} %get-tuple-element.53.own_ref), channel_id=1, source_target_pairs={{0,16},{16,0},{1,17},{17,1},{2,18},{18,2},{3,19},{19,3},{4,20},{20... | collective-permute-start | bytes 98312 | tf_op jit(solution)/shard_map/ppermute | solution.py:875
  42.6 0.0 copy-done.2
  42.6 0.0 copy-done.3
  42.6 0.0 copy-done.4
  42.6 1.4 %shard_map.109 = (f32[1152,128]{1,0:T(8,128)S(1)}, f32[1152,128]{1,0:T(8,128)S(1)}) custom-call(s32[1]{0:T(128)} %bitcast.member_ref, f32[2,12,8,128]{3,2,1,0:T(8,128)S(1)} %copy-done.1, f32[2,10,5,18,128]{4,3,2,1,0:T(8,128)S(1)} %copy-done, s32[64,128]{1,0:T(8,128)S(1)} %copy-done.2, ...), custom_call_target="tpu_custom_call", output_to_operand_aliasing={{0}: (9, {}), {1}: (10, {})} | custom-call | flops 4915200 | bytes 1638400 | tf_op jit(solution)/shard_map/pallas_call | solution.py:1013
  44.0 1.0 %collective-permute-done.4.other_ref = f32[64,128]{1,0:T(8,128)S(1)} collective-permute-done((f32[64,128]{1,0:T(8,128)S(1)}, f32[64,128]{1,0:T(8,128)S(1)}, u32[]{:S(2)}, u32[]{:S(2)}) %collective-permute-start.4) | collective-permute-done | bytes 32800 | tf_op jit(solution)/shard_map/ppermute | solution.py:875
  45.0 1.0 %shard_map.110 = (f32[3,64,128]{2,1,0:T(8,128)S(1)}, f32[18,64,128]{2,1,0:T(8,128)S(1)}) custom-call(s32[1]{0:T(128)} %bitcast.member_ref, f32[1800]{0:T(1024)S(1)} %copy-done.5, f32[64,128]{1,0:T(8,128)S(1)} %get-tuple-element.33.wet_ref, f32[1152,128]{1,0:T(8,128)S(1)} %get-tuple-element.51.a_ref, f32[1152,128]{1,0:T(8,128)S(1)} %get-tuple-element.52.b_ref, ...), custom_call_target="tpu_custom_call" | custom-call | flops 1769472 | bytes 1179648 | tf_op jit(solution)/shard_map/pallas_call | solution.py:1026
  46.0 1.6 %collective-permute-start.5 = (f32[3,64,128]{2,1,0:T(8,128)S(1)}, f32[3,64,128]{2,1,0:T(8,128)S(1)}, u32[]{:S(2)}, u32[]{:S(2)}) collective-permute-start(f32[3,64,128]{2,1,0:T(8,128)S(1)} %get-tuple-element.55.own_ref), channel_id=1, source_target_pairs={{0,16},{16,0},{1,17},{17,1},{2,18},{18,2},{3,19},{19,3},{4,20},{20... | collective-permute-start | bytes 294920 | tf_op jit(solution)/shard_map/ppermute | solution.py:875
  47.5 3.1 %collective-permute-done.5.other_ref = f32[3,64,128]{2,1,0:T(8,128)S(1)} collective-permute-done((f32[3,64,128]{2,1,0:T(8,128)S(1)}, f32[3,64,128]{2,1,0:T(8,128)S(1)}, u32[]{:S(2)}, u32[]{:S(2)}) %collective-permute-start.5) | collective-permute-done | bytes 98336 | tf_op jit(solution)/shard_map/ppermute | solution.py:875
  50.7 1.9 %collective-permute-start.7 = (f32[2,64,128]{2,1,0:T(8,128)S(1)}, f32[2,64,128]{2,1,0:T(8,128)S(1)}, u32[]{:S(2)}, u32[]{:S(2)}) collective-permute-start(f32[2,64,128]{2,1,0:T(8,128)S(1)} %get-tuple-element.57.stress_ref), channel_id=1, source_target_pairs={{4,8},{8,4},{5,9},{9,5},{6,10},{10,6},{7,11},{11,7},{20,24},{24,20... | collective-permute-start | bytes 196616 | tf_op jit(solution)/shard_map/ppermute | solution.py:868
  52.6 0.1 collective-permute-start.6
  52.7 3.6 %collective-permute-done.7.other_ref = f32[2,64,128]{2,1,0:T(8,128)S(1)} collective-permute-done((f32[2,64,128]{2,1,0:T(8,128)S(1)}, f32[2,64,128]{2,1,0:T(8,128)S(1)}, u32[]{:S(2)}, u32[]{:S(2)}) %collective-permute-start.7) | collective-permute-done | bytes 65568 | tf_op jit(solution)/shard_map/ppermute | solution.py:868
  56.2 0.0 collective-permute-done.6.swapped_ref
  56.3 2.0 %collective-permute-start.8 = (f32[2,8,256]{2,1,0:T(8,128)S(1)}, f32[2,8,256]{2,1,0:T(8,128)S(1)}, u32[]{:S(2)}, u32[]{:S(2)}) collective-permute-start(f32[2,8,256]{2,1,0:T(8,128)S(1)} %get-tuple-element.59), channel_id=1, source_target_pairs={{0,1},{2,3},{1,0},{3,2},{4,5},{6,7},{5,4},{7,6},{8,9},{10,11},{9,8... | collective-permute-start | bytes 49160 | tf_op jit(solution)/shard_map/ppermute | solution.py:868
  58.3 2.3 %collective-permute-start.9 = (f32[2,8,256]{2,1,0:T(8,128)S(1)}, f32[2,8,256]{2,1,0:T(8,128)S(1)}, u32[]{:S(2)}, u32[]{:S(2)}) collective-permute-start(f32[2,8,256]{2,1,0:T(8,128)S(1)} %get-tuple-element.60), channel_id=1, source_target_pairs={{1,2},{2,1},{5,6},{6,5},{9,10},{10,9},{13,14},{14,13},{17,18},{18,... | collective-permute-start | bytes 49160 | tf_op jit(solution)/shard_map/ppermute | solution.py:868
  60.7 0.0 collective-permute-done.8.swapped_ref
  60.7 3.3 %collective-permute-done.9.other_ref = f32[2,8,256]{2,1,0:T(8,128)S(1)} collective-permute-done((f32[2,8,256]{2,1,0:T(8,128)S(1)}, f32[2,8,256]{2,1,0:T(8,128)S(1)}, u32[]{:S(2)}, u32[]{:S(2)}) %collective-permute-start.9) | collective-permute-done | bytes 16416 | tf_op jit(solution)/shard_map/ppermute | solution.py:868
  63.9 0.0 copy-done.6
  63.9 12.2 %shard_map.113 = (f32[18,36,64,128]{3,2,1,0:T(8,128)}, f32[64,128]{1,0:T(8,128)}) custom-call(s32[1]{0:T(128)} %bitcast.member_ref, f32[1800]{0:T(1024)S(1)} %copy-done.5, f32[64,128]{1,0:T(8,128)S(1)} %copy-done.6, f32[18,64,128]{2,1,0:T(8,128)S(1)} %get-tuple-element.54.ratios_ref, f32[3,64,128]{2,1,0:T(8,128)S(1)} %get-tuple-element.56.sums_ref, ...), custom_call_target="tpu_custom_call" | custom-call | flops 31850496 | bytes 42467328 | tf_op jit(solution)/shard_map/pallas_call | solution.py:1052
  (2 shorter events, 0.0 us)
Async XLA Ops:
  0.6 14.5 %copy-start.5 = (f32[1800]{0:T(1024)S(1)}, f32[1800]{0:T(1024)}, u32[]{:S(2)}) copy-start(f32[1800]{0:T(1024)} %constant.12.clone.scalar_ref) | copy-start | bytes 21604
  12.6 10.3 %collective-permute-start = (f32[6,64,128]{2,1,0:T(8,128)S(1)}, f32[6,64,128]{2,1,0:T(8,128)S(1)}, u32[]{:S(2)}, u32[]{:S(2)}) collective-permute-start(f32[6,64,128]{2,1,0:T(8,128)S(1)} %get-tuple-element.35), channel_id=1, source_target_pairs={{0,4},{8,12},{4,0},{12,8},{1,5},{9,13},{5,1},{13,9},{2,6},{10,14},... | collective-permute-start | bytes 589832 | tf_op jit(solution)/shard_map/ppermute | solution.py:868
  12.6 10.3 %collective-permute-start.1 = (f32[6,64,128]{2,1,0:T(8,128)S(1)}, f32[6,64,128]{2,1,0:T(8,128)S(1)}, u32[]{:S(2)}, u32[]{:S(2)}) collective-permute-start(f32[6,64,128]{2,1,0:T(8,128)S(1)} %get-tuple-element.36), channel_id=1, source_target_pairs={{4,8},{8,4},{5,9},{9,5},{6,10},{10,6},{7,11},{11,7},{20,24},{24,20... | collective-permute-start | bytes 589832 | tf_op jit(solution)/shard_map/ppermute | solution.py:868
  23.0 16.8 %collective-permute-start.3 = (f32[656,128]{1,0:T(8,128)S(1)}, f32[656,128]{1,0:T(8,128)S(1)}, u32[]{:S(2)}, u32[]{:S(2)}) collective-permute-start(f32[656,128]{1,0:T(8,128)S(1)} %get-tuple-element.41), channel_id=1, source_target_pairs={{1,2},{2,1},{5,6},{6,5},{9,10},{10,9},{13,14},{14,13},{17,18},{18,... | collective-permute-start | bytes 1007624 | tf_op jit(solution)/shard_map/ppermute | solution.py:868
  26.5 13.3 %collective-permute-start.2 = (f32[656,128]{1,0:T(8,128)S(1)}, f32[656,128]{1,0:T(8,128)S(1)}, u32[]{:S(2)}, u32[]{:S(2)}) collective-permute-start(f32[656,128]{1,0:T(8,128)S(1)} %get-tuple-element.40.refs_0_), channel_id=1, source_target_pairs={{0,1},{2,3},{1,0},{3,2},{4,5},{6,7},{5,4},{7,6},{8,9},{10,11},{9,8... | collective-permute-start | bytes 1007624 | tf_op jit(solution)/shard_map/ppermute | solution.py:868
  26.6 13.2 %copy-start = (f32[2,10,5,18,128]{4,3,2,1,0:T(8,128)S(1)}, f32[2,10,5,18,128]{4,3,2,1,0:T(8,128)}, u32[]{:S(2)}) copy-start(f32[2,10,5,18,128]{4,3,2,1,0:T(8,128)} %constant.14.clone.table_hbm.table_ref) | copy-start | bytes 2764804
  26.6 13.2 %copy-start.1 = (f32[2,12,8,128]{3,2,1,0:T(8,128)S(1)}, f32[2,12,8,128]{3,2,1,0:T(8,128)}, u32[]{:S(2)}) copy-start(f32[2,12,8,128]{3,2,1,0:T(8,128)} %constant.13.clone.lanes_hbm.lanes_ref) | copy-start | bytes 294916
  26.6 15.9 %copy-start.2 = (s32[64,128]{1,0:T(8,128)S(1)}, s32[64,128]{1,0:T(8,128)}, u32[]{:S(2)}) copy-start(s32[64,128]{1,0:T(8,128)} %ice_ref.1) | copy-start | bytes 98308
  26.7 15.9 %copy-start.3 = (f32[64,128]{1,0:T(8,128)S(1)}, f32[64,128]{1,0:T(8,128)}, u32[]{:S(2)}) copy-start(f32[64,128]{1,0:T(8,128)} %east_ref.1) | copy-start | bytes 98308
  26.7 15.9 %copy-start.4 = (f32[64,128]{1,0:T(8,128)S(1)}, f32[64,128]{1,0:T(8,128)}, u32[]{:S(2)}) copy-start(f32[64,128]{1,0:T(8,128)} %north_ref.1) | copy-start | bytes 98308
  26.7 37.3 %copy-start.6 = (f32[64,128]{1,0:T(8,128)S(1)}, f32[64,128]{1,0:T(8,128)}, u32[]{:S(2)}) copy-start(f32[64,128]{1,0:T(8,128)} %depth_ref.1) | copy-start | bytes 98308
  41.0 4.0 %collective-permute-start.4 = (f32[64,128]{1,0:T(8,128)S(1)}, f32[64,128]{1,0:T(8,128)S(1)}, u32[]{:S(2)}, u32[]{:S(2)}) collective-permute-start(f32[64,128]{1,0:T(8,128)S(1)} %get-tuple-element.53.own_ref), channel_id=1, source_target_pairs={{0,16},{16,0},{1,17},{17,1},{2,18},{18,2},{3,19},{19,3},{4,20},{20... | collective-permute-start | bytes 98312 | tf_op jit(solution)/shard_map/ppermute | solution.py:875
  46.0 4.7 %collective-permute-start.5 = (f32[3,64,128]{2,1,0:T(8,128)S(1)}, f32[3,64,128]{2,1,0:T(8,128)S(1)}, u32[]{:S(2)}, u32[]{:S(2)}) collective-permute-start(f32[3,64,128]{2,1,0:T(8,128)S(1)} %get-tuple-element.55.own_ref), channel_id=1, source_target_pairs={{0,16},{16,0},{1,17},{17,1},{2,18},{18,2},{3,19},{19,3},{4,20},{20... | collective-permute-start | bytes 294920 | tf_op jit(solution)/shard_map/ppermute | solution.py:875
  50.7 5.6 %collective-permute-start.7 = (f32[2,64,128]{2,1,0:T(8,128)S(1)}, f32[2,64,128]{2,1,0:T(8,128)S(1)}, u32[]{:S(2)}, u32[]{:S(2)}) collective-permute-start(f32[2,64,128]{2,1,0:T(8,128)S(1)} %get-tuple-element.57.stress_ref), channel_id=1, source_target_pairs={{4,8},{8,4},{5,9},{9,5},{6,10},{10,6},{7,11},{11,7},{20,24},{24,20... | collective-permute-start | bytes 196616 | tf_op jit(solution)/shard_map/ppermute | solution.py:868
  52.6 3.7 %collective-permute-start.6 = (f32[2,64,128]{2,1,0:T(8,128)S(1)}, f32[2,64,128]{2,1,0:T(8,128)S(1)}, u32[]{:S(2)}, u32[]{:S(2)}) collective-permute-start(f32[2,64,128]{2,1,0:T(8,128)S(1)} %get-tuple-element.57.stress_ref), channel_id=1, source_target_pairs={{0,4},{8,12},{4,0},{12,8},{1,5},{9,13},{5,1},{13,9},{2,6},{10,14},... | collective-permute-start | bytes 196616 | tf_op jit(solution)/shard_map/ppermute | solution.py:868
  56.3 4.4 %collective-permute-start.8 = (f32[2,8,256]{2,1,0:T(8,128)S(1)}, f32[2,8,256]{2,1,0:T(8,128)S(1)}, u32[]{:S(2)}, u32[]{:S(2)}) collective-permute-start(f32[2,8,256]{2,1,0:T(8,128)S(1)} %get-tuple-element.59), channel_id=1, source_target_pairs={{0,1},{2,3},{1,0},{3,2},{4,5},{6,7},{5,4},{7,6},{8,9},{10,11},{9,8... | collective-permute-start | bytes 49160 | tf_op jit(solution)/shard_map/ppermute | solution.py:868
  58.3 5.6 %collective-permute-start.9 = (f32[2,8,256]{2,1,0:T(8,128)S(1)}, f32[2,8,256]{2,1,0:T(8,128)S(1)}, u32[]{:S(2)}, u32[]{:S(2)}) collective-permute-start(f32[2,8,256]{2,1,0:T(8,128)S(1)} %get-tuple-element.60), channel_id=1, source_target_pairs={{1,2},{2,1},{5,6},{6,5},{9,10},{10,9},{13,14},{14,13},{17,18},{18,... | collective-permute-start | bytes 49160 | tf_op jit(solution)/shard_map/ppermute | solution.py:868

commit v10 on v9

--- a/solution.py
+++ b/solution.py
@@ -227,6 +227,16 @@
     return scalars.reshape(-1), lanes, rows
 
 
+def begin(copies):
+    for copy in copies:
+        copy.start()
+
+
+def finish(copies):
+    for copy in copies:
+        copy.wait()
+
+
 def odd_position(axis):
     return lax.rem(lax.axis_index(axis), 2) == 1
 
@@ -253,7 +263,8 @@
     return jnp.where(iota(values.shape, 1) == edge, 0.0, moved)
 
 
-DEPTH = 2
+DEPTH = 4
+SHARES = 3
 
 
 def sides(quadrant):
@@ -286,10 +297,20 @@
     blocks_ref = kept_ref.reshape(freqs, ND, rows, LANES)
 
     def fetch(group):
-        part = (slice(None), pl.ds(group * GROUP, GROUP))
-        return pltpu.make_async_copy(spectrum_ref.at[part], blocks_ref.at[part], sems.at[group])
-
-    fetch(0).start()
+        ends = [share * freqs // SHARES for share in range(SHARES + 1)]
+        parts = [
+            (pl.ds(first, last - first), pl.ds(group * GROUP, GROUP))
+            for first, last in zip(ends, ends[1:])
+            if last > first
+        ]
+        return [
+            pltpu.make_async_copy(
+                spectrum_ref.at[part], blocks_ref.at[part], sems.at[group, share]
+            )
+            for share, part in enumerate(parts)
+        ]
+
+    begin(fetch(0))
     edges_ref[...] = jnp.zeros_like(edges_ref)
     for copy in small:
         copy.wait()
@@ -305,7 +326,7 @@
         growth_ref[direction] = open_water * jnp.square(jnp.maximum(project, 0.0))
 
     for group in range(1, DEPTH):
-        fetch(group).start()
+        begin(fetch(group))
     lane = iota(shape, 1)
     even = lane % 2 == 0
     tile_lane = iota((SUB, LANES), 1)
@@ -320,11 +341,11 @@
 
         def gather(index, carry):
             group = index + (0 if to_right else half)
-            fetch(group).wait()
+            finish(fetch(group))
 
             @pl.when(group + DEPTH < GROUPS)
             def _():
-                fetch(group + DEPTH).start()
+                begin(fetch(group + DEPTH))
 
             packed = [jnp.zeros((SUB, LANES), jnp.float32) for _ in range(tiles)]
             for i in range(GROUP):
@@ -421,7 +442,8 @@
         copy.wait()
 
 
-AHEAD = 3
+AHEAD = 6
+PIECES = 4
 
 
 def main_kernel(
@@ -437,9 +459,15 @@
 
     def fetch(j):
         slot = lax.rem(j, AHEAD)
-        return pltpu.make_async_copy(spectrum_ref.at[j], ring_ref.at[slot], sems.at[slot])
-
-    fetch(jnp.int32(start)).start()
+        parts = [pl.ds(piece * (ND // PIECES), ND // PIECES) for piece in range(PIECES)]
+        return [
+            pltpu.make_async_copy(
+                spectrum_ref.at[j, part], ring_ref.at[slot, part], sems.at[slot, piece]
+            )
+            for piece, part in enumerate(parts)
+        ]
+
+    begin(fetch(jnp.int32(start)))
 
     lane = iota((SUB, LANES), 1)
     sub = iota((SUB, LANES), 0)
@@ -462,12 +490,12 @@
         return ((kind, 0, kind), (18 - kind, 1, kind), (18 + kind, 2, kind), (36 - kind, 3, kind))
 
     def frequency(j, carry):
-        fetch(j).wait()
+        finish(fetch(j))
 
         @pl.when(j == start)
         def _():
             for later in range(start + 1, min(start + AHEAD, stop)):
-                fetch(jnp.int32(later)).start()
+                begin(fetch(jnp.int32(later)))
 
         slot = lax.rem(j, AHEAD)
         sums = [[None] * tiles for _ in range(3)]
@@ -545,7 +573,7 @@
 
         @pl.when(j + AHEAD < stop)
         def _():
-            fetch(j + AHEAD).start()
+            begin(fetch(j + AHEAD))
 
         return carry
 
@@ -946,7 +974,7 @@
             pltpu.VMEM((rows, lanes), jnp.float32),
             pltpu.VMEM((rows, lanes), jnp.float32),
             pltpu.SemaphoreType.DMA((6,)),
-            pltpu.SemaphoreType.DMA((GROUPS,)),
+            pltpu.SemaphoreType.DMA((GROUPS, SHARES)),
         ],
         limit=30,
     )(
@@ -969,11 +997,11 @@
             moved=local_comp * cells * 8 * (stop - start) // freqs,
             scratch=[
                 pltpu.VMEM((AHEAD, ND, rows, lanes), jnp.float32),
-                pltpu.SemaphoreType.DMA((AHEAD,)),
+                pltpu.SemaphoreType.DMA((AHEAD, PIECES)),
             ]
             + [pltpu.VMEM((rows + 2 * SUB, lanes), jnp.float32)] * 8,
             aliases={6 + index: index for index in range(4)} if before else {},
-            limit=8,
+            limit=12,
         )(member, scalars, wet, growth, in_hbm(spectrum), *before)
 
     early = max(1, freqs // 3)

time: 76.4 us -> 75.1 us (0.983)
  Pallas kernels: 48.6 us -> 47.4 us
    pallas_call x1, Pallas kernels: 11.9 us -> 10.1 us  [resident(): call(functools.partial(pack_kernel, freqs), [SMEM] + [HBM] * 7, (in_any(N...]
  transfers between devices with their start and end apart: 10 -> 10, of which waited for: 4 -> 4; matrix products, arithmetic and copies ran while one was open for 0% -> 0% of each run, Pallas kernels for 29% -> 31%
where the time goes in v10:
time: 75.1 us; the launch traced here: 74.9 us
  Pallas kernels  47.4 us (63%)
  starting transfers between devices  15.6 us (21%)
  waiting for transfers between devices  11 us (15%)
  between operations  0.87 us (1%)
    pallas_call x2, Pallas kernels, main_part(): call(functools.partial(main_kernel, freqs, start, stop), [SMEM, SMEM, VME...  21.4 us
    ppermute x8, starting transfers between devices, swap(): return lax.ppermute(values, axis, pairs + [(b, a) for a, b in pairs])  12.5 us
    pallas_call x1, Pallas kernels, resident(): call(functools.partial(final_kernel, freqs), [SMEM, SMEM] + [VMEM] * 10,...  12.2 us
    pallas_call x1, Pallas kernels, resident(): call(functools.partial(pack_kernel, freqs), [SMEM] + [HBM] * 7, (in_any(N...  10.1 us
    ppermute x8, waiting for transfers between devices, swap(): return lax.ppermute(values, axis, pairs + [(b, a) for a, b in pairs])  6.85 us
    ppermute x2, waiting for transfers between devices, others_sum(): lax.ppermute(values, axis, [(i, (i + step) % count) for i in range(count)])  4.13 us
    ppermute x2, starting transfers between devices, others_sum(): lax.ppermute(values, axis, [(i, (i + step) % count) for i in range(count)])  3.11 us
  transfers between devices with their start and end apart: 10, of which 4 were waited for; matrix products, arithmetic and copies ran while one was open for 0% of the time, Pallas kernels for 31%

profile of v10, /device:TPU:12, one launch (start us, length us, event | category | flops | bytes accessed | tf_op | source)
XLA Modules:
  0.0 74.9 jit_solution(13956273509426141133)
XLA Ops:
  0.6 0.0 copy-start.5
  0.6 10.1 %shard_map.104 = (f32[36,64,128]{2,1,0:T(8,128)S(1)}, f32[64,128]{1,0:T(8,128)S(1)}, f32[6,64,128]{2,1,0:T(8,128)S(1)}, f32[6,64,128]{2,1,0:T(8,128)S(1)}, f32[6...) custom-call(s32[1]{0:T(128)} %bitcast.member_ref, ...), custom_call_target="tpu_custom_call" | custom-call | flops 21233664 | bytes 21233664 | tf_op jit(solution)/shard_map/pallas_call | solution.py:951
  10.7 0.1 collective-permute-start
  10.8 2.5 %collective-permute-start.1 = (f32[6,64,128]{2,1,0:T(8,128)S(1)}, f32[6,64,128]{2,1,0:T(8,128)S(1)}, u32[]{:S(2)}, u32[]{:S(2)}) collective-permute-start(f32[6,64,128]{2,1,0:T(8,128)S(1)} %get-tuple-element.36), channel_id=1, source_target_pairs={{4,8},{8,4},{5,9},{9,5},{6,10},{10,6},{7,11},{11,7},{20,24},{24,20... | collective-permute-start | bytes 589832 | tf_op jit(solution)/shard_map/ppermute | solution.py:896
  13.3 0.0 copy-done.5
  13.3 7.9 %shard_map.105 = (f32[18,36,64,128]{3,2,1,0:T(8,128)S(1)}, f32[1152,128]{1,0:T(8,128)S(1)}, f32[1152,128]{1,0:T(8,128)S(1)}, f32[64,128]{1,0:T(8,128)S(1)}) custom-call(s32[1]{0:T(128)} %bitcast.member_ref, f32[1800]{0:T(1024)S(1)} %copy-done.5, f32[64,128]{1,0:T(8,128)S(1)} %get-tuple-element.33.wet_ref, f32[36,64,128]{2,1,0:T(8,128)S(1)} %get-tuple-element.34.growth_ref, ...), custom_call_target="tpu_custom_call" | custom-call | flops 28311552 | bytes 14155776 | tf_op jit(solution)/shard_map/pallas_call | solution.py:986
  21.3 0.0 collective-permute-done.swapped_ref.swap_side_ref
  21.3 0.0 collective-permute-done.1.other_ref.other_side_ref
  21.3 0.1 shard_map.106
  21.4 3.5 %collective-permute-start.3 = (f32[656,128]{1,0:T(8,128)S(1)}, f32[656,128]{1,0:T(8,128)S(1)}, u32[]{:S(2)}, u32[]{:S(2)}) collective-permute-start(f32[656,128]{1,0:T(8,128)S(1)} %get-tuple-element.41), channel_id=1, source_target_pairs={{1,2},{2,1},{5,6},{6,5},{9,10},{10,9},{13,14},{14,13},{17,18},{18,... | collective-permute-start | bytes 1007624 | tf_op jit(solution)/shard_map/ppermute | solution.py:896
  24.9 0.1 collective-permute-start.2
  25.0 0.0 copy-start
  25.0 0.0 copy-start.1
  25.0 0.0 copy-start.2
  25.0 0.0 copy-start.3
  25.1 0.0 copy-start.4
  25.1 0.0 copy-start.6
  25.1 13.5 %shard_map.107 = (f32[18,36,64,128]{3,2,1,0:T(8,128)S(1)}, f32[1152,128]{1,0:T(8,128)S(1)}, f32[1152,128]{1,0:T(8,128)S(1)}, f32[64,128]{1,0:T(8,128)S(1)}) custom-call(s32[1]{0:T(128)} %bitcast.member_ref, f32[1800]{0:T(1024)S(1)} %copy-done.5, ...), custom_call_target="tpu_custom_call", output_to_operand_aliasing={{0}: (6, {}), {1}: (7, {}), {2}: (8, {}), {3}: (9, {})} | custom-call | flops 56623104 | bytes 28311552 | tf_op jit(solution)/shard_map/pallas_call | solution.py:986
  38.6 0.0 collective-permute-done.3.other_row_ref
  38.6 0.0 collective-permute-done.2.swap_row_ref
  38.6 0.0 copy-done
  38.6 0.0 copy-done.1
  38.6 1.1 %shard_map.108 = (f32[12,64,128]{2,1,0:T(8,128)S(1)}, f32[5184,128]{1,0:T(8,128)S(1)}, f32[64,128]{1,0:T(8,128)S(1)}) custom-call(s32[1]{0:T(128)} %bitcast.member_ref, f32[2,12,8,128]{3,2,1,0:T(8,128)S(1)} %copy-done.1, f32[2,10,5,18,128]{4,3,2,1,0:T(8,128)S(1)} %copy-done, ...), custom_call_target="tpu_custom_call", output_to_operand_aliasing={{1}: (8, {}), {2}: (9, {})} | custom-call | flops 4915200 | bytes 1638400 | tf_op jit(solution)/shard_map/pallas_call | solution.py:1024
  39.8 1.6 %collective-permute-start.4 = (f32[64,128]{1,0:T(8,128)S(1)}, f32[64,128]{1,0:T(8,128)S(1)}, u32[]{:S(2)}, u32[]{:S(2)}) collective-permute-start(f32[64,128]{1,0:T(8,128)S(1)} %get-tuple-element.53.own_ref), channel_id=1, source_target_pairs={{0,16},{16,0},{1,17},{17,1},{2,18},{18,2},{3,19},{19,3},{4,20},{20... | collective-permute-start | bytes 98312 | tf_op jit(solution)/shard_map/ppermute | solution.py:903
  41.3 0.0 copy-done.2
  41.3 0.0 copy-done.3
  41.3 0.0 copy-done.4
  41.3 1.4 %shard_map.109 = (f32[1152,128]{1,0:T(8,128)S(1)}, f32[1152,128]{1,0:T(8,128)S(1)}) custom-call(s32[1]{0:T(128)} %bitcast.member_ref, f32[2,12,8,128]{3,2,1,0:T(8,128)S(1)} %copy-done.1, f32[2,10,5,18,128]{4,3,2,1,0:T(8,128)S(1)} %copy-done, s32[64,128]{1,0:T(8,128)S(1)} %copy-done.2, ...), custom_call_target="tpu_custom_call", output_to_operand_aliasing={{0}: (9, {}), {1}: (10, {})} | custom-call | flops 4915200 | bytes 1638400 | tf_op jit(solution)/shard_map/pallas_call | solution.py:1041
  42.7 1.0 %collective-permute-done.4.other_ref = f32[64,128]{1,0:T(8,128)S(1)} collective-permute-done((f32[64,128]{1,0:T(8,128)S(1)}, f32[64,128]{1,0:T(8,128)S(1)}, u32[]{:S(2)}, u32[]{:S(2)}) %collective-permute-start.4) | collective-permute-done | bytes 32800 | tf_op jit(solution)/shard_map/ppermute | solution.py:903
  43.7 1.0 %shard_map.110 = (f32[3,64,128]{2,1,0:T(8,128)S(1)}, f32[18,64,128]{2,1,0:T(8,128)S(1)}) custom-call(s32[1]{0:T(128)} %bitcast.member_ref, f32[1800]{0:T(1024)S(1)} %copy-done.5, f32[64,128]{1,0:T(8,128)S(1)} %get-tuple-element.33.wet_ref, f32[1152,128]{1,0:T(8,128)S(1)} %get-tuple-element.51.a_ref, f32[1152,128]{1,0:T(8,128)S(1)} %get-tuple-element.52.b_ref, ...), custom_call_target="tpu_custom_call" | custom-call | flops 1769472 | bytes 1179648 | tf_op jit(solution)/shard_map/pallas_call | solution.py:1054
  44.7 1.6 %collective-permute-start.5 = (f32[3,64,128]{2,1,0:T(8,128)S(1)}, f32[3,64,128]{2,1,0:T(8,128)S(1)}, u32[]{:S(2)}, u32[]{:S(2)}) collective-permute-start(f32[3,64,128]{2,1,0:T(8,128)S(1)} %get-tuple-element.55.own_ref), channel_id=1, source_target_pairs={{0,16},{16,0},{1,17},{17,1},{2,18},{18,2},{3,19},{19,3},{4,20},{20... | collective-permute-start | bytes 294920 | tf_op jit(solution)/shard_map/ppermute | solution.py:903
  46.3 3.1 %collective-permute-done.5.other_ref = f32[3,64,128]{2,1,0:T(8,128)S(1)} collective-permute-done((f32[3,64,128]{2,1,0:T(8,128)S(1)}, f32[3,64,128]{2,1,0:T(8,128)S(1)}, u32[]{:S(2)}, u32[]{:S(2)}) %collective-permute-start.5) | collective-permute-done | bytes 98336 | tf_op jit(solution)/shard_map/ppermute | solution.py:903
  49.4 1.9 %collective-permute-start.7 = (f32[2,64,128]{2,1,0:T(8,128)S(1)}, f32[2,64,128]{2,1,0:T(8,128)S(1)}, u32[]{:S(2)}, u32[]{:S(2)}) collective-permute-start(f32[2,64,128]{2,1,0:T(8,128)S(1)} %get-tuple-element.57.stress_ref), channel_id=1, source_target_pairs={{4,8},{8,4},{5,9},{9,5},{6,10},{10,6},{7,11},{11,7},{20,24},{24,20... | collective-permute-start | bytes 196616 | tf_op jit(solution)/shard_map/ppermute | solution.py:896
  51.4 0.1 collective-permute-start.6
  51.4 3.6 %collective-permute-done.7.other_ref = f32[2,64,128]{2,1,0:T(8,128)S(1)} collective-permute-done((f32[2,64,128]{2,1,0:T(8,128)S(1)}, f32[2,64,128]{2,1,0:T(8,128)S(1)}, u32[]{:S(2)}, u32[]{:S(2)}) %collective-permute-start.7) | collective-permute-done | bytes 65568 | tf_op jit(solution)/shard_map/ppermute | solution.py:896
  55.0 0.0 collective-permute-done.6.swapped_ref
  55.0 2.0 %collective-permute-start.8 = (f32[2,8,256]{2,1,0:T(8,128)S(1)}, f32[2,8,256]{2,1,0:T(8,128)S(1)}, u32[]{:S(2)}, u32[]{:S(2)}) collective-permute-start(f32[2,8,256]{2,1,0:T(8,128)S(1)} %get-tuple-element.59), channel_id=1, source_target_pairs={{0,1},{2,3},{1,0},{3,2},{4,5},{6,7},{5,4},{7,6},{8,9},{10,11},{9,8... | collective-permute-start | bytes 49160 | tf_op jit(solution)/shard_map/ppermute | solution.py:896
  57.1 2.3 %collective-permute-start.9 = (f32[2,8,256]{2,1,0:T(8,128)S(1)}, f32[2,8,256]{2,1,0:T(8,128)S(1)}, u32[]{:S(2)}, u32[]{:S(2)}) collective-permute-start(f32[2,8,256]{2,1,0:T(8,128)S(1)} %get-tuple-element.60), channel_id=1, source_target_pairs={{1,2},{2,1},{5,6},{6,5},{9,10},{10,9},{13,14},{14,13},{17,18},{18,... | collective-permute-start | bytes 49160 | tf_op jit(solution)/shard_map/ppermute | solution.py:896
  59.4 0.0 collective-permute-done.8.swapped_ref
  59.4 3.3 %collective-permute-done.9.other_ref = f32[2,8,256]{2,1,0:T(8,128)S(1)} collective-permute-done((f32[2,8,256]{2,1,0:T(8,128)S(1)}, f32[2,8,256]{2,1,0:T(8,128)S(1)}, u32[]{:S(2)}, u32[]{:S(2)}) %collective-permute-start.9) | collective-permute-done | bytes 16416 | tf_op jit(solution)/shard_map/ppermute | solution.py:896
  62.7 0.0 copy-done.6
  62.7 12.2 %shard_map.113 = (f32[18,36,64,128]{3,2,1,0:T(8,128)}, f32[64,128]{1,0:T(8,128)}) custom-call(s32[1]{0:T(128)} %bitcast.member_ref, f32[1800]{0:T(1024)S(1)} %copy-done.5, f32[64,128]{1,0:T(8,128)S(1)} %copy-done.6, f32[18,64,128]{2,1,0:T(8,128)S(1)} %get-tuple-element.54.ratios_ref, f32[3,64,128]{2,1,0:T(8,128)S(1)} %get-tuple-element.56.sums_ref, ...), custom_call_target="tpu_custom_call" | custom-call | flops 31850496 | bytes 42467328 | tf_op jit(solution)/shard_map/pallas_call | solution.py:1080
  (2 shorter events, 0.0 us)
Async XLA Ops:
  0.6 12.7 %copy-start.5 = (f32[1800]{0:T(1024)S(1)}, f32[1800]{0:T(1024)}, u32[]{:S(2)}) copy-start(f32[1800]{0:T(1024)} %constant.12.clone.scalar_ref) | copy-start | bytes 21604
  10.7 10.5 %collective-permute-start = (f32[6,64,128]{2,1,0:T(8,128)S(1)}, f32[6,64,128]{2,1,0:T(8,128)S(1)}, u32[]{:S(2)}, u32[]{:S(2)}) collective-permute-start(f32[6,64,128]{2,1,0:T(8,128)S(1)} %get-tuple-element.35), channel_id=1, source_target_pairs={{0,4},{8,12},{4,0},{12,8},{1,5},{9,13},{5,1},{13,9},{2,6},{10,14},... | collective-permute-start | bytes 589832 | tf_op jit(solution)/shard_map/ppermute | solution.py:896
  10.8 10.5 %collective-permute-start.1 = (f32[6,64,128]{2,1,0:T(8,128)S(1)}, f32[6,64,128]{2,1,0:T(8,128)S(1)}, u32[]{:S(2)}, u32[]{:S(2)}) collective-permute-start(f32[6,64,128]{2,1,0:T(8,128)S(1)} %get-tuple-element.36), channel_id=1, source_target_pairs={{4,8},{8,4},{5,9},{9,5},{6,10},{10,6},{7,11},{11,7},{20,24},{24,20... | collective-permute-start | bytes 589832 | tf_op jit(solution)/shard_map/ppermute | solution.py:896
  21.4 17.2 %collective-permute-start.3 = (f32[656,128]{1,0:T(8,128)S(1)}, f32[656,128]{1,0:T(8,128)S(1)}, u32[]{:S(2)}, u32[]{:S(2)}) collective-permute-start(f32[656,128]{1,0:T(8,128)S(1)} %get-tuple-element.41), channel_id=1, source_target_pairs={{1,2},{2,1},{5,6},{6,5},{9,10},{10,9},{13,14},{14,13},{17,18},{18,... | collective-permute-start | bytes 1007624 | tf_op jit(solution)/shard_map/ppermute | solution.py:896
  24.9 13.7 %collective-permute-start.2 = (f32[656,128]{1,0:T(8,128)S(1)}, f32[656,128]{1,0:T(8,128)S(1)}, u32[]{:S(2)}, u32[]{:S(2)}) collective-permute-start(f32[656,128]{1,0:T(8,128)S(1)} %get-tuple-element.40.refs_0_), channel_id=1, source_target_pairs={{0,1},{2,3},{1,0},{3,2},{4,5},{6,7},{5,4},{7,6},{8,9},{10,11},{9,8... | collective-permute-start | bytes 1007624 | tf_op jit(solution)/shard_map/ppermute | solution.py:896
  25.0 13.6 %copy-start = (f32[2,10,5,18,128]{4,3,2,1,0:T(8,128)S(1)}, f32[2,10,5,18,128]{4,3,2,1,0:T(8,128)}, u32[]{:S(2)}) copy-start(f32[2,10,5,18,128]{4,3,2,1,0:T(8,128)} %constant.14.clone.table_hbm.table_ref) | copy-start | bytes 2764804
  25.0 13.6 %copy-start.1 = (f32[2,12,8,128]{3,2,1,0:T(8,128)S(1)}, f32[2,12,8,128]{3,2,1,0:T(8,128)}, u32[]{:S(2)}) copy-start(f32[2,12,8,128]{3,2,1,0:T(8,128)} %constant.13.clone.lanes_hbm.lanes_ref) | copy-start | bytes 294916
  25.0 16.3 %copy-start.2 = (s32[64,128]{1,0:T(8,128)S(1)}, s32[64,128]{1,0:T(8,128)}, u32[]{:S(2)}) copy-start(s32[64,128]{1,0:T(8,128)} %ice_ref.1) | copy-start | bytes 98308
  25.0 16.3 %copy-start.3 = (f32[64,128]{1,0:T(8,128)S(1)}, f32[64,128]{1,0:T(8,128)}, u32[]{:S(2)}) copy-start(f32[64,128]{1,0:T(8,128)} %east_ref.1) | copy-start | bytes 98308
  25.1 16.3 %copy-start.4 = (f32[64,128]{1,0:T(8,128)S(1)}, f32[64,128]{1,0:T(8,128)}, u32[]{:S(2)}) copy-start(f32[64,128]{1,0:T(8,128)} %north_ref.1) | copy-start | bytes 98308
  25.1 37.6 %copy-start.6 = (f32[64,128]{1,0:T(8,128)S(1)}, f32[64,128]{1,0:T(8,128)}, u32[]{:S(2)}) copy-start(f32[64,128]{1,0:T(8,128)} %depth_ref.1) | copy-start | bytes 98308
  39.8 4.0 %collective-permute-start.4 = (f32[64,128]{1,0:T(8,128)S(1)}, f32[64,128]{1,0:T(8,128)S(1)}, u32[]{:S(2)}, u32[]{:S(2)}) collective-permute-start(f32[64,128]{1,0:T(8,128)S(1)} %get-tuple-element.53.own_ref), channel_id=1, source_target_pairs={{0,16},{16,0},{1,17},{17,1},{2,18},{18,2},{3,19},{19,3},{4,20},{20... | collective-permute-start | bytes 98312 | tf_op jit(solution)/shard_map/ppermute | solution.py:903
  44.7 4.7 %collective-permute-start.5 = (f32[3,64,128]{2,1,0:T(8,128)S(1)}, f32[3,64,128]{2,1,0:T(8,128)S(1)}, u32[]{:S(2)}, u32[]{:S(2)}) collective-permute-start(f32[3,64,128]{2,1,0:T(8,128)S(1)} %get-tuple-element.55.own_ref), channel_id=1, source_target_pairs={{0,16},{16,0},{1,17},{17,1},{2,18},{18,2},{3,19},{19,3},{4,20},{20... | collective-permute-start | bytes 294920 | tf_op jit(solution)/shard_map/ppermute | solution.py:903
  49.4 5.6 %collective-permute-start.7 = (f32[2,64,128]{2,1,0:T(8,128)S(1)}, f32[2,64,128]{2,1,0:T(8,128)S(1)}, u32[]{:S(2)}, u32[]{:S(2)}) collective-permute-start(f32[2,64,128]{2,1,0:T(8,128)S(1)} %get-tuple-element.57.stress_ref), channel_id=1, source_target_pairs={{4,8},{8,4},{5,9},{9,5},{6,10},{10,6},{7,11},{11,7},{20,24},{24,20... | collective-permute-start | bytes 196616 | tf_op jit(solution)/shard_map/ppermute | solution.py:896
  51.4 3.7 %collective-permute-start.6 = (f32[2,64,128]{2,1,0:T(8,128)S(1)}, f32[2,64,128]{2,1,0:T(8,128)S(1)}, u32[]{:S(2)}, u32[]{:S(2)}) collective-permute-start(f32[2,64,128]{2,1,0:T(8,128)S(1)} %get-tuple-element.57.stress_ref), channel_id=1, source_target_pairs={{0,4},{8,12},{4,0},{12,8},{1,5},{9,13},{5,1},{13,9},{2,6},{10,14},... | collective-permute-start | bytes 196616 | tf_op jit(solution)/shard_map/ppermute | solution.py:896
  55.0 4.4 %collective-permute-start.8 = (f32[2,8,256]{2,1,0:T(8,128)S(1)}, f32[2,8,256]{2,1,0:T(8,128)S(1)}, u32[]{:S(2)}, u32[]{:S(2)}) collective-permute-start(f32[2,8,256]{2,1,0:T(8,128)S(1)} %get-tuple-element.59), channel_id=1, source_target_pairs={{0,1},{2,3},{1,0},{3,2},{4,5},{6,7},{5,4},{7,6},{8,9},{10,11},{9,8... | collective-permute-start | bytes 49160 | tf_op jit(solution)/shard_map/ppermute | solution.py:896
  57.1 5.6 %collective-permute-start.9 = (f32[2,8,256]{2,1,0:T(8,128)S(1)}, f32[2,8,256]{2,1,0:T(8,128)S(1)}, u32[]{:S(2)}, u32[]{:S(2)}) collective-permute-start(f32[2,8,256]{2,1,0:T(8,128)S(1)} %get-tuple-element.60), channel_id=1, source_target_pairs={{1,2},{2,1},{5,6},{6,5},{9,10},{10,9},{13,14},{14,13},{17,18},{18,... | collective-permute-start | bytes 49160 | tf_op jit(solution)/shard_map/ppermute | solution.py:896

commit v11 on v9

--- a/solution.py
+++ b/solution.py
@@ -253,7 +253,7 @@
     return jnp.where(iota(values.shape, 1) == edge, 0.0, moved)
 
 
-DEPTH = 2
+DEPTH = 3
 
 
 def sides(quadrant):
@@ -289,7 +289,8 @@
         part = (slice(None), pl.ds(group * GROUP, GROUP))
         return pltpu.make_async_copy(spectrum_ref.at[part], blocks_ref.at[part], sems.at[group])
 
-    fetch(0).start()
+    for group in range(DEPTH):
+        fetch(group).start()
     edges_ref[...] = jnp.zeros_like(edges_ref)
     for copy in small:
         copy.wait()
@@ -304,8 +305,6 @@
         project = math.cos(angle) * east_ref[...] + math.sin(angle) * north_ref[...]
         growth_ref[direction] = open_water * jnp.square(jnp.maximum(project, 0.0))
 
-    for group in range(1, DEPTH):
-        fetch(group).start()
     lane = iota(shape, 1)
     even = lane % 2 == 0
     tile_lane = iota((SUB, LANES), 1)
@@ -439,7 +438,8 @@
         slot = lax.rem(j, AHEAD)
         return pltpu.make_async_copy(spectrum_ref.at[j], ring_ref.at[slot], sems.at[slot])
 
-    fetch(jnp.int32(start)).start()
+    for j in range(start, min(start + AHEAD, stop)):
+        fetch(jnp.int32(j)).start()
 
     lane = iota((SUB, LANES), 1)
     sub = iota((SUB, LANES), 0)
@@ -463,12 +463,6 @@
 
     def frequency(j, carry):
         fetch(j).wait()
-
-        @pl.when(j == start)
-        def _():
-            for later in range(start + 1, min(start + AHEAD, stop)):
-                fetch(jnp.int32(later)).start()
-
         slot = lax.rem(j, AHEAD)
         sums = [[None] * tiles for _ in range(3)]
 

time: 76.4 us -> 73.7 us (0.965)
  Pallas kernels: 48.6 us -> 46 us
    pallas_call x1, Pallas kernels: 11.9 us -> 9.98 us  [resident(): call(functools.partial(pack_kernel, freqs), [SMEM] + [HBM] * 7, (in_any(N...]
where the time goes in v11:
time: 73.7 us; the launch traced here: 73.5 us
  Pallas kernels  46 us (62%)
  starting transfers between devices  15.6 us (21%)
  waiting for transfers between devices  11 us (15%)
  between operations  0.87 us (1%)
    pallas_call x2, Pallas kernels, main_part(): call(functools.partial(main_kernel, freqs, start, stop), [SMEM, SMEM, VME...  20.2 us
    ppermute x8, starting transfers between devices, swap(): return lax.ppermute(values, axis, pairs + [(b, a) for a, b in pairs])  12.5 us
    pallas_call x1, Pallas kernels, resident(): call(functools.partial(final_kernel, freqs), [SMEM, SMEM] + [VMEM] * 10,...  12.2 us
    pallas_call x1, Pallas kernels, resident(): call(functools.partial(pack_kernel, freqs), [SMEM] + [HBM] * 7, (in_any(N...  9.98 us
    ppermute x8, waiting for transfers between devices, swap(): return lax.ppermute(values, axis, pairs + [(b, a) for a, b in pairs])  6.85 us
    ppermute x2, waiting for transfers between devices, others_sum(): lax.ppermute(values, axis, [(i, (i + step) % count) for i in range(count)])  4.14 us
    ppermute x2, starting transfers between devices, others_sum(): lax.ppermute(values, axis, [(i, (i + step) % count) for i in range(count)])  3.11 us
  transfers between devices with their start and end apart: 10, of which 4 were waited for; matrix products, arithmetic and copies ran while one was open for 0% of the time, Pallas kernels for 29%

profile of v11, /device:TPU:12, one launch (start us, length us, event | category | flops | bytes accessed | tf_op | source)
XLA Modules:
  0.0 73.5 jit_solution(12861091843160465431)
XLA Ops:
  0.6 0.0 copy-start.5
  0.6 10.0 %shard_map.104 = (f32[36,64,128]{2,1,0:T(8,128)S(1)}, f32[64,128]{1,0:T(8,128)S(1)}, f32[6,64,128]{2,1,0:T(8,128)S(1)}, f32[6,64,128]{2,1,0:T(8,128)S(1)}, f32[6...) custom-call(s32[1]{0:T(128)} %bitcast.member_ref, ...), custom_call_target="tpu_custom_call" | custom-call | flops 21233664 | bytes 21233664 | tf_op jit(solution)/shard_map/pallas_call | solution.py:917
  10.6 0.1 collective-permute-start
  10.7 2.5 %collective-permute-start.1 = (f32[6,64,128]{2,1,0:T(8,128)S(1)}, f32[6,64,128]{2,1,0:T(8,128)S(1)}, u32[]{:S(2)}, u32[]{:S(2)}) collective-permute-start(f32[6,64,128]{2,1,0:T(8,128)S(1)} %get-tuple-element.36), channel_id=1, source_target_pairs={{4,8},{8,4},{5,9},{9,5},{6,10},{10,6},{7,11},{11,7},{20,24},{24,20... | collective-permute-start | bytes 589832 | tf_op jit(solution)/shard_map/ppermute | solution.py:862
  13.2 0.0 copy-done.5
  13.2 7.4 %shard_map.105 = (f32[18,36,64,128]{3,2,1,0:T(8,128)S(1)}, f32[1152,128]{1,0:T(8,128)S(1)}, f32[1152,128]{1,0:T(8,128)S(1)}, f32[64,128]{1,0:T(8,128)S(1)}) custom-call(s32[1]{0:T(128)} %bitcast.member_ref, f32[1800]{0:T(1024)S(1)} %copy-done.5, f32[64,128]{1,0:T(8,128)S(1)} %get-tuple-element.33.wet_ref, f32[36,64,128]{2,1,0:T(8,128)S(1)} %get-tuple-element.34.growth_ref, ...), custom_call_target="tpu_custom_call" | custom-call | flops 28311552 | bytes 14155776 | tf_op jit(solution)/shard_map/pallas_call | solution.py:952
  20.6 0.0 collective-permute-done.swapped_ref.swap_side_ref
  20.6 0.0 collective-permute-done.1.other_ref.other_side_ref
  20.6 0.1 shard_map.106
  20.8 3.5 %collective-permute-start.3 = (f32[656,128]{1,0:T(8,128)S(1)}, f32[656,128]{1,0:T(8,128)S(1)}, u32[]{:S(2)}, u32[]{:S(2)}) collective-permute-start(f32[656,128]{1,0:T(8,128)S(1)} %get-tuple-element.41), channel_id=1, source_target_pairs={{1,2},{2,1},{5,6},{6,5},{9,10},{10,9},{13,14},{14,13},{17,18},{18,... | collective-permute-start | bytes 1007624 | tf_op jit(solution)/shard_map/ppermute | solution.py:862
  24.3 0.1 collective-permute-start.2
  24.3 0.0 copy-start
  24.3 0.0 copy-start.1
  24.4 0.0 copy-start.2
  24.4 0.0 copy-start.3
  24.4 0.0 copy-start.4
  24.4 0.0 copy-start.6
  24.4 12.8 %shard_map.107 = (f32[18,36,64,128]{3,2,1,0:T(8,128)S(1)}, f32[1152,128]{1,0:T(8,128)S(1)}, f32[1152,128]{1,0:T(8,128)S(1)}, f32[64,128]{1,0:T(8,128)S(1)}) custom-call(s32[1]{0:T(128)} %bitcast.member_ref, f32[1800]{0:T(1024)S(1)} %copy-done.5, ...), custom_call_target="tpu_custom_call", output_to_operand_aliasing={{0}: (6, {}), {1}: (7, {}), {2}: (8, {}), {3}: (9, {})} | custom-call | flops 56623104 | bytes 28311552 | tf_op jit(solution)/shard_map/pallas_call | solution.py:952
  37.2 0.0 collective-permute-done.3.other_row_ref
  37.2 0.0 collective-permute-done.2.swap_row_ref
  37.2 0.0 copy-done
  37.2 0.0 copy-done.1
  37.3 1.1 %shard_map.108 = (f32[12,64,128]{2,1,0:T(8,128)S(1)}, f32[5184,128]{1,0:T(8,128)S(1)}, f32[64,128]{1,0:T(8,128)S(1)}) custom-call(s32[1]{0:T(128)} %bitcast.member_ref, f32[2,12,8,128]{3,2,1,0:T(8,128)S(1)} %copy-done.1, f32[2,10,5,18,128]{4,3,2,1,0:T(8,128)S(1)} %copy-done, ...), custom_call_target="tpu_custom_call", output_to_operand_aliasing={{1}: (8, {}), {2}: (9, {})} | custom-call | flops 4915200 | bytes 1638400 | tf_op jit(solution)/shard_map/pallas_call | solution.py:990
  38.4 1.6 %collective-permute-start.4 = (f32[64,128]{1,0:T(8,128)S(1)}, f32[64,128]{1,0:T(8,128)S(1)}, u32[]{:S(2)}, u32[]{:S(2)}) collective-permute-start(f32[64,128]{1,0:T(8,128)S(1)} %get-tuple-element.53.own_ref), channel_id=1, source_target_pairs={{0,16},{16,0},{1,17},{17,1},{2,18},{18,2},{3,19},{19,3},{4,20},{20... | collective-permute-start | bytes 98312 | tf_op jit(solution)/shard_map/ppermute | solution.py:869
  39.9 0.0 copy-done.2
  39.9 0.0 copy-done.3
  39.9 0.0 copy-done.4
  39.9 1.4 %shard_map.109 = (f32[1152,128]{1,0:T(8,128)S(1)}, f32[1152,128]{1,0:T(8,128)S(1)}) custom-call(s32[1]{0:T(128)} %bitcast.member_ref, f32[2,12,8,128]{3,2,1,0:T(8,128)S(1)} %copy-done.1, f32[2,10,5,18,128]{4,3,2,1,0:T(8,128)S(1)} %copy-done, s32[64,128]{1,0:T(8,128)S(1)} %copy-done.2, ...), custom_call_target="tpu_custom_call", output_to_operand_aliasing={{0}: (9, {}), {1}: (10, {})} | custom-call | flops 4915200 | bytes 1638400 | tf_op jit(solution)/shard_map/pallas_call | solution.py:1007
  41.4 1.0 %collective-permute-done.4.other_ref = f32[64,128]{1,0:T(8,128)S(1)} collective-permute-done((f32[64,128]{1,0:T(8,128)S(1)}, f32[64,128]{1,0:T(8,128)S(1)}, u32[]{:S(2)}, u32[]{:S(2)}) %collective-permute-start.4) | collective-permute-done | bytes 32800 | tf_op jit(solution)/shard_map/ppermute | solution.py:869
  42.4 1.0 %shard_map.110 = (f32[3,64,128]{2,1,0:T(8,128)S(1)}, f32[18,64,128]{2,1,0:T(8,128)S(1)}) custom-call(s32[1]{0:T(128)} %bitcast.member_ref, f32[1800]{0:T(1024)S(1)} %copy-done.5, f32[64,128]{1,0:T(8,128)S(1)} %get-tuple-element.33.wet_ref, f32[1152,128]{1,0:T(8,128)S(1)} %get-tuple-element.51.a_ref, f32[1152,128]{1,0:T(8,128)S(1)} %get-tuple-element.52.b_ref, ...), custom_call_target="tpu_custom_call" | custom-call | flops 1769472 | bytes 1179648 | tf_op jit(solution)/shard_map/pallas_call | solution.py:1020
  43.3 1.6 %collective-permute-start.5 = (f32[3,64,128]{2,1,0:T(8,128)S(1)}, f32[3,64,128]{2,1,0:T(8,128)S(1)}, u32[]{:S(2)}, u32[]{:S(2)}) collective-permute-start(f32[3,64,128]{2,1,0:T(8,128)S(1)} %get-tuple-element.55.own_ref), channel_id=1, source_target_pairs={{0,16},{16,0},{1,17},{17,1},{2,18},{18,2},{3,19},{19,3},{4,20},{20... | collective-permute-start | bytes 294920 | tf_op jit(solution)/shard_map/ppermute | solution.py:869
  44.9 3.1 %collective-permute-done.5.other_ref = f32[3,64,128]{2,1,0:T(8,128)S(1)} collective-permute-done((f32[3,64,128]{2,1,0:T(8,128)S(1)}, f32[3,64,128]{2,1,0:T(8,128)S(1)}, u32[]{:S(2)}, u32[]{:S(2)}) %collective-permute-start.5) | collective-permute-done | bytes 98336 | tf_op jit(solution)/shard_map/ppermute | solution.py:869
  48.0 1.9 %collective-permute-start.7 = (f32[2,64,128]{2,1,0:T(8,128)S(1)}, f32[2,64,128]{2,1,0:T(8,128)S(1)}, u32[]{:S(2)}, u32[]{:S(2)}) collective-permute-start(f32[2,64,128]{2,1,0:T(8,128)S(1)} %get-tuple-element.57.stress_ref), channel_id=1, source_target_pairs={{4,8},{8,4},{5,9},{9,5},{6,10},{10,6},{7,11},{11,7},{20,24},{24,20... | collective-permute-start | bytes 196616 | tf_op jit(solution)/shard_map/ppermute | solution.py:862
  50.0 0.1 collective-permute-start.6
  50.1 3.6 %collective-permute-done.7.other_ref = f32[2,64,128]{2,1,0:T(8,128)S(1)} collective-permute-done((f32[2,64,128]{2,1,0:T(8,128)S(1)}, f32[2,64,128]{2,1,0:T(8,128)S(1)}, u32[]{:S(2)}, u32[]{:S(2)}) %collective-permute-start.7) | collective-permute-done | bytes 65568 | tf_op jit(solution)/shard_map/ppermute | solution.py:862
  53.6 0.0 collective-permute-done.6.swapped_ref
  53.7 2.0 %collective-permute-start.8 = (f32[2,8,256]{2,1,0:T(8,128)S(1)}, f32[2,8,256]{2,1,0:T(8,128)S(1)}, u32[]{:S(2)}, u32[]{:S(2)}) collective-permute-start(f32[2,8,256]{2,1,0:T(8,128)S(1)} %get-tuple-element.59), channel_id=1, source_target_pairs={{0,1},{2,3},{1,0},{3,2},{4,5},{6,7},{5,4},{7,6},{8,9},{10,11},{9,8... | collective-permute-start | bytes 49160 | tf_op jit(solution)/shard_map/ppermute | solution.py:862
  55.7 2.3 %collective-permute-start.9 = (f32[2,8,256]{2,1,0:T(8,128)S(1)}, f32[2,8,256]{2,1,0:T(8,128)S(1)}, u32[]{:S(2)}, u32[]{:S(2)}) collective-permute-start(f32[2,8,256]{2,1,0:T(8,128)S(1)} %get-tuple-element.60), channel_id=1, source_target_pairs={{1,2},{2,1},{5,6},{6,5},{9,10},{10,9},{13,14},{14,13},{17,18},{18,... | collective-permute-start | bytes 49160 | tf_op jit(solution)/shard_map/ppermute | solution.py:862
  58.1 0.0 collective-permute-done.8.swapped_ref
  58.1 3.3 %collective-permute-done.9.other_ref = f32[2,8,256]{2,1,0:T(8,128)S(1)} collective-permute-done((f32[2,8,256]{2,1,0:T(8,128)S(1)}, f32[2,8,256]{2,1,0:T(8,128)S(1)}, u32[]{:S(2)}, u32[]{:S(2)}) %collective-permute-start.9) | collective-permute-done | bytes 16416 | tf_op jit(solution)/shard_map/ppermute | solution.py:862
  61.3 0.0 copy-done.6
  61.3 12.2 %shard_map.113 = (f32[18,36,64,128]{3,2,1,0:T(8,128)}, f32[64,128]{1,0:T(8,128)}) custom-call(s32[1]{0:T(128)} %bitcast.member_ref, f32[1800]{0:T(1024)S(1)} %copy-done.5, f32[64,128]{1,0:T(8,128)S(1)} %copy-done.6, f32[18,64,128]{2,1,0:T(8,128)S(1)} %get-tuple-element.54.ratios_ref, f32[3,64,128]{2,1,0:T(8,128)S(1)} %get-tuple-element.56.sums_ref, ...), custom_call_target="tpu_custom_call" | custom-call | flops 31850496 | bytes 42467328 | tf_op jit(solution)/shard_map/pallas_call | solution.py:1046
  (2 shorter events, 0.0 us)
Async XLA Ops:
  0.6 12.6 %copy-start.5 = (f32[1800]{0:T(1024)S(1)}, f32[1800]{0:T(1024)}, u32[]{:S(2)}) copy-start(f32[1800]{0:T(1024)} %constant.12.clone.scalar_ref) | copy-start | bytes 21604
  10.6 10.0 %collective-permute-start = (f32[6,64,128]{2,1,0:T(8,128)S(1)}, f32[6,64,128]{2,1,0:T(8,128)S(1)}, u32[]{:S(2)}, u32[]{:S(2)}) collective-permute-start(f32[6,64,128]{2,1,0:T(8,128)S(1)} %get-tuple-element.35), channel_id=1, source_target_pairs={{0,4},{8,12},{4,0},{12,8},{1,5},{9,13},{5,1},{13,9},{2,6},{10,14},... | collective-permute-start | bytes 589832 | tf_op jit(solution)/shard_map/ppermute | solution.py:862
  10.7 9.9 %collective-permute-start.1 = (f32[6,64,128]{2,1,0:T(8,128)S(1)}, f32[6,64,128]{2,1,0:T(8,128)S(1)}, u32[]{:S(2)}, u32[]{:S(2)}) collective-permute-start(f32[6,64,128]{2,1,0:T(8,128)S(1)} %get-tuple-element.36), channel_id=1, source_target_pairs={{4,8},{8,4},{5,9},{9,5},{6,10},{10,6},{7,11},{11,7},{20,24},{24,20... | collective-permute-start | bytes 589832 | tf_op jit(solution)/shard_map/ppermute | solution.py:862
  20.8 16.5 %collective-permute-start.3 = (f32[656,128]{1,0:T(8,128)S(1)}, f32[656,128]{1,0:T(8,128)S(1)}, u32[]{:S(2)}, u32[]{:S(2)}) collective-permute-start(f32[656,128]{1,0:T(8,128)S(1)} %get-tuple-element.41), channel_id=1, source_target_pairs={{1,2},{2,1},{5,6},{6,5},{9,10},{10,9},{13,14},{14,13},{17,18},{18,... | collective-permute-start | bytes 1007624 | tf_op jit(solution)/shard_map/ppermute | solution.py:862
  24.3 13.0 %collective-permute-start.2 = (f32[656,128]{1,0:T(8,128)S(1)}, f32[656,128]{1,0:T(8,128)S(1)}, u32[]{:S(2)}, u32[]{:S(2)}) collective-permute-start(f32[656,128]{1,0:T(8,128)S(1)} %get-tuple-element.40.refs_0_), channel_id=1, source_target_pairs={{0,1},{2,3},{1,0},{3,2},{4,5},{6,7},{5,4},{7,6},{8,9},{10,11},{9,8... | collective-permute-start | bytes 1007624 | tf_op jit(solution)/shard_map/ppermute | solution.py:862
  24.3 12.9 %copy-start = (f32[2,10,5,18,128]{4,3,2,1,0:T(8,128)S(1)}, f32[2,10,5,18,128]{4,3,2,1,0:T(8,128)}, u32[]{:S(2)}) copy-start(f32[2,10,5,18,128]{4,3,2,1,0:T(8,128)} %constant.14.clone.table_hbm.table_ref) | copy-start | bytes 2764804
  24.3 12.9 %copy-start.1 = (f32[2,12,8,128]{3,2,1,0:T(8,128)S(1)}, f32[2,12,8,128]{3,2,1,0:T(8,128)}, u32[]{:S(2)}) copy-start(f32[2,12,8,128]{3,2,1,0:T(8,128)} %constant.13.clone.lanes_hbm.lanes_ref) | copy-start | bytes 294916
  24.4 15.6 %copy-start.2 = (s32[64,128]{1,0:T(8,128)S(1)}, s32[64,128]{1,0:T(8,128)}, u32[]{:S(2)}) copy-start(s32[64,128]{1,0:T(8,128)} %ice_ref.1) | copy-start | bytes 98308
  24.4 15.6 %copy-start.3 = (f32[64,128]{1,0:T(8,128)S(1)}, f32[64,128]{1,0:T(8,128)}, u32[]{:S(2)}) copy-start(f32[64,128]{1,0:T(8,128)} %east_ref.1) | copy-start | bytes 98308
  24.4 15.6 %copy-start.4 = (f32[64,128]{1,0:T(8,128)S(1)}, f32[64,128]{1,0:T(8,128)}, u32[]{:S(2)}) copy-start(f32[64,128]{1,0:T(8,128)} %north_ref.1) | copy-start | bytes 98308
  24.4 36.9 %copy-start.6 = (f32[64,128]{1,0:T(8,128)S(1)}, f32[64,128]{1,0:T(8,128)}, u32[]{:S(2)}) copy-start(f32[64,128]{1,0:T(8,128)} %depth_ref.1) | copy-start | bytes 98308
  38.4 4.0 %collective-permute-start.4 = (f32[64,128]{1,0:T(8,128)S(1)}, f32[64,128]{1,0:T(8,128)S(1)}, u32[]{:S(2)}, u32[]{:S(2)}) collective-permute-start(f32[64,128]{1,0:T(8,128)S(1)} %get-tuple-element.53.own_ref), channel_id=1, source_target_pairs={{0,16},{16,0},{1,17},{17,1},{2,18},{18,2},{3,19},{19,3},{4,20},{20... | collective-permute-start | bytes 98312 | tf_op jit(solution)/shard_map/ppermute | solution.py:869
  43.3 4.7 %collective-permute-start.5 = (f32[3,64,128]{2,1,0:T(8,128)S(1)}, f32[3,64,128]{2,1,0:T(8,128)S(1)}, u32[]{:S(2)}, u32[]{:S(2)}) collective-permute-start(f32[3,64,128]{2,1,0:T(8,128)S(1)} %get-tuple-element.55.own_ref), channel_id=1, source_target_pairs={{0,16},{16,0},{1,17},{17,1},{2,18},{18,2},{3,19},{19,3},{4,20},{20... | collective-permute-start | bytes 294920 | tf_op jit(solution)/shard_map/ppermute | solution.py:869
  48.0 5.6 %collective-permute-start.7 = (f32[2,64,128]{2,1,0:T(8,128)S(1)}, f32[2,64,128]{2,1,0:T(8,128)S(1)}, u32[]{:S(2)}, u32[]{:S(2)}) collective-permute-start(f32[2,64,128]{2,1,0:T(8,128)S(1)} %get-tuple-element.57.stress_ref), channel_id=1, source_target_pairs={{4,8},{8,4},{5,9},{9,5},{6,10},{10,6},{7,11},{11,7},{20,24},{24,20... | collective-permute-start | bytes 196616 | tf_op jit(solution)/shard_map/ppermute | solution.py:862
  50.0 3.7 %collective-permute-start.6 = (f32[2,64,128]{2,1,0:T(8,128)S(1)}, f32[2,64,128]{2,1,0:T(8,128)S(1)}, u32[]{:S(2)}, u32[]{:S(2)}) collective-permute-start(f32[2,64,128]{2,1,0:T(8,128)S(1)} %get-tuple-element.57.stress_ref), channel_id=1, source_target_pairs={{0,4},{8,12},{4,0},{12,8},{1,5},{9,13},{5,1},{13,9},{2,6},{10,14},... | collective-permute-start | bytes 196616 | tf_op jit(solution)/shard_map/ppermute | solution.py:862
  53.7 4.4 %collective-permute-start.8 = (f32[2,8,256]{2,1,0:T(8,128)S(1)}, f32[2,8,256]{2,1,0:T(8,128)S(1)}, u32[]{:S(2)}, u32[]{:S(2)}) collective-permute-start(f32[2,8,256]{2,1,0:T(8,128)S(1)} %get-tuple-element.59), channel_id=1, source_target_pairs={{0,1},{2,3},{1,0},{3,2},{4,5},{6,7},{5,4},{7,6},{8,9},{10,11},{9,8... | collective-permute-start | bytes 49160 | tf_op jit(solution)/shard_map/ppermute | solution.py:862
  55.7 5.6 %collective-permute-start.9 = (f32[2,8,256]{2,1,0:T(8,128)S(1)}, f32[2,8,256]{2,1,0:T(8,128)S(1)}, u32[]{:S(2)}, u32[]{:S(2)}) collective-permute-start(f32[2,8,256]{2,1,0:T(8,128)S(1)} %get-tuple-element.60), channel_id=1, source_target_pairs={{1,2},{2,1},{5,6},{6,5},{9,10},{10,9},{13,14},{14,13},{17,18},{18,... | collective-permute-start | bytes 49160 | tf_op jit(solution)/shard_map/ppermute | solution.py:862
